TPU v7x, 32 devices: a whole 2x2x4 slice. The times are simulated.
32 devices in a mesh: rep: 2 (over y), date: 4 (over x, core), tile: 4 (over z).
Axes of the slice: x: 2, y: 2, z: 4, core: 2. Of those that a mesh axis runs over, the one named last changes fastest.
Arguments:
- tokens: bfloat16 [32, 128, 1280], P(('rep', 'tile'), 'date'), parts along dimension 0, may hold values from -6 to 6
- cotangent: bfloat16 [32, 128, 1280], P(('rep', 'tile'), 'date'), parts along dimension 0, may hold values from -6 to 6
- valid: int32 [32, 128], P(('rep', 'tile')), parts along dimension 0, may hold values from 0 to 1, as said below
- visible: int32 [32], P(('rep', 'tile')), parts along dimension 0, may hold values from 0 to 255
- live: int32 [8], P('rep'), parts along dimension 0, may hold values from 1 to 4, as said below
- pos_table: bfloat16 [256, 1280], replicated, may hold values from -6 to 6
- norm_gain: float32 [1280], replicated, may hold values from 0.5 to 1.5
- norm_bias: float32 [1280], replicated, may hold values from -2 to 2
- w_qkv: bfloat16 [1280, 3840], P('tile'), may hold values from -0.1118034 to 0.1118034
Outputs:
- attended: bfloat16 [32, 128, 1280], P(('rep', 'tile'), 'date'), parts along dimension 0
- grad_tokens: bfloat16 [32, 128, 1280], P(('rep', 'tile'), 'date'), parts along dimension 0
- grad_norm: float32 [4, 1280], P('rep'), parts along dimension 0
There are 2 independent parts, one for each index of `rep`. A program takes and returns all parts, laid end to end along the dimension named above; an argument that names none is the same for every part. Nothing has to cross between parts.
Inputs may be any that keep to these rules, and one draw needn't show every extreme that they name: `valid`: every patch slot has data on at least one date. Whenever a tile owner holds 4 live blocks, the next owner on the tile cycle (index plus one, the last followed by the first) holds at most 2 and the previous owner fewer than 4.
All inputs are finite; a program needn't handle non-finite values.
Results may differ from a plain program's by a relative error of at most 0.04.
Values may be sent and summed in bfloat16 or wider, within the bound.
No kernel may reach another device: no remote copies, remote signals or barrier semaphores. Data moves between devices by JAX's collectives and lax.ppermute only.
A program may use at most 64 MiB of HBM per device.

v0:
```python
import jax
import jax.numpy as jnp
from jax import lax
from jax.sharding import PartitionSpec as P

HEAD_DIM = 80
DG = 32
BLOCK_ROWS = 32


def norm_forward(embedded, norm_gain, norm_bias):
    hidden = embedded.astype(jnp.float32)
    centred = hidden - jnp.mean(hidden, axis=-1, keepdims=True)
    inv_std = lax.rsqrt(jnp.mean(centred * centred, axis=-1, keepdims=True) + 1e-06)
    unit_rows = centred * inv_std
    normed = (unit_rows * norm_gain + norm_bias).astype(jnp.bfloat16)
    return (unit_rows, inv_std, normed)


def norm_backward(grad_normed, unit_rows, inv_std, norm_gain):
    scaled = grad_normed * norm_gain
    grad_hidden = inv_std * (
        scaled
        - jnp.mean(scaled, axis=-1, keepdims=True)
        - unit_rows * jnp.mean(scaled * unit_rows, axis=-1, keepdims=True)
    )
    norm_terms = jnp.stack([jnp.sum(grad_normed * unit_rows, axis=0), jnp.sum(grad_normed, axis=0)])
    return (grad_hidden.astype(jnp.bfloat16), norm_terms)


def project(normed, weights):
    return jnp.dot(normed, weights, preferred_element_type=jnp.float32).astype(jnp.bfloat16)


def back_project(grad_qkv, weights):
    return lax.dot_general(
        grad_qkv, weights, (((1,), (1,)), ((), ())), preferred_element_type=jnp.float32
    )


def attend_both(qkv_rows, upstream, mask_part):
    slot_count, date_count, triple = qkv_rows.shape
    channels = triple // 3
    head_count = triple // (3 * HEAD_DIM)
    inv_scale = 1.0 / HEAD_DIM**0.5
    split_qkv = qkv_rows.reshape(slot_count, date_count, 3, head_count, HEAD_DIM)
    queries = split_qkv[:, :, 0]
    key_rows = split_qkv[:, :, 1]
    values = split_qkv[:, :, 2]
    scores = (
        jnp.einsum("pthe,puhe->phtu", queries, key_rows, preferred_element_type=jnp.float32)
        * inv_scale
    )
    allowed = (mask_part > 0)[:, None, None, :]
    scores = jnp.where(allowed, scores, -1e30)
    top_score = jnp.max(scores, axis=-1, keepdims=True)
    exp_scores = jnp.exp(scores - top_score)
    probs_all = exp_scores / jnp.sum(exp_scores, axis=-1, keepdims=True)
    probs_low = probs_all.astype(jnp.bfloat16)
    context = jnp.einsum("phtu,puhe->pthe", probs_low, values, preferred_element_type=jnp.float32)
    grad_out = upstream.reshape(slot_count, date_count, head_count, HEAD_DIM)
    grad_values = jnp.einsum(
        "phtu,pthe->puhe", probs_low, grad_out, preferred_element_type=jnp.float32
    )
    grad_probs = jnp.einsum("pthe,puhe->phtu", grad_out, values, preferred_element_type=jnp.float32)
    grad_scores = (
        probs_all
        * (grad_probs - jnp.sum(probs_all * grad_probs, axis=-1, keepdims=True))
        * inv_scale
    )
    grad_low = grad_scores.astype(jnp.bfloat16)
    grad_queries = jnp.einsum(
        "phtu,puhe->pthe", grad_low, key_rows, preferred_element_type=jnp.float32
    )
    grad_keys = jnp.einsum("phtu,pthe->puhe", grad_low, queries, preferred_element_type=jnp.float32)
    grad_qkv = jnp.stack([grad_queries, grad_keys, grad_values], axis=2)
    grad_qkv = grad_qkv.reshape(slot_count, date_count, triple).astype(jnp.bfloat16)
    return (context.reshape(slot_count, date_count, channels).astype(jnp.bfloat16), grad_qkv)


def local(tokens, cotangent, valid, visible, live, pos_table, norm_gain, norm_bias, w_qkv):
    slot_count, date_local, model_width = tokens.shape
    group_count = lax.axis_size("date")
    group_index = lax.axis_index("date")
    owner_index = lax.axis_index("tile")
    block_patches = BLOCK_ROWS // DG
    live_here = lax.dynamic_index_in_dim(live, owner_index, 0, keepdims=False)
    slot_live = jnp.arange(slot_count, dtype=jnp.int32) // block_patches < live_here
    live_low = slot_live.astype(jnp.bfloat16)[:, None, None]
    onehot = (visible[:, None] == jnp.arange(pos_table.shape[0], dtype=jnp.int32)[None, :]).astype(
        jnp.bfloat16
    )
    position = jnp.dot(onehot, pos_table, preferred_element_type=jnp.float32)
    embedded = (tokens.astype(jnp.float32) + position[:, None, :]).astype(jnp.bfloat16)
    upstream = cotangent * live_low
    weights = lax.all_gather(w_qkv, "tile", axis=0, tiled=True)
    triple = weights.shape[1]
    part_slots = slot_count // group_count
    mask_part = lax.dynamic_slice_in_dim(valid, group_index * part_slots, part_slots, 0)
    unit_rows, inv_std, normed = norm_forward(
        embedded.reshape(-1, model_width), norm_gain, norm_bias
    )
    qkv_rows = project(normed, weights).reshape(slot_count, date_local, triple)
    sent_qkv, sent_up = (
        lax.all_to_all(qkv_rows, "date", split_axis=0, concat_axis=1, tiled=True),
        lax.all_to_all(upstream, "date", split_axis=0, concat_axis=1, tiled=True),
    )
    context, grad_qkv = attend_both(sent_qkv, sent_up, mask_part)
    context_home, grad_home = (
        lax.all_to_all(context, "date", split_axis=1, concat_axis=0, tiled=True),
        lax.all_to_all(grad_qkv, "date", split_axis=1, concat_axis=0, tiled=True),
    )
    grad_normed = back_project(grad_home.reshape(-1, triple), weights)
    grad_tokens, norm_sums = norm_backward(grad_normed, unit_rows, inv_std, norm_gain)
    grad_tokens = grad_tokens.reshape(slot_count, date_local, model_width) * live_low
    attended = context_home * live_low
    grad_norm = lax.psum(norm_sums, ("date", "tile"))
    return (attended, grad_tokens, grad_norm)


def solution(mesh):
    in_specs = (
        P(("rep", "tile"), "date", None),
        P(("rep", "tile"), "date", None),
        P(("rep", "tile"), None),
        P(("rep", "tile")),
        P("rep"),
        P(),
        P(),
        P(),
        P("tile", None),
    )
    out_specs = (P(("rep", "tile"), "date", None), P(("rep", "tile"), "date", None), P("rep", None))
    return jax.shard_map(local, mesh=mesh, in_specs=in_specs, out_specs=out_specs, check_vma=False)
```

profile of v0, /device:TPU:0, one launch (start us, length us, event | category | flops | bytes accessed | tf_op | source)
XLA Modules:
  0.0 349.5 jit_solution(16507767950990516526)
XLA Ops:
  10.1 4.2 %all-to-all-start.2 = ((bf16[4,32,1280]{2,1,0:T(8,128)(2,1)}), bf16[4,32,1280]{2,1,0:T(8,128)(2,1)S(1)}, u32[]{:S(2)}, u32[]{:S(2)}) async-start(bf16[4,32,1280]{2,1,0:T(8,128)(2,1)} %broadcast_multiply_fusion.1), calls=%async_computation.2 | async-start | bytes 655360 | tf_op jit(solution)/shard_map/all_to_all | solution.py:106
  15.3 170.3 %all-gather.2.cloned.1.call-done = bf16[1280,3840]{1,0:T(8,128)(2,1)} async-done(((bf16[320,3840]{1,0:T(8,128)(2,1)}), bf16[1280,3840]{1,0:T(8,128)(2,1)}) %all-gather.2.cloned.1.call-update) | async-done | bytes 9830416 | tf_op jit(solution)/shard_map/all_gather | solution.py:96
  185.6 6.2 %convolution_convert_fusion = bf16[128,3840]{1,0:T(8,128)(2,1)} fusion(bf16[128,1280]{1,0:T(8,128)(2,1)S(1)} %add_convert_fusion, bf16[1280,3840]{1,0:T(8,128)(2,1)} %all-gather.2.cloned.1.call-done), kind=kOutput, calls=%fused_computation.2 | convolution fusion | flops 1258782720 | bytes 11141120 | tf_op jit(solution)/shard_map/dot_general | solution.py:32
  191.8 3.5 %all-to-all-start = ((bf16[4,32,3840]{2,1,0:T(8,128)(2,1)}), bf16[4,32,3840]{2,1,0:T(8,128)(2,1)S(1)}, u32[]{:S(2)}, u32[]{:S(2)}) async-start(bf16[4,32,3840]{2,1,0:T(8,128)(2,1)} %bitcast.1), calls=%async_computation | async-start | bytes 1966080 | tf_op jit(solution)/shard_map/all_to_all | solution.py:105
  198.5 10.6 %all-to-all-done = bf16[4,32,3840]{2,1,0:T(8,128)(2,1)S(1)} async-done(((bf16[4,32,3840]{2,1,0:T(8,128)(2,1)}), bf16[4,32,3840]{2,1,0:T(8,128)(2,1)S(1)}, u32[]{:S(2)}, u32[]{:S(2)}) %all-to-all-start) | async-done | bytes 983072 | tf_op jit(solution)/shard_map/all_to_all | solution.py:105
  209.1 2.6 reshape.186
  211.7 1.3 fusion.49
  213.0 1.5 copy.58
  214.5 1.6 copy.57
  217.6 2.7 fusion.50
  220.3 2.5 fusion.11
  223.9 2.9 fusion.9
  227.9 2.6 reduce.9
  231.3 3.6 %all-to-all-start.1 = ((bf16[4,2,20480]{2,1,0:T(2,128)(2,1)}), bf16[4,2,20480]{2,1,0:T(2,128)(2,1)S(1)}, u32[]{:S(2)}, u32[]{:S(2)}) async-start(bf16[4,2,20480]{2,1,0:T(2,128)(2,1)} %reshape.194), calls=%async_computation.1 | async-start | bytes 655360 | tf_op jit(solution)/shard_map/all_to_all | solution.py:110
  235.0 2.8 fusion.10
  238.9 3.8 %copy.50 = bf16[1,128,3840]{2,0,1:T(2,128)(2,1)S(1)} copy(bf16[1,128,3840]{1,2,0:T(8,128)(2,1)} %bitcast.86) | data formatting | bytes 1966080 | tf_op jit(solution)/shard_map/convert_element_type | solution.py:77
  242.6 7.6 %reduce.8 = bf16[128,3840]{1,0:T(8,128)(2,1)} reduce(bf16[128,1,3840]{2,1,0:T(2,128)(2,1)S(1)} %bitcast.85, bf16[]{:T(256)} %broadcast.105), dimensions={1}, to_apply=%bitcast.70.reduce_sub_computation | reduce | bytes 1966082
  250.3 3.4 reshape.196
  253.7 4.2 %all-to-all-start.3 = ((bf16[4,2,61440]{2,1,0:T(2,128)(2,1)}), bf16[4,2,61440]{2,1,0:T(2,128)(2,1)}, u32[]{:S(2)}, u32[]{:S(2)}) async-start(bf16[4,2,61440]{2,1,0:T(2,128)(2,1)} %reshape.196), calls=%async_computation.3 | async-start | bytes 1966080 | tf_op jit(solution)/shard_map/all_to_all | solution.py:111
  258.3 13.4 %all-to-all-done.3 = bf16[4,2,61440]{2,1,0:T(2,128)(2,1)} async-done(((bf16[4,2,61440]{2,1,0:T(2,128)(2,1)}), bf16[4,2,61440]{2,1,0:T(2,128)(2,1)}, u32[]{:S(2)}, u32[]{:S(2)}) %all-to-all-start.3) | async-done | bytes 983072 | tf_op jit(solution)/shard_map/all_to_all | solution.py:111
  271.8 2.6 reshape.197
  274.4 7.9 %multiply_reduce_fusion.1 = (f32[1280]{0:T(1024)S(1)}, f32[128]{0:T(128)S(1)}, f32[128]{0:T(128)S(1)}, f32[1280]{0:T(1024)S(1)}, f32[128,1280]{1,0:T(8,128)}) fusion(f32[128]{0:T(128)S(1)} %rsqrt.12, f32[128]{0:T(128)S(1)} %div.28, f32[4,1280]{1,0:T(4,128)S(1)} %copy-done.5, bf16[4,32,1280]{2,1,0:T(8,128)(2,1)S(1)} %copy-done.1, f32[1280]{0:T(1024)S(1)} %copy-done.12, ...), kind=kOutput, calls=%fused_computation.26 | convolution fusion | flops 1260418304 | bytes 11834368 | tf_op jit(solution)/shard_map/dot_general | solution.py:36
  282.3 58.0 %psum.7 = f32[2,1280]{1,0:T(2,128)} all-reduce(f32[2,1280]{1,0:T(2,128)S(1)} %pad_maximum_fusion.1), channel_id=1, replica_groups=mesh['rep'=2,'date'=4,'tile'=4] {'date','tile'}, use_global_device_ids=true, to_apply=%region_9.10 | all-reduce | flops 2560 | bytes 20480 | tf_op jit(solution)/shard_map/psum | solution.py:117
  340.3 1.4 multiply_convert_fusion
  (72 shorter events, 13.8 us)
Async XLA Ops:
  7.2 7.1 %copy-start = (bf16[256,1280]{1,0:T(8,128)(2,1)S(1)}, bf16[256,1280]{1,0:T(8,128)(2,1)}, u32[]{:S(2)}) copy-start(bf16[256,1280]{1,0:T(8,128)(2,1)} %param.14) | copy-start | bytes 1966084
  7.2 2.0 copy-start.9
  7.2 7.1 %copy-start.16 = (s32[4]{0:T(128)S(1)}, s32[4]{0:T(128)}, u32[]{:S(2)}) copy-start(s32[4]{0:T(128)} %param.12) | copy-start | bytes 52
  7.2 7.3 %copy-start.1 = (bf16[4,32,1280]{2,1,0:T(8,128)(2,1)S(1)}, bf16[4,32,1280]{2,1,0:T(8,128)(2,1)}, u32[]{:S(2)}) copy-start(bf16[4,32,1280]{2,1,0:T(8,128)(2,1)} %param.9) | copy-start | bytes 983044
  7.2 7.9 %copy-start.12 = (f32[1280]{0:T(1024)S(1)}, f32[1280]{0:T(1024)}, u32[]{:S(2)}) copy-start(f32[1280]{0:T(1024)} %param.15) | copy-start | bytes 15364
  7.2 7.9 %copy-start.13 = (f32[1280]{0:T(1024)S(1)}, f32[1280]{0:T(1024)}, u32[]{:S(2)}) copy-start(f32[1280]{0:T(1024)} %param.16) | copy-start | bytes 15364
  7.2 178.3 %all-gather.2.cloned.1.call-start = ((), (), s32[]{:S(2)}) async-start(), calls=%async_computation.4 | async-start | bytes 12288000 | tf_op jit(solution)/shard_map/all_gather | solution.py:96
  9.2 182.6 %copy-start.14 = (bf16[4]{0:T(256)(128)(2,1)}, bf16[4]{0:T(256)(128)(2,1)S(1)}, u32[]{:S(2)}) copy-start(bf16[4]{0:T(256)(128)(2,1)S(1)} %compare_convert_fusion) | copy-start | bytes 28
  10.1 181.7 %all-to-all-start.2 = ((bf16[4,32,1280]{2,1,0:T(8,128)(2,1)}), bf16[4,32,1280]{2,1,0:T(8,128)(2,1)S(1)}, u32[]{:S(2)}, u32[]{:S(2)}) async-start(bf16[4,32,1280]{2,1,0:T(8,128)(2,1)} %broadcast_multiply_fusion.1), calls=%async_computation.2 | async-start | bytes 655360 | tf_op jit(solution)/shard_map/all_to_all | solution.py:106
  14.5 177.3 %copy-start.4 = (f32[4,1280]{1,0:T(4,128)}, f32[4,1280]{1,0:T(4,128)S(1)}, u32[]{:S(2)}) copy-start(f32[4,1280]{1,0:T(4,128)S(1)} %fusion.36) | copy-start | bytes 61444
  191.8 17.3 %all-to-all-start = ((bf16[4,32,3840]{2,1,0:T(8,128)(2,1)}), bf16[4,32,3840]{2,1,0:T(8,128)(2,1)S(1)}, u32[]{:S(2)}, u32[]{:S(2)}) async-start(bf16[4,32,3840]{2,1,0:T(8,128)(2,1)} %bitcast.1), calls=%async_computation | async-start | bytes 1966080 | tf_op jit(solution)/shard_map/all_to_all | solution.py:105
  211.7 5.5 %copy-start.2 = (bf16[128,16,80]{0,2,1:T(8,128)(2,1)S(1)}, bf16[128,16,80]{0,2,1:T(8,128)(2,1)}, u32[]{:S(2)}) copy-start(bf16[128,16,80]{0,2,1:T(8,128)(2,1)} %copy.45) | copy-start | bytes 983044
  214.5 5.9 %copy-start.6 = (bf16[1,128,1,16,80]{1,4,3,2,0:T(8,128)(2,1)}, bf16[1,128,1,16,80]{1,4,3,2,0:T(8,128)(2,1)S(1)}, u32[]{:S(2)}) copy-start(bf16[1,128,1,16,80]{1,4,3,2,0:T(8,128)(2,1)S(1)} %copy.58) | copy-start | bytes 983044
  217.6 5.6 %copy-start.3 = (f32[16,128,128]{1,2,0:T(8,128)}, f32[16,128,128]{1,2,0:T(8,128)S(1)}, u32[]{:S(2)}) copy-start(f32[16,128,128]{1,2,0:T(8,128)S(1)} %fusion.27) | copy-start | bytes 3145732
  220.3 2.9 copy-start.19
  220.3 2.5 copy-start.18
  222.9 1.0 copy-start.8
  226.7 8.2 %copy-start.7 = (bf16[1,128,1,16,80]{1,4,3,2,0:T(8,128)(2,1)S(1)}, bf16[1,128,1,16,80]{1,4,3,2,0:T(8,128)(2,1)}, u32[]{:S(2)}) copy-start(bf16[1,128,1,16,80]{1,4,3,2,0:T(8,128)(2,1)} %copy-done.6) | copy-start | bytes 983044
  231.3 22.4 %all-to-all-start.1 = ((bf16[4,2,20480]{2,1,0:T(2,128)(2,1)}), bf16[4,2,20480]{2,1,0:T(2,128)(2,1)S(1)}, u32[]{:S(2)}, u32[]{:S(2)}) async-start(bf16[4,2,20480]{2,1,0:T(2,128)(2,1)} %reshape.194), calls=%async_computation.1 | async-start | bytes 655360 | tf_op jit(solution)/shard_map/all_to_all | solution.py:110
  235.0 2.8 copy-start.10
  235.0 2.8 copy-start.11
  253.7 18.1 %all-to-all-start.3 = ((bf16[4,2,61440]{2,1,0:T(2,128)(2,1)}), bf16[4,2,61440]{2,1,0:T(2,128)(2,1)}, u32[]{:S(2)}, u32[]{:S(2)}) async-start(bf16[4,2,61440]{2,1,0:T(2,128)(2,1)} %reshape.196), calls=%async_computation.3 | async-start | bytes 1966080 | tf_op jit(solution)/shard_map/all_to_all | solution.py:111
  257.9 16.4 %copy-start.5 = (f32[4,1280]{1,0:T(4,128)S(1)}, f32[4,1280]{1,0:T(4,128)}, u32[]{:S(2)}) copy-start(f32[4,1280]{1,0:T(4,128)} %copy-done.4) | copy-start | bytes 61444
  274.4 67.3 %copy-start.15 = (bf16[4]{0:T(256)(128)(2,1)S(1)}, bf16[4]{0:T(256)(128)(2,1)}, u32[]{:S(2)}) copy-start(bf16[4]{0:T(256)(128)(2,1)} %copy-done.14) | copy-start | bytes 28
  (1 other events, 0.8 us)
Sparse Core Ops, SparseCore 0:
  9.6 175.8 all-gather.1
where the time goes:
time: 350 us; the launch traced here: 349 us
  waiting for transfers between devices  195 us (56%)
  blocking collectives  58 us (17%)
  matrix products  26 us (7%)
  local copies, waits for them, and re-layouts  23.7 us (7%)
  other arithmetic  16.9 us (5%)
  starting transfers between devices  15.6 us (4%)
  between operations  14.4 us (4%)
    all_gather x1, waiting for transfers between devices, local(): weights = lax.all_gather(w_qkv, 'tile', axis=0, tiled=True)  170 us
    psum x1, blocking collectives, local(): grad_norm = lax.psum(norm_sums, ('date', 'tile'))  58 us
    all_to_all x1, waiting for transfers between devices, local(): lax.all_to_all(grad_qkv, 'date', split_axis=1, concat_axis=0, tiled=True)  13.4 us
    unnamed x49, local copies, waits for them, and re-layouts  12.7 us
    all_to_all x1, waiting for transfers between devices, local(): lax.all_to_all(qkv_rows, 'date', split_axis=0, concat_axis=1, tiled=True)  10.6 us
    unnamed x2, other arithmetic  10.2 us
    dot_general x1, matrix products, back_project(): lax.dot_general(grad_qkv, weights, (((1,), (1,)), ((), ())), preferred_el...  7.92 us
  transfers between devices with their start and end apart: 5, of which 3 were waited for; matrix products, arithmetic and copies ran while one was open for 9% of the time, Pallas kernels for 0%

commit v1 on v0

v1 whole, which is shorter than its diff:
```python
import functools

import jax
import jax.numpy as jnp
from jax import lax
from jax.experimental import pallas as pl
from jax.experimental.pallas import tpu as pltpu
from jax.sharding import PartitionSpec as P

HEAD_DIM = 80
HEADS = 16
DG = 32
BLOCK_ROWS = 32
F32 = jnp.float32
BF16 = jnp.bfloat16
VMEM_LIMIT = 48 * 1024 * 1024

VMEM = pl.BlockSpec(memory_space=pltpu.VMEM)
SMEM = pl.BlockSpec(memory_space=pltpu.SMEM)
ANY = pl.BlockSpec(memory_space=pl.ANY)


def dot(a, b):
    return jnp.dot(a, b, preferred_element_type=F32)


def dot_nt(a, b):
    return lax.dot_general(a, b, (((1,), (1,)), ((), ())), preferred_element_type=F32)


def dot_tn(a, b):
    return lax.dot_general(a, b, (((0,), (0,)), ((), ())), preferred_element_type=F32)


def norm_kernel(groups, where_ref, visible_ref, pos_ref, gain_ref, bias_ref, *refs):
    token_refs = refs[:groups]
    normed_ref, unit_ref, own_unit_ref, own_inv_ref = refs[groups:]
    slots, rows, width = token_refs[0].shape
    gain = gain_ref[...]
    bias = bias_ref[...]
    positions = []
    for p in range(slots):
        iota = lax.broadcasted_iota(jnp.int32, (8, pos_ref.shape[0]), 1)
        onehot = (iota == visible_ref[p]).astype(F32).astype(BF16)
        positions.append(dot(onehot, pos_ref[...])[0:1])
    for s in range(groups):
        for p in range(slots):
            embedded = (token_refs[s][p].astype(F32) + positions[p]).astype(BF16).astype(F32)
            centred = embedded - jnp.mean(embedded, axis=-1, keepdims=True)
            inv_std = lax.rsqrt(jnp.mean(centred * centred, axis=-1, keepdims=True) + 1e-06)
            unit = centred * inv_std
            normed_ref[p, where_ref[s]] = (unit * gain + bias).astype(BF16)
            unit_ref[p, where_ref[s]] = unit.astype(BF16)
            if s == 0:
                own_unit_ref[p] = unit
                own_inv_ref[p] = jnp.broadcast_to(inv_std, own_inv_ref.shape[1:])


def attend_kernel(chunks, copies, where_ref, live_ref, normed_ref, unit_ref, up_ref, valid_ref, *refs):
    chunk_refs = refs[:chunks]
    context_ref, grad_ref, sums_ref, weights, qkv_ref, gqkv_ref, sems = refs[chunks:]
    groups, slots, rows, channels = up_ref.shape
    dates = groups * rows
    heads = channels // HEAD_DIM
    inv_scale = 1.0 / HEAD_DIM**0.5
    moves = []
    for c, ref in enumerate(chunk_refs):
        at = pl.multiple_of(where_ref[c], 16)
        moves.append(
            pltpu.make_async_copy(ref, weights.at[pl.ds(at, ref.shape[0]), :], sems.at[c])
        )
    for move in moves:
        move.start()
    for move in moves:
        move.wait()
    qkv_ref[...] = dot(normed_ref[...], weights[...]).astype(BF16)
    for p in range(slots):
        span = slice(p * dates, (p + 1) * dates)
        alive = (live_ref[0] > p // (BLOCK_ROWS // DG)).astype(F32)
        rows_qkv = qkv_ref[span, :]
        upstream = jnp.concatenate([up_ref[g, p] for g in range(groups)], axis=0)
        upstream = upstream * alive.astype(BF16)
        allowed = valid_ref[:, p : p + 1] > 0
        grads = [[], [], []]
        contexts = []
        for h in range(heads):
            q, k, v = (
                rows_qkv[:, i * channels + h * HEAD_DIM : i * channels + (h + 1) * HEAD_DIM]
                for i in range(3)
            )
            up = upstream[:, h * HEAD_DIM : (h + 1) * HEAD_DIM]
            scores = jnp.where(allowed, dot_nt(k, q) * inv_scale, -1e30)
            exps = jnp.exp(scores - jnp.max(scores, axis=0, keepdims=True))
            probs = exps / jnp.sum(exps, axis=0, keepdims=True)
            low = probs.astype(BF16)
            contexts.append(dot_tn(low, v) * alive)
            grads[2].append(dot(low, up))
            gprobs = dot_nt(v, up)
            gscores = probs * (gprobs - jnp.sum(probs * gprobs, axis=0, keepdims=True)) * inv_scale
            glow = gscores.astype(BF16)
            grads[0].append(dot_tn(glow, k))
            grads[1].append(dot(glow, q))
        gqkv_ref[span, :] = jnp.concatenate(grads[0] + grads[1] + grads[2], axis=1).astype(BF16)
        context = jnp.concatenate(contexts, axis=1).astype(BF16)
        for g in range(groups):
            context_ref[g, p] = context[g * rows : (g + 1) * rows]
    gain_sum = None
    for p in range(slots):
        span = slice(p * dates, (p + 1) * dates)
        partial = dot_nt(gqkv_ref[span, :], weights[...])
        for g in range(groups):
            grad_ref[g, p] = partial[g * rows : (g + 1) * rows].astype(BF16)
        gain_part = jnp.sum(partial * unit_ref[span, :].astype(F32), axis=0, keepdims=True)
        bias_part = jnp.sum(partial, axis=0, keepdims=True)
        gain_sum = gain_part if gain_sum is None else gain_sum + gain_part
        bias_sum = bias_part if p == 0 else bias_sum + bias_part
    both = jnp.concatenate([gain_sum, bias_sum], axis=0)
    for c in range(copies):
        sums_ref[c] = both


def finish_kernel(live_ref, grad_ref, unit_ref, inv_ref, gain_ref, context_ref, sums_ref, attended_ref, out_ref, norm_ref):
    groups, slots, rows, width = grad_ref.shape
    gain = gain_ref[...]
    for p in range(slots):
        alive = (live_ref[0] > p // (BLOCK_ROWS // DG)).astype(F32)
        grad = grad_ref[0, p].astype(F32)
        for g in range(1, groups):
            grad = grad + grad_ref[g, p].astype(F32)
        unit = unit_ref[p]
        scaled = grad * gain
        out = inv_ref[p][:, 0:1] * (
            scaled
            - jnp.mean(scaled, axis=-1, keepdims=True)
            - unit * jnp.mean(scaled * unit, axis=-1, keepdims=True)
        )
        out_ref[p] = (out * alive).astype(BF16)
        attended_ref[p] = jnp.concatenate([context_ref[g, p] for g in range(groups)], axis=1)
    norm_ref[...] = jnp.sum(sums_ref[...], axis=0)


def local(tokens, cotangent, valid, visible, live, pos_table, norm_gain, norm_bias, w_qkv):
    slots, rows, width = tokens.shape
    groups = lax.axis_size("date")
    owners = lax.axis_size("tile")
    reps = lax.axis_size("rep")
    group = lax.axis_index("date")
    owner = lax.axis_index("tile")
    rep = lax.axis_index("rep")
    depth, triple = w_qkv.shape
    channels = triple // 3
    part = channels // groups
    dates = rows * groups
    live_here = lax.dynamic_slice_in_dim(live, owner, 1, 0)

    mine = lax.dynamic_slice_in_dim(w_qkv.reshape(depth, 3, channels), group * part, part, 2)
    mine = mine.reshape(depth, 3 * part)
    if owners == 4 and reps == 2 and depth % 32 == 0:
        half_rows = depth // 2
        half = lax.dynamic_slice_in_dim(mine, rep * half_rows, half_rows, 0)
        chunks, places = [mine], [owner * depth]
        for shift in (2, 1, 3):
            got = lax.ppermute(half, "tile", [(i, (i + shift) % owners) for i in range(owners)])
            other = lax.ppermute(got, "rep", [(0, 1), (1, 0)])
            source = (owner - shift) % owners
            chunks += [got, other]
            places += [source * depth + rep * half_rows, source * depth + (1 - rep) * half_rows]
    else:
        chunks, places = [lax.all_gather(mine, "tile", axis=0, tiled=True)], [0]
    places = jnp.stack([jnp.asarray(p, jnp.int32) for p in places])

    gathered = [tokens] + [
        lax.ppermute(tokens, "date", [(i, (i + s) % groups) for i in range(groups)])
        for s in range(1, groups)
    ]
    where = jnp.stack([(group - s) % groups for s in range(groups)]).astype(jnp.int32)
    columns = cotangent.reshape(slots, rows, groups, part).transpose(2, 0, 1, 3)
    upstream = lax.all_to_all(columns, "date", split_axis=0, concat_axis=0, tiled=True)

    params = pltpu.CompilerParams(vmem_limit_bytes=VMEM_LIMIT)
    gain2, bias2 = norm_gain.reshape(1, width), norm_bias.reshape(1, width)
    normed, unit, own_unit, own_inv = pl.pallas_call(
        functools.partial(norm_kernel, groups),
        out_shape=(
            jax.ShapeDtypeStruct((slots, groups, rows, width), BF16),
            jax.ShapeDtypeStruct((slots, groups, rows, width), BF16),
            jax.ShapeDtypeStruct((slots, rows, width), F32),
            jax.ShapeDtypeStruct((slots, rows, 128), F32),
        ),
        in_specs=[SMEM, SMEM] + [VMEM] * (3 + groups),
        out_specs=(VMEM,) * 4,
        compiler_params=params,
        cost_estimate=pl.CostEstimate(flops=10**7, bytes_accessed=6 * 10**6, transcendentals=1000),
        name="norm",
    )(where, visible, pos_table, gain2, bias2, *gathered)

    copies = groups * owners if owners == 4 else 1
    context, grad, sums = pl.pallas_call(
        functools.partial(attend_kernel, len(chunks), copies),
        out_shape=(
            jax.ShapeDtypeStruct((groups, slots, rows, part), BF16),
            jax.ShapeDtypeStruct((groups, slots, rows, width), BF16),
            jax.ShapeDtypeStruct((copies, 2, width), F32),
        ),
        in_specs=[SMEM, SMEM] + [VMEM] * 4 + [ANY] * len(chunks),
        out_specs=(VMEM,) * 3,
        scratch_shapes=[
            pltpu.VMEM((width, 3 * part), BF16),
            pltpu.VMEM((slots * dates, 3 * part), BF16),
            pltpu.VMEM((slots * dates, 3 * part), BF16),
            pltpu.SemaphoreType.DMA((len(chunks),)),
        ],
        compiler_params=params,
        cost_estimate=pl.CostEstimate(flops=3 * 10**9, bytes_accessed=10**7, transcendentals=10**6),
        name="attend",
    )(
        places,
        live_here,
        normed.reshape(slots * dates, width),
        unit.reshape(slots * dates, width),
        upstream,
        valid.T,
        *chunks,
    )

    context_home = lax.all_to_all(context, "date", split_axis=0, concat_axis=0, tiled=True)
    grad_home = lax.all_to_all(grad, "date", split_axis=0, concat_axis=0, tiled=True)
    if copies > 1:
        sums = lax.all_to_all(sums, ("date", "tile"), split_axis=0, concat_axis=0, tiled=True)
    else:
        sums = lax.psum(sums, ("date", "tile"))

    return pl.pallas_call(
        finish_kernel,
        out_shape=(
            jax.ShapeDtypeStruct((slots, rows, channels), BF16),
            jax.ShapeDtypeStruct((slots, rows, width), BF16),
            jax.ShapeDtypeStruct((2, width), F32),
        ),
        in_specs=[SMEM] + [VMEM] * 6,
        out_specs=(VMEM,) * 3,
        compiler_params=params,
        cost_estimate=pl.CostEstimate(flops=10**7, bytes_accessed=4 * 10**6, transcendentals=0),
        name="finish",
    )(live_here, grad_home, own_unit, own_inv, gain2, context_home, sums)


def solution(mesh):
    in_specs = (
        P(("rep", "tile"), "date", None),
        P(("rep", "tile"), "date", None),
        P(("rep", "tile"), None),
        P(("rep", "tile")),
        P("rep"),
        P(),
        P(),
        P(),
        P("tile", None),
    )
    out_specs = (P(("rep", "tile"), "date", None), P(("rep", "tile"), "date", None), P("rep", None))
    return jax.shard_map(local, mesh=mesh, in_specs=in_specs, out_specs=out_specs, check_vma=False)
```

time: 350 us -> 111 us (0.32)
  waiting for transfers between devices: 195 us -> 26.1 us
  matrix products: 26 us -> 0 us
  other arithmetic: 16.9 us -> 0.08 us
  blocking collectives: 58 us -> 42.6 us
  Pallas kernels: 0 us -> 14.5 us
  between operations: 14.4 us -> 0.97 us
  local copies, waits for them, and re-layouts: 23.7 us -> 12.1 us
    all_gather x1 -> x0, waiting for transfers between devices: 170 us -> none  [local(): weights = lax.all_gather(w_qkv, 'tile', axis=0, tiled=True)]
    psum x1 -> x0, blocking collectives: 58 us -> none  [local(): grad_norm = lax.psum(norm_sums, ('date', 'tile'))]
    all_to_all x0 -> x3, blocking collectives: none -> 42.6 us  [the longest x1 19.7 us: local(): lax.all_to_all(grad, 'date', split_axis=0, concat_axis=0, tiled=True)]
    ppermute x0 -> x9, waiting for transfers between devices: none -> 25.8 us  [the longest x3 24 us: local(): lax.ppermute(half, 'tile', [(i, (i + shift) % owners) for i in range(owne...]
    all_to_all x4 -> x1, waiting for transfers between devices: 24 us -> 0.36 us  [local(): lax.all_to_all(columns, 'date', split_axis=0, concat_axis=0, tiled=True)]
    dot_general x8 -> x0, matrix products: 23.2 us -> none  [the longest x1 7.92 us: back_project(): lax.dot_general(grad_qkv, weights, (((1,), (1,)), ((), ())), preferred_el...]
    pallas_call x0 -> x3, Pallas kernels: none -> 14.5 us  [the longest x1 10.5 us: local(): pl.pallas_call(functools.partial(attend_kernel, len(chunks), copies), out...]
    all_to_all x4 -> x1, starting transfers between devices: 15.6 us -> 3.46 us  [local(): lax.all_to_all(columns, 'date', split_axis=0, concat_axis=0, tiled=True)]
  transfers between devices with their start and end apart: 5 -> 10, of which waited for: 3 -> 5; matrix products, arithmetic and copies ran while one was open for 9% -> 2% of each run, Pallas kernels for 0% -> 2%
where the time goes in v1:
time: 111 us
  blocking collectives  42.6 us (38%)
  waiting for transfers between devices  26.1 us (24%)
  starting transfers between devices  14.6 us (13%)
  Pallas kernels  14.5 us (13%)
  local copies, waits for them, and re-layouts  12.1 us (11%)
    ppermute x3, waiting for transfers between devices, local(): lax.ppermute(half, 'tile', [(i, (i + shift) % owners) for i in range(owne...  24 us
    all_to_all x1, blocking collectives, local(): lax.all_to_all(grad, 'date', split_axis=0, concat_axis=0, tiled=True)  19.7 us
    all_to_all x1, blocking collectives, local(): lax.all_to_all(sums, ('date', 'tile'), split_axis=0, concat_axis=0, tiled...  12.9 us
    pallas_call x1, Pallas kernels, local(): pl.pallas_call(functools.partial(attend_kernel, len(chunks), copies), out...  10.5 us
    all_to_all x1, blocking collectives, local(): lax.all_to_all(context, 'date', split_axis=0, concat_axis=0, tiled=True)  9.99 us
    unnamed x26, local copies, waits for them, and re-layouts  7.61 us
    ppermute x3, starting transfers between devices, local(): lax.ppermute(half, 'tile', [(i, (i + shift) % owners) for i in range(owne...  6.11 us
    ppermute x3, starting transfers between devices, local(): other = lax.ppermute(got, 'rep', [(0, 1), (1, 0)])  3.55 us
  transfers between devices with their start and end apart: 10, of which 5 were waited for; matrix products, arithmetic and copies ran while one was open for 2% of the time, Pallas kernels for 2%

profile of v1, /device:TPU:0, one launch (start us, length us, event | category | flops | bytes accessed | tf_op | source)
XLA Modules:
  0.0 111.0 jit_solution(14800876785262634115)
XLA Ops:
  0.6 3.6 %copy.15 = bf16[320,3840]{0,1:T(8,128)(2,1)S(1)} copy(bf16[320,3840]{1,0:T(8,128)(2,1)} %param.17) | data formatting | bytes 4915200 | tf_op args[8]
  4.3 0.9 constant_dynamic-slice_fusion.1
  5.2 1.4 %copy.17.refs_0_ = bf16[320,960]{1,0:T(8,128)(2,1)S(1)} copy(bf16[320,960]{0,1:T(8,128)(2,1)} %bitcast.23) | data formatting | bytes 1228800 | tf_op jit(solution)/shard_map/reshape | solution.py:157
  6.8 5.1 %collective-permute-start.7 = (bf16[160,960]{1,0:T(8,128)(2,1)S(1)}, bf16[160,960]{1,0:T(8,128)(2,1)}, u32[]{:S(2)}, u32[]{:S(2)}) collective-permute-start(bf16[160,960]{1,0:T(8,128)(2,1)S(1)} %constant_dynamic-slice_fusion), channel_id=1, source_target_pairs={{0,3},{1,0},{2,1},{3,2},{4,7},{5,4},{6,5},{7,6},{8,11},{9,8},{10,9... | collective-permute-start | bytes 921608 | tf_op jit(solution)/shard_map/ppermute | solution.py:163
  11.9 1.5 %collective-permute-start.1 = (bf16[4,32,1280]{2,1,0:T(8,128)(2,1)S(1)}, bf16[4,32,1280]{2,1,0:T(8,128)(2,1)S(1)}, u32[]{:S(2)}, u32[]{:S(2)}) collective-permute-start(bf16[4,32,1280]{2,1,0:T(8,128)(2,1)S(1)} %copy-done.1), channel_id=1, source_target_pairs={{0,8},{4,12},{8,0},{12,4},{1,9},{5,13},{9,1},{13,5},{2,10},{6,14},... | collective-permute-start | bytes 983048 | tf_op jit(solution)/shard_map/ppermute | solution.py:173
  13.4 1.0 collective-permute-start.3
  14.4 5.6 %collective-permute-done.7.refs_5_ = bf16[160,960]{1,0:T(8,128)(2,1)} collective-permute-done((bf16[160,960]{1,0:T(8,128)(2,1)S(1)}, bf16[160,960]{1,0:T(8,128)(2,1)}, u32[]{:S(2)}, u32[]{:S(2)}) %collective-permute-start.7) | collective-permute-done | bytes 307232 | tf_op jit(solution)/shard_map/ppermute | solution.py:163
  20.0 8.1 %collective-permute-done.5.refs_3_ = bf16[160,960]{1,0:T(8,128)(2,1)} collective-permute-done((bf16[160,960]{1,0:T(8,128)(2,1)S(1)}, bf16[160,960]{1,0:T(8,128)(2,1)}, u32[]{:S(2)}, u32[]{:S(2)}) %collective-permute-start.5) | collective-permute-done | bytes 307232 | tf_op jit(solution)/shard_map/ppermute | solution.py:163
  28.1 1.5 %collective-permute-start.8 = (bf16[160,960]{1,0:T(8,128)(2,1)}, bf16[160,960]{1,0:T(8,128)(2,1)}, u32[]{:S(2)}, u32[]{:S(2)}) collective-permute-start(bf16[160,960]{1,0:T(8,128)(2,1)} %collective-permute-done.7.refs_5_), channel_id=1, source_target_pairs={{0,16},{16,0},{1,17},{17,1},{2,18},{18,2},{3,19},{19,3},{4,20},{20... | collective-permute-start | bytes 921608 | tf_op jit(solution)/shard_map/ppermute | solution.py:164
  29.7 10.3 %collective-permute-done.3.refs_1_ = bf16[160,960]{1,0:T(8,128)(2,1)} collective-permute-done((bf16[160,960]{1,0:T(8,128)(2,1)S(1)}, bf16[160,960]{1,0:T(8,128)(2,1)}, u32[]{:S(2)}, u32[]{:S(2)}) %collective-permute-start.3) | collective-permute-done | bytes 307232 | tf_op jit(solution)/shard_map/ppermute | solution.py:163
  39.9 1.5 %collective-permute-start.6 = (bf16[160,960]{1,0:T(8,128)(2,1)}, bf16[160,960]{1,0:T(8,128)(2,1)}, u32[]{:S(2)}, u32[]{:S(2)}) collective-permute-start(bf16[160,960]{1,0:T(8,128)(2,1)} %collective-permute-done.5.refs_3_), channel_id=1, source_target_pairs={{0,16},{16,0},{1,17},{17,1},{2,18},{18,2},{3,19},{19,3},{4,20},{20... | collective-permute-start | bytes 921608 | tf_op jit(solution)/shard_map/ppermute | solution.py:164
  42.4 0.8 copy.19
  43.2 3.5 %all-to-all-start = ((bf16[4,4,32,320]{3,2,1,0:T(8,128)(2,1)}), bf16[4,4,32,320]{3,2,1,0:T(8,128)(2,1)S(1)}, u32[]{:S(2)}, u32[]{:S(2)}) async-start(bf16[4,4,32,320]{3,2,1,0:T(8,128)(2,1)} %bitcast.24), calls=%async_computation | async-start | bytes 786432 | tf_op jit(solution)/shard_map/all_to_all | solution.py:178
  47.9 0.7 copy-done.2
  48.6 1.0 copy-done.3
  49.6 2.0 %norm.1 = (bf16[4,4,32,1280]{3,2,1,0:T(8,128)(2,1)S(1)}, bf16[4,4,32,1280]{3,2,1,0:T(8,128)(2,1)S(1)}, f32[4,32,1280]{2,1,0:T(8,128)S(1)}, f32[4,32,128]{2,1,0:T(8,128)S(1)}) custom-call(s32[4]{0:T(128)S(1)} %pad_add_fusion.where_ref, s32[4]{0:T(128)S(1)} %copy-done.4, bf16[256,1280]{1,0:T(8,128)(2,1)S(1)} %copy-done, f32[1,1280]{1,0:T(1,128)S(1)} %reshape.27.gain_ref, ...), custom_call_target="tpu_custom_call" | custom-call | flops 10000000 | bytes 6000000 | tf_op jit(solution)/shard_map/norm/pallas_call | solution.py:182
  51.6 1.1 copy-done.5
  52.7 1.1 copy-done.6
  54.1 1.7 %collective-permute-done.4.refs_2_ = bf16[160,960]{1,0:T(8,128)(2,1)} collective-permute-done((bf16[160,960]{1,0:T(8,128)(2,1)}, bf16[160,960]{1,0:T(8,128)(2,1)}, u32[]{:S(2)}, u32[]{:S(2)}) %collective-permute-start.4) | collective-permute-done | bytes 307232 | tf_op jit(solution)/shard_map/ppermute | solution.py:164
  55.8 10.5 %attend.1 = (bf16[4,4,32,320]{3,2,1,0:T(8,128)(2,1)S(1)}, bf16[4,4,32,1280]{3,2,1,0:T(8,128)(2,1)S(1)}, f32[16,2,1280]{2,1,0:T(2,128)S(1)}) custom-call(s32[7]{0:T(128)S(1)} %stack.46.where_ref, s32[1]{0:T(128)} %dynamic_slice.9.live_ref, bf16[512,1280]{1,0:T(8,128)(2,1)} %bitcast.20, bf16[512,1280]{1,0:T(8,128)(2,1)} %bitcast.21, ...), custom_call_target="tpu_custom_call" | custom-call | flops 3000000000 | bytes 10000000 | tf_op jit(solution)/shard_map/attend/pallas_call | solution.py:198
  66.4 10.0 %all_to_all.20.context_ref = bf16[4,4,32,320]{3,2,1,0:T(8,128)(2,1)S(1)} all-to-all(bf16[4,4,32,320]{3,2,1,0:T(8,128)(2,1)S(1)} %get-tuple-element.15), channel_id=1, replica_groups=mesh['rep'=2,'date'=4,'tile'=4] {'date'}, dimensions={0} | all-to-all | bytes 655360 | tf_op jit(solution)/shard_map/all_to_all | solution.py:226
  76.4 12.9 %all_to_all.21.sums_ref = f32[16,2,1280]{2,1,0:T(2,128)S(1)} all-to-all(f32[16,2,1280]{2,1,0:T(2,128)S(1)} %get-tuple-element.16), channel_id=1, replica_groups=mesh['rep'=2,'date'=4,'tile'=4] {'date','tile'}, dimensions={0} | all-to-all | bytes 327680 | tf_op jit(solution)/shard_map/all_to_all | solution.py:229
  89.3 19.7 %all_to_all.22.grad_ref = bf16[4,4,32,1280]{3,2,1,0:T(8,128)(2,1)S(1)} all-to-all(bf16[4,4,32,1280]{3,2,1,0:T(8,128)(2,1)S(1)} %get-tuple-element.12), channel_id=1, replica_groups=mesh['rep'=2,'date'=4,'tile'=4] {'date'}, dimensions={0} | all-to-all | bytes 2621440 | tf_op jit(solution)/shard_map/all_to_all | solution.py:227
  109.0 2.0 %finish.1 = (bf16[4,32,1280]{2,1,0:T(8,128)(2,1)}, bf16[4,32,1280]{2,1,0:T(8,128)(2,1)}, f32[2,1280]{1,0:T(2,128)}) custom-call(s32[1]{0:T(128)} %dynamic_slice.9.live_ref, bf16[4,4,32,1280]{3,2,1,0:T(8,128)(2,1)S(1)} %all_to_all.22.grad_ref, f32[4,32,1280]{2,1,0:T(8,128)S(1)} %get-tuple-element.13.unit_ref, f32[4,32,128]{2,1,0:T(8,128)S(1)} %get-tuple-element.14.inv_ref, ...), custom_call_target="tpu_custom_call" | custom-call | flops 10000000 | bytes 4000000 | tf_op jit(solution)/shard_map/finish/pallas_call | solution.py:233
  (38 shorter events, 2.4 us)
Async XLA Ops:
  5.2 6.7 %copy-start.1 = (bf16[4,32,1280]{2,1,0:T(8,128)(2,1)S(1)}, bf16[4,32,1280]{2,1,0:T(8,128)(2,1)}, u32[]{:S(2)}) copy-start(bf16[4,32,1280]{2,1,0:T(8,128)(2,1)} %refs_0_.1) | copy-start | bytes 983044
  5.2 36.7 %copy-start.7 = (bf16[4,32,1280]{2,1,0:T(8,128)(2,1)S(1)}, bf16[4,32,1280]{2,1,0:T(8,128)(2,1)}, u32[]{:S(2)}) copy-start(bf16[4,32,1280]{2,1,0:T(8,128)(2,1)} %param.10) | copy-start | bytes 983044
  6.7 40.1 %copy-start.8 = (f32[1280]{0:T(1024)S(1)}, f32[1280]{0:T(1024)}, u32[]{:S(2)}) copy-start(f32[1280]{0:T(1024)} %param.15) | copy-start | bytes 15364
  6.7 40.1 %copy-start.9 = (f32[1280]{0:T(1024)S(1)}, f32[1280]{0:T(1024)}, u32[]{:S(2)}) copy-start(f32[1280]{0:T(1024)} %param.16) | copy-start | bytes 15364
  6.7 40.1 %copy-start.10 = (s32[4,128]{1,0:T(4,128)S(1)}, s32[4,128]{1,0:T(4,128)}, u32[]{:S(2)}) copy-start(s32[4,128]{1,0:T(4,128)} %param.11) | copy-start | bytes 6148
  6.8 40.3 %copy-start.11 = (s32[4]{0:T(128)S(1)}, s32[4]{0:T(128)}, u32[]{:S(2)}) copy-start(s32[4]{0:T(128)} %param.13) | copy-start | bytes 52
  6.8 41.8 %copy-start = (bf16[256,1280]{1,0:T(8,128)(2,1)S(1)}, bf16[256,1280]{1,0:T(8,128)(2,1)}, u32[]{:S(2)}) copy-start(bf16[256,1280]{1,0:T(8,128)(2,1)} %pos_ref.1) | copy-start | bytes 1966084
  6.8 41.8 %copy-start.4 = (s32[4]{0:T(128)S(1)}, s32[4]{0:T(128)}, u32[]{:S(2)}) copy-start(s32[4]{0:T(128)} %visible_ref.1) | copy-start | bytes 52
  6.8 13.2 %collective-permute-start.7 = (bf16[160,960]{1,0:T(8,128)(2,1)S(1)}, bf16[160,960]{1,0:T(8,128)(2,1)}, u32[]{:S(2)}, u32[]{:S(2)}) collective-permute-start(bf16[160,960]{1,0:T(8,128)(2,1)S(1)} %constant_dynamic-slice_fusion), channel_id=1, source_target_pairs={{0,3},{1,0},{2,1},{3,2},{4,7},{5,4},{6,5},{7,6},{8,11},{9,8},{10,9... | collective-permute-start | bytes 921608 | tf_op jit(solution)/shard_map/ppermute | solution.py:163
  11.9 29.6 %collective-permute-start.1 = (bf16[4,32,1280]{2,1,0:T(8,128)(2,1)S(1)}, bf16[4,32,1280]{2,1,0:T(8,128)(2,1)S(1)}, u32[]{:S(2)}, u32[]{:S(2)}) collective-permute-start(bf16[4,32,1280]{2,1,0:T(8,128)(2,1)S(1)} %copy-done.1), channel_id=1, source_target_pairs={{0,8},{4,12},{8,0},{12,4},{1,9},{5,13},{9,1},{13,5},{2,10},{6,14},... | collective-permute-start | bytes 983048 | tf_op jit(solution)/shard_map/ppermute | solution.py:173
  13.4 14.8 %collective-permute-start.5 = (bf16[160,960]{1,0:T(8,128)(2,1)S(1)}, bf16[160,960]{1,0:T(8,128)(2,1)}, u32[]{:S(2)}, u32[]{:S(2)}) collective-permute-start(bf16[160,960]{1,0:T(8,128)(2,1)S(1)} %constant_dynamic-slice_fusion), channel_id=1, source_target_pairs={{0,1},{1,2},{2,3},{3,0},{4,5},{5,6},{6,7},{7,4},{8,9},{9,10},{10,1... | collective-permute-start | bytes 921608 | tf_op jit(solution)/shard_map/ppermute | solution.py:163
  13.4 26.5 %collective-permute-start.3 = (bf16[160,960]{1,0:T(8,128)(2,1)S(1)}, bf16[160,960]{1,0:T(8,128)(2,1)}, u32[]{:S(2)}, u32[]{:S(2)}) collective-permute-start(bf16[160,960]{1,0:T(8,128)(2,1)S(1)} %constant_dynamic-slice_fusion), channel_id=1, source_target_pairs={{0,2},{1,3},{2,0},{3,1},{4,6},{5,7},{6,4},{7,5},{8,10},{9,11},{10,... | collective-permute-start | bytes 921608 | tf_op jit(solution)/shard_map/ppermute | solution.py:163
  14.4 33.5 %collective-permute-start = (bf16[4,32,1280]{2,1,0:T(8,128)(2,1)S(1)}, bf16[4,32,1280]{2,1,0:T(8,128)(2,1)S(1)}, u32[]{:S(2)}, u32[]{:S(2)}) collective-permute-start(bf16[4,32,1280]{2,1,0:T(8,128)(2,1)S(1)} %copy-done.1), channel_id=1, source_target_pairs={{0,4},{4,8},{8,12},{12,0},{1,5},{5,9},{9,13},{13,1},{2,6},{6,10},{... | collective-permute-start | bytes 983048 | tf_op jit(solution)/shard_map/ppermute | solution.py:173
  20.0 27.8 %collective-permute-start.2 = (bf16[4,32,1280]{2,1,0:T(8,128)(2,1)S(1)}, bf16[4,32,1280]{2,1,0:T(8,128)(2,1)S(1)}, u32[]{:S(2)}, u32[]{:S(2)}) collective-permute-start(bf16[4,32,1280]{2,1,0:T(8,128)(2,1)S(1)} %copy-done.1), channel_id=1, source_target_pairs={{0,12},{4,0},{8,4},{12,8},{1,13},{5,1},{9,5},{13,9},{2,14},{6,2},{... | collective-permute-start | bytes 983048 | tf_op jit(solution)/shard_map/ppermute | solution.py:173
  28.1 26.0 %collective-permute-start.8 = (bf16[160,960]{1,0:T(8,128)(2,1)}, bf16[160,960]{1,0:T(8,128)(2,1)}, u32[]{:S(2)}, u32[]{:S(2)}) collective-permute-start(bf16[160,960]{1,0:T(8,128)(2,1)} %collective-permute-done.7.refs_5_), channel_id=1, source_target_pairs={{0,16},{16,0},{1,17},{17,1},{2,18},{18,2},{3,19},{19,3},{4,20},{20... | collective-permute-start | bytes 921608 | tf_op jit(solution)/shard_map/ppermute | solution.py:164
  39.9 14.2 %collective-permute-start.6 = (bf16[160,960]{1,0:T(8,128)(2,1)}, bf16[160,960]{1,0:T(8,128)(2,1)}, u32[]{:S(2)}, u32[]{:S(2)}) collective-permute-start(bf16[160,960]{1,0:T(8,128)(2,1)} %collective-permute-done.5.refs_3_), channel_id=1, source_target_pairs={{0,16},{16,0},{1,17},{17,1},{2,18},{18,2},{3,19},{19,3},{4,20},{20... | collective-permute-start | bytes 921608 | tf_op jit(solution)/shard_map/ppermute | solution.py:164
  41.4 14.4 %collective-permute-start.4 = (bf16[160,960]{1,0:T(8,128)(2,1)}, bf16[160,960]{1,0:T(8,128)(2,1)}, u32[]{:S(2)}, u32[]{:S(2)}) collective-permute-start(bf16[160,960]{1,0:T(8,128)(2,1)} %collective-permute-done.3.refs_1_), channel_id=1, source_target_pairs={{0,16},{16,0},{1,17},{17,1},{2,18},{18,2},{3,19},{19,3},{4,20},{20... | collective-permute-start | bytes 921608 | tf_op jit(solution)/shard_map/ppermute | solution.py:164
  43.2 10.9 %all-to-all-start = ((bf16[4,4,32,320]{3,2,1,0:T(8,128)(2,1)}), bf16[4,4,32,320]{3,2,1,0:T(8,128)(2,1)S(1)}, u32[]{:S(2)}, u32[]{:S(2)}) async-start(bf16[4,4,32,320]{3,2,1,0:T(8,128)(2,1)} %bitcast.24), calls=%async_computation | async-start | bytes 786432 | tf_op jit(solution)/shard_map/all_to_all | solution.py:178
  47.9 0.7 copy-start.2
  48.6 1.0 copy-start.3
  51.6 1.1 copy-start.5
  52.7 1.1 copy-start.6

commit v2 on v1

v2 whole, which is shorter than its diff:
```python
import functools

import jax
import jax.numpy as jnp
from jax import lax
from jax.experimental import pallas as pl
from jax.experimental.pallas import tpu as pltpu
from jax.sharding import PartitionSpec as P

HEAD_DIM = 80
DG = 32
BLOCK_ROWS = 32
F32 = jnp.float32
BF16 = jnp.bfloat16

VMEM = pl.BlockSpec(memory_space=pltpu.VMEM)
SMEM = pl.BlockSpec(memory_space=pltpu.SMEM)
HBM = pl.BlockSpec(memory_space=pltpu.HBM)


def dot(a, b):
    return jnp.dot(a, b, preferred_element_type=F32)


def dot_nt(a, b):
    return lax.dot_general(a, b, (((1,), (1,)), ((), ())), preferred_element_type=F32)


def dot_tn(a, b):
    return lax.dot_general(a, b, (((0,), (0,)), ((), ())), preferred_element_type=F32)


def norm_kernel(visible_ref, pos_ref, gain_ref, bias_ref, *refs):
    groups = len(refs) - 4
    token_refs = refs[:groups]
    normed_ref, unit_ref, own_unit_ref, own_inv_ref = refs[groups:]
    slots, rows, width = token_refs[0].shape
    gain = gain_ref[...]
    bias = bias_ref[...]
    for p in range(slots):
        iota = lax.broadcasted_iota(jnp.int32, (8, pos_ref.shape[0]), 1)
        onehot = (iota == visible_ref[p]).astype(F32).astype(BF16)
        position = dot(onehot, pos_ref[...])[0:1]
        for s in range(groups):
            embedded = (token_refs[s][p].astype(F32) + position).astype(BF16).astype(F32)
            centred = embedded - jnp.mean(embedded, axis=-1, keepdims=True)
            inv_std = lax.rsqrt(jnp.mean(centred * centred, axis=-1, keepdims=True) + 1e-06)
            unit = centred * inv_std
            normed_ref[p, s] = (unit * gain + bias).astype(BF16)
            unit_ref[p, s] = unit.astype(BF16)
            if s == 0:
                own_unit_ref[p] = unit
                own_inv_ref[p] = jnp.broadcast_to(inv_std, own_inv_ref.shape[1:])


def attend_kernel(
    places, copies, where_ref, live_ref, normed_ref, unit_ref, up_ref, valid_ref, gathered, *refs
):
    groups, slots, rows, channels = up_ref.shape
    context_refs, grad_refs = refs[:groups], refs[groups : 2 * groups]
    sums_ref, weights, qkv_ref, gqkv_ref, sems = refs[2 * groups :]
    dates = groups * rows
    heads = channels // HEAD_DIM
    inv_scale = 1.0 / HEAD_DIM**0.5
    height = gathered.shape[0] // len(places)
    moves = [
        pltpu.make_async_copy(
            gathered.at[pl.ds(c * height, height)], weights.at[pl.ds(place, height)], sems.at[c]
        )
        for c, place in enumerate(places)
    ]
    for move in moves:
        move.start()
    for move in moves:
        move.wait()
    qkv_ref[...] = dot(normed_ref[...], weights[...]).astype(BF16)
    valid_rows = jnp.concatenate(
        [valid_ref[pl.ds(pl.multiple_of(where_ref[s] * rows, rows), rows), :] for s in range(groups)],
        axis=0,
    )
    for p in range(slots):
        span = slice(p * dates, (p + 1) * dates)
        alive = (live_ref[0] > p // (BLOCK_ROWS // DG)).astype(F32)
        rows_qkv = qkv_ref[span, :]
        upstream = jnp.concatenate([up_ref[where_ref[s], p] for s in range(groups)], axis=0)
        upstream = upstream * alive.astype(BF16)
        allowed = valid_rows[:, p : p + 1] > 0
        grads = [[], [], []]
        contexts = []
        for h in range(heads):
            q, k, v = (
                rows_qkv[:, i * channels + h * HEAD_DIM : i * channels + (h + 1) * HEAD_DIM]
                for i in range(3)
            )
            up = upstream[:, h * HEAD_DIM : (h + 1) * HEAD_DIM]
            scores = jnp.where(allowed, dot_nt(k, q) * inv_scale, -1e30)
            exps = jnp.exp(scores - jnp.max(scores, axis=0, keepdims=True))
            probs = exps / jnp.sum(exps, axis=0, keepdims=True)
            low = probs.astype(BF16)
            contexts.append(dot_tn(low, v) * alive)
            grads[2].append(dot(low, up))
            gprobs = dot_nt(v, up)
            gscores = probs * (gprobs - jnp.sum(probs * gprobs, axis=0, keepdims=True)) * inv_scale
            glow = gscores.astype(BF16)
            grads[0].append(dot_tn(glow, k))
            grads[1].append(dot(glow, q))
        gqkv_ref[span, :] = jnp.concatenate(grads[0] + grads[1] + grads[2], axis=1).astype(BF16)
        context = jnp.concatenate(contexts, axis=1).astype(BF16)
        for s in range(groups):
            context_refs[s][p] = context[s * rows : (s + 1) * rows]
    gain_sum = None
    for p in range(slots):
        span = slice(p * dates, (p + 1) * dates)
        partial = dot_nt(gqkv_ref[span, :], weights[...])
        for s in range(groups):
            grad_refs[s][p] = partial[s * rows : (s + 1) * rows].astype(BF16)
        gain_part = jnp.sum(partial * unit_ref[span, :].astype(F32), axis=0, keepdims=True)
        bias_part = jnp.sum(partial, axis=0, keepdims=True)
        gain_sum = gain_part if gain_sum is None else gain_sum + gain_part
        bias_sum = bias_part if p == 0 else bias_sum + bias_part
    both = jnp.concatenate([gain_sum, bias_sum], axis=0)
    for c in range(copies):
        sums_ref[c] = both


def finish_kernel(where_ref, live_ref, unit_ref, inv_ref, gain_ref, sums_ref, *refs):
    groups = (len(refs) - 4) // 2
    context_refs, grad_refs = refs[:groups], refs[groups : 2 * groups]
    attended_ref, out_ref, norm_ref, held = refs[2 * groups :]
    slots, rows, width = unit_ref.shape
    gain = gain_ref[...]
    for s in range(groups):
        held[where_ref[s]] = context_refs[s][...]
    for p in range(slots):
        alive = (live_ref[0] > p // (BLOCK_ROWS // DG)).astype(F32)
        grad = grad_refs[0][p].astype(F32)
        for s in range(1, groups):
            grad = grad + grad_refs[s][p].astype(F32)
        unit = unit_ref[p]
        scaled = grad * gain
        out = inv_ref[p][:, 0:1] * (
            scaled
            - jnp.mean(scaled, axis=-1, keepdims=True)
            - unit * jnp.mean(scaled * unit, axis=-1, keepdims=True)
        )
        out_ref[p] = (out * alive).astype(BF16)
        attended_ref[p] = jnp.concatenate([held[g, p] for g in range(groups)], axis=1)
    norm_ref[...] = jnp.sum(sums_ref[...], axis=0)


def shifted(array, axis, shift):
    size = lax.axis_size(axis)
    return lax.ppermute(array, axis, [(i, (i + shift) % size) for i in range(size)])


def params(megabytes):
    return pltpu.CompilerParams(vmem_limit_bytes=megabytes * 1024 * 1024)


def local(tokens, cotangent, valid, visible, live, pos_table, norm_gain, norm_bias, w_qkv):
    slots, rows, width = tokens.shape
    groups = lax.axis_size("date")
    owners = lax.axis_size("tile")
    reps = lax.axis_size("rep")
    group = lax.axis_index("date")
    owner = lax.axis_index("tile")
    rep = lax.axis_index("rep")
    depth, triple = w_qkv.shape
    channels = triple // 3
    part = channels // groups
    dates = rows * groups
    live_here = lax.dynamic_slice_in_dim(live, owner, 1, 0)

    share = depth // reps
    spread = share % 16 == 0
    first, height = (rep * share, share) if spread else (0, depth)
    mine = jnp.concatenate(
        [
            lax.dynamic_slice(w_qkv, (first, i * channels + group * part), (height, part))
            for i in range(3)
        ],
        axis=1,
    )
    if spread:
        weights = lax.all_gather(mine, ("rep", "tile"), axis=0, tiled=True)
        places = [k * depth + r * share for r in range(reps) for k in range(owners)]
    else:
        weights = lax.all_gather(mine, "tile", axis=0, tiled=True)
        places = [0]

    gathered = [tokens] + [shifted(tokens, "date", s) for s in range(1, groups)]
    columns = cotangent.reshape(slots, rows, groups, part).transpose(2, 0, 1, 3)
    upstream = lax.all_to_all(columns, "date", split_axis=0, concat_axis=0, tiled=True)
    where = jnp.stack([(group - s) % groups for s in range(groups)]).astype(jnp.int32)
    whence = jnp.stack([(group + s) % groups for s in range(groups)]).astype(jnp.int32)

    gain2, bias2 = norm_gain.reshape(1, width), norm_bias.reshape(1, width)
    normed, unit, own_unit, own_inv = pl.pallas_call(
        norm_kernel,
        out_shape=(
            jax.ShapeDtypeStruct((slots, groups, rows, width), BF16),
            jax.ShapeDtypeStruct((slots, groups, rows, width), BF16),
            jax.ShapeDtypeStruct((slots, rows, width), F32),
            jax.ShapeDtypeStruct((slots, rows, 128), F32),
        ),
        in_specs=[SMEM] + [VMEM] * (3 + groups),
        out_specs=(VMEM,) * 4,
        compiler_params=params(16),
        cost_estimate=pl.CostEstimate(flops=10**7, bytes_accessed=6 * 10**6, transcendentals=1000),
        name="norm",
    )(visible, pos_table, gain2, bias2, *gathered)

    copies = groups * owners if owners == 4 else 1
    results = pl.pallas_call(
        functools.partial(attend_kernel, places, copies),
        out_shape=(jax.ShapeDtypeStruct((slots, rows, part), BF16),) * groups
        + (jax.ShapeDtypeStruct((slots, rows, width), BF16),) * groups
        + (jax.ShapeDtypeStruct((copies, 2, width), F32),),
        in_specs=[SMEM, SMEM] + [VMEM] * 4 + [HBM],
        out_specs=(VMEM,) * (2 * groups + 1),
        scratch_shapes=[
            pltpu.VMEM((width, 3 * part), BF16),
            pltpu.VMEM((slots * dates, 3 * part), BF16),
            pltpu.VMEM((slots * dates, 3 * part), BF16),
            pltpu.SemaphoreType.DMA((len(places),)),
        ],
        compiler_params=params(24),
        cost_estimate=pl.CostEstimate(flops=3 * 10**9, bytes_accessed=10**7, transcendentals=10**6),
        name="attend",
    )(
        where,
        live_here,
        normed.reshape(slots * dates, width),
        unit.reshape(slots * dates, width),
        upstream,
        valid.T,
        weights,
    )
    contexts, grads, sums = results[:groups], results[groups : 2 * groups], results[-1]

    grad_home = [grads[0]] + [shifted(grads[s], "date", -s) for s in range(1, groups)]
    context_home = [contexts[0]] + [shifted(contexts[s], "date", -s) for s in range(1, groups)]
    if copies > 1:
        sums = lax.all_to_all(sums, ("date", "tile"), split_axis=0, concat_axis=0, tiled=True)
    else:
        sums = lax.psum(sums, ("date", "tile"))

    return pl.pallas_call(
        finish_kernel,
        out_shape=(
            jax.ShapeDtypeStruct((slots, rows, channels), BF16),
            jax.ShapeDtypeStruct((slots, rows, width), BF16),
            jax.ShapeDtypeStruct((2, width), F32),
        ),
        in_specs=[SMEM, SMEM] + [VMEM] * (4 + 2 * groups),
        out_specs=(VMEM,) * 3,
        scratch_shapes=[pltpu.VMEM((groups, slots, rows, part), BF16)],
        compiler_params=params(16),
        cost_estimate=pl.CostEstimate(flops=10**7, bytes_accessed=4 * 10**6, transcendentals=0),
        name="finish",
    )(whence, live_here, own_unit, own_inv, gain2, sums, *context_home, *grad_home)


def solution(mesh):
    in_specs = (
        P(("rep", "tile"), "date", None),
        P(("rep", "tile"), "date", None),
        P(("rep", "tile"), None),
        P(("rep", "tile")),
        P("rep"),
        P(),
        P(),
        P(),
        P("tile", None),
    )
    out_specs = (P(("rep", "tile"), "date", None), P(("rep", "tile"), "date", None), P("rep", None))
    return jax.shard_map(local, mesh=mesh, in_specs=in_specs, out_specs=out_specs, check_vma=False)
```

time: 111 us -> 117 us (1.054)
  blocking collectives: 42.6 us -> 0 us
  waiting for transfers between devices: 26.1 us -> 56 us
  between operations: 0.97 us -> 14.3 us
  starting transfers between devices: 14.6 us -> 18.5 us
    all_to_all x3 -> x0, blocking collectives: 42.6 us -> none  [the longest x1 19.7 us: local(): lax.all_to_all(grad, 'date', split_axis=0, concat_axis=0, tiled=True)]
    all_gather x0 -> x1, waiting for transfers between devices: none -> 35.9 us  [local(): weights = lax.all_gather(mine, ('rep', 'tile'), axis=0, tiled=True)]
    ppermute x9, waiting for transfers between devices: 25.8 us -> 20.1 us  [shifted(): lax.ppermute(array, axis, [(i, (i + shift) % size) for i in range(size)])]
    all_to_all x0 -> x1, starting transfers between devices: none -> 4.24 us  [local(): lax.all_to_all(sums, ('date', 'tile'), split_axis=0, concat_axis=0, tiled...]
    reshape x1 -> x0, local copies, waits for them, and re-layouts: 1.44 us -> none  [local(): mine = mine.reshape(depth, 3 * part)]
    pallas_call x2, Pallas kernels: 12.6 us -> 11.2 us  [the longest x1 9.24 us: local(): pl.pallas_call(functools.partial(attend_kernel, places, copies), out_shap...]
    unnamed x26 -> x31, local copies, waits for them, and re-layouts: 7.61 us -> 8.59 us
  transfers between devices with their start and end apart: 10 -> 12, of which waited for: 5 -> 6; matrix products, arithmetic and copies ran while one was open for 2% -> 3% of each run, Pallas kernels for 2% -> 2%
where the time goes in v2:
time: 117 us; the launch traced here: 116 us
  waiting for transfers between devices  56 us (48%)
  starting transfers between devices  18.5 us (16%)
  between operations  14.3 us (12%)
  Pallas kernels  13.6 us (12%)
  local copies, waits for them, and re-layouts  12.8 us (11%)
    all_gather x1, waiting for transfers between devices, local(): weights = lax.all_gather(mine, ('rep', 'tile'), axis=0, tiled=True)  35.9 us
    ppermute x9, waiting for transfers between devices, shifted(): lax.ppermute(array, axis, [(i, (i + shift) % size) for i in range(size)])  20.1 us
    ppermute x9, starting transfers between devices, shifted(): lax.ppermute(array, axis, [(i, (i + shift) % size) for i in range(size)])  10.8 us
    pallas_call x1, Pallas kernels, local(): pl.pallas_call(functools.partial(attend_kernel, places, copies), out_shap...  9.24 us
    unnamed x31, local copies, waits for them, and re-layouts  8.59 us
    all_to_all x1, starting transfers between devices, local(): lax.all_to_all(sums, ('date', 'tile'), split_axis=0, concat_axis=0, tiled...  4.24 us
    all_to_all x1, starting transfers between devices, local(): lax.all_to_all(columns, 'date', split_axis=0, concat_axis=0, tiled=True)  3.46 us
    pallas_call x1, Pallas kernels, local(): pl.pallas_call(finish_kernel, out_shape=(jax.ShapeDtypeStruct((slots, row...  2.43 us
  transfers between devices with their start and end apart: 12, of which 6 were waited for; matrix products, arithmetic and copies ran while one was open for 3% of the time, Pallas kernels for 2%

profile of v2, /device:TPU:0, one launch (start us, length us, event | category | flops | bytes accessed | tf_op | source)
XLA Modules:
  0.0 116.2 jit_solution(15680306946613892373)
XLA Ops:
  7.3 1.4 %fusion = (bf16[160,320]{1,0:T(8,128)(2,1)S(1)}, bf16[160,320]{1,0:T(8,128)(2,1)S(1)}, bf16[160,320]{1,0:T(8,128)(2,1)S(1)}) fusion(bf16[320,3840]{1,0:T(8,128)(2,1)} %param.17, s32[]{:T(128)S(6)} %select_n.58, s32[]{:T(128)S(6)} %select_n.59, s32[]{:T(128)S(6)} %select_n.61, s32[]{:T(128)S(6)} %select_n.60), kind=kLoop, calls=%fused_computation.4 | loop fusion | bytes 614416 | tf_op jit(solution)/shard_map/dynamic_slice | solution.py:179
  8.7 0.8 pad_maximum_fusion
  10.1 2.6 %collective-permute-start.1 = (bf16[4,32,1280]{2,1,0:T(8,128)(2,1)}, bf16[4,32,1280]{2,1,0:T(8,128)(2,1)S(1)}, u32[]{:S(2)}, u32[]{:S(2)}) collective-permute-start(bf16[4,32,1280]{2,1,0:T(8,128)(2,1)} %refs_0_.1), channel_id=1, source_target_pairs={{0,8},{4,12},{8,0},{12,4},{1,9},{5,13},{9,1},{13,5},{2,10},{6,14},... | collective-permute-start | bytes 983048 | tf_op jit(solution)/shard_map/ppermute | solution.py:153
  12.7 1.4 %collective-permute-start.2 = (bf16[4,32,1280]{2,1,0:T(8,128)(2,1)}, bf16[4,32,1280]{2,1,0:T(8,128)(2,1)S(1)}, u32[]{:S(2)}, u32[]{:S(2)}) collective-permute-start(bf16[4,32,1280]{2,1,0:T(8,128)(2,1)} %refs_0_.1), channel_id=1, source_target_pairs={{0,12},{4,0},{8,4},{12,8},{1,13},{5,1},{9,5},{13,9},{2,14},{6,2},{... | collective-permute-start | bytes 983048 | tf_op jit(solution)/shard_map/ppermute | solution.py:153
  14.1 1.4 %reshape.25 = bf16[4,32,4,320]{3,2,1,0:T(4,128)(2,1)S(1)} reshape(bf16[4,32,1280]{2,1,0:T(8,128)(2,1)} %param.10) | data formatting | bytes 655360 | tf_op jit(solution)/shard_map/reshape | solution.py:192
  15.5 0.8 copy.16
  16.3 3.5 %all-to-all-start = ((bf16[4,4,32,320]{3,2,1,0:T(8,128)(2,1)}), bf16[4,4,32,320]{3,2,1,0:T(8,128)(2,1)S(1)}, u32[]{:S(2)}, u32[]{:S(2)}) async-start(bf16[4,4,32,320]{3,2,1,0:T(8,128)(2,1)} %bitcast.12), calls=%async_computation | async-start | bytes 786432 | tf_op jit(solution)/shard_map/all_to_all | solution.py:193
  20.6 0.8 collective-permute-done.1.refs_2_
  21.4 6.6 %collective-permute-done.2.refs_3_ = bf16[4,32,1280]{2,1,0:T(8,128)(2,1)S(1)} collective-permute-done((bf16[4,32,1280]{2,1,0:T(8,128)(2,1)}, bf16[4,32,1280]{2,1,0:T(8,128)(2,1)S(1)}, u32[]{:S(2)}, u32[]{:S(2)}) %collective-permute-start.2) | collective-permute-done | bytes 327712 | tf_op jit(solution)/shard_map/ppermute | solution.py:153
  28.1 1.9 %norm.1 = (bf16[4,4,32,1280]{3,2,1,0:T(8,128)(2,1)S(1)}, bf16[4,4,32,1280]{3,2,1,0:T(8,128)(2,1)S(1)}, f32[4,32,1280]{2,1,0:T(8,128)S(1)}, f32[4,32,128]{2,1,0:T(8,128)S(1)}) custom-call(s32[4]{0:T(128)S(1)} %copy-done.2, bf16[256,1280]{1,0:T(8,128)(2,1)S(1)} %copy-done, f32[1,1280]{1,0:T(1,128)S(1)} %reshape.21.gain_ref, f32[1,1280]{1,0:T(1,128)S(1)} %reshape.22.bias_ref, ...), custom_call_target="tpu_custom_call" | custom-call | flops 10000000 | bytes 6000000 | tf_op jit(solution)/shard_map/norm/pallas_call | solution.py:198
  30.0 1.1 copy-done.4
  31.1 1.1 copy-done.6
  32.2 35.9 %all-gather.2.cloned.1.call-done.gathered = bf16[1280,960]{1,0:T(8,128)(2,1)} async-done(((bf16[160,960]{1,0:T(8,128)(2,1)}), bf16[1280,960]{1,0:T(8,128)(2,1)}) %all-gather.2.cloned.1.call-update) | async-done | bytes 2457616 | tf_op jit(solution)/shard_map/all_gather | solution.py:185
  68.1 1.7 %copy-done.3 = bf16[1280,960]{1,0:T(8,128)(2,1)S(1)} copy-done((bf16[1280,960]{1,0:T(8,128)(2,1)S(1)}, bf16[1280,960]{1,0:T(8,128)(2,1)}, u32[]{:S(2)}) %copy-start.3) | copy-done | bytes 2457624
  69.9 1.3 %copy-done.5 = bf16[4,4,32,1280]{3,2,1,0:T(8,128)(2,1)S(1)} copy-done((bf16[4,4,32,1280]{3,2,1,0:T(8,128)(2,1)S(1)}, bf16[4,4,32,1280]{3,2,1,0:T(8,128)(2,1)}, u32[]{:S(2)}) %copy-start.5) | copy-done | bytes 1310744
  71.2 1.3 %copy-done.7 = bf16[4,4,32,1280]{3,2,1,0:T(8,128)(2,1)S(1)} copy-done((bf16[4,4,32,1280]{3,2,1,0:T(8,128)(2,1)S(1)}, bf16[4,4,32,1280]{3,2,1,0:T(8,128)(2,1)}, u32[]{:S(2)}) %copy-start.7) | copy-done | bytes 1310744
  72.5 9.2 %attend.1 = (bf16[4,32,320]{2,1,0:T(8,128)(2,1)S(1)}, bf16[4,32,320]{2,1,0:T(8,128)(2,1)S(1)}, bf16[4,32,320]{2,1,0:T(8,128)(2,1)S(1)}, bf16[4,32,320]{2,1,0:T(8...) custom-call(s32[4]{0:T(128)S(1)} %pad_add_fusion.1.where_ref, ...), custom_call_target="tpu_custom_call" | custom-call | flops 3000000000 | bytes 10000000 | tf_op jit(solution)/shard_map/attend/pallas_call | solution.py:214
  83.7 1.5 %collective-permute-start.7 = (bf16[4,32,1280]{2,1,0:T(8,128)(2,1)}, bf16[4,32,1280]{2,1,0:T(8,128)(2,1)S(1)}, u32[]{:S(2)}, u32[]{:S(2)}) collective-permute-start(bf16[4,32,1280]{2,1,0:T(8,128)(2,1)} %get-tuple-element.27), channel_id=1, source_target_pairs={{0,8},{4,12},{8,0},{12,4},{1,9},{5,13},{9,1},{13,5},{2,10},{6,14},... | collective-permute-start | bytes 983048 | tf_op jit(solution)/shard_map/ppermute | solution.py:153
  85.4 4.2 %all-to-all-start.1 = ((f32[16,2,1280]{2,1,0:T(2,128)}), f32[16,2,1280]{2,1,0:T(2,128)S(1)}, u32[]{:S(2)}, u32[]{:S(2)}) async-start(f32[16,2,1280]{2,1,0:T(2,128)} %get-tuple-element.20), calls=%async_computation.1 | async-start | bytes 327680 | tf_op jit(solution)/shard_map/all_to_all | solution.py:244
  89.6 1.7 %collective-permute-start.3 = (bf16[4,32,320]{2,1,0:T(8,128)(2,1)}, bf16[4,32,320]{2,1,0:T(8,128)(2,1)S(1)}, u32[]{:S(2)}, u32[]{:S(2)}) collective-permute-start(bf16[4,32,320]{2,1,0:T(8,128)(2,1)} %copy-done.10), channel_id=1, source_target_pairs={{0,12},{4,0},{8,4},{12,8},{1,13},{5,1},{9,5},{13,9},{2,14},{6,2},{... | collective-permute-start | bytes 245768 | tf_op jit(solution)/shard_map/ppermute | solution.py:153
  91.7 10.3 %collective-permute-done.3.refs_1_ = bf16[4,32,320]{2,1,0:T(8,128)(2,1)S(1)} collective-permute-done((bf16[4,32,320]{2,1,0:T(8,128)(2,1)}, bf16[4,32,320]{2,1,0:T(8,128)(2,1)S(1)}, u32[]{:S(2)}, u32[]{:S(2)}) %collective-permute-start.3) | collective-permute-done | bytes 81952 | tf_op jit(solution)/shard_map/ppermute | solution.py:153
  102.0 2.6 %collective-permute-start.5 = (bf16[4,32,320]{2,1,0:T(8,128)(2,1)}, bf16[4,32,320]{2,1,0:T(8,128)(2,1)S(1)}, u32[]{:S(2)}, u32[]{:S(2)}) collective-permute-start(bf16[4,32,320]{2,1,0:T(8,128)(2,1)} %copy-done.8), channel_id=1, source_target_pairs={{0,4},{4,8},{8,12},{12,0},{1,5},{5,9},{9,13},{13,1},{2,6},{6,10},{... | collective-permute-start | bytes 245768 | tf_op jit(solution)/shard_map/ppermute | solution.py:153
  104.6 1.8 %collective-permute-done.4.refs_2_ = bf16[4,32,320]{2,1,0:T(8,128)(2,1)S(1)} collective-permute-done((bf16[4,32,320]{2,1,0:T(8,128)(2,1)}, bf16[4,32,320]{2,1,0:T(8,128)(2,1)S(1)}, u32[]{:S(2)}, u32[]{:S(2)}) %collective-permute-start.4) | collective-permute-done | bytes 81952 | tf_op jit(solution)/shard_map/ppermute | solution.py:153
  106.9 2.4 %finish.1 = (bf16[4,32,1280]{2,1,0:T(8,128)(2,1)}, bf16[4,32,1280]{2,1,0:T(8,128)(2,1)}, f32[2,1280]{1,0:T(2,128)}) custom-call(s32[4]{0:T(128)S(1)} %pad_add_fusion.where_ref, s32[1]{0:T(128)} %dynamic_slice.12.live_ref, f32[4,32,1280]{2,1,0:T(8,128)S(1)} %get-tuple-element.16.unit_ref, f32[4,32,128]{2,1,0:T(8,128)S(1)} %get-tuple-element.17.inv_ref, ...), custom_call_target="tpu_custom_call" | custom-call | flops 10000000 | bytes 4000000 | tf_op jit(solution)/shard_map/finish/pallas_call | solution.py:248
  (44 shorter events, 4.4 us)
Async XLA Ops:
  7.2 20.9 %copy-start.1 = (bf16[4,32,1280]{2,1,0:T(8,128)(2,1)S(1)}, bf16[4,32,1280]{2,1,0:T(8,128)(2,1)}, u32[]{:S(2)}) copy-start(bf16[4,32,1280]{2,1,0:T(8,128)(2,1)} %refs_0_.1) | copy-start | bytes 983044
  7.2 12.6 %copy-start.11 = (f32[1280]{0:T(1024)S(1)}, f32[1280]{0:T(1024)}, u32[]{:S(2)}) copy-start(f32[1280]{0:T(1024)} %param.15) | copy-start | bytes 15364
  7.2 12.6 %copy-start.12 = (f32[1280]{0:T(1024)S(1)}, f32[1280]{0:T(1024)}, u32[]{:S(2)}) copy-start(f32[1280]{0:T(1024)} %param.16) | copy-start | bytes 15364
  7.2 12.6 %copy-start.13 = (s32[4,128]{1,0:T(4,128)S(1)}, s32[4,128]{1,0:T(4,128)}, u32[]{:S(2)}) copy-start(s32[4,128]{1,0:T(4,128)} %param.11) | copy-start | bytes 6148
  7.2 12.8 %copy-start.14 = (s32[4]{0:T(128)S(1)}, s32[4]{0:T(128)}, u32[]{:S(2)}) copy-start(s32[4]{0:T(128)} %param.13) | copy-start | bytes 52
  7.2 20.9 %copy-start.2 = (s32[4]{0:T(128)S(1)}, s32[4]{0:T(128)}, u32[]{:S(2)}) copy-start(s32[4]{0:T(128)} %visible_ref.1) | copy-start | bytes 52
  7.2 20.9 %copy-start = (bf16[256,1280]{1,0:T(8,128)(2,1)S(1)}, bf16[256,1280]{1,0:T(8,128)(2,1)}, u32[]{:S(2)}) copy-start(bf16[256,1280]{1,0:T(8,128)(2,1)} %pos_ref.1) | copy-start | bytes 1966084
  7.2 60.9 %all-gather.2.cloned.1.call-start = ((), (), s32[]{:S(2)}) async-start(), calls=%async_computation.2 | async-start | bytes 2949120 | tf_op jit(solution)/shard_map/all_gather | solution.py:185
  9.6 11.0 %collective-permute-start = (bf16[4,32,1280]{2,1,0:T(8,128)(2,1)}, bf16[4,32,1280]{2,1,0:T(8,128)(2,1)S(1)}, u32[]{:S(2)}, u32[]{:S(2)}) collective-permute-start(bf16[4,32,1280]{2,1,0:T(8,128)(2,1)} %refs_0_.1), channel_id=1, source_target_pairs={{0,4},{4,8},{8,12},{12,0},{1,5},{5,9},{9,13},{13,1},{2,6},{6,10},{... | collective-permute-start | bytes 983048 | tf_op jit(solution)/shard_map/ppermute | solution.py:153
  10.1 11.3 %collective-permute-start.1 = (bf16[4,32,1280]{2,1,0:T(8,128)(2,1)}, bf16[4,32,1280]{2,1,0:T(8,128)(2,1)S(1)}, u32[]{:S(2)}, u32[]{:S(2)}) collective-permute-start(bf16[4,32,1280]{2,1,0:T(8,128)(2,1)} %refs_0_.1), channel_id=1, source_target_pairs={{0,8},{4,12},{8,0},{12,4},{1,9},{5,13},{9,1},{13,5},{2,10},{6,14},... | collective-permute-start | bytes 983048 | tf_op jit(solution)/shard_map/ppermute | solution.py:153
  12.7 15.4 %collective-permute-start.2 = (bf16[4,32,1280]{2,1,0:T(8,128)(2,1)}, bf16[4,32,1280]{2,1,0:T(8,128)(2,1)S(1)}, u32[]{:S(2)}, u32[]{:S(2)}) collective-permute-start(bf16[4,32,1280]{2,1,0:T(8,128)(2,1)} %refs_0_.1), channel_id=1, source_target_pairs={{0,12},{4,0},{8,4},{12,8},{1,13},{5,1},{9,5},{13,9},{2,14},{6,2},{... | collective-permute-start | bytes 983048 | tf_op jit(solution)/shard_map/ppermute | solution.py:153
  16.3 15.9 %all-to-all-start = ((bf16[4,4,32,320]{3,2,1,0:T(8,128)(2,1)}), bf16[4,4,32,320]{3,2,1,0:T(8,128)(2,1)S(1)}, u32[]{:S(2)}, u32[]{:S(2)}) async-start(bf16[4,4,32,320]{3,2,1,0:T(8,128)(2,1)} %bitcast.12), calls=%async_computation | async-start | bytes 786432 | tf_op jit(solution)/shard_map/all_to_all | solution.py:193
  30.0 1.1 copy-start.4
  31.1 1.1 copy-start.6
  68.1 1.7 %copy-start.3 = (bf16[1280,960]{1,0:T(8,128)(2,1)S(1)}, bf16[1280,960]{1,0:T(8,128)(2,1)}, u32[]{:S(2)}) copy-start(bf16[1280,960]{1,0:T(8,128)(2,1)} %all-gather.2.cloned.1.call-done.gathered) | copy-start | bytes 7372804
  69.9 1.3 %copy-start.5 = (bf16[4,4,32,1280]{3,2,1,0:T(8,128)(2,1)S(1)}, bf16[4,4,32,1280]{3,2,1,0:T(8,128)(2,1)}, u32[]{:S(2)}) copy-start(bf16[4,4,32,1280]{3,2,1,0:T(8,128)(2,1)} %copy-done.4) | copy-start | bytes 3932164
  71.2 1.3 %copy-start.7 = (bf16[4,4,32,1280]{3,2,1,0:T(8,128)(2,1)S(1)}, bf16[4,4,32,1280]{3,2,1,0:T(8,128)(2,1)}, u32[]{:S(2)}) copy-start(bf16[4,4,32,1280]{3,2,1,0:T(8,128)(2,1)} %copy-done.6) | copy-start | bytes 3932164
  83.7 23.2 %collective-permute-start.6 = (bf16[4,32,1280]{2,1,0:T(8,128)(2,1)}, bf16[4,32,1280]{2,1,0:T(8,128)(2,1)S(1)}, u32[]{:S(2)}, u32[]{:S(2)}) collective-permute-start(bf16[4,32,1280]{2,1,0:T(8,128)(2,1)} %get-tuple-element.26), channel_id=1, source_target_pairs={{0,12},{4,0},{8,4},{12,8},{1,13},{5,1},{9,5},{13,9},{2,14},{6,2},{... | collective-permute-start | bytes 983048 | tf_op jit(solution)/shard_map/ppermute | solution.py:153
  83.7 23.2 %collective-permute-start.7 = (bf16[4,32,1280]{2,1,0:T(8,128)(2,1)}, bf16[4,32,1280]{2,1,0:T(8,128)(2,1)S(1)}, u32[]{:S(2)}, u32[]{:S(2)}) collective-permute-start(bf16[4,32,1280]{2,1,0:T(8,128)(2,1)} %get-tuple-element.27), channel_id=1, source_target_pairs={{0,8},{4,12},{8,0},{12,4},{1,9},{5,13},{9,1},{13,5},{2,10},{6,14},... | collective-permute-start | bytes 983048 | tf_op jit(solution)/shard_map/ppermute | solution.py:153
  85.1 21.8 %collective-permute-start.8 = (bf16[4,32,1280]{2,1,0:T(8,128)(2,1)S(1)}, bf16[4,32,1280]{2,1,0:T(8,128)(2,1)S(1)}, u32[]{:S(2)}, u32[]{:S(2)}) collective-permute-start(bf16[4,32,1280]{2,1,0:T(8,128)(2,1)S(1)} %get-tuple-element.28), channel_id=1, source_target_pairs={{0,4},{4,8},{8,12},{12,0},{1,5},{5,9},{9,13},{13,1},{2,6},{6,10},{... | collective-permute-start | bytes 983048 | tf_op jit(solution)/shard_map/ppermute | solution.py:153
  85.4 21.5 %all-to-all-start.1 = ((f32[16,2,1280]{2,1,0:T(2,128)}), f32[16,2,1280]{2,1,0:T(2,128)S(1)}, u32[]{:S(2)}, u32[]{:S(2)}) async-start(f32[16,2,1280]{2,1,0:T(2,128)} %get-tuple-element.20), calls=%async_computation.1 | async-start | bytes 327680 | tf_op jit(solution)/shard_map/all_to_all | solution.py:244
  89.6 12.3 %collective-permute-start.3 = (bf16[4,32,320]{2,1,0:T(8,128)(2,1)}, bf16[4,32,320]{2,1,0:T(8,128)(2,1)S(1)}, u32[]{:S(2)}, u32[]{:S(2)}) collective-permute-start(bf16[4,32,320]{2,1,0:T(8,128)(2,1)} %copy-done.10), channel_id=1, source_target_pairs={{0,12},{4,0},{8,4},{12,8},{1,13},{5,1},{9,5},{13,9},{2,14},{6,2},{... | collective-permute-start | bytes 245768 | tf_op jit(solution)/shard_map/ppermute | solution.py:153
  91.3 15.1 %collective-permute-start.4 = (bf16[4,32,320]{2,1,0:T(8,128)(2,1)}, bf16[4,32,320]{2,1,0:T(8,128)(2,1)S(1)}, u32[]{:S(2)}, u32[]{:S(2)}) collective-permute-start(bf16[4,32,320]{2,1,0:T(8,128)(2,1)} %copy-done.9), channel_id=1, source_target_pairs={{0,8},{4,12},{8,0},{12,4},{1,9},{5,13},{9,1},{13,5},{2,10},{6,14},... | collective-permute-start | bytes 245768 | tf_op jit(solution)/shard_map/ppermute | solution.py:153
  102.0 4.9 %collective-permute-start.5 = (bf16[4,32,320]{2,1,0:T(8,128)(2,1)}, bf16[4,32,320]{2,1,0:T(8,128)(2,1)S(1)}, u32[]{:S(2)}, u32[]{:S(2)}) collective-permute-start(bf16[4,32,320]{2,1,0:T(8,128)(2,1)} %copy-done.8), channel_id=1, source_target_pairs={{0,4},{4,8},{8,12},{12,0},{1,5},{5,9},{9,13},{13,1},{2,6},{6,10},{... | collective-permute-start | bytes 245768 | tf_op jit(solution)/shard_map/ppermute | solution.py:153
  (3 other events, 1.9 us)
Sparse Core Ops, SparseCore 0:
  10.7 57.3 all-gather.1

commit v3 on v2

v3 whole, which is shorter than its diff:
```python
import functools

import jax
import jax.numpy as jnp
from jax import lax
from jax.experimental import pallas as pl
from jax.experimental.pallas import tpu as pltpu
from jax.sharding import PartitionSpec as P

HEAD_DIM = 80
DG = 32
BLOCK_ROWS = 32
F32 = jnp.float32
BF16 = jnp.bfloat16

VMEM = pl.BlockSpec(memory_space=pltpu.VMEM)
SMEM = pl.BlockSpec(memory_space=pltpu.SMEM)
HBM = pl.BlockSpec(memory_space=pltpu.HBM)


def dot(a, b):
    return jnp.dot(a, b, preferred_element_type=F32)


def dot_nt(a, b):
    return lax.dot_general(a, b, (((1,), (1,)), ((), ())), preferred_element_type=F32)


def dot_tn(a, b):
    return lax.dot_general(a, b, (((0,), (0,)), ((), ())), preferred_element_type=F32)


def run_all(moves):
    for move in moves:
        move.start()
    for move in moves:
        move.wait()


def pick_kernel(part, spot_ref, w_ref, out_ref, windows, sems):
    height = out_ref.shape[0]
    channels = w_ref.shape[1] // 3
    first = pl.multiple_of(spot_ref[0], 16)
    group = spot_ref[1]
    odd = lax.rem(group, 2)
    wide = windows.shape[2]
    start = (group // 2) * (2 * part) + odd * (2 * part - wide)
    run_all(
        [
            pltpu.make_async_copy(
                w_ref.at[
                    pl.ds(first, height), pl.ds(pl.multiple_of(i * channels + start, 128), wide)
                ],
                windows.at[i],
                sems.at[i],
            )
            for i in range(3)
        ]
    )
    pieces = []
    for i in range(3):
        window = windows[i]
        pieces.append(jnp.where(odd == 1, window[:, wide - part :], window[:, :part]))
    out_ref[...] = jnp.concatenate(pieces, axis=1)


def norm_kernel(visible_ref, pos_ref, gain_ref, bias_ref, *refs):
    groups = len(refs) - 7
    token_refs = refs[:groups]
    normed_out, unit_out, own_unit_ref, own_inv_ref, normed_ref, unit_ref, sems = refs[groups:]
    slots, rows, width = token_refs[0].shape
    gain = gain_ref[...]
    bias = bias_ref[...]
    moves = []
    for p in range(slots):
        iota = lax.broadcasted_iota(jnp.int32, (8, pos_ref.shape[0]), 1)
        onehot = (iota == visible_ref[p]).astype(F32).astype(BF16)
        position = dot(onehot, pos_ref[...])[0:1]
        for s in range(groups):
            embedded = (token_refs[s][p].astype(F32) + position).astype(BF16).astype(F32)
            centred = embedded - jnp.mean(embedded, axis=-1, keepdims=True)
            inv_std = lax.rsqrt(jnp.mean(centred * centred, axis=-1, keepdims=True) + 1e-06)
            unit = centred * inv_std
            normed_ref[p, s] = (unit * gain + bias).astype(BF16)
            unit_ref[p, s] = unit.astype(BF16)
            if s == 0:
                own_unit_ref[p] = unit
                own_inv_ref[p] = jnp.broadcast_to(inv_std, own_inv_ref.shape[1:])
        for i, (here, out) in enumerate(((normed_ref, normed_out), (unit_ref, unit_out))):
            moves.append(pltpu.make_async_copy(here.at[p], out.at[p], sems.at[2 * p + i]))
            moves[-1].start()
    for move in moves:
        move.wait()


def weight_moves(places_ref, chunk_refs, weights, sems):
    return [
        pltpu.make_async_copy(
            ref,
            weights.at[pl.ds(pl.multiple_of(places_ref[c], 16), ref.shape[0]), :],
            sems.at[c],
        )
        for c, ref in enumerate(chunk_refs)
    ]


def attend_kernel(chunks, where_ref, live_ref, places_ref, normed_hbm, up_ref, valid_ref, *refs):
    groups, slots, rows, channels = up_ref.shape
    chunk_refs = refs[:chunks]
    context_outs = refs[chunks : chunks + groups]
    gqkv_out, weights, normed, qkv_ref, gqkv_ref, context_ref, sems, out_sems = refs[chunks + groups :]
    dates = groups * rows
    heads = channels // HEAD_DIM
    inv_scale = 1.0 / HEAD_DIM**0.5
    run_all(
        weight_moves(places_ref, chunk_refs, weights, sems)
        + [pltpu.make_async_copy(normed_hbm, normed, sems.at[chunks])]
    )
    qkv_ref[...] = dot(normed[...], weights[...]).astype(BF16)
    valid_rows = jnp.concatenate(
        [valid_ref[pl.ds(pl.multiple_of(where_ref[s] * rows, rows), rows), :] for s in range(groups)],
        axis=0,
    )
    moves = []
    for p in range(slots):
        span = slice(p * dates, (p + 1) * dates)
        alive = (live_ref[0] > p // (BLOCK_ROWS // DG)).astype(F32)
        rows_qkv = qkv_ref[span, :]
        upstream = jnp.concatenate([up_ref[where_ref[s], p] for s in range(groups)], axis=0)
        upstream = upstream * alive.astype(BF16)
        allowed = valid_rows[:, p : p + 1] > 0
        grads = [[], [], []]
        contexts = []
        for h in range(heads):
            q, k, v = (
                rows_qkv[:, i * channels + h * HEAD_DIM : i * channels + (h + 1) * HEAD_DIM]
                for i in range(3)
            )
            up = upstream[:, h * HEAD_DIM : (h + 1) * HEAD_DIM]
            scores = jnp.where(allowed, dot_nt(k, q) * inv_scale, -1e30)
            exps = jnp.exp(scores - jnp.max(scores, axis=0, keepdims=True))
            probs = exps * (1.0 / jnp.sum(exps, axis=0, keepdims=True))
            low = probs.astype(BF16)
            contexts.append(dot_tn(low, v) * alive)
            grads[2].append(dot(low, up))
            gprobs = dot_nt(v, up)
            gscores = probs * (gprobs - jnp.sum(probs * gprobs, axis=0, keepdims=True)) * inv_scale
            glow = gscores.astype(BF16)
            grads[0].append(dot_tn(glow, k))
            grads[1].append(dot(glow, q))
        gqkv_ref[span, :] = jnp.concatenate(grads[0] + grads[1] + grads[2], axis=1).astype(BF16)
        context_ref[span, :] = jnp.concatenate(contexts, axis=1).astype(BF16)
        first = len(moves)
        moves.append(pltpu.make_async_copy(gqkv_ref.at[span], gqkv_out.at[span], out_sems.at[first]))
        for s in range(groups):
            piece = context_ref.at[pl.ds(p * dates + s * rows, rows)]
            moves.append(
                pltpu.make_async_copy(piece, context_outs[s].at[p], out_sems.at[first + 1 + s])
            )
        for move in moves[first:]:
            move.start()
    for move in moves:
        move.wait()


def back_kernel(chunks, copies, places_ref, gqkv_hbm, unit_hbm, *refs):
    chunk_refs = refs[:chunks]
    stay_out, cross_out, sums_ref, weights, gqkv, unit, stay, cross, sems, out_sems = refs[chunks:]
    halves, slots, rows, width = stay.shape
    groups = 2 * halves
    dates = groups * rows
    unit_move = pltpu.make_async_copy(unit_hbm, unit, sems.at[chunks + 1])
    unit_move.start()
    run_all(
        weight_moves(places_ref, chunk_refs, weights, sems)
        + [pltpu.make_async_copy(gqkv_hbm, gqkv, sems.at[chunks])]
    )
    unit_move.wait()
    step = 256
    moves = []
    for n in range(width // step):
        lanes = slice(n * step, (n + 1) * step)
        partial = dot_nt(gqkv[...], weights[lanes, :])
        low = partial.astype(BF16)
        for p in range(slots):
            for s in range(groups):
                at = p * dates + s * rows
                (cross if s % 2 else stay)[s // 2, p, :, lanes] = low[at : at + rows]
        sums_ref[0, 0:1, lanes] = jnp.sum(partial * unit[:, lanes].astype(F32), axis=0, keepdims=True)
        sums_ref[0, 1:2, lanes] = jnp.sum(partial, axis=0, keepdims=True)
        for i, (here, out) in enumerate(((cross, cross_out), (stay, stay_out))):
            spot = pl.ds(n * step, step)
            moves.append(
                pltpu.make_async_copy(
                    here.at[:, :, :, spot], out.at[:, :, :, spot], out_sems.at[2 * n + i]
                )
            )
            moves[-1].start()
    for c in range(1, copies):
        sums_ref[c] = sums_ref[0]
    for move in moves:
        move.wait()


def finish_kernel(where_ref, live_ref, unit_ref, inv_ref, gain_ref, sums_ref, stay_ref, near_ref, far_ref, *refs):
    groups = len(refs) - 4
    context_refs = refs[:groups]
    attended_ref, out_ref, norm_ref, held = refs[groups:]
    slots, rows, width = unit_ref.shape
    gain = gain_ref[...]
    for s in range(groups):
        held[where_ref[s]] = context_refs[s][...]
    for p in range(slots):
        alive = (live_ref[0] > p // (BLOCK_ROWS // DG)).astype(F32)
        grad = stay_ref[p].astype(F32) + near_ref[p].astype(F32) + far_ref[p].astype(F32)
        unit = unit_ref[p]
        scaled = grad * gain
        out = inv_ref[p][:, 0:1] * (
            scaled
            - jnp.mean(scaled, axis=-1, keepdims=True)
            - unit * jnp.mean(scaled * unit, axis=-1, keepdims=True)
        )
        out_ref[p] = (out * alive).astype(BF16)
        attended_ref[p] = jnp.concatenate([held[g, p] for g in range(groups)], axis=1)
    norm_ref[...] = jnp.sum(sums_ref[...], axis=0)


def swapped(array, axis, bits):
    return lax.ppermute(array, axis, [(i, i ^ bits) for i in range(lax.axis_size(axis))])


def params(megabytes):
    return pltpu.CompilerParams(vmem_limit_bytes=megabytes * 1024 * 1024)


def pick(w_qkv, first, height, group, part):
    wide = -(-part // 128) * 128
    spot = jnp.stack([jnp.asarray(first, jnp.int32), group.astype(jnp.int32)])
    return pl.pallas_call(
        functools.partial(pick_kernel, part),
        out_shape=jax.ShapeDtypeStruct((height, 3 * part), BF16),
        in_specs=[SMEM, HBM],
        out_specs=VMEM,
        scratch_shapes=[pltpu.VMEM((3, height, wide), BF16), pltpu.SemaphoreType.DMA((3,))],
        compiler_params=params(4),
        cost_estimate=pl.CostEstimate(flops=10**5, bytes_accessed=10**6, transcendentals=0),
        name="pick",
    )(spot, w_qkv)


def gather_weights(w_qkv, group, part):
    owners = lax.axis_size("tile")
    owner = lax.axis_index("tile")
    rep = lax.axis_index("rep")
    depth, triple = w_qkv.shape
    share = depth // 2
    if owners != 4 or lax.axis_size("rep") != 2 or share % 16:
        mine = jnp.concatenate(
            [
                lax.dynamic_slice_in_dim(w_qkv, i * (triple // 3) + group * part, part, 1)
                for i in range(3)
            ],
            axis=1,
        )
        return [lax.all_gather(mine, "tile", axis=0, tiled=True)], [0]
    ring = [0, 1, 3, 2]
    held = pick(w_qkv, rep * share, share, group, part)
    rest = pick(w_qkv, (1 - rep) * share, share, group, part)
    pieces = [held, rest]
    places = [owner * depth + rep * share, owner * depth + (1 - rep) * share]
    spot = owner ^ (owner >> 1)
    for step in range(1, owners):
        held = lax.ppermute(held, "tile", [(ring[i], ring[(i + 1) % owners]) for i in range(owners)])
        back = (spot - step) % owners
        source = back ^ (back >> 1)
        pieces += [held, swapped(held, "rep", 1)]
        places += [source * depth + rep * share, source * depth + (1 - rep) * share]
    return pieces, places


def local(tokens, cotangent, valid, visible, live, pos_table, norm_gain, norm_bias, w_qkv):
    slots, rows, width = tokens.shape
    groups = lax.axis_size("date")
    owners = lax.axis_size("tile")
    group = lax.axis_index("date")
    owner = lax.axis_index("tile")
    channels = w_qkv.shape[1] // 3
    part = channels // groups
    dates = rows * groups
    live_here = lax.dynamic_slice_in_dim(live, owner, 1, 0)
    where = jnp.stack([group ^ s for s in range(groups)]).astype(jnp.int32)

    pieces, places = gather_weights(w_qkv, group, part)
    places = jnp.stack([jnp.asarray(p, jnp.int32) for p in places])
    chunks = len(pieces)

    across = swapped(tokens, "date", 2)
    gathered = [tokens, swapped(tokens, "date", 1), across, swapped(across, "date", 1)]
    columns = cotangent.reshape(slots, rows, groups, part).transpose(2, 0, 1, 3)
    upstream = lax.all_to_all(columns, "date", split_axis=0, concat_axis=0, tiled=True)

    gain2, bias2 = norm_gain.reshape(1, width), norm_bias.reshape(1, width)
    normed, unit, own_unit, own_inv = pl.pallas_call(
        norm_kernel,
        out_shape=(
            jax.ShapeDtypeStruct((slots, groups, rows, width), BF16),
            jax.ShapeDtypeStruct((slots, groups, rows, width), BF16),
            jax.ShapeDtypeStruct((slots, rows, width), F32),
            jax.ShapeDtypeStruct((slots, rows, 128), F32),
        ),
        in_specs=[SMEM] + [VMEM] * (3 + groups),
        out_specs=(HBM, HBM, VMEM, VMEM),
        scratch_shapes=[
            pltpu.VMEM((slots, groups, rows, width), BF16),
            pltpu.VMEM((slots, groups, rows, width), BF16),
            pltpu.SemaphoreType.DMA((2 * slots,)),
        ],
        compiler_params=params(12),
        cost_estimate=pl.CostEstimate(flops=10**7, bytes_accessed=6 * 10**6, transcendentals=1000),
        name="norm",
    )(visible, pos_table, gain2, bias2, *gathered)

    results = pl.pallas_call(
        functools.partial(attend_kernel, chunks),
        out_shape=(jax.ShapeDtypeStruct((slots, rows, part), BF16),) * groups
        + (jax.ShapeDtypeStruct((slots * dates, 3 * part), BF16),),
        in_specs=[SMEM, SMEM, SMEM, HBM, VMEM, VMEM] + [HBM] * chunks,
        out_specs=(HBM,) * (groups + 1),
        scratch_shapes=[
            pltpu.VMEM((width, 3 * part), BF16),
            pltpu.VMEM((slots * dates, width), BF16),
            pltpu.VMEM((slots * dates, 3 * part), BF16),
            pltpu.VMEM((slots * dates, 3 * part), BF16),
            pltpu.VMEM((slots * dates, part), BF16),
            pltpu.SemaphoreType.DMA((chunks + 1,)),
            pltpu.SemaphoreType.DMA((slots * (groups + 1),)),
        ],
        compiler_params=params(20),
        cost_estimate=pl.CostEstimate(flops=3 * 10**9, bytes_accessed=10**7, transcendentals=10**6),
        name="attend",
    )(where, live_here, places, normed.reshape(slots * dates, width), upstream, valid.T, *pieces)
    contexts, gqkv = results[:groups], results[-1]

    copies = groups * owners if owners == 4 else 1
    half = (groups // 2, slots, rows, width)
    stay, cross, sums = pl.pallas_call(
        functools.partial(back_kernel, chunks, copies),
        out_shape=(
            jax.ShapeDtypeStruct(half, BF16),
            jax.ShapeDtypeStruct(half, BF16),
            jax.ShapeDtypeStruct((copies, 2, width), F32),
        ),
        in_specs=[SMEM, HBM, HBM] + [HBM] * chunks,
        out_specs=(HBM, HBM, VMEM),
        scratch_shapes=[
            pltpu.VMEM((width, 3 * part), BF16),
            pltpu.VMEM((slots * dates, 3 * part), BF16),
            pltpu.VMEM((slots * dates, width), BF16),
            pltpu.VMEM(half, BF16),
            pltpu.VMEM(half, BF16),
            pltpu.SemaphoreType.DMA((chunks + 2,)),
            pltpu.SemaphoreType.DMA((2 * (width // 256),)),
        ],
        compiler_params=params(20),
        cost_estimate=pl.CostEstimate(flops=2 * 10**9, bytes_accessed=10**7, transcendentals=0),
        name="back",
    )(places, gqkv, unit.reshape(slots * dates, width), *pieces)

    context_home = [contexts[0]] + [swapped(contexts[s], "date", s) for s in range(1, groups)]
    near = swapped(cross, "date", 1)
    chip_sum = (stay[1].astype(F32) + near[1].astype(F32)).astype(BF16)
    far = swapped(chip_sum, "date", 2)
    if copies > 1:
        sums = lax.all_to_all(sums, ("date", "tile"), split_axis=0, concat_axis=0, tiled=True)
    else:
        sums = lax.psum(sums, ("date", "tile"))

    return pl.pallas_call(
        finish_kernel,
        out_shape=(
            jax.ShapeDtypeStruct((slots, rows, channels), BF16),
            jax.ShapeDtypeStruct((slots, rows, width), BF16),
            jax.ShapeDtypeStruct((2, width), F32),
        ),
        in_specs=[SMEM, SMEM] + [VMEM] * (7 + groups),
        out_specs=(VMEM,) * 3,
        scratch_shapes=[pltpu.VMEM((groups, slots, rows, part), BF16)],
        compiler_params=params(12),
        cost_estimate=pl.CostEstimate(flops=10**7, bytes_accessed=4 * 10**6, transcendentals=0),
        name="finish",
    )(where, live_here, own_unit, own_inv, gain2, sums, stay[0], near[0], far, *context_home)


def solution(mesh):
    in_specs = (
        P(("rep", "tile"), "date", None),
        P(("rep", "tile"), "date", None),
        P(("rep", "tile"), None),
        P(("rep", "tile")),
        P("rep"),
        P(),
        P(),
        P(),
        P("tile", None),
    )
    out_specs = (P(("rep", "tile"), "date", None), P(("rep", "tile"), "date", None), P("rep", None))
    return jax.shard_map(local, mesh=mesh, in_specs=in_specs, out_specs=out_specs, check_vma=False)
```

time: 117 us -> 92.6 us (0.79)
  waiting for transfers between devices: 56 us -> 33.5 us
  between operations: 14.3 us -> 0.89 us
  Pallas kernels: 13.6 us -> 24.1 us
  starting transfers between devices: 18.5 us -> 22.6 us
  local copies, waits for them, and re-layouts: 12.8 us -> 9.72 us
    all_gather x1 -> x0, waiting for transfers between devices: 35.9 us -> none  [local(): weights = lax.all_gather(mine, ('rep', 'tile'), axis=0, tiled=True)]
    ppermute x9 -> x14, waiting for transfers between devices: 20.1 us -> 33.5 us  [the longest x3 22.1 us: gather_weights(): lax.ppermute(held, 'tile', [(ring[i], ring[(i + 1) % owners]) for i in ra...]
    pallas_call x1 -> x4, Pallas kernels: 9.24 us -> 17.4 us  [the longest x1 8.91 us: local(): pl.pallas_call(functools.partial(attend_kernel, chunks), out_shape=(jax.S...]
    ppermute x9 -> x14, starting transfers between devices: 10.8 us -> 13.2 us  [the longest x11 8.89 us: swapped(): lax.ppermute(array, axis, [(i, i ^ bits) for i in range(lax.axis_size(axi...]
    pallas_call x1, Pallas kernels: 1.94 us -> 4.25 us  [local(): pl.pallas_call(norm_kernel, out_shape=(jax.ShapeDtypeStruct((slots, group...]
    unnamed x31 -> x39, local copies, waits for them, and re-layouts: 8.59 us -> 6.77 us
    all_to_all x1, starting transfers between devices: 4.24 us -> 5.9 us  [local(): lax.all_to_all(sums, ('date', 'tile'), split_axis=0, concat_axis=0, tiled...]
    dynamic_slice x1 -> x0, local copies, waits for them, and re-layouts: 1.45 us -> none  [local(): lax.dynamic_slice(w_qkv, (first, i * channels + group * part), (height, p...]
  transfers between devices with their start and end apart: 12 -> 16, of which waited for: 6 -> 7; matrix products, arithmetic and copies ran while one was open for 3% -> 5% of each run, Pallas kernels for 2% -> 6%
where the time goes in v3:
time: 92.6 us; the launch traced here: 92 us
  waiting for transfers between devices  33.5 us (36%)
  Pallas kernels  24.1 us (26%)
  starting transfers between devices  22.6 us (24%)
  local copies, waits for them, and re-layouts  9.72 us (10%)
  other arithmetic  1.28 us (1%)
    ppermute x3, waiting for transfers between devices, gather_weights(): lax.ppermute(held, 'tile', [(ring[i], ring[(i + 1) % owners]) for i in ra...  22.1 us
    ppermute x11, waiting for transfers between devices, swapped(): lax.ppermute(array, axis, [(i, i ^ bits) for i in range(lax.axis_size(axi...  11.4 us
    pallas_call x1, Pallas kernels, local(): pl.pallas_call(functools.partial(attend_kernel, chunks), out_shape=(jax.S...  8.91 us
    ppermute x11, starting transfers between devices, swapped(): lax.ppermute(array, axis, [(i, i ^ bits) for i in range(lax.axis_size(axi...  8.89 us
    unnamed x39, local copies, waits for them, and re-layouts  6.77 us
    pallas_call x1, Pallas kernels, local(): pl.pallas_call(functools.partial(back_kernel, chunks, copies), out_shape=...  6.71 us
    all_to_all x1, starting transfers between devices, local(): lax.all_to_all(sums, ('date', 'tile'), split_axis=0, concat_axis=0, tiled...  5.9 us
    ppermute x3, starting transfers between devices, gather_weights(): lax.ppermute(held, 'tile', [(ring[i], ring[(i + 1) % owners]) for i in ra...  4.32 us
  transfers between devices with their start and end apart: 16, of which 7 were waited for; matrix products, arithmetic and copies ran while one was open for 5% of the time, Pallas kernels for 6%

profile of v3, /device:TPU:0, one launch (start us, length us, event | category | flops | bytes accessed | tf_op | source)
XLA Modules:
  0.0 92.0 jit_solution(3296818423028173164)
XLA Ops:
  0.7 1.7 %copy-done = bf16[320,3840]{1,0:T(8,128)(2,1)S(1)} copy-done((bf16[320,3840]{1,0:T(8,128)(2,1)S(1)}, bf16[320,3840]{1,0:T(8,128)(2,1)}, u32[]{:S(2)}) %copy-start) | copy-done | bytes 2457624
  3.3 3.1 %collective-permute-start.3 = (bf16[160,960]{1,0:T(8,128)(2,1)S(1)}, bf16[160,960]{1,0:T(8,128)(2,1)}, u32[]{:S(2)}, u32[]{:S(2)}) collective-permute-start(bf16[160,960]{1,0:T(8,128)(2,1)S(1)} %pick.2.refs_0_), channel_id=1, source_target_pairs={{0,1},{1,3},{3,2},{2,0},{4,5},{5,7},{7,6},{6,4},{8,9},{9,11},{11,1... | collective-permute-start | bytes 921608 | tf_op jit(solution)/shard_map/ppermute | solution.py:273
  7.1 8.1 %collective-permute-done.3.refs_2_ = bf16[160,960]{1,0:T(8,128)(2,1)} collective-permute-done((bf16[160,960]{1,0:T(8,128)(2,1)S(1)}, bf16[160,960]{1,0:T(8,128)(2,1)}, u32[]{:S(2)}, u32[]{:S(2)}) %collective-permute-start.3) | collective-permute-done | bytes 307232 | tf_op jit(solution)/shard_map/ppermute | solution.py:273
  16.0 1.5 %collective-permute-start.1 = (bf16[4,32,1280]{2,1,0:T(8,128)(2,1)}, bf16[4,32,1280]{2,1,0:T(8,128)(2,1)}, u32[]{:S(2)}, u32[]{:S(2)}) collective-permute-start(bf16[4,32,1280]{2,1,0:T(8,128)(2,1)} %refs_0_.1), channel_id=1, source_target_pairs={{0,8},{4,12},{8,0},{12,4},{1,9},{5,13},{9,1},{13,5},{2,10},{6,14},... | collective-permute-start | bytes 983048 | tf_op jit(solution)/shard_map/ppermute | solution.py:229
  17.4 7.9 %collective-permute-done.5.refs_4_ = bf16[160,960]{1,0:T(8,128)(2,1)} collective-permute-done((bf16[160,960]{1,0:T(8,128)(2,1)}, bf16[160,960]{1,0:T(8,128)(2,1)}, u32[]{:S(2)}, u32[]{:S(2)}) %collective-permute-start.5) | collective-permute-done | bytes 307232 | tf_op jit(solution)/shard_map/ppermute | solution.py:273
  26.4 1.5 %collective-permute-start.4 = (bf16[160,960]{1,0:T(8,128)(2,1)}, bf16[160,960]{1,0:T(8,128)(2,1)}, u32[]{:S(2)}, u32[]{:S(2)}) collective-permute-start(bf16[160,960]{1,0:T(8,128)(2,1)} %collective-permute-done.3.refs_2_), channel_id=1, source_target_pairs={{0,16},{16,0},{1,17},{17,1},{2,18},{18,2},{3,19},{19,3},{4,20},{20... | collective-permute-start | bytes 921608 | tf_op jit(solution)/shard_map/ppermute | solution.py:229
  28.4 6.1 %collective-permute-done.7.refs_6_ = bf16[160,960]{1,0:T(8,128)(2,1)} collective-permute-done((bf16[160,960]{1,0:T(8,128)(2,1)}, bf16[160,960]{1,0:T(8,128)(2,1)}, u32[]{:S(2)}, u32[]{:S(2)}) %collective-permute-start.7) | collective-permute-done | bytes 307232 | tf_op jit(solution)/shard_map/ppermute | solution.py:273
  36.7 3.5 %all-to-all-start = ((bf16[4,4,32,320]{3,2,1,0:T(8,128)(2,1)}), bf16[4,4,32,320]{3,2,1,0:T(8,128)(2,1)S(1)}, u32[]{:S(2)}, u32[]{:S(2)}) async-start(bf16[4,4,32,320]{3,2,1,0:T(8,128)(2,1)} %bitcast.25), calls=%async_computation | async-start | bytes 786432 | tf_op jit(solution)/shard_map/all_to_all | solution.py:300
  42.9 4.3 %norm.1 = (bf16[4,4,32,1280]{3,2,1,0:T(8,128)(2,1)S(1)}, bf16[4,4,32,1280]{3,2,1,0:T(8,128)(2,1)S(1)}, f32[4,32,1280]{2,1,0:T(8,128)S(1)}, f32[4,32,128]{2,1,0:T(8,128)S(1)}) custom-call(s32[4]{0:T(128)S(1)} %copy-done.9, bf16[256,1280]{1,0:T(8,128)(2,1)S(1)} %copy-done.2, f32[1,1280]{1,0:T(1,128)S(1)} %reshape.25.gain_ref, f32[1,1280]{1,0:T(1,128)S(1)} %reshape.26.bias_ref, ...), custom_call_target="tpu_custom_call" | custom-call | flops 10000000 | bytes 6000000 | tf_op jit(solution)/shard_map/norm/pallas_call | solution.py:303
  47.1 1.1 %copy-done.10 = bf16[4,4,32,1280]{3,2,1,0:T(8,128)(2,1)} copy-done((bf16[4,4,32,1280]{3,2,1,0:T(8,128)(2,1)}, bf16[4,4,32,1280]{3,2,1,0:T(8,128)(2,1)S(1)}, u32[]{:S(2)}) %copy-start.10) | copy-done | bytes 1310744
  48.2 1.1 %copy-done.12 = bf16[4,4,32,1280]{3,2,1,0:T(8,128)(2,1)} copy-done((bf16[4,4,32,1280]{3,2,1,0:T(8,128)(2,1)}, bf16[4,4,32,1280]{3,2,1,0:T(8,128)(2,1)S(1)}, u32[]{:S(2)}) %copy-start.12) | copy-done | bytes 1310744
  49.3 1.0 %collective-permute-done.8.refs_7_ = bf16[160,960]{1,0:T(8,128)(2,1)} collective-permute-done((bf16[160,960]{1,0:T(8,128)(2,1)}, bf16[160,960]{1,0:T(8,128)(2,1)}, u32[]{:S(2)}, u32[]{:S(2)}) %collective-permute-start.8) | collective-permute-done | bytes 307232 | tf_op jit(solution)/shard_map/ppermute | solution.py:229
  50.4 1.3 %copy-done.13 = bf16[4,4,32,1280]{3,2,1,0:T(8,128)(2,1)S(1)} copy-done((bf16[4,4,32,1280]{3,2,1,0:T(8,128)(2,1)S(1)}, bf16[4,4,32,1280]{3,2,1,0:T(8,128)(2,1)}, u32[]{:S(2)}) %copy-start.13) | copy-done | bytes 1310744
  51.7 8.9 %attend.1 = (bf16[4,32,320]{2,1,0:T(8,128)(2,1)S(1)}, bf16[4,32,320]{2,1,0:T(8,128)(2,1)}, bf16[4,32,320]{2,1,0:T(8,128)(2,1)}, bf16[4,32,320]{2,1,0:T(8,128)(2,1)}, bf16[512,960]{1,0:T(8,128)(2,1)S(1)}) custom-call(s32[4]{0:T(128)S(1)} %pad_add_fusion.where_ref, s32[1]{0:T(128)} %dynamic_slice.3.live_ref, s32[8]{0:T(128)S(1)} %stack.69.places_ref, ...), custom_call_target="tpu_custom_call" | custom-call | flops 3000000000 | bytes 10000000 | tf_op jit(solution)/shard_map/attend/pallas_call | solution.py:323
  60.6 6.7 %back.1 = (bf16[2,4,32,1280]{3,2,1,0:T(8,128)(2,1)S(1)}, bf16[2,4,32,1280]{3,2,1,0:T(8,128)(2,1)S(1)}, f32[16,2,1280]{2,1,0:T(2,128)}) custom-call(s32[8]{0:T(128)S(1)} %stack.69.places_ref, bf16[512,960]{1,0:T(8,128)(2,1)S(1)} %get-tuple-element.18.gqkv_hbm, bf16[512,1280]{1,0:T(8,128)(2,1)S(1)} %bitcast.27, bf16[160,960]{1,0:T(8,128)(2,1)S(1)} %copy-done.4, ...), custom_call_target="tpu_custom_call" | custom-call | flops 2000000000 | bytes 10000000 | tf_op jit(solution)/shard_map/back/pallas_call | solution.py:346
  67.4 5.9 %all-to-all-start.1 = ((f32[16,2,1280]{2,1,0:T(2,128)}), f32[16,2,1280]{2,1,0:T(2,128)S(1)}, u32[]{:S(2)}, u32[]{:S(2)}) async-start(f32[16,2,1280]{2,1,0:T(2,128)} %get-tuple-element.20), calls=%async_computation.1 | async-start | bytes 327680 | tf_op jit(solution)/shard_map/all_to_all | solution.py:374
  73.7 1.7 %collective-permute-start.12 = (bf16[4,32,320]{2,1,0:T(8,128)(2,1)}, bf16[4,32,320]{2,1,0:T(8,128)(2,1)S(1)}, u32[]{:S(2)}, u32[]{:S(2)}) collective-permute-start(bf16[4,32,320]{2,1,0:T(8,128)(2,1)} %get-tuple-element.25), channel_id=1, source_target_pairs={{0,8},{4,12},{8,0},{12,4},{1,9},{5,13},{9,1},{13,5},{2,10},{6,14},... | collective-permute-start | bytes 245768 | tf_op jit(solution)/shard_map/ppermute | solution.py:229
  75.5 1.1 %fusion = bf16[4,32,1280]{2,1,0:T(8,128)(2,1)S(1)} fusion(bf16[2,4,32,1280]{3,2,1,0:T(8,128)(2,1)} %collective-permute-done.9, bf16[2,4,32,1280]{3,2,1,0:T(8,128)(2,1)S(1)} %get-tuple-element.21), kind=kLoop, calls=%fused_computation.2 | loop fusion | flops 655360 | bytes 983040 | tf_op jit(solution)/shard_map/convert_element_type | solution.py:371
  76.5 1.8 %collective-permute-start.10 = (bf16[4,32,1280]{2,1,0:T(8,128)(2,1)S(1)}, bf16[4,32,1280]{2,1,0:T(8,128)(2,1)S(1)}, u32[]{:S(2)}, u32[]{:S(2)}) collective-permute-start(bf16[4,32,1280]{2,1,0:T(8,128)(2,1)S(1)} %fusion), channel_id=1, source_target_pairs={{0,8},{4,12},{8,0},{12,4},{1,9},{5,13},{9,1},{13,5},{2,10},{6,14},... | collective-permute-start | bytes 983048 | tf_op jit(solution)/shard_map/ppermute | solution.py:229
  78.3 1.0 %slice_bitcast_fusion.near_ref = bf16[4,32,1280]{2,1,0:T(8,128)(2,1)S(1)} fusion(bf16[2,4,32,1280]{3,2,1,0:T(8,128)(2,1)} %collective-permute-done.9), kind=kLoop, calls=%fused_computation.3 | loop fusion | bytes 655360 | tf_op jit(solution)/shard_map/squeeze | solution.py:391
  79.3 1.3 %collective-permute-done.12.refs_2_ = bf16[4,32,320]{2,1,0:T(8,128)(2,1)S(1)} collective-permute-done((bf16[4,32,320]{2,1,0:T(8,128)(2,1)}, bf16[4,32,320]{2,1,0:T(8,128)(2,1)S(1)}, u32[]{:S(2)}, u32[]{:S(2)}) %collective-permute-start.12) | collective-permute-done | bytes 81952 | tf_op jit(solution)/shard_map/ppermute | solution.py:229
  80.6 1.6 %collective-permute-done.13.refs_3_ = bf16[4,32,320]{2,1,0:T(8,128)(2,1)S(1)} collective-permute-done((bf16[4,32,320]{2,1,0:T(8,128)(2,1)}, bf16[4,32,320]{2,1,0:T(8,128)(2,1)S(1)}, u32[]{:S(2)}, u32[]{:S(2)}) %collective-permute-start.13) | collective-permute-done | bytes 81952 | tf_op jit(solution)/shard_map/ppermute | solution.py:229
  82.2 7.4 %collective-permute-done.10.far_ref = bf16[4,32,1280]{2,1,0:T(8,128)(2,1)S(1)} collective-permute-done((bf16[4,32,1280]{2,1,0:T(8,128)(2,1)S(1)}, bf16[4,32,1280]{2,1,0:T(8,128)(2,1)S(1)}, u32[]{:S(2)}, u32[]{:S(2)}) %collective-permute-start.10) | collective-permute-done | bytes 327712 | tf_op jit(solution)/shard_map/ppermute | solution.py:229
  89.6 2.4 %finish.1 = (bf16[4,32,1280]{2,1,0:T(8,128)(2,1)}, bf16[4,32,1280]{2,1,0:T(8,128)(2,1)}, f32[2,1280]{1,0:T(2,128)}) custom-call(s32[4]{0:T(128)S(1)} %pad_add_fusion.where_ref, s32[1]{0:T(128)} %dynamic_slice.3.live_ref, f32[4,32,1280]{2,1,0:T(8,128)S(1)} %get-tuple-element.15.unit_ref, f32[4,32,128]{2,1,0:T(8,128)S(1)} %copy-done.8, ...), custom_call_target="tpu_custom_call" | custom-call | flops 10000000 | bytes 4000000 | tf_op jit(solution)/shard_map/finish/pallas_call | solution.py:378
  (65 shorter events, 9.3 us)
Async XLA Ops:
  2.4 33.0 %copy-start.14 = (bf16[4,32,1280]{2,1,0:T(8,128)(2,1)S(1)}, bf16[4,32,1280]{2,1,0:T(8,128)(2,1)}, u32[]{:S(2)}) copy-start(bf16[4,32,1280]{2,1,0:T(8,128)(2,1)} %param.10) | copy-start | bytes 983044
  2.4 37.8 %copy-start.1 = (bf16[320,3840]{1,0:T(8,128)(2,1)S(1)}, bf16[320,3840]{1,0:T(8,128)(2,1)}, u32[]{:S(2)}) copy-start(bf16[320,3840]{1,0:T(8,128)(2,1)} %w_ref.3) | copy-start | bytes 7372804
  3.3 11.9 %collective-permute-start.3 = (bf16[160,960]{1,0:T(8,128)(2,1)S(1)}, bf16[160,960]{1,0:T(8,128)(2,1)}, u32[]{:S(2)}, u32[]{:S(2)}) collective-permute-start(bf16[160,960]{1,0:T(8,128)(2,1)S(1)} %pick.2.refs_0_), channel_id=1, source_target_pairs={{0,1},{1,3},{3,2},{2,0},{4,5},{5,7},{7,6},{6,4},{8,9},{9,11},{11,1... | collective-permute-start | bytes 921608 | tf_op jit(solution)/shard_map/ppermute | solution.py:273
  15.2 10.1 %collective-permute-start.5 = (bf16[160,960]{1,0:T(8,128)(2,1)}, bf16[160,960]{1,0:T(8,128)(2,1)}, u32[]{:S(2)}, u32[]{:S(2)}) collective-permute-start(bf16[160,960]{1,0:T(8,128)(2,1)} %collective-permute-done.3.refs_2_), channel_id=1, source_target_pairs={{0,1},{1,3},{3,2},{2,0},{4,5},{5,7},{7,6},{6,4},{8,9},{9,11},{11,1... | collective-permute-start | bytes 921608 | tf_op jit(solution)/shard_map/ppermute | solution.py:273
  16.0 9.9 %collective-permute-start.1 = (bf16[4,32,1280]{2,1,0:T(8,128)(2,1)}, bf16[4,32,1280]{2,1,0:T(8,128)(2,1)}, u32[]{:S(2)}, u32[]{:S(2)}) collective-permute-start(bf16[4,32,1280]{2,1,0:T(8,128)(2,1)} %refs_0_.1), channel_id=1, source_target_pairs={{0,8},{4,12},{8,0},{12,4},{1,9},{5,13},{9,1},{13,5},{2,10},{6,14},... | collective-permute-start | bytes 983048 | tf_op jit(solution)/shard_map/ppermute | solution.py:229
  25.3 9.2 %collective-permute-start.7 = (bf16[160,960]{1,0:T(8,128)(2,1)}, bf16[160,960]{1,0:T(8,128)(2,1)}, u32[]{:S(2)}, u32[]{:S(2)}) collective-permute-start(bf16[160,960]{1,0:T(8,128)(2,1)} %collective-permute-done.5.refs_4_), channel_id=1, source_target_pairs={{0,1},{1,3},{3,2},{2,0},{4,5},{5,7},{7,6},{6,4},{8,9},{9,11},{11,1... | collective-permute-start | bytes 921608 | tf_op jit(solution)/shard_map/ppermute | solution.py:273
  25.9 17.0 %collective-permute-start = (bf16[4,32,1280]{2,1,0:T(8,128)(2,1)}, bf16[4,32,1280]{2,1,0:T(8,128)(2,1)}, u32[]{:S(2)}, u32[]{:S(2)}) collective-permute-start(bf16[4,32,1280]{2,1,0:T(8,128)(2,1)} %refs_0_.1), channel_id=1, source_target_pairs={{0,4},{4,0},{8,12},{12,8},{1,5},{5,1},{9,13},{13,9},{2,6},{6,2},{1... | collective-permute-start | bytes 983048 | tf_op jit(solution)/shard_map/ppermute | solution.py:229
  25.9 17.0 %collective-permute-start.2 = (bf16[4,32,1280]{2,1,0:T(8,128)(2,1)}, bf16[4,32,1280]{2,1,0:T(8,128)(2,1)}, u32[]{:S(2)}, u32[]{:S(2)}) collective-permute-start(bf16[4,32,1280]{2,1,0:T(8,128)(2,1)} %collective-permute-done.1.refs_2_), channel_id=1, source_target_pairs={{0,4},{4,0},{8,12},{12,8},{1,5},{5,1},{9,13},{13,9},{2,6},{6,2},{1... | collective-permute-start | bytes 983048 | tf_op jit(solution)/shard_map/ppermute | solution.py:229
  26.4 22.9 %collective-permute-start.4 = (bf16[160,960]{1,0:T(8,128)(2,1)}, bf16[160,960]{1,0:T(8,128)(2,1)}, u32[]{:S(2)}, u32[]{:S(2)}) collective-permute-start(bf16[160,960]{1,0:T(8,128)(2,1)} %collective-permute-done.3.refs_2_), channel_id=1, source_target_pairs={{0,16},{16,0},{1,17},{17,1},{2,18},{18,2},{3,19},{19,3},{4,20},{20... | collective-permute-start | bytes 921608 | tf_op jit(solution)/shard_map/ppermute | solution.py:229
  27.9 21.4 %collective-permute-start.6 = (bf16[160,960]{1,0:T(8,128)(2,1)}, bf16[160,960]{1,0:T(8,128)(2,1)}, u32[]{:S(2)}, u32[]{:S(2)}) collective-permute-start(bf16[160,960]{1,0:T(8,128)(2,1)} %collective-permute-done.5.refs_4_), channel_id=1, source_target_pairs={{0,16},{16,0},{1,17},{17,1},{2,18},{18,2},{3,19},{19,3},{4,20},{20... | collective-permute-start | bytes 921608 | tf_op jit(solution)/shard_map/ppermute | solution.py:229
  34.5 15.8 %collective-permute-start.8 = (bf16[160,960]{1,0:T(8,128)(2,1)}, bf16[160,960]{1,0:T(8,128)(2,1)}, u32[]{:S(2)}, u32[]{:S(2)}) collective-permute-start(bf16[160,960]{1,0:T(8,128)(2,1)} %collective-permute-done.7.refs_6_), channel_id=1, source_target_pairs={{0,16},{16,0},{1,17},{17,1},{2,18},{18,2},{3,19},{19,3},{4,20},{20... | collective-permute-start | bytes 921608 | tf_op jit(solution)/shard_map/ppermute | solution.py:229
  36.7 12.6 %all-to-all-start = ((bf16[4,4,32,320]{3,2,1,0:T(8,128)(2,1)}), bf16[4,4,32,320]{3,2,1,0:T(8,128)(2,1)S(1)}, u32[]{:S(2)}, u32[]{:S(2)}) async-start(bf16[4,4,32,320]{3,2,1,0:T(8,128)(2,1)} %bitcast.25), calls=%async_computation | async-start | bytes 786432 | tf_op jit(solution)/shard_map/all_to_all | solution.py:300
  40.3 2.6 %copy-start.2 = (bf16[256,1280]{1,0:T(8,128)(2,1)S(1)}, bf16[256,1280]{1,0:T(8,128)(2,1)}, u32[]{:S(2)}) copy-start(bf16[256,1280]{1,0:T(8,128)(2,1)} %pos_ref.1) | copy-start | bytes 1966084
  41.9 8.4 %copy-start.4 = (bf16[160,960]{1,0:T(8,128)(2,1)S(1)}, bf16[160,960]{1,0:T(8,128)(2,1)}, u32[]{:S(2)}) copy-start(bf16[160,960]{1,0:T(8,128)(2,1)} %copy-done.3) | copy-start | bytes 921604
  41.9 8.4 %copy-start.6 = (bf16[160,960]{1,0:T(8,128)(2,1)S(1)}, bf16[160,960]{1,0:T(8,128)(2,1)}, u32[]{:S(2)}) copy-start(bf16[160,960]{1,0:T(8,128)(2,1)} %copy-done.5) | copy-start | bytes 921604
  49.3 11.3 %copy-start.7 = (f32[4,32,128]{2,1,0:T(8,128)}, f32[4,32,128]{2,1,0:T(8,128)S(1)}, u32[]{:S(2)}) copy-start(f32[4,32,128]{2,1,0:T(8,128)S(1)} %get-tuple-element.16.inv_ref) | copy-start | bytes 196612
  51.7 8.9 %copy-start.11 = (bf16[4,4,32,1280]{3,2,1,0:T(8,128)(2,1)S(1)}, bf16[4,4,32,1280]{3,2,1,0:T(8,128)(2,1)}, u32[]{:S(2)}) copy-start(bf16[4,4,32,1280]{3,2,1,0:T(8,128)(2,1)} %copy-done.10) | copy-start | bytes 3932164
  67.3 8.1 %collective-permute-start.9 = (bf16[2,4,32,1280]{3,2,1,0:T(8,128)(2,1)S(1)}, bf16[2,4,32,1280]{3,2,1,0:T(8,128)(2,1)}, u32[]{:S(2)}, u32[]{:S(2)}) collective-permute-start(bf16[2,4,32,1280]{3,2,1,0:T(8,128)(2,1)S(1)} %get-tuple-element.22), channel_id=1, source_target_pairs={{0,4},{4,0},{8,12},{12,8},{1,5},{5,1},{9,13},{13,9},{2,6},{6,2},{1... | collective-permute-start | bytes 1966088 | tf_op jit(solution)/shard_map/ppermute | solution.py:229
  67.4 22.2 %copy-start.8 = (f32[4,32,128]{2,1,0:T(8,128)S(1)}, f32[4,32,128]{2,1,0:T(8,128)}, u32[]{:S(2)}) copy-start(f32[4,32,128]{2,1,0:T(8,128)} %copy-done.7) | copy-start | bytes 196612
  67.4 14.8 %all-to-all-start.1 = ((f32[16,2,1280]{2,1,0:T(2,128)}), f32[16,2,1280]{2,1,0:T(2,128)S(1)}, u32[]{:S(2)}, u32[]{:S(2)}) async-start(f32[16,2,1280]{2,1,0:T(2,128)} %get-tuple-element.20), calls=%async_computation.1 | async-start | bytes 327680 | tf_op jit(solution)/shard_map/all_to_all | solution.py:374
  73.3 5.9 %collective-permute-start.11 = (bf16[4,32,320]{2,1,0:T(8,128)(2,1)}, bf16[4,32,320]{2,1,0:T(8,128)(2,1)S(1)}, u32[]{:S(2)}, u32[]{:S(2)}) collective-permute-start(bf16[4,32,320]{2,1,0:T(8,128)(2,1)} %get-tuple-element.24), channel_id=1, source_target_pairs={{0,4},{4,0},{8,12},{12,8},{1,5},{5,1},{9,13},{13,9},{2,6},{6,2},{1... | collective-permute-start | bytes 245768 | tf_op jit(solution)/shard_map/ppermute | solution.py:229
  73.7 6.8 %collective-permute-start.12 = (bf16[4,32,320]{2,1,0:T(8,128)(2,1)}, bf16[4,32,320]{2,1,0:T(8,128)(2,1)S(1)}, u32[]{:S(2)}, u32[]{:S(2)}) collective-permute-start(bf16[4,32,320]{2,1,0:T(8,128)(2,1)} %get-tuple-element.25), channel_id=1, source_target_pairs={{0,8},{4,12},{8,0},{12,4},{1,9},{5,13},{9,1},{13,5},{2,10},{6,14},... | collective-permute-start | bytes 245768 | tf_op jit(solution)/shard_map/ppermute | solution.py:229
  75.4 6.8 %collective-permute-start.13 = (bf16[4,32,320]{2,1,0:T(8,128)(2,1)}, bf16[4,32,320]{2,1,0:T(8,128)(2,1)S(1)}, u32[]{:S(2)}, u32[]{:S(2)}) collective-permute-start(bf16[4,32,320]{2,1,0:T(8,128)(2,1)} %get-tuple-element.26), channel_id=1, source_target_pairs={{0,12},{4,8},{8,4},{12,0},{1,13},{5,9},{9,5},{13,1},{2,14},{6,10},... | collective-permute-start | bytes 245768 | tf_op jit(solution)/shard_map/ppermute | solution.py:229
  76.5 13.1 %collective-permute-start.10 = (bf16[4,32,1280]{2,1,0:T(8,128)(2,1)S(1)}, bf16[4,32,1280]{2,1,0:T(8,128)(2,1)S(1)}, u32[]{:S(2)}, u32[]{:S(2)}) collective-permute-start(bf16[4,32,1280]{2,1,0:T(8,128)(2,1)S(1)} %fusion), channel_id=1, source_target_pairs={{0,8},{4,12},{8,0},{12,4},{1,9},{5,13},{9,1},{13,5},{2,10},{6,14},... | collective-permute-start | bytes 983048 | tf_op jit(solution)/shard_map/ppermute | solution.py:229
  (11 other events, 16.1 us)

commit v4 on v2

v4 whole, which is shorter than its diff:
```python
import functools

import jax
import jax.numpy as jnp
from jax import lax
from jax.experimental import pallas as pl
from jax.experimental.pallas import tpu as pltpu
from jax.sharding import PartitionSpec as P

HEAD_DIM = 80
DG = 32
BLOCK_ROWS = 32
F32 = jnp.float32
BF16 = jnp.bfloat16

VMEM = pl.BlockSpec(memory_space=pltpu.VMEM)
SMEM = pl.BlockSpec(memory_space=pltpu.SMEM)
HBM = pl.BlockSpec(memory_space=pltpu.HBM)


def dot(a, b):
    return jnp.dot(a, b, preferred_element_type=F32)


def dot_nt(a, b):
    return lax.dot_general(a, b, (((1,), (1,)), ((), ())), preferred_element_type=F32)


def dot_tn(a, b):
    return lax.dot_general(a, b, (((0,), (0,)), ((), ())), preferred_element_type=F32)


def window_of(group, part):
    wide = -(-part // 128) * 128
    odd = lax.rem(group, 2)
    start = (group // 2) * (2 * part) + odd * (2 * part - wide)
    return start, wide, odd == 1


def pick_kernel(part, other, ids_ref, w_ref, out_ref, windows, sems):
    height = out_ref.shape[0]
    channels = w_ref.shape[1] // 3
    half = 1 - ids_ref[0] if other else ids_ref[0]
    first = pl.multiple_of(half * height, 16)
    start, wide, odd = window_of(ids_ref[1], part)
    moves = [
        pltpu.make_async_copy(
            w_ref.at[pl.ds(first, height), pl.ds(pl.multiple_of(i * channels + start, 128), wide)],
            windows.at[i],
            sems.at[i],
        )
        for i in range(3)
    ]
    for move in moves:
        move.start()
    for move in moves:
        move.wait()
    pieces = []
    for i in range(3):
        window = windows[i]
        pieces.append(jnp.where(odd, window[:, wide - part :], window[:, :part]))
    out_ref[...] = jnp.concatenate(pieces, axis=1)


def columns_kernel(ids_ref, cotangent_ref, *out_refs):
    part = out_refs[0].shape[2]
    for s, out_ref in enumerate(out_refs):
        start, wide, odd = window_of(ids_ref[1] ^ s, part)
        window = cotangent_ref[:, :, pl.ds(pl.multiple_of(start, 128), wide)]
        out_ref[...] = jnp.where(odd, window[:, :, wide - part :], window[:, :, :part])


def norm_kernel(visible_ref, pos_ref, gain_ref, bias_ref, *refs):
    groups = len(refs) - 4
    token_refs = refs[:groups]
    normed_ref, unit_ref, own_unit_ref, own_inv_ref = refs[groups:]
    slots, rows, width = token_refs[0].shape
    gain = gain_ref[...]
    bias = bias_ref[...]
    for p in range(slots):
        iota = lax.broadcasted_iota(jnp.int32, (8, pos_ref.shape[0]), 1)
        onehot = (iota == visible_ref[p]).astype(F32).astype(BF16)
        position = dot(onehot, pos_ref[...])[0:1]
        for s in range(groups):
            embedded = (token_refs[s][p].astype(F32) + position).astype(BF16).astype(F32)
            centred = embedded - jnp.mean(embedded, axis=-1, keepdims=True)
            inv_std = lax.rsqrt(jnp.mean(centred * centred, axis=-1, keepdims=True) + 1e-06)
            unit = centred * inv_std
            at = (p * groups + s) * rows
            normed_ref[at : at + rows] = (unit * gain + bias).astype(BF16)
            unit_ref[at : at + rows] = unit.astype(BF16)
            if s == 0:
                own_unit_ref[p] = unit
                own_inv_ref[p] = jnp.broadcast_to(inv_std, own_inv_ref.shape[1:])


def piece_rows(ids_ref, count, depth):
    if count == 1:
        return [0]
    rep, owner = ids_ref[0], ids_ref[2]
    owners = count // 2
    share = depth // 2
    spot = owner ^ (owner >> 1)
    firsts = []
    for step in range(owners):
        back = lax.rem(spot + owners - step, owners)
        source = back ^ (back >> 1)
        firsts.append(pl.multiple_of(source * depth + rep * share, 16))
        firsts.append(pl.multiple_of(source * depth + (1 - rep) * share, 16))
    return firsts


def attend_kernel(count, depth, ids_ref, live_ref, normed_ref, valid_ref, *refs):
    groups = (len(refs) - count - 3) // 2
    up_refs, piece_refs = refs[:groups], refs[groups : groups + count]
    context_refs = refs[groups + count : 2 * groups + count]
    gqkv_ref, weights, qkv_ref = refs[2 * groups + count :]
    slots, rows, channels = up_refs[0].shape
    dates = groups * rows
    heads = channels // HEAD_DIM
    inv_scale = 1.0 / HEAD_DIM**0.5
    for first, ref in zip(piece_rows(ids_ref, count, depth), piece_refs):
        weights[pl.ds(first, ref.shape[0]), :] = ref[...]
    qkv_ref[...] = dot(normed_ref[...], weights[...]).astype(BF16)
    valid_rows = jnp.concatenate(
        [
            valid_ref[pl.ds(pl.multiple_of((ids_ref[1] ^ s) * rows, rows), rows), :]
            for s in range(groups)
        ],
        axis=0,
    )
    for p in range(slots):
        span = slice(p * dates, (p + 1) * dates)
        alive = (live_ref[ids_ref[2]] > p // (BLOCK_ROWS // DG)).astype(F32)
        rows_qkv = qkv_ref[span, :]
        upstream = jnp.concatenate([ref[p] for ref in up_refs], axis=0) * alive.astype(BF16)
        allowed = valid_rows[:, p : p + 1] > 0
        grads = [[], [], []]
        contexts = []
        for h in range(heads):
            q, k, v = (
                rows_qkv[:, i * channels + h * HEAD_DIM : i * channels + (h + 1) * HEAD_DIM]
                for i in range(3)
            )
            up = upstream[:, h * HEAD_DIM : (h + 1) * HEAD_DIM]
            scores = jnp.where(allowed, dot_nt(k, q) * inv_scale, -1e30)
            exps = jnp.exp(scores - jnp.max(scores, axis=0, keepdims=True))
            probs = exps * (1.0 / jnp.sum(exps, axis=0, keepdims=True))
            low = probs.astype(BF16)
            contexts.append(dot_tn(low, v) * alive)
            grads[2].append(dot(low, up))
            gprobs = dot_nt(v, up)
            gscores = probs * (gprobs - jnp.sum(probs * gprobs, axis=0, keepdims=True)) * inv_scale
            glow = gscores.astype(BF16)
            grads[0].append(dot_tn(glow, k))
            grads[1].append(dot(glow, q))
        gqkv_ref[span, :] = jnp.concatenate(grads[0] + grads[1] + grads[2], axis=1).astype(BF16)
        context = jnp.concatenate(contexts, axis=1).astype(BF16)
        for s in range(groups):
            context_refs[s][p] = context[s * rows : (s + 1) * rows]


def back_kernel(gqkv_ref, unit_ref, weights, stay_ref, pass_ref, cross_ref, sums_ref):
    slots, rows, width = stay_ref.shape
    groups = 4
    dates = groups * rows
    step = 256
    for n in range(width // step):
        lanes = slice(n * step, (n + 1) * step)
        partial = dot_nt(gqkv_ref[...], weights[lanes, :])
        low = partial.astype(BF16)
        for p in range(slots):
            for s, out in enumerate((stay_ref, cross_ref.at[0], pass_ref, cross_ref.at[1])):
                at = p * dates + s * rows
                out[p, :, lanes] = low[at : at + rows]
        sums_ref[0:1, lanes] = jnp.sum(partial * unit_ref[:, lanes].astype(F32), axis=0, keepdims=True)
        sums_ref[1:2, lanes] = jnp.sum(partial, axis=0, keepdims=True)


def merge_kernel(pass_ref, near_ref, *refs):
    out_ref, total_ref = refs[-2:]
    out_ref[...] = (pass_ref[...].astype(F32) + near_ref[1].astype(F32)).astype(BF16)
    total = refs[0][...]
    for ref in refs[1:-2]:
        total = total + ref[...]
    total_ref[...] = total


def home_kernel(ids_ref, stay_ref, near_ref, *refs):
    groups = len(refs) - 3
    context_refs = refs[:groups]
    grad_ref, attended_ref, held = refs[groups:]
    grad_ref[...] = stay_ref[...].astype(F32) + near_ref[0].astype(F32)
    for s in range(groups):
        held[ids_ref[1] ^ s] = context_refs[s][...]
    for p in range(attended_ref.shape[0]):
        attended_ref[p] = jnp.concatenate([held[g, p] for g in range(groups)], axis=1)


def finish_kernel(ids_ref, live_ref, unit_ref, inv_ref, gain_ref, grad_ref, far_ref, *refs):
    out_ref, norm_ref = refs[-2:]
    slots = unit_ref.shape[0]
    gain = gain_ref[...]
    for p in range(slots):
        alive = (live_ref[ids_ref[2]] > p // (BLOCK_ROWS // DG)).astype(F32)
        unit = unit_ref[p]
        scaled = (grad_ref[p] + far_ref[p].astype(F32)) * gain
        out = inv_ref[p][:, 0:1] * (
            scaled
            - jnp.mean(scaled, axis=-1, keepdims=True)
            - unit * jnp.mean(scaled * unit, axis=-1, keepdims=True)
        )
        out_ref[p] = (out * alive).astype(BF16)
    total = refs[0][...]
    for ref in refs[1:-2]:
        total = total + ref[...]
    norm_ref[...] = total


def swapped(array, axis, bits):
    return lax.ppermute(array, axis, [(i, i ^ bits) for i in range(lax.axis_size(axis))])


def after(array, *others):
    return lax.optimization_barrier((array, *others))[0]


def near(array):
    return pltpu.with_memory_space_constraint(array, pltpu.VMEM)


def call(kernel, name, out_shape, in_specs, args, megabytes, flops=10**6, size=10**6, scratch=()):
    return pl.pallas_call(
        kernel,
        out_shape=out_shape,
        in_specs=in_specs,
        out_specs=jax.tree.map(lambda _: VMEM, out_shape),
        scratch_shapes=list(scratch),
        compiler_params=pltpu.CompilerParams(vmem_limit_bytes=megabytes * 1024 * 1024),
        cost_estimate=pl.CostEstimate(flops=flops, bytes_accessed=size, transcendentals=0),
        name=name,
    )(*args)


def pick(w_qkv, ids, share, part, other):
    wide = -(-part // 128) * 128
    return call(
        functools.partial(pick_kernel, part, other),
        "pick",
        pltpu.VMEM((share, 3 * part), BF16),
        [SMEM, HBM],
        (ids, pltpu.with_memory_space_constraint(w_qkv, pltpu.HBM)),
        4,
        scratch=(pltpu.VMEM((3, share, wide), BF16), pltpu.SemaphoreType.DMA((3,))),
    )


def local(tokens, cotangent, valid, visible, live, pos_table, norm_gain, norm_bias, w_qkv):
    slots, rows, width = tokens.shape
    groups = lax.axis_size("date")
    owners = lax.axis_size("tile")
    depth, triple = w_qkv.shape
    channels = triple // 3
    part = channels // groups
    dates = rows * groups
    ids = jnp.stack([lax.axis_index(name) for name in ("rep", "date", "tile")]).astype(jnp.int32)
    gain2, bias2 = norm_gain.reshape(1, width), norm_bias.reshape(1, width)
    valid_t = valid.T

    chain = owners == 4 and lax.axis_size("rep") == 2 and depth % 32 == 0
    ring = [(0, 1), (1, 3), (3, 2), (2, 0)]
    share = depth // 2
    if chain:
        held = pick(w_qkv, ids, share, part, False)
        first = lax.ppermute(held, "tile", ring)
        rest = pick(w_qkv, ids, share, part, True)
    across = swapped(tokens, "date", 2)
    beside = swapped(tokens, "date", 1)
    ups = call(
        columns_kernel,
        "columns",
        (jax.ShapeDtypeStruct((slots, rows, part), BF16),) * groups,
        [SMEM, VMEM],
        (ids, cotangent),
        4,
    )
    ups = [ups[0]] + [swapped(ups[s], "date", s) for s in range(1, groups)]
    beyond = swapped(across, "date", 1)
    if chain:
        first = after(first, across, *ups[1:])
        second = lax.ppermute(first, "tile", ring)
        first_other = swapped(first, "rep", 1)
        second = after(second, beside, beyond, first_other)
        third = lax.ppermute(second, "tile", ring)
        second_other = swapped(second, "rep", 1)
    gathered = [tokens, beside, across, beyond]

    normed, unit, own_unit, own_inv = call(
        norm_kernel,
        "norm",
        (
            pltpu.VMEM((slots * dates, width), BF16),
            pltpu.VMEM((slots * dates, width), BF16),
            pltpu.VMEM((slots, rows, width), F32),
            pltpu.VMEM((slots, rows, 128), F32),
        ),
        [SMEM] + [VMEM] * (3 + groups),
        (visible, pos_table, gain2, bias2, *gathered),
        12,
        flops=10**7,
        size=6 * 10**6,
    )
    if chain:
        third = after(third, normed, second_other)
        third_other = swapped(third, "rep", 1)
        pieces = [held, rest, first, first_other, second, second_other, third, third_other]
    else:
        group = lax.axis_index("date")
        mine = [
            lax.dynamic_slice_in_dim(w_qkv, i * channels + group * part, part, 1) for i in range(3)
        ]
        pieces = [lax.all_gather(jnp.concatenate(mine, axis=1), "tile", axis=0, tiled=True)]
    pieces = [near(piece) for piece in pieces]

    results = call(
        functools.partial(attend_kernel, len(pieces), depth),
        "attend",
        (pltpu.VMEM((slots, rows, part), BF16),) * groups
        + (pltpu.VMEM((slots * dates, 3 * part), BF16), pltpu.VMEM((width, 3 * part), BF16)),
        [SMEM] * 2 + [VMEM] * (2 + groups + len(pieces)),
        (ids, live, near(normed), valid_t, *ups, *pieces),
        20,
        flops=3 * 10**9,
        size=10**7,
        scratch=(pltpu.VMEM((slots * dates, 3 * part), BF16),),
    )
    contexts, gqkv, weights = results[:groups], results[groups], results[groups + 1]
    contexts = [contexts[0]] + [swapped(contexts[s], "date", s) for s in range(1, groups)]

    block = pltpu.VMEM((slots, rows, width), BF16)
    stay, passing, cross, sums = call(
        back_kernel,
        "back",
        (block, block, pltpu.VMEM((2, slots, rows, width), BF16), pltpu.VMEM((2, width), F32)),
        [VMEM] * 3,
        (near(gqkv), near(unit), near(weights)),
        12,
        flops=4 * 10**9,
        size=10**7,
    )

    close = swapped(cross, "date", 1)
    close = after(close, *contexts[1:])
    if owners == 4:
        tiles = [sums] + [swapped(sums, "tile", s) for s in range(1, owners)]
    else:
        tiles = [lax.psum(sums, ("date", "tile"))]
    chip, total = call(
        merge_kernel,
        "merge",
        (block, pltpu.VMEM((2, width), F32)),
        [VMEM] * (2 + len(tiles)),
        (passing, close, *tiles),
        6,
    )
    far = swapped(chip, "date", 2)
    totals = [total] + [swapped(total, "date", s) for s in range(1, groups)] if owners == 4 else [total]
    home, attended = call(
        home_kernel,
        "home",
        (pltpu.VMEM((slots, rows, width), F32), jax.ShapeDtypeStruct((slots, rows, channels), BF16)),
        [SMEM] + [VMEM] * (2 + groups),
        (ids, stay, close, *contexts),
        6,
        scratch=(pltpu.VMEM((groups, slots, rows, part), BF16),),
    )
    grad_tokens, grad_norm = call(
        finish_kernel,
        "finish",
        (
            jax.ShapeDtypeStruct((slots, rows, width), BF16),
            jax.ShapeDtypeStruct((2, width), F32),
        ),
        [SMEM] * 2 + [VMEM] * (5 + len(totals)),
        (ids, live, near(own_unit), near(own_inv), gain2, near(home), far, *totals),
        6,
    )
    return attended, grad_tokens, grad_norm


def solution(mesh):
    in_specs = (
        P(("rep", "tile"), "date", None),
        P(("rep", "tile"), "date", None),
        P(("rep", "tile"), None),
        P(("rep", "tile")),
        P("rep"),
        P(),
        P(),
        P(),
        P("tile", None),
    )
    out_specs = (P(("rep", "tile"), "date", None), P(("rep", "tile"), "date", None), P("rep", None))
    return jax.shard_map(local, mesh=mesh, in_specs=in_specs, out_specs=out_specs, check_vma=False)
```

time: 117 us -> 74.4 us (0.64)
  waiting for transfers between devices: 56 us -> 25 us
  between operations: 14.3 us -> 0.88 us
  starting transfers between devices: 18.5 us -> 26.8 us
  local copies, waits for them, and re-layouts: 12.8 us -> 4.99 us
  Pallas kernels: 13.6 us -> 16.5 us
    all_gather x1 -> x0, waiting for transfers between devices: 35.9 us -> none  [local(): weights = lax.all_gather(mine, ('rep', 'tile'), axis=0, tiled=True)]
    ppermute x9 -> x23, starting transfers between devices: 10.8 us -> 26.8 us  [the longest x20 20.8 us: swapped(): lax.ppermute(array, axis, [(i, i ^ bits) for i in range(lax.axis_size(axi...]
    all_to_all x2 -> x0, starting transfers between devices: 7.69 us -> none  [the longest x1 4.24 us: local(): lax.all_to_all(sums, ('date', 'tile'), split_axis=0, concat_axis=0, tiled...]
    ppermute x9 -> x23, waiting for transfers between devices: 20.1 us -> 25 us  [the longest x20 15.8 us: swapped(): lax.ppermute(array, axis, [(i, i ^ bits) for i in range(lax.axis_size(axi...]
    unnamed x31 -> x41, local copies, waits for them, and re-layouts: 8.59 us -> 4.98 us
    pallas_call x3 -> x9, Pallas kernels: 13.6 us -> 16.5 us  [call(): pl.pallas_call(kernel, out_shape=out_shape, in_specs=in_specs, out_specs=...]
    reshape x2 -> x0, local copies, waits for them, and re-layouts: 2.21 us -> none  [local(): columns = cotangent.reshape(slots, rows, groups, part).transpose(2, 0, 1, 3)]
    dynamic_slice x2 -> x0, local copies, waits for them, and re-layouts: 2 us -> none  [the longest x1 1.45 us: local(): lax.dynamic_slice(w_qkv, (first, i * channels + group * part), (height, p...]
  transfers between devices with their start and end apart: 12 -> 23, of which waited for: 6 -> 13; matrix products, arithmetic and copies ran while one was open for 3% -> 0% of each run, Pallas kernels for 2% -> 11%
where the time goes in v4:
time: 74.4 us; the launch traced here: 74.2 us
  starting transfers between devices  26.8 us (36%)
  waiting for transfers between devices  25 us (34%)
  Pallas kernels  16.5 us (22%)
  local copies, waits for them, and re-layouts  4.99 us (7%)
  between operations  0.88 us (1%)
    ppermute x20, starting transfers between devices, swapped(): lax.ppermute(array, axis, [(i, i ^ bits) for i in range(lax.axis_size(axi...  20.8 us
    pallas_call x9, Pallas kernels, call(): pl.pallas_call(kernel, out_shape=out_shape, in_specs=in_specs, out_specs=...  16.5 us
    ppermute x20, waiting for transfers between devices, swapped(): lax.ppermute(array, axis, [(i, i ^ bits) for i in range(lax.axis_size(axi...  15.8 us
    ppermute x1, waiting for transfers between devices, local(): second = lax.ppermute(first, 'tile', ring)  7.05 us
    unnamed x41, local copies, waits for them, and re-layouts  4.98 us
    ppermute x1, starting transfers between devices, local(): second = lax.ppermute(first, 'tile', ring)  2.37 us
    ppermute x1, waiting for transfers between devices, local(): third = lax.ppermute(second, 'tile', ring)  2.15 us
    ppermute x1, starting transfers between devices, local(): third = lax.ppermute(second, 'tile', ring)  1.94 us
  transfers between devices with their start and end apart: 23, of which 13 were waited for; matrix products, arithmetic and copies ran while one was open for 0% of the time, Pallas kernels for 11%

profile of v4, /device:TPU:0, one launch (start us, length us, event | category | flops | bytes accessed | tf_op | source)
XLA Modules:
  0.0 74.2 jit_solution(17804729150078206472)
XLA Ops:
  0.7 3.0 %collective-permute-start.1 = (bf16[4,32,1280]{2,1,0:T(8,128)(2,1)}, bf16[4,32,1280]{2,1,0:T(8,128)(2,1)S(1)}, u32[]{:S(2)}, u32[]{:S(2)}) collective-permute-start(bf16[4,32,1280]{2,1,0:T(8,128)(2,1)} %refs_0_.1), channel_id=1, source_target_pairs={{0,8},{4,12},{8,0},{12,4},{1,9},{5,13},{9,1},{13,5},{2,10},{6,14},... | collective-permute-start | bytes 983048 | tf_op jit(solution)/shard_map/ppermute | solution.py:221
  3.8 1.9 %pick.2.refs_4_ = bf16[160,960]{1,0:T(8,128)(2,1)S(1)} custom-call(s32[3]{0:T(128)S(1)} %pad_add_fusion.ids_ref, bf16[320,3840]{1,0:T(8,128)(2,1)} %w_ref.3), custom_call_target="tpu_custom_call" | custom-call | flops 1000000 | bytes 1000000 | tf_op jit(solution)/shard_map/pick/pallas_call | solution.py:233
  5.6 1.6 %collective-permute-start.6 = (bf16[160,960]{1,0:T(8,128)(2,1)S(1)}, bf16[160,960]{1,0:T(8,128)(2,1)S(1)}, u32[]{:S(2)}, u32[]{:S(2)}) collective-permute-start(bf16[160,960]{1,0:T(8,128)(2,1)S(1)} %pick.2.refs_4_), channel_id=1, source_target_pairs={{0,1},{1,3},{3,2},{2,0},{4,5},{5,7},{7,6},{6,4},{8,9},{9,11},{11,1... | collective-permute-start | bytes 921608 | tf_op jit(solution)/shard_map/ppermute | solution.py:275
  12.1 1.9 %collective-permute-done.4.refs_2_ = bf16[4,32,320]{2,1,0:T(8,128)(2,1)S(1)} collective-permute-done((bf16[4,32,320]{2,1,0:T(8,128)(2,1)S(1)}, bf16[4,32,320]{2,1,0:T(8,128)(2,1)S(1)}, u32[]{:S(2)}, u32[]{:S(2)}) %collective-permute-start.4) | collective-permute-done | bytes 81952 | tf_op jit(solution)/shard_map/ppermute | solution.py:221
  16.1 2.4 %collective-permute-start.8 = (bf16[160,960]{1,0:T(8,128)(2,1)S(1)}, bf16[160,960]{1,0:T(8,128)(2,1)S(1)}, u32[]{:S(2)}, u32[]{:S(2)}) collective-permute-start(bf16[160,960]{1,0:T(8,128)(2,1)S(1)} %collective-permute-done.6.refs_6_), channel_id=1, source_target_pairs={{0,1},{1,3},{3,2},{2,0},{4,5},{5,7},{7,6},{6,4},{8,9},{9,11},{11,1... | collective-permute-start | bytes 921608 | tf_op jit(solution)/shard_map/ppermute | solution.py:291
  18.5 1.5 %collective-permute-start.7 = (bf16[160,960]{1,0:T(8,128)(2,1)S(1)}, bf16[160,960]{1,0:T(8,128)(2,1)S(1)}, u32[]{:S(2)}, u32[]{:S(2)}) collective-permute-start(bf16[160,960]{1,0:T(8,128)(2,1)S(1)} %collective-permute-done.6.refs_6_), channel_id=1, source_target_pairs={{0,16},{16,0},{1,17},{17,1},{2,18},{18,2},{3,19},{19,3},{4,20},{20... | collective-permute-start | bytes 921608 | tf_op jit(solution)/shard_map/ppermute | solution.py:221
  20.0 7.1 %collective-permute-done.8.refs_8_ = bf16[160,960]{1,0:T(8,128)(2,1)S(1)} collective-permute-done((bf16[160,960]{1,0:T(8,128)(2,1)S(1)}, bf16[160,960]{1,0:T(8,128)(2,1)S(1)}, u32[]{:S(2)}, u32[]{:S(2)}) %collective-permute-start.8) | collective-permute-done | bytes 307232 | tf_op jit(solution)/shard_map/ppermute | solution.py:291
  28.1 1.9 %collective-permute-start.10 = (bf16[160,960]{1,0:T(8,128)(2,1)S(1)}, bf16[160,960]{1,0:T(8,128)(2,1)}, u32[]{:S(2)}, u32[]{:S(2)}) collective-permute-start(bf16[160,960]{1,0:T(8,128)(2,1)S(1)} %collective-permute-done.8.refs_8_), channel_id=1, source_target_pairs={{0,1},{1,3},{3,2},{2,0},{4,5},{5,7},{7,6},{6,4},{8,9},{9,11},{11,1... | collective-permute-start | bytes 921608 | tf_op jit(solution)/shard_map/ppermute | solution.py:294
  30.1 1.5 %collective-permute-start.9 = (bf16[160,960]{1,0:T(8,128)(2,1)S(1)}, bf16[160,960]{1,0:T(8,128)(2,1)S(1)}, u32[]{:S(2)}, u32[]{:S(2)}) collective-permute-start(bf16[160,960]{1,0:T(8,128)(2,1)S(1)} %collective-permute-done.8.refs_8_), channel_id=1, source_target_pairs={{0,16},{16,0},{1,17},{17,1},{2,18},{18,2},{3,19},{19,3},{4,20},{20... | collective-permute-start | bytes 921608 | tf_op jit(solution)/shard_map/ppermute | solution.py:221
  31.6 1.9 %norm.1 = (bf16[512,1280]{1,0:T(8,128)(2,1)S(1)}, bf16[512,1280]{1,0:T(8,128)(2,1)S(1)}, f32[4,32,1280]{2,1,0:T(8,128)S(1)}, f32[4,32,128]{2,1,0:T(8,128)S(1)}) custom-call(s32[4]{0:T(128)S(1)} %copy-done.3, bf16[256,1280]{1,0:T(8,128)(2,1)S(1)} %copy-done, f32[1,1280]{1,0:T(1,128)S(1)} %reshape.12.gain_ref, f32[1,1280]{1,0:T(1,128)S(1)} %reshape.13.bias_ref, ...), custom_call_target="tpu_custom_call" | custom-call | flops 10000000 | bytes 6000000 | tf_op jit(solution)/shard_map/norm/pallas_call | solution.py:233
  35.7 2.2 %collective-permute-done.10.refs_10_ = bf16[160,960]{1,0:T(8,128)(2,1)} collective-permute-done((bf16[160,960]{1,0:T(8,128)(2,1)S(1)}, bf16[160,960]{1,0:T(8,128)(2,1)}, u32[]{:S(2)}, u32[]{:S(2)}) %collective-permute-start.10) | collective-permute-done | bytes 307232 | tf_op jit(solution)/shard_map/ppermute | solution.py:294
  39.2 1.5 %collective-permute-start.11 = (bf16[160,960]{1,0:T(8,128)(2,1)}, bf16[160,960]{1,0:T(8,128)(2,1)S(1)}, u32[]{:S(2)}, u32[]{:S(2)}) collective-permute-start(bf16[160,960]{1,0:T(8,128)(2,1)} %collective-permute-done.10.refs_10_), channel_id=1, source_target_pairs={{0,16},{16,0},{1,17},{17,1},{2,18},{18,2},{3,19},{19,3},{4,20},{20... | collective-permute-start | bytes 921608 | tf_op jit(solution)/shard_map/ppermute | solution.py:221
  40.9 1.9 %pick.3.refs_5_ = bf16[160,960]{1,0:T(8,128)(2,1)S(1)} custom-call(s32[3]{0:T(128)S(1)} %pad_add_fusion.ids_ref, bf16[320,3840]{1,0:T(8,128)(2,1)} %w_ref.3), custom_call_target="tpu_custom_call" | custom-call | flops 1000000 | bytes 1000000 | tf_op jit(solution)/shard_map/pick/pallas_call | solution.py:233
  42.7 4.3 %collective-permute-done.11.refs_11_ = bf16[160,960]{1,0:T(8,128)(2,1)S(1)} collective-permute-done((bf16[160,960]{1,0:T(8,128)(2,1)}, bf16[160,960]{1,0:T(8,128)(2,1)S(1)}, u32[]{:S(2)}, u32[]{:S(2)}) %collective-permute-start.11) | collective-permute-done | bytes 307232 | tf_op jit(solution)/shard_map/ppermute | solution.py:221
  47.1 5.1 %attend.1 = (bf16[4,32,320]{2,1,0:T(8,128)(2,1)S(1)}, bf16[4,32,320]{2,1,0:T(8,128)(2,1)S(1)}, bf16[4,32,320]{2,1,0:T(8,128)(2,1)S(1)}, bf16[4,32,320]{2,1,0:T(8...) custom-call(s32[3]{0:T(128)S(1)} %pad_add_fusion.ids_ref, s32[4]{0:T(128)S(1)} %copy-done.4, ...), custom_call_target="tpu_custom_call" | custom-call | flops 3000000000 | bytes 10000000 | tf_op jit(solution)/shard_map/attend/pallas_call | solution.py:233
  52.2 1.6 %back.1 = (bf16[4,32,1280]{2,1,0:T(8,128)(2,1)S(1)}, bf16[4,32,1280]{2,1,0:T(8,128)(2,1)S(1)}, bf16[2,4,32,1280]{3,2,1,0:T(8,128)(2,1)S(1)}, f32[2,1280]{1,0:T(2,128)S(1)}) custom-call(bf16[512,960]{1,0:T(8,128)(2,1)S(1)} %get-tuple-element.39.gqkv_ref, bf16[512,1280]{1,0:T(8,128)(2,1)S(1)} %copy-done.6, bf16[1280,960]{1,0:T(8,128)(2,1)S(1)} %get-tuple-element.41.weights), custom_call_target="tpu_custom_call" | custom-call | flops 4000000000 | bytes 10000000 | tf_op jit(solution)/shard_map/back/pallas_call | solution.py:233
  54.4 1.5 %collective-permute-start.14 = (bf16[4,32,320]{2,1,0:T(8,128)(2,1)S(1)}, bf16[4,32,320]{2,1,0:T(8,128)(2,1)S(1)}, u32[]{:S(2)}, u32[]{:S(2)}) collective-permute-start(bf16[4,32,320]{2,1,0:T(8,128)(2,1)S(1)} %get-tuple-element.45), channel_id=1, source_target_pairs={{0,8},{4,12},{8,0},{12,4},{1,9},{5,13},{9,1},{13,5},{2,10},{6,14},... | collective-permute-start | bytes 245768 | tf_op jit(solution)/shard_map/ppermute | solution.py:221
  55.9 2.7 %collective-permute-start.18 = (f32[2,1280]{1,0:T(2,128)S(1)}, f32[2,1280]{1,0:T(2,128)S(1)}, u32[]{:S(2)}, u32[]{:S(2)}) collective-permute-start(f32[2,1280]{1,0:T(2,128)S(1)} %get-tuple-element.54.refs_0_), channel_id=1, source_target_pairs={{0,3},{1,2},{2,1},{3,0},{4,7},{5,6},{6,5},{7,4},{8,11},{9,10},{10,... | collective-permute-start | bytes 30728 | tf_op jit(solution)/shard_map/ppermute | solution.py:221
  59.5 1.8 %collective-permute-start.16 = (f32[2,1280]{1,0:T(2,128)S(1)}, f32[2,1280]{1,0:T(2,128)S(1)}, u32[]{:S(2)}, u32[]{:S(2)}) collective-permute-start(f32[2,1280]{1,0:T(2,128)S(1)} %get-tuple-element.54.refs_0_), channel_id=1, source_target_pairs={{0,1},{1,0},{2,3},{3,2},{4,5},{5,4},{6,7},{7,6},{8,9},{9,8},{10,11... | collective-permute-start | bytes 30728 | tf_op jit(solution)/shard_map/ppermute | solution.py:221
  61.5 1.8 %collective-permute-done.17.refs_2_ = f32[2,1280]{1,0:T(2,128)S(1)} collective-permute-done((f32[2,1280]{1,0:T(2,128)S(1)}, f32[2,1280]{1,0:T(2,128)S(1)}, u32[]{:S(2)}, u32[]{:S(2)}) %collective-permute-start.17) | collective-permute-done | bytes 10272 | tf_op jit(solution)/shard_map/ppermute | solution.py:221
  63.4 2.0 %collective-permute-start.19 = (bf16[4,32,1280]{2,1,0:T(8,128)(2,1)S(1)}, bf16[4,32,1280]{2,1,0:T(8,128)(2,1)S(1)}, u32[]{:S(2)}, u32[]{:S(2)}) collective-permute-start(bf16[4,32,1280]{2,1,0:T(8,128)(2,1)S(1)} %get-tuple-element.55), channel_id=1, source_target_pairs={{0,8},{4,12},{8,0},{12,4},{1,9},{5,13},{9,1},{13,5},{2,10},{6,14},... | collective-permute-start | bytes 983048 | tf_op jit(solution)/shard_map/ppermute | solution.py:221
  65.6 1.7 %collective-permute-start.20 = (f32[2,1280]{1,0:T(2,128)S(1)}, f32[2,1280]{1,0:T(2,128)S(1)}, u32[]{:S(2)}, u32[]{:S(2)}) collective-permute-start(f32[2,1280]{1,0:T(2,128)S(1)} %get-tuple-element.56.refs_0_), channel_id=1, source_target_pairs={{0,4},{4,0},{8,12},{12,8},{1,5},{5,1},{9,13},{13,9},{2,6},{6,2},{1... | collective-permute-start | bytes 30728 | tf_op jit(solution)/shard_map/ppermute | solution.py:221
  68.7 2.9 %collective-permute-done.22.refs_3_ = f32[2,1280]{1,0:T(2,128)S(1)} collective-permute-done((f32[2,1280]{1,0:T(2,128)S(1)}, f32[2,1280]{1,0:T(2,128)S(1)}, u32[]{:S(2)}, u32[]{:S(2)}) %collective-permute-start.22) | collective-permute-done | bytes 10272 | tf_op jit(solution)/shard_map/ppermute | solution.py:221
  72.6 1.6 %finish.1 = (bf16[4,32,1280]{2,1,0:T(8,128)(2,1)}, f32[2,1280]{1,0:T(2,128)}) custom-call(s32[3]{0:T(128)S(1)} %pad_add_fusion.ids_ref, s32[4]{0:T(128)S(1)} %copy-done.4, f32[4,32,1280]{2,1,0:T(8,128)S(1)} %get-tuple-element.50.unit_ref, f32[4,32,128]{2,1,0:T(8,128)S(1)} %get-tuple-element.51.inv_ref, f32[1,1280]{1,0:T(1,128)S(1)} %reshape.12.gain_ref, ...), custom_call_target="tpu_custom_call" | custom-call | flops 1000000 | bytes 1000000 | tf_op jit(solution)/shard_map/finish/pallas_call | solution.py:233
  (75 shorter events, 16.0 us)
Async XLA Ops:
  0.7 11.4 %collective-permute-start.1 = (bf16[4,32,1280]{2,1,0:T(8,128)(2,1)}, bf16[4,32,1280]{2,1,0:T(8,128)(2,1)S(1)}, u32[]{:S(2)}, u32[]{:S(2)}) collective-permute-start(bf16[4,32,1280]{2,1,0:T(8,128)(2,1)} %refs_0_.1), channel_id=1, source_target_pairs={{0,8},{4,12},{8,0},{12,4},{1,9},{5,13},{9,1},{13,5},{2,10},{6,14},... | collective-permute-start | bytes 983048 | tf_op jit(solution)/shard_map/ppermute | solution.py:221
  5.6 10.5 %collective-permute-start.6 = (bf16[160,960]{1,0:T(8,128)(2,1)S(1)}, bf16[160,960]{1,0:T(8,128)(2,1)S(1)}, u32[]{:S(2)}, u32[]{:S(2)}) collective-permute-start(bf16[160,960]{1,0:T(8,128)(2,1)S(1)} %pick.2.refs_4_), channel_id=1, source_target_pairs={{0,1},{1,3},{3,2},{2,0},{4,5},{5,7},{7,6},{6,4},{8,9},{9,11},{11,1... | collective-permute-start | bytes 921608 | tf_op jit(solution)/shard_map/ppermute | solution.py:275
  8.3 38.7 %copy-start.4 = (s32[4]{0:T(128)S(1)}, s32[4]{0:T(128)}, u32[]{:S(2)}) copy-start(s32[4]{0:T(128)} %live_ref.3) | copy-start | bytes 52
  8.3 1.9 %collective-permute-start.3 = (bf16[4,32,320]{2,1,0:T(8,128)(2,1)S(1)}, bf16[4,32,320]{2,1,0:T(8,128)(2,1)S(1)}, u32[]{:S(2)}, u32[]{:S(2)}) collective-permute-start(bf16[4,32,320]{2,1,0:T(8,128)(2,1)S(1)} %get-tuple-element.33), channel_id=1, source_target_pairs={{0,4},{4,0},{8,12},{12,8},{1,5},{5,1},{9,13},{13,9},{2,6},{6,2},{1... | collective-permute-start | bytes 245768 | tf_op jit(solution)/shard_map/ppermute | solution.py:221
  8.4 5.7 %collective-permute-start.4 = (bf16[4,32,320]{2,1,0:T(8,128)(2,1)S(1)}, bf16[4,32,320]{2,1,0:T(8,128)(2,1)S(1)}, u32[]{:S(2)}, u32[]{:S(2)}) collective-permute-start(bf16[4,32,320]{2,1,0:T(8,128)(2,1)S(1)} %get-tuple-element.34), channel_id=1, source_target_pairs={{0,8},{4,12},{8,0},{12,4},{1,9},{5,13},{9,1},{13,5},{2,10},{6,14},... | collective-permute-start | bytes 245768 | tf_op jit(solution)/shard_map/ppermute | solution.py:221
  9.0 6.5 %collective-permute-start.5 = (bf16[4,32,320]{2,1,0:T(8,128)(2,1)S(1)}, bf16[4,32,320]{2,1,0:T(8,128)(2,1)S(1)}, u32[]{:S(2)}, u32[]{:S(2)}) collective-permute-start(bf16[4,32,320]{2,1,0:T(8,128)(2,1)S(1)} %get-tuple-element.35), channel_id=1, source_target_pairs={{0,12},{4,8},{8,4},{12,0},{1,13},{5,9},{9,5},{13,1},{2,14},{6,10},... | collective-permute-start | bytes 245768 | tf_op jit(solution)/shard_map/ppermute | solution.py:221
  10.9 9.1 %collective-permute-start = (bf16[4,32,1280]{2,1,0:T(8,128)(2,1)S(1)}, bf16[4,32,1280]{2,1,0:T(8,128)(2,1)S(1)}, u32[]{:S(2)}, u32[]{:S(2)}) collective-permute-start(bf16[4,32,1280]{2,1,0:T(8,128)(2,1)S(1)} %copy-done.1), channel_id=1, source_target_pairs={{0,4},{4,0},{8,12},{12,8},{1,5},{5,1},{9,13},{13,9},{2,6},{6,2},{1... | collective-permute-start | bytes 983048 | tf_op jit(solution)/shard_map/ppermute | solution.py:221
  12.1 16.0 %collective-permute-start.2 = (bf16[4,32,1280]{2,1,0:T(8,128)(2,1)S(1)}, bf16[4,32,1280]{2,1,0:T(8,128)(2,1)S(1)}, u32[]{:S(2)}, u32[]{:S(2)}) collective-permute-start(bf16[4,32,1280]{2,1,0:T(8,128)(2,1)S(1)} %collective-permute-done.1.refs_2_), channel_id=1, source_target_pairs={{0,4},{4,0},{8,12},{12,8},{1,5},{5,1},{9,13},{13,9},{2,6},{6,2},{1... | collective-permute-start | bytes 983048 | tf_op jit(solution)/shard_map/ppermute | solution.py:221
  16.1 10.9 %collective-permute-start.8 = (bf16[160,960]{1,0:T(8,128)(2,1)S(1)}, bf16[160,960]{1,0:T(8,128)(2,1)S(1)}, u32[]{:S(2)}, u32[]{:S(2)}) collective-permute-start(bf16[160,960]{1,0:T(8,128)(2,1)S(1)} %collective-permute-done.6.refs_6_), channel_id=1, source_target_pairs={{0,1},{1,3},{3,2},{2,0},{4,5},{5,7},{7,6},{6,4},{8,9},{9,11},{11,1... | collective-permute-start | bytes 921608 | tf_op jit(solution)/shard_map/ppermute | solution.py:291
  18.5 9.6 %collective-permute-start.7 = (bf16[160,960]{1,0:T(8,128)(2,1)S(1)}, bf16[160,960]{1,0:T(8,128)(2,1)S(1)}, u32[]{:S(2)}, u32[]{:S(2)}) collective-permute-start(bf16[160,960]{1,0:T(8,128)(2,1)S(1)} %collective-permute-done.6.refs_6_), channel_id=1, source_target_pairs={{0,16},{16,0},{1,17},{17,1},{2,18},{18,2},{3,19},{19,3},{4,20},{20... | collective-permute-start | bytes 921608 | tf_op jit(solution)/shard_map/ppermute | solution.py:221
  28.1 9.8 %collective-permute-start.10 = (bf16[160,960]{1,0:T(8,128)(2,1)S(1)}, bf16[160,960]{1,0:T(8,128)(2,1)}, u32[]{:S(2)}, u32[]{:S(2)}) collective-permute-start(bf16[160,960]{1,0:T(8,128)(2,1)S(1)} %collective-permute-done.8.refs_8_), channel_id=1, source_target_pairs={{0,1},{1,3},{3,2},{2,0},{4,5},{5,7},{7,6},{6,4},{8,9},{9,11},{11,1... | collective-permute-start | bytes 921608 | tf_op jit(solution)/shard_map/ppermute | solution.py:294
  30.1 8.4 %collective-permute-start.9 = (bf16[160,960]{1,0:T(8,128)(2,1)S(1)}, bf16[160,960]{1,0:T(8,128)(2,1)S(1)}, u32[]{:S(2)}, u32[]{:S(2)}) collective-permute-start(bf16[160,960]{1,0:T(8,128)(2,1)S(1)} %collective-permute-done.8.refs_8_), channel_id=1, source_target_pairs={{0,16},{16,0},{1,17},{17,1},{2,18},{18,2},{3,19},{19,3},{4,20},{20... | collective-permute-start | bytes 921608 | tf_op jit(solution)/shard_map/ppermute | solution.py:221
  39.2 7.8 %collective-permute-start.11 = (bf16[160,960]{1,0:T(8,128)(2,1)}, bf16[160,960]{1,0:T(8,128)(2,1)S(1)}, u32[]{:S(2)}, u32[]{:S(2)}) collective-permute-start(bf16[160,960]{1,0:T(8,128)(2,1)} %collective-permute-done.10.refs_10_), channel_id=1, source_target_pairs={{0,16},{16,0},{1,17},{17,1},{2,18},{18,2},{3,19},{19,3},{4,20},{20... | collective-permute-start | bytes 921608 | tf_op jit(solution)/shard_map/ppermute | solution.py:221
  53.8 7.5 %collective-permute-start.12 = (bf16[2,4,32,1280]{3,2,1,0:T(8,128)(2,1)S(1)}, bf16[2,4,32,1280]{3,2,1,0:T(8,128)(2,1)S(1)}, u32[]{:S(2)}, u32[]{:S(2)}) collective-permute-start(bf16[2,4,32,1280]{3,2,1,0:T(8,128)(2,1)S(1)} %get-tuple-element.43), channel_id=1, source_target_pairs={{0,4},{4,0},{8,12},{12,8},{1,5},{5,1},{9,13},{13,9},{2,6},{6,2},{1... | collective-permute-start | bytes 1966088 | tf_op jit(solution)/shard_map/ppermute | solution.py:221
  53.9 4.7 %collective-permute-start.13 = (bf16[4,32,320]{2,1,0:T(8,128)(2,1)S(1)}, bf16[4,32,320]{2,1,0:T(8,128)(2,1)S(1)}, u32[]{:S(2)}, u32[]{:S(2)}) collective-permute-start(bf16[4,32,320]{2,1,0:T(8,128)(2,1)S(1)} %get-tuple-element.44), channel_id=1, source_target_pairs={{0,4},{4,0},{8,12},{12,8},{1,5},{5,1},{9,13},{13,9},{2,6},{6,2},{1... | collective-permute-start | bytes 245768 | tf_op jit(solution)/shard_map/ppermute | solution.py:221
  54.4 5.1 %collective-permute-start.14 = (bf16[4,32,320]{2,1,0:T(8,128)(2,1)S(1)}, bf16[4,32,320]{2,1,0:T(8,128)(2,1)S(1)}, u32[]{:S(2)}, u32[]{:S(2)}) collective-permute-start(bf16[4,32,320]{2,1,0:T(8,128)(2,1)S(1)} %get-tuple-element.45), channel_id=1, source_target_pairs={{0,8},{4,12},{8,0},{12,4},{1,9},{5,13},{9,1},{13,5},{2,10},{6,14},... | collective-permute-start | bytes 245768 | tf_op jit(solution)/shard_map/ppermute | solution.py:221
  55.9 5.4 %collective-permute-start.15 = (bf16[4,32,320]{2,1,0:T(8,128)(2,1)S(1)}, bf16[4,32,320]{2,1,0:T(8,128)(2,1)S(1)}, u32[]{:S(2)}, u32[]{:S(2)}) collective-permute-start(bf16[4,32,320]{2,1,0:T(8,128)(2,1)S(1)} %get-tuple-element.46), channel_id=1, source_target_pairs={{0,12},{4,8},{8,4},{12,0},{1,13},{5,9},{9,5},{13,1},{2,14},{6,10},... | collective-permute-start | bytes 245768 | tf_op jit(solution)/shard_map/ppermute | solution.py:221
  55.9 5.5 %collective-permute-start.18 = (f32[2,1280]{1,0:T(2,128)S(1)}, f32[2,1280]{1,0:T(2,128)S(1)}, u32[]{:S(2)}, u32[]{:S(2)}) collective-permute-start(f32[2,1280]{1,0:T(2,128)S(1)} %get-tuple-element.54.refs_0_), channel_id=1, source_target_pairs={{0,3},{1,2},{2,1},{3,0},{4,7},{5,6},{6,5},{7,4},{8,11},{9,10},{10,... | collective-permute-start | bytes 30728 | tf_op jit(solution)/shard_map/ppermute | solution.py:221
  58.6 4.7 %collective-permute-start.17 = (f32[2,1280]{1,0:T(2,128)S(1)}, f32[2,1280]{1,0:T(2,128)S(1)}, u32[]{:S(2)}, u32[]{:S(2)}) collective-permute-start(f32[2,1280]{1,0:T(2,128)S(1)} %get-tuple-element.54.refs_0_), channel_id=1, source_target_pairs={{0,2},{1,3},{2,0},{3,1},{4,6},{5,7},{6,4},{7,5},{8,10},{9,11},{10,... | collective-permute-start | bytes 30728 | tf_op jit(solution)/shard_map/ppermute | solution.py:221
  59.5 3.8 %collective-permute-start.16 = (f32[2,1280]{1,0:T(2,128)S(1)}, f32[2,1280]{1,0:T(2,128)S(1)}, u32[]{:S(2)}, u32[]{:S(2)}) collective-permute-start(f32[2,1280]{1,0:T(2,128)S(1)} %get-tuple-element.54.refs_0_), channel_id=1, source_target_pairs={{0,1},{1,0},{2,3},{3,2},{4,5},{5,4},{6,7},{7,6},{8,9},{9,8},{10,11... | collective-permute-start | bytes 30728 | tf_op jit(solution)/shard_map/ppermute | solution.py:221
  63.4 9.2 %collective-permute-start.19 = (bf16[4,32,1280]{2,1,0:T(8,128)(2,1)S(1)}, bf16[4,32,1280]{2,1,0:T(8,128)(2,1)S(1)}, u32[]{:S(2)}, u32[]{:S(2)}) collective-permute-start(bf16[4,32,1280]{2,1,0:T(8,128)(2,1)S(1)} %get-tuple-element.55), channel_id=1, source_target_pairs={{0,8},{4,12},{8,0},{12,4},{1,9},{5,13},{9,1},{13,5},{2,10},{6,14},... | collective-permute-start | bytes 983048 | tf_op jit(solution)/shard_map/ppermute | solution.py:221
  65.4 6.2 %collective-permute-start.22 = (f32[2,1280]{1,0:T(2,128)S(1)}, f32[2,1280]{1,0:T(2,128)S(1)}, u32[]{:S(2)}, u32[]{:S(2)}) collective-permute-start(f32[2,1280]{1,0:T(2,128)S(1)} %get-tuple-element.56.refs_0_), channel_id=1, source_target_pairs={{0,12},{4,8},{8,4},{12,0},{1,13},{5,9},{9,5},{13,1},{2,14},{6,10},... | collective-permute-start | bytes 30728 | tf_op jit(solution)/shard_map/ppermute | solution.py:221
  65.4 7.2 %collective-permute-start.21 = (f32[2,1280]{1,0:T(2,128)S(1)}, f32[2,1280]{1,0:T(2,128)S(1)}, u32[]{:S(2)}, u32[]{:S(2)}) collective-permute-start(f32[2,1280]{1,0:T(2,128)S(1)} %get-tuple-element.56.refs_0_), channel_id=1, source_target_pairs={{0,8},{4,12},{8,0},{12,4},{1,9},{5,13},{9,1},{13,5},{2,10},{6,14},... | collective-permute-start | bytes 30728 | tf_op jit(solution)/shard_map/ppermute | solution.py:221
  65.6 7.1 %collective-permute-start.20 = (f32[2,1280]{1,0:T(2,128)S(1)}, f32[2,1280]{1,0:T(2,128)S(1)}, u32[]{:S(2)}, u32[]{:S(2)}) collective-permute-start(f32[2,1280]{1,0:T(2,128)S(1)} %get-tuple-element.56.refs_0_), channel_id=1, source_target_pairs={{0,4},{4,0},{8,12},{12,8},{1,5},{5,1},{9,13},{13,9},{2,6},{6,2},{1... | collective-permute-start | bytes 30728 | tf_op jit(solution)/shard_map/ppermute | solution.py:221
  (19 other events, 230.5 us)

commit v5 on v4

--- a/solution.py
+++ b/solution.py
@@ -62,18 +62,23 @@
     out_ref[...] = jnp.concatenate(pieces, axis=1)
 
 
-def columns_kernel(ids_ref, cotangent_ref, *out_refs):
-    part = out_refs[0].shape[2]
-    for s, out_ref in enumerate(out_refs):
-        start, wide, odd = window_of(ids_ref[1] ^ s, part)
-        window = cotangent_ref[:, :, pl.ds(pl.multiple_of(start, 128), wide)]
-        out_ref[...] = jnp.where(odd, window[:, :, wide - part :], window[:, :, :part])
+def columns_kernel(part, ids_ref, cotangent_ref, out_ref):
+    theirs = (1 - ids_ref[1] // 2) * (2 * part)
+    out_ref[...] = cotangent_ref[:, :, pl.ds(pl.multiple_of(theirs, 128), 2 * part)]
+
+
+def part_kernel(part, ids_ref, cotangent_ref, columns_ref, up_ref, out_ref):
+    ours = pl.multiple_of(ids_ref[1] // 2 * (2 * part), 128)
+    odd = lax.rem(ids_ref[1], 2) == 1
+    for i, block in enumerate((cotangent_ref[:, :, pl.ds(ours, 2 * part)], columns_ref[...])):
+        low, high = block[:, :, :part], block[:, :, part:]
+        up_ref[i] = jnp.where(odd, high, low)
+        out_ref[i] = jnp.where(odd, low, high)
 
 
 def norm_kernel(visible_ref, pos_ref, gain_ref, bias_ref, *refs):
-    groups = len(refs) - 4
-    token_refs = refs[:groups]
-    normed_ref, unit_ref, own_unit_ref, own_inv_ref = refs[groups:]
+    token_refs = refs[:-4]
+    normed_ref, unit_ref, own_unit_ref, own_inv_ref = refs[-4:]
     slots, rows, width = token_refs[0].shape
     gain = gain_ref[...]
     bias = bias_ref[...]
@@ -81,12 +86,12 @@
         iota = lax.broadcasted_iota(jnp.int32, (8, pos_ref.shape[0]), 1)
         onehot = (iota == visible_ref[p]).astype(F32).astype(BF16)
         position = dot(onehot, pos_ref[...])[0:1]
-        for s in range(groups):
-            embedded = (token_refs[s][p].astype(F32) + position).astype(BF16).astype(F32)
+        for s, tokens_ref in enumerate(token_refs):
+            embedded = (tokens_ref[p].astype(F32) + position).astype(BF16).astype(F32)
             centred = embedded - jnp.mean(embedded, axis=-1, keepdims=True)
             inv_std = lax.rsqrt(jnp.mean(centred * centred, axis=-1, keepdims=True) + 1e-06)
             unit = centred * inv_std
-            at = (p * groups + s) * rows
+            at = (p * len(token_refs) + s) * rows
             normed_ref[at : at + rows] = (unit * gain + bias).astype(BF16)
             unit_ref[at : at + rows] = unit.astype(BF16)
             if s == 0:
@@ -110,31 +115,27 @@
     return firsts
 
 
-def attend_kernel(count, depth, ids_ref, live_ref, normed_ref, valid_ref, *refs):
-    groups = (len(refs) - count - 3) // 2
-    up_refs, piece_refs = refs[:groups], refs[groups : groups + count]
-    context_refs = refs[groups + count : 2 * groups + count]
-    gqkv_ref, weights, qkv_ref = refs[2 * groups + count :]
-    slots, rows, channels = up_refs[0].shape
-    dates = groups * rows
+def attend_kernel(count, depth, ids_ref, live_ref, normed_ref, valid_ref, up_ref, beside_ref, *refs):
+    piece_refs = refs[:count]
+    own_ref, close_ref, across_ref, gqkv_ref, weights, qkv_ref = refs[-6:]
+    _, slots, rows, channels = up_ref.shape
+    dates = valid_ref.shape[1]
     heads = channels // HEAD_DIM
     inv_scale = 1.0 / HEAD_DIM**0.5
     for first, ref in zip(piece_rows(ids_ref, count, depth), piece_refs):
         weights[pl.ds(first, ref.shape[0]), :] = ref[...]
     qkv_ref[...] = dot(normed_ref[...], weights[...]).astype(BF16)
-    valid_rows = jnp.concatenate(
-        [
-            valid_ref[pl.ds(pl.multiple_of((ids_ref[1] ^ s) * rows, rows), rows), :]
-            for s in range(groups)
-        ],
-        axis=0,
-    )
+    row = lax.broadcasted_iota(jnp.int32, (dates, dates), 0)
+    column = lax.broadcasted_iota(jnp.int32, (dates, dates), 1)
+    same_date = column == (row ^ (ids_ref[1] * rows))
     for p in range(slots):
         span = slice(p * dates, (p + 1) * dates)
         alive = (live_ref[ids_ref[2]] > p // (BLOCK_ROWS // DG)).astype(F32)
         rows_qkv = qkv_ref[span, :]
-        upstream = jnp.concatenate([ref[p] for ref in up_refs], axis=0) * alive.astype(BF16)
-        allowed = valid_rows[:, p : p + 1] > 0
+        upstream = [up_ref[0, p], beside_ref[0, p], up_ref[1, p], beside_ref[1, p]]
+        upstream = jnp.concatenate(upstream, axis=0) * alive.astype(BF16)
+        valid = valid_ref[p : p + 1, :].astype(F32)
+        allowed = jnp.sum(jnp.where(same_date, valid, 0.0), axis=1, keepdims=True) > 0
         grads = [[], [], []]
         contexts = []
         for h in range(heads):
@@ -156,45 +157,68 @@
             grads[1].append(dot(glow, q))
         gqkv_ref[span, :] = jnp.concatenate(grads[0] + grads[1] + grads[2], axis=1).astype(BF16)
         context = jnp.concatenate(contexts, axis=1).astype(BF16)
-        for s in range(groups):
-            context_refs[s][p] = context[s * rows : (s + 1) * rows]
+        for s, out in enumerate((own_ref, close_ref, across_ref.at[0], across_ref.at[1])):
+            out[p] = context[s * rows : (s + 1) * rows]
 
 
 def back_kernel(gqkv_ref, unit_ref, weights, stay_ref, pass_ref, cross_ref, sums_ref):
     slots, rows, width = stay_ref.shape
-    groups = 4
-    dates = groups * rows
+    dates = gqkv_ref.shape[0] // slots
+    tail = 2 * slots * rows
     step = 256
     for n in range(width // step):
         lanes = slice(n * step, (n + 1) * step)
         partial = dot_nt(gqkv_ref[...], weights[lanes, :])
         low = partial.astype(BF16)
         for p in range(slots):
-            for s, out in enumerate((stay_ref, cross_ref.at[0], pass_ref, cross_ref.at[1])):
-                at = p * dates + s * rows
-                out[p, :, lanes] = low[at : at + rows]
-        sums_ref[0:1, lanes] = jnp.sum(partial * unit_ref[:, lanes].astype(F32), axis=0, keepdims=True)
-        sums_ref[1:2, lanes] = jnp.sum(partial, axis=0, keepdims=True)
-
-
-def merge_kernel(pass_ref, near_ref, *refs):
-    out_ref, total_ref = refs[-2:]
-    out_ref[...] = (pass_ref[...].astype(F32) + near_ref[1].astype(F32)).astype(BF16)
+            for s in range(dates // rows):
+                block = low[p * dates + s * rows : p * dates + (s + 1) * rows]
+                if s % 2:
+                    at = (s // 2 * slots + p) * rows
+                    cross_ref[at : at + rows, lanes] = block
+                else:
+                    (pass_ref if s else stay_ref)[p, :, lanes] = block
+        gain_sum = jnp.sum(partial * unit_ref[:, lanes].astype(F32), axis=0, keepdims=True)
+        sums = jnp.concatenate([gain_sum, jnp.sum(partial, axis=0, keepdims=True)], axis=0)
+        sums_ref[:, lanes] = sums
+        high = sums.astype(BF16)
+        rest = (sums - high.astype(F32)).astype(BF16)
+        fill = jnp.zeros((cross_ref.shape[0] - tail - 4, step), BF16)
+        cross_ref[tail:, lanes] = jnp.concatenate([high, rest, fill], axis=0)
+
+
+def merge_kernel(pass_ref, close_ref, sums_ref, out_ref, total_ref):
+    slots, rows, width = out_ref.shape
+    for p in range(slots):
+        at = (slots + p) * rows
+        out_ref[p] = (pass_ref[p].astype(F32) + close_ref[at : at + rows].astype(F32)).astype(BF16)
+    sums = close_ref[2 * slots * rows :].astype(F32)
+    total_ref[...] = sums_ref[...] + sums[0:2] + sums[2:4]
+
+
+def both_kernel(close_ref, far_ref, both_ref):
+    both_ref[0] = close_ref[...]
+    both_ref[1] = far_ref[1]
+
+
+def add_kernel(*refs):
     total = refs[0][...]
-    for ref in refs[1:-2]:
+    for ref in refs[1:-1]:
         total = total + ref[...]
-    total_ref[...] = total
-
-
-def home_kernel(ids_ref, stay_ref, near_ref, *refs):
-    groups = len(refs) - 3
-    context_refs = refs[:groups]
-    grad_ref, attended_ref, held = refs[groups:]
-    grad_ref[...] = stay_ref[...].astype(F32) + near_ref[0].astype(F32)
-    for s in range(groups):
-        held[ids_ref[1] ^ s] = context_refs[s][...]
-    for p in range(attended_ref.shape[0]):
-        attended_ref[p] = jnp.concatenate([held[g, p] for g in range(groups)], axis=1)
+    refs[-1][...] = total
+
+
+def home_kernel(ids_ref, stay_ref, close_ref, own_ref, beside_ref, across_ref, grad_ref, attended_ref, held):
+    slots, rows, width = grad_ref.shape
+    group = ids_ref[1]
+    held[group] = own_ref[...]
+    held[group ^ 1] = beside_ref[0]
+    held[group ^ 2] = across_ref[0]
+    held[group ^ 3] = beside_ref[1]
+    for p in range(slots):
+        close = close_ref[p * rows : (p + 1) * rows].astype(F32)
+        grad_ref[p] = stay_ref[p].astype(F32) + close
+        attended_ref[p] = jnp.concatenate([held[g, p] for g in range(held.shape[0])], axis=1)
 
 
 def finish_kernel(ids_ref, live_ref, unit_ref, inv_ref, gain_ref, grad_ref, far_ref, *refs):
@@ -229,7 +253,7 @@
     return pltpu.with_memory_space_constraint(array, pltpu.VMEM)
 
 
-def call(kernel, name, out_shape, in_specs, args, megabytes, flops=10**6, size=10**6, scratch=()):
+def call(kernel, name, out_shape, in_specs, args, megabytes, scratch=()):
     return pl.pallas_call(
         kernel,
         out_shape=out_shape,
@@ -237,7 +261,7 @@
         out_specs=jax.tree.map(lambda _: VMEM, out_shape),
         scratch_shapes=list(scratch),
         compiler_params=pltpu.CompilerParams(vmem_limit_bytes=megabytes * 1024 * 1024),
-        cost_estimate=pl.CostEstimate(flops=flops, bytes_accessed=size, transcendentals=0),
+        cost_estimate=pl.CostEstimate(flops=1000, bytes_accessed=1000, transcendentals=0),
         name=name,
     )(*args)
 
@@ -265,35 +289,49 @@
     dates = rows * groups
     ids = jnp.stack([lax.axis_index(name) for name in ("rep", "date", "tile")]).astype(jnp.int32)
     gain2, bias2 = norm_gain.reshape(1, width), norm_bias.reshape(1, width)
-    valid_t = valid.T
 
     chain = owners == 4 and lax.axis_size("rep") == 2 and depth % 32 == 0
     ring = [(0, 1), (1, 3), (3, 2), (2, 0)]
     share = depth // 2
+
+    held = pick(w_qkv, ids, share, part, False) if chain else ids
+    sooner = after(tokens, held)
+    across = swapped(sooner, "date", 2)
+    beside = swapped(sooner, "date", 1)
     if chain:
-        held = pick(w_qkv, ids, share, part, False)
         first = lax.ppermute(held, "tile", ring)
-        rest = pick(w_qkv, ids, share, part, True)
-    across = swapped(tokens, "date", 2)
-    beside = swapped(tokens, "date", 1)
-    ups = call(
-        columns_kernel,
-        "columns",
-        (jax.ShapeDtypeStruct((slots, rows, part), BF16),) * groups,
-        [SMEM, VMEM],
-        (ids, cotangent),
-        4,
-    )
-    ups = [ups[0]] + [swapped(ups[s], "date", s) for s in range(1, groups)]
-    beyond = swapped(across, "date", 1)
-    if chain:
-        first = after(first, across, *ups[1:])
+        first = after(first, across, beside)
         second = lax.ppermute(first, "tile", ring)
         first_other = swapped(first, "rep", 1)
-        second = after(second, beside, beyond, first_other)
+        rest = pick(w_qkv, after(ids, first), share, part, True)
+    else:
+        first = ids
+    across = after(across, first)
+    beyond = swapped(across, "date", 1)
+    pair = pltpu.VMEM((2, slots, rows, part), BF16)
+    columns = call(
+        functools.partial(columns_kernel, part),
+        "columns",
+        pltpu.VMEM((slots, rows, 2 * part), BF16),
+        [SMEM, VMEM],
+        (after(ids, first), cotangent),
+        4,
+    )
+    columns = swapped(columns, "date", 2)
+    if chain:
+        second = after(second, first_other, beyond, columns, rest)
         third = lax.ppermute(second, "tile", ring)
         second_other = swapped(second, "rep", 1)
-    gathered = [tokens, beside, across, beyond]
+        columns = after(columns, second)
+    ups, ups_beside = call(
+        functools.partial(part_kernel, part),
+        "part",
+        (pair, pair),
+        [SMEM, VMEM, VMEM],
+        (ids, cotangent, near(columns)),
+        4,
+    )
+    ups_beside = swapped(ups_beside, "date", 1)
 
     normed, unit, own_unit, own_inv = call(
         norm_kernel,
@@ -305,13 +343,11 @@
             pltpu.VMEM((slots, rows, 128), F32),
         ),
         [SMEM] + [VMEM] * (3 + groups),
-        (visible, pos_table, gain2, bias2, *gathered),
+        (visible, pos_table, gain2, bias2, tokens, near(beside), near(across), near(beyond)),
         12,
-        flops=10**7,
-        size=6 * 10**6,
     )
     if chain:
-        third = after(third, normed, second_other)
+        third = after(third, second_other, ups_beside, normed)
         third_other = swapped(third, "rep", 1)
         pieces = [held, rest, first, first_other, second, second_other, third, third_other]
     else:
@@ -322,55 +358,66 @@
         pieces = [lax.all_gather(jnp.concatenate(mine, axis=1), "tile", axis=0, tiled=True)]
     pieces = [near(piece) for piece in pieces]
 
-    results = call(
+    piece = pltpu.VMEM((slots, rows, part), BF16)
+    context, close_context, far_context, gqkv, weights = call(
         functools.partial(attend_kernel, len(pieces), depth),
         "attend",
-        (pltpu.VMEM((slots, rows, part), BF16),) * groups
-        + (pltpu.VMEM((slots * dates, 3 * part), BF16), pltpu.VMEM((width, 3 * part), BF16)),
-        [SMEM] * 2 + [VMEM] * (2 + groups + len(pieces)),
-        (ids, live, near(normed), valid_t, *ups, *pieces),
+        (
+            piece,
+            piece,
+            pair,
+            pltpu.VMEM((slots * dates, 3 * part), BF16),
+            pltpu.VMEM((width, 3 * part), BF16),
+        ),
+        [SMEM] * 2 + [VMEM] * (4 + len(pieces)),
+        (ids, live, near(normed), valid, near(ups), near(ups_beside), *pieces),
         20,
-        flops=3 * 10**9,
-        size=10**7,
         scratch=(pltpu.VMEM((slots * dates, 3 * part), BF16),),
     )
-    contexts, gqkv, weights = results[:groups], results[groups], results[groups + 1]
-    contexts = [contexts[0]] + [swapped(contexts[s], "date", s) for s in range(1, groups)]
+    far_context = swapped(far_context, "date", 2)
 
     block = pltpu.VMEM((slots, rows, width), BF16)
+    pairs = pltpu.VMEM((2, width), F32)
     stay, passing, cross, sums = call(
         back_kernel,
         "back",
-        (block, block, pltpu.VMEM((2, slots, rows, width), BF16), pltpu.VMEM((2, width), F32)),
+        (block, block, pltpu.VMEM((2 * slots * rows + 16, width), BF16), pairs),
         [VMEM] * 3,
         (near(gqkv), near(unit), near(weights)),
         12,
-        flops=4 * 10**9,
-        size=10**7,
     )
 
     close = swapped(cross, "date", 1)
-    close = after(close, *contexts[1:])
-    if owners == 4:
-        tiles = [sums] + [swapped(sums, "tile", s) for s in range(1, owners)]
-    else:
-        tiles = [lax.psum(sums, ("date", "tile"))]
     chip, total = call(
         merge_kernel,
         "merge",
-        (block, pltpu.VMEM((2, width), F32)),
-        [VMEM] * (2 + len(tiles)),
-        (passing, close, *tiles),
+        (block, pairs),
+        [VMEM] * 3,
+        (near(passing), near(close), near(sums)),
         6,
     )
+    far_context = after(far_context, chip)
+    both = call(both_kernel, "both", pair, [VMEM] * 2, (near(close_context), near(far_context)), 2)
     far = swapped(chip, "date", 2)
-    totals = [total] + [swapped(total, "date", s) for s in range(1, groups)] if owners == 4 else [total]
+    if owners == 4:
+        total = call(
+            add_kernel,
+            "add",
+            pairs,
+            [VMEM] * owners,
+            [near(total)] + [near(swapped(total, "tile", s)) for s in range(1, owners)],
+            2,
+        )
+    else:
+        total = lax.psum(total, "tile")
+    far_total = swapped(total, "date", 2)
+    both = swapped(both, "date", 1)
     home, attended = call(
         home_kernel,
         "home",
         (pltpu.VMEM((slots, rows, width), F32), jax.ShapeDtypeStruct((slots, rows, channels), BF16)),
-        [SMEM] + [VMEM] * (2 + groups),
-        (ids, stay, close, *contexts),
+        [SMEM] + [VMEM] * 5,
+        (ids, near(stay), near(close), near(context), near(both), near(far_context)),
         6,
         scratch=(pltpu.VMEM((groups, slots, rows, part), BF16),),
     )
@@ -381,8 +428,8 @@
             jax.ShapeDtypeStruct((slots, rows, width), BF16),
             jax.ShapeDtypeStruct((2, width), F32),
         ),
-        [SMEM] * 2 + [VMEM] * (5 + len(totals)),
-        (ids, live, near(own_unit), near(own_inv), gain2, near(home), far, *totals),
+        [SMEM] * 2 + [VMEM] * 7,
+        (ids, live, near(own_unit), near(own_inv), gain2, near(home), near(far), total, far_total),
         6,
     )
     return attended, grad_tokens, grad_norm

time: 74.4 us -> 74.6 us (level)
  waiting for transfers between devices: 25 us -> 41.3 us
  starting transfers between devices: 26.8 us -> 15.8 us
  local copies, waits for them, and re-layouts: 4.99 us -> 0.06 us
    ppermute x1, waiting for transfers between devices: 0.01 us -> 9.45 us  [local(): first = lax.ppermute(held, 'tile', ring)]
    ppermute x20 -> x16, waiting for transfers between devices: 15.8 us -> 24.2 us  [swapped(): lax.ppermute(array, axis, [(i, i ^ bits) for i in range(lax.axis_size(axi...]
    ppermute x20 -> x16, starting transfers between devices: 20.8 us -> 12.7 us  [swapped(): lax.ppermute(array, axis, [(i, i ^ bits) for i in range(lax.axis_size(axi...]
    unnamed x41 -> x16, local copies, waits for them, and re-layouts: 4.98 us -> 0.05 us
    ppermute x1, waiting for transfers between devices: 7.05 us -> 2.14 us  [local(): second = lax.ppermute(first, 'tile', ring)]
    ppermute x1, waiting for transfers between devices: 2.15 us -> 5.6 us  [local(): third = lax.ppermute(second, 'tile', ring)]
    ppermute x1, starting transfers between devices: 2.37 us -> 0.78 us  [local(): second = lax.ppermute(first, 'tile', ring)]
    ppermute x1, starting transfers between devices: 1.94 us -> 0.79 us  [local(): third = lax.ppermute(second, 'tile', ring)]
  transfers between devices with their start and end apart: 23 -> 19, of which waited for: 13 -> 11; matrix products, arithmetic and copies ran while one was open for 0% -> 0% of each run, Pallas kernels for 11% -> 9%
where the time goes in v5:
time: 74.6 us; the launch traced here: 74.4 us
  waiting for transfers between devices  41.3 us (55%)
  Pallas kernels  16.2 us (22%)
  starting transfers between devices  15.8 us (21%)
  between operations  0.87 us (1%)
    ppermute x16, waiting for transfers between devices, swapped(): lax.ppermute(array, axis, [(i, i ^ bits) for i in range(lax.axis_size(axi...  24.2 us
    pallas_call x12, Pallas kernels, call(): pl.pallas_call(kernel, out_shape=out_shape, in_specs=in_specs, out_specs=...  16.2 us
    ppermute x16, starting transfers between devices, swapped(): lax.ppermute(array, axis, [(i, i ^ bits) for i in range(lax.axis_size(axi...  12.7 us
    ppermute x1, waiting for transfers between devices, local(): first = lax.ppermute(held, 'tile', ring)  9.45 us
    ppermute x1, waiting for transfers between devices, local(): third = lax.ppermute(second, 'tile', ring)  5.6 us
    ppermute x1, waiting for transfers between devices, local(): second = lax.ppermute(first, 'tile', ring)  2.14 us
    ppermute x1, starting transfers between devices, local(): first = lax.ppermute(held, 'tile', ring)  1.58 us
  transfers between devices with their start and end apart: 19, of which 11 were waited for; matrix products, arithmetic and copies ran while one was open for 0% of the time, Pallas kernels for 9%

profile of v5, /device:TPU:0, one launch (start us, length us, event | category | flops | bytes accessed | tf_op | source)
XLA Modules:
  0.0 74.4 jit_solution(13095582274446719397)
XLA Ops:
  0.7 1.9 %pick.2.refs_0_ = bf16[160,960]{1,0:T(8,128)(2,1)S(1)} custom-call(s32[3]{0:T(128)S(1)} %pad_add_fusion.ids_ref, bf16[320,3840]{1,0:T(8,128)(2,1)} %w_ref.3), custom_call_target="tpu_custom_call" | custom-call | flops 1000 | bytes 1000 | tf_op jit(solution)/shard_map/pick/pallas_call | solution.py:257
  2.7 3.0 %collective-permute-start.1 = (bf16[4,32,1280]{2,1,0:T(8,128)(2,1)S(1)}, bf16[4,32,1280]{2,1,0:T(8,128)(2,1)S(1)}, u32[]{:S(2)}, u32[]{:S(2)}) collective-permute-start(bf16[4,32,1280]{2,1,0:T(8,128)(2,1)S(1)} %copy-done.2), channel_id=1, source_target_pairs={{0,8},{4,12},{8,0},{12,4},{1,9},{5,13},{9,1},{13,5},{2,10},{6,14},... | collective-permute-start | bytes 983048 | tf_op jit(solution)/shard_map/ppermute | solution.py:245
  5.7 1.6 %collective-permute-start.2 = (bf16[160,960]{1,0:T(8,128)(2,1)S(1)}, bf16[160,960]{1,0:T(8,128)(2,1)S(1)}, u32[]{:S(2)}, u32[]{:S(2)}) collective-permute-start(bf16[160,960]{1,0:T(8,128)(2,1)S(1)} %pick.2.refs_0_), channel_id=1, source_target_pairs={{0,1},{1,3},{3,2},{2,0},{4,5},{5,7},{7,6},{6,4},{8,9},{9,11},{11,1... | collective-permute-start | bytes 921608 | tf_op jit(solution)/shard_map/ppermute | solution.py:302
  7.2 9.4 %collective-permute-done.2.refs_2_ = bf16[160,960]{1,0:T(8,128)(2,1)S(1)} collective-permute-done((bf16[160,960]{1,0:T(8,128)(2,1)S(1)}, bf16[160,960]{1,0:T(8,128)(2,1)S(1)}, u32[]{:S(2)}, u32[]{:S(2)}) %collective-permute-start.2) | collective-permute-done | bytes 307232 | tf_op jit(solution)/shard_map/ppermute | solution.py:302
  16.7 1.6 %collective-permute-start.6 = (bf16[160,960]{1,0:T(8,128)(2,1)S(1)}, bf16[160,960]{1,0:T(8,128)(2,1)S(1)}, u32[]{:S(2)}, u32[]{:S(2)}) collective-permute-start(bf16[160,960]{1,0:T(8,128)(2,1)S(1)} %collective-permute-done.2.refs_2_), channel_id=1, source_target_pairs={{0,16},{16,0},{1,17},{17,1},{2,18},{18,2},{3,19},{19,3},{4,20},{20... | collective-permute-start | bytes 921608 | tf_op jit(solution)/shard_map/ppermute | solution.py:245
  20.3 1.9 %pick.3.refs_1_ = bf16[160,960]{1,0:T(8,128)(2,1)S(1)} custom-call(s32[3]{0:T(128)S(1)} %pad_add_fusion.ids_ref, bf16[320,3840]{1,0:T(8,128)(2,1)} %w_ref.3), custom_call_target="tpu_custom_call" | custom-call | flops 1000 | bytes 1000 | tf_op jit(solution)/shard_map/pick/pallas_call | solution.py:257
  22.2 3.6 %collective-permute-done.4.columns_ref = bf16[4,32,640]{2,1,0:T(8,128)(2,1)S(1)} collective-permute-done((bf16[4,32,640]{2,1,0:T(8,128)(2,1)S(1)}, bf16[4,32,640]{2,1,0:T(8,128)(2,1)S(1)}, u32[]{:S(2)}, u32[]{:S(2)}) %collective-permute-start.4) | collective-permute-done | bytes 163872 | tf_op jit(solution)/shard_map/ppermute | solution.py:245
  25.7 1.1 %collective-permute-done.6.refs_3_ = bf16[160,960]{1,0:T(8,128)(2,1)S(1)} collective-permute-done((bf16[160,960]{1,0:T(8,128)(2,1)S(1)}, bf16[160,960]{1,0:T(8,128)(2,1)S(1)}, u32[]{:S(2)}, u32[]{:S(2)}) %collective-permute-start.6) | collective-permute-done | bytes 307232 | tf_op jit(solution)/shard_map/ppermute | solution.py:245
  26.8 2.1 %collective-permute-done.5.refs_4_ = bf16[160,960]{1,0:T(8,128)(2,1)S(1)} collective-permute-done((bf16[160,960]{1,0:T(8,128)(2,1)S(1)}, bf16[160,960]{1,0:T(8,128)(2,1)S(1)}, u32[]{:S(2)}, u32[]{:S(2)}) %collective-permute-start.5) | collective-permute-done | bytes 307232 | tf_op jit(solution)/shard_map/ppermute | solution.py:304
  29.0 0.8 %collective-permute-start.9 = (bf16[160,960]{1,0:T(8,128)(2,1)S(1)}, bf16[160,960]{1,0:T(8,128)(2,1)S(1)}, u32[]{:S(2)}, u32[]{:S(2)}) collective-permute-start(bf16[160,960]{1,0:T(8,128)(2,1)S(1)} %collective-permute-done.5.refs_4_), channel_id=1, source_target_pairs={{0,1},{1,3},{3,2},{2,0},{4,5},{5,7},{7,6},{6,4},{8,9},{9,11},{11,1... | collective-permute-start | bytes 921608 | tf_op jit(solution)/shard_map/ppermute | solution.py:323
  30.3 0.8 %part.1 = (bf16[2,4,32,320]{3,2,1,0:T(8,128)(2,1)S(1)}, bf16[2,4,32,320]{3,2,1,0:T(8,128)(2,1)S(1)}) custom-call(s32[3]{0:T(128)S(1)} %pad_add_fusion.ids_ref, bf16[4,32,1280]{2,1,0:T(8,128)(2,1)S(1)} %copy-done, bf16[4,32,640]{2,1,0:T(8,128)(2,1)S(1)} %collective-permute-done.4.columns_ref), custom_call_target="tpu_custom_call" | custom-call | flops 1000 | bytes 1000 | tf_op jit(solution)/shard_map/part/pallas_call | solution.py:257
  31.3 1.9 %norm.1 = (bf16[512,1280]{1,0:T(8,128)(2,1)S(1)}, bf16[512,1280]{1,0:T(8,128)(2,1)S(1)}, f32[4,32,1280]{2,1,0:T(8,128)S(1)}, f32[4,32,128]{2,1,0:T(8,128)S(1)}) custom-call(s32[4]{0:T(128)S(1)} %copy-done.5, bf16[256,1280]{1,0:T(8,128)(2,1)S(1)} %copy-done.1, f32[1,1280]{1,0:T(1,128)S(1)} %reshape.12.gain_ref, f32[1,1280]{1,0:T(1,128)S(1)} %reshape.13.bias_ref, ...), custom_call_target="tpu_custom_call" | custom-call | flops 1000 | bytes 1000 | tf_op jit(solution)/shard_map/norm/pallas_call | solution.py:257
  33.2 5.6 %collective-permute-done.9.refs_6_ = bf16[160,960]{1,0:T(8,128)(2,1)S(1)} collective-permute-done((bf16[160,960]{1,0:T(8,128)(2,1)S(1)}, bf16[160,960]{1,0:T(8,128)(2,1)S(1)}, u32[]{:S(2)}, u32[]{:S(2)}) %collective-permute-start.9) | collective-permute-done | bytes 307232 | tf_op jit(solution)/shard_map/ppermute | solution.py:323
  39.3 7.5 %collective-permute-done.10.refs_7_ = bf16[160,960]{1,0:T(8,128)(2,1)S(1)} collective-permute-done((bf16[160,960]{1,0:T(8,128)(2,1)S(1)}, bf16[160,960]{1,0:T(8,128)(2,1)S(1)}, u32[]{:S(2)}, u32[]{:S(2)}) %collective-permute-start.10) | collective-permute-done | bytes 307232 | tf_op jit(solution)/shard_map/ppermute | solution.py:245
  46.8 4.4 %attend.1 = (bf16[4,32,320]{2,1,0:T(8,128)(2,1)S(1)}, bf16[4,32,320]{2,1,0:T(8,128)(2,1)S(1)}, bf16[2,4,32,320]{3,2,1,0:T(8,128)(2,1)S(1)}, bf16[512,960]{1,0:T(8,128)(2,1)S(1)}, bf16[1280,960]{1,0:T(8,128)(2,1)S(1)}) custom-call(s32[3]{0:T(128)S(1)} %pad_add_fusion.ids_ref, s32[4]{0:T(128)S(1)} %copy-done.4, ...), custom_call_target="tpu_custom_call" | custom-call | flops 1000 | bytes 1000 | tf_op jit(solution)/shard_map/attend/pallas_call | solution.py:257
  51.2 1.6 %back.1 = (bf16[4,32,1280]{2,1,0:T(8,128)(2,1)S(1)}, bf16[4,32,1280]{2,1,0:T(8,128)(2,1)S(1)}, bf16[272,1280]{1,0:T(8,128)(2,1)S(1)}, f32[2,1280]{1,0:T(2,128)S(1)}) custom-call(bf16[512,960]{1,0:T(8,128)(2,1)S(1)} %get-tuple-element.42.gqkv_ref, bf16[512,1280]{1,0:T(8,128)(2,1)S(1)} %get-tuple-element.43.unit_ref, ...), custom_call_target="tpu_custom_call" | custom-call | flops 1000 | bytes 1000 | tf_op jit(solution)/shard_map/back/pallas_call | solution.py:257
  53.5 1.5 %collective-permute-done.11.close_ref = bf16[272,1280]{1,0:T(8,128)(2,1)S(1)} collective-permute-done((bf16[272,1280]{1,0:T(8,128)(2,1)S(1)}, bf16[272,1280]{1,0:T(8,128)(2,1)S(1)}, u32[]{:S(2)}, u32[]{:S(2)}) %collective-permute-start.11) | collective-permute-done | bytes 696352 | tf_op jit(solution)/shard_map/ppermute | solution.py:245
  55.8 4.9 %collective-permute-done.12.far_ref.across_ref = bf16[2,4,32,320]{3,2,1,0:T(8,128)(2,1)S(1)} collective-permute-done((bf16[2,4,32,320]{3,2,1,0:T(8,128)(2,1)S(1)}, bf16[2,4,32,320]{3,2,1,0:T(8,128)(2,1)S(1)}, u32[]{:S(2)}, u32[]{:S(2)}) %collective-permute-start.12) | collective-permute-done | bytes 163872 | tf_op jit(solution)/shard_map/ppermute | solution.py:245
  60.8 3.7 %collective-permute-start.17 = (f32[2,1280]{1,0:T(2,128)S(1)}, f32[2,1280]{1,0:T(2,128)S(1)}, u32[]{:S(2)}, u32[]{:S(2)}) collective-permute-start(f32[2,1280]{1,0:T(2,128)S(1)} %get-tuple-element.58.refs_0_), channel_id=1, source_target_pairs={{0,3},{1,2},{2,1},{3,0},{4,7},{5,6},{6,5},{7,4},{8,11},{9,10},{10,... | collective-permute-start | bytes 30728 | tf_op jit(solution)/shard_map/ppermute | solution.py:245
  65.3 1.1 %collective-permute-done.17.refs_3_ = f32[2,1280]{1,0:T(2,128)S(1)} collective-permute-done((f32[2,1280]{1,0:T(2,128)S(1)}, f32[2,1280]{1,0:T(2,128)S(1)}, u32[]{:S(2)}, u32[]{:S(2)}) %collective-permute-start.17) | collective-permute-done | bytes 10272 | tf_op jit(solution)/shard_map/ppermute | solution.py:245
  66.3 2.7 %collective-permute-done.16.refs_2_ = f32[2,1280]{1,0:T(2,128)S(1)} collective-permute-done((f32[2,1280]{1,0:T(2,128)S(1)}, f32[2,1280]{1,0:T(2,128)S(1)}, u32[]{:S(2)}, u32[]{:S(2)}) %collective-permute-start.16) | collective-permute-done | bytes 10272 | tf_op jit(solution)/shard_map/ppermute | solution.py:245
  69.7 1.4 %home.1 = (f32[4,32,1280]{2,1,0:T(8,128)S(1)}, bf16[4,32,1280]{2,1,0:T(8,128)(2,1)}) custom-call(s32[3]{0:T(128)S(1)} %pad_add_fusion.ids_ref, bf16[4,32,1280]{2,1,0:T(8,128)(2,1)S(1)} %get-tuple-element.45.stay_ref, bf16[272,1280]{1,0:T(8,128)(2,1)S(1)} %collective-permute-done.11.close_ref, bf16[4,32,320]{2,1,0:T(8,128)(2,1)S(1)} %get-tuple-element.47.own_ref, ...), custom_call_target="tpu_custom_call" | custom-call | flops 1000 | bytes 1000 | tf_op jit(solution)/shard_map/home/pallas_call | solution.py:257
  71.1 1.7 %collective-permute-done.18.refs_1_ = f32[2,1280]{1,0:T(2,128)S(1)} collective-permute-done((f32[2,1280]{1,0:T(2,128)S(1)}, f32[2,1280]{1,0:T(2,128)S(1)}, u32[]{:S(2)}, u32[]{:S(2)}) %collective-permute-start.18) | collective-permute-done | bytes 10272 | tf_op jit(solution)/shard_map/ppermute | solution.py:245
  72.8 1.6 %finish.1 = (bf16[4,32,1280]{2,1,0:T(8,128)(2,1)}, f32[2,1280]{1,0:T(2,128)}) custom-call(s32[3]{0:T(128)S(1)} %pad_add_fusion.ids_ref, s32[4]{0:T(128)S(1)} %copy-done.4, f32[4,32,1280]{2,1,0:T(8,128)S(1)} %get-tuple-element.55.unit_ref, f32[4,32,128]{2,1,0:T(8,128)S(1)} %get-tuple-element.56.inv_ref, f32[1,1280]{1,0:T(1,128)S(1)} %reshape.12.gain_ref, ...), custom_call_target="tpu_custom_call" | custom-call | flops 1000 | bytes 1000 | tf_op jit(solution)/shard_map/finish/pallas_call | solution.py:257
  (45 shorter events, 6.0 us)
Async XLA Ops:
  2.6 28.6 %copy-start.6 = (f32[1280]{0:T(1024)S(1)}, f32[1280]{0:T(1024)}, u32[]{:S(2)}) copy-start(f32[1280]{0:T(1024)} %param.15) | copy-start | bytes 15364
  2.6 28.6 %copy-start.7 = (f32[1280]{0:T(1024)S(1)}, f32[1280]{0:T(1024)}, u32[]{:S(2)}) copy-start(f32[1280]{0:T(1024)} %param.16) | copy-start | bytes 15364
  2.6 28.6 %copy-start.1 = (bf16[256,1280]{1,0:T(8,128)(2,1)S(1)}, bf16[256,1280]{1,0:T(8,128)(2,1)}, u32[]{:S(2)}) copy-start(bf16[256,1280]{1,0:T(8,128)(2,1)} %pos_ref.1) | copy-start | bytes 1966084
  2.7 28.6 %copy-start.5 = (s32[4]{0:T(128)S(1)}, s32[4]{0:T(128)}, u32[]{:S(2)}) copy-start(s32[4]{0:T(128)} %visible_ref.1) | copy-start | bytes 52
  2.7 14.0 %collective-permute-start.1 = (bf16[4,32,1280]{2,1,0:T(8,128)(2,1)S(1)}, bf16[4,32,1280]{2,1,0:T(8,128)(2,1)S(1)}, u32[]{:S(2)}, u32[]{:S(2)}) collective-permute-start(bf16[4,32,1280]{2,1,0:T(8,128)(2,1)S(1)} %copy-done.2), channel_id=1, source_target_pairs={{0,8},{4,12},{8,0},{12,4},{1,9},{5,13},{9,1},{13,5},{2,10},{6,14},... | collective-permute-start | bytes 983048 | tf_op jit(solution)/shard_map/ppermute | solution.py:245
  5.7 11.0 %collective-permute-start = (bf16[4,32,1280]{2,1,0:T(8,128)(2,1)S(1)}, bf16[4,32,1280]{2,1,0:T(8,128)(2,1)S(1)}, u32[]{:S(2)}, u32[]{:S(2)}) collective-permute-start(bf16[4,32,1280]{2,1,0:T(8,128)(2,1)S(1)} %copy-done.2), channel_id=1, source_target_pairs={{0,4},{4,0},{8,12},{12,8},{1,5},{5,1},{9,13},{13,9},{2,6},{6,2},{1... | collective-permute-start | bytes 983048 | tf_op jit(solution)/shard_map/ppermute | solution.py:245
  5.7 11.0 %collective-permute-start.2 = (bf16[160,960]{1,0:T(8,128)(2,1)S(1)}, bf16[160,960]{1,0:T(8,128)(2,1)S(1)}, u32[]{:S(2)}, u32[]{:S(2)}) collective-permute-start(bf16[160,960]{1,0:T(8,128)(2,1)S(1)} %pick.2.refs_0_), channel_id=1, source_target_pairs={{0,1},{1,3},{3,2},{2,0},{4,5},{5,7},{7,6},{6,4},{8,9},{9,11},{11,1... | collective-permute-start | bytes 921608 | tf_op jit(solution)/shard_map/ppermute | solution.py:302
  16.7 12.3 %collective-permute-start.3 = (bf16[4,32,1280]{2,1,0:T(8,128)(2,1)S(1)}, bf16[4,32,1280]{2,1,0:T(8,128)(2,1)S(1)}, u32[]{:S(2)}, u32[]{:S(2)}) collective-permute-start(bf16[4,32,1280]{2,1,0:T(8,128)(2,1)S(1)} %collective-permute-done.1.refs_2_), channel_id=1, source_target_pairs={{0,4},{4,0},{8,12},{12,8},{1,5},{5,1},{9,13},{13,9},{2,6},{6,2},{1... | collective-permute-start | bytes 983048 | tf_op jit(solution)/shard_map/ppermute | solution.py:245
  16.7 10.1 %collective-permute-start.6 = (bf16[160,960]{1,0:T(8,128)(2,1)S(1)}, bf16[160,960]{1,0:T(8,128)(2,1)S(1)}, u32[]{:S(2)}, u32[]{:S(2)}) collective-permute-start(bf16[160,960]{1,0:T(8,128)(2,1)S(1)} %collective-permute-done.2.refs_2_), channel_id=1, source_target_pairs={{0,16},{16,0},{1,17},{17,1},{2,18},{18,2},{3,19},{19,3},{4,20},{20... | collective-permute-start | bytes 921608 | tf_op jit(solution)/shard_map/ppermute | solution.py:245
  18.3 10.7 %collective-permute-start.5 = (bf16[160,960]{1,0:T(8,128)(2,1)S(1)}, bf16[160,960]{1,0:T(8,128)(2,1)S(1)}, u32[]{:S(2)}, u32[]{:S(2)}) collective-permute-start(bf16[160,960]{1,0:T(8,128)(2,1)S(1)} %collective-permute-done.2.refs_2_), channel_id=1, source_target_pairs={{0,1},{1,3},{3,2},{2,0},{4,5},{5,7},{7,6},{6,4},{8,9},{9,11},{11,1... | collective-permute-start | bytes 921608 | tf_op jit(solution)/shard_map/ppermute | solution.py:304
  19.7 27.2 %copy-start.3 = (s32[4,128]{1,0:T(4,128)S(1)}, s32[4,128]{1,0:T(4,128)}, u32[]{:S(2)}) copy-start(s32[4,128]{1,0:T(4,128)} %valid_ref.1) | copy-start | bytes 6148
  19.7 6.1 %collective-permute-start.4 = (bf16[4,32,640]{2,1,0:T(8,128)(2,1)S(1)}, bf16[4,32,640]{2,1,0:T(8,128)(2,1)S(1)}, u32[]{:S(2)}, u32[]{:S(2)}) collective-permute-start(bf16[4,32,640]{2,1,0:T(8,128)(2,1)S(1)} %columns.1), channel_id=1, source_target_pairs={{0,8},{4,12},{8,0},{12,4},{1,9},{5,13},{9,1},{13,5},{2,10},{6,14},... | collective-permute-start | bytes 491528 | tf_op jit(solution)/shard_map/ppermute | solution.py:245
  29.0 9.8 %collective-permute-start.9 = (bf16[160,960]{1,0:T(8,128)(2,1)S(1)}, bf16[160,960]{1,0:T(8,128)(2,1)S(1)}, u32[]{:S(2)}, u32[]{:S(2)}) collective-permute-start(bf16[160,960]{1,0:T(8,128)(2,1)S(1)} %collective-permute-done.5.refs_4_), channel_id=1, source_target_pairs={{0,1},{1,3},{3,2},{2,0},{4,5},{5,7},{7,6},{6,4},{8,9},{9,11},{11,1... | collective-permute-start | bytes 921608 | tf_op jit(solution)/shard_map/ppermute | solution.py:323
  29.8 9.1 %collective-permute-start.8 = (bf16[160,960]{1,0:T(8,128)(2,1)S(1)}, bf16[160,960]{1,0:T(8,128)(2,1)S(1)}, u32[]{:S(2)}, u32[]{:S(2)}) collective-permute-start(bf16[160,960]{1,0:T(8,128)(2,1)S(1)} %collective-permute-done.5.refs_4_), channel_id=1, source_target_pairs={{0,16},{16,0},{1,17},{17,1},{2,18},{18,2},{3,19},{19,3},{4,20},{20... | collective-permute-start | bytes 921608 | tf_op jit(solution)/shard_map/ppermute | solution.py:245
  31.1 2.1 %collective-permute-start.7 = (bf16[2,4,32,320]{3,2,1,0:T(8,128)(2,1)S(1)}, bf16[2,4,32,320]{3,2,1,0:T(8,128)(2,1)S(1)}, u32[]{:S(2)}, u32[]{:S(2)}) collective-permute-start(bf16[2,4,32,320]{3,2,1,0:T(8,128)(2,1)S(1)} %get-tuple-element.40), channel_id=1, source_target_pairs={{0,4},{4,0},{8,12},{12,8},{1,5},{5,1},{9,13},{13,9},{2,6},{6,2},{1... | collective-permute-start | bytes 491528 | tf_op jit(solution)/shard_map/ppermute | solution.py:245
  38.8 8.0 %collective-permute-start.10 = (bf16[160,960]{1,0:T(8,128)(2,1)S(1)}, bf16[160,960]{1,0:T(8,128)(2,1)S(1)}, u32[]{:S(2)}, u32[]{:S(2)}) collective-permute-start(bf16[160,960]{1,0:T(8,128)(2,1)S(1)} %collective-permute-done.9.refs_6_), channel_id=1, source_target_pairs={{0,16},{16,0},{1,17},{17,1},{2,18},{18,2},{3,19},{19,3},{4,20},{20... | collective-permute-start | bytes 921608 | tf_op jit(solution)/shard_map/ppermute | solution.py:245
  52.9 2.2 %collective-permute-start.11 = (bf16[272,1280]{1,0:T(8,128)(2,1)S(1)}, bf16[272,1280]{1,0:T(8,128)(2,1)S(1)}, u32[]{:S(2)}, u32[]{:S(2)}) collective-permute-start(bf16[272,1280]{1,0:T(8,128)(2,1)S(1)} %get-tuple-element.46), channel_id=1, source_target_pairs={{0,4},{4,0},{8,12},{12,8},{1,5},{5,1},{9,13},{13,9},{2,6},{6,2},{1... | collective-permute-start | bytes 2088968 | tf_op jit(solution)/shard_map/ppermute | solution.py:245
  52.9 7.8 %collective-permute-start.12 = (bf16[2,4,32,320]{3,2,1,0:T(8,128)(2,1)S(1)}, bf16[2,4,32,320]{3,2,1,0:T(8,128)(2,1)S(1)}, u32[]{:S(2)}, u32[]{:S(2)}) collective-permute-start(bf16[2,4,32,320]{3,2,1,0:T(8,128)(2,1)S(1)} %get-tuple-element.49), channel_id=1, source_target_pairs={{0,8},{4,12},{8,0},{12,4},{1,9},{5,13},{9,1},{13,5},{2,10},{6,14},... | collective-permute-start | bytes 491528 | tf_op jit(solution)/shard_map/ppermute | solution.py:245
  55.2 17.6 %collective-permute-start.14 = (bf16[4,32,1280]{2,1,0:T(8,128)(2,1)S(1)}, bf16[4,32,1280]{2,1,0:T(8,128)(2,1)S(1)}, u32[]{:S(2)}, u32[]{:S(2)}) collective-permute-start(bf16[4,32,1280]{2,1,0:T(8,128)(2,1)S(1)} %get-tuple-element.52), channel_id=1, source_target_pairs={{0,8},{4,12},{8,0},{12,4},{1,9},{5,13},{9,1},{13,5},{2,10},{6,14},... | collective-permute-start | bytes 983048 | tf_op jit(solution)/shard_map/ppermute | solution.py:245
  60.7 8.9 %collective-permute-start.13 = (bf16[2,4,32,320]{3,2,1,0:T(8,128)(2,1)S(1)}, bf16[2,4,32,320]{3,2,1,0:T(8,128)(2,1)S(1)}, u32[]{:S(2)}, u32[]{:S(2)}) collective-permute-start(bf16[2,4,32,320]{3,2,1,0:T(8,128)(2,1)S(1)} %both.1), channel_id=1, source_target_pairs={{0,4},{4,0},{8,12},{12,8},{1,5},{5,1},{9,13},{13,9},{2,6},{6,2},{1... | collective-permute-start | bytes 491528 | tf_op jit(solution)/shard_map/ppermute | solution.py:245
  60.8 5.5 %collective-permute-start.17 = (f32[2,1280]{1,0:T(2,128)S(1)}, f32[2,1280]{1,0:T(2,128)S(1)}, u32[]{:S(2)}, u32[]{:S(2)}) collective-permute-start(f32[2,1280]{1,0:T(2,128)S(1)} %get-tuple-element.58.refs_0_), channel_id=1, source_target_pairs={{0,3},{1,2},{2,1},{3,0},{4,7},{5,6},{6,5},{7,4},{8,11},{9,10},{10,... | collective-permute-start | bytes 30728 | tf_op jit(solution)/shard_map/ppermute | solution.py:245
  64.5 4.6 %collective-permute-start.16 = (f32[2,1280]{1,0:T(2,128)S(1)}, f32[2,1280]{1,0:T(2,128)S(1)}, u32[]{:S(2)}, u32[]{:S(2)}) collective-permute-start(f32[2,1280]{1,0:T(2,128)S(1)} %get-tuple-element.58.refs_0_), channel_id=1, source_target_pairs={{0,2},{1,3},{2,0},{3,1},{4,6},{5,7},{6,4},{7,5},{8,10},{9,11},{10,... | collective-permute-start | bytes 30728 | tf_op jit(solution)/shard_map/ppermute | solution.py:245
  65.0 4.0 %collective-permute-start.15 = (f32[2,1280]{1,0:T(2,128)S(1)}, f32[2,1280]{1,0:T(2,128)S(1)}, u32[]{:S(2)}, u32[]{:S(2)}) collective-permute-start(f32[2,1280]{1,0:T(2,128)S(1)} %get-tuple-element.58.refs_0_), channel_id=1, source_target_pairs={{0,1},{1,0},{2,3},{3,2},{4,5},{5,4},{6,7},{7,6},{8,9},{9,8},{10,11... | collective-permute-start | bytes 30728 | tf_op jit(solution)/shard_map/ppermute | solution.py:245
  69.1 3.7 %collective-permute-start.18 = (f32[2,1280]{1,0:T(2,128)S(1)}, f32[2,1280]{1,0:T(2,128)S(1)}, u32[]{:S(2)}, u32[]{:S(2)}) collective-permute-start(f32[2,1280]{1,0:T(2,128)S(1)} %add.5.refs_0_), channel_id=1, source_target_pairs={{0,8},{4,12},{8,0},{12,4},{1,9},{5,13},{9,1},{13,5},{2,10},{6,14},... | collective-permute-start | bytes 30728 | tf_op jit(solution)/shard_map/ppermute | solution.py:245
  (3 other events, 47.6 us)

commit v6 on v5

--- a/solution.py
+++ b/solution.py
@@ -107,7 +107,7 @@
     share = depth // 2
     spot = owner ^ (owner >> 1)
     firsts = []
-    for step in range(owners):
+    for step in (0, 1, 3, 2):
         back = lax.rem(spot + owners - step, owners)
         source = back ^ (back >> 1)
         firsts.append(pl.multiple_of(source * depth + rep * share, 16))
@@ -253,7 +253,7 @@
     return pltpu.with_memory_space_constraint(array, pltpu.VMEM)
 
 
-def call(kernel, name, out_shape, in_specs, args, megabytes, scratch=()):
+def call(kernel, name, out_shape, in_specs, args, megabytes, scratch=(), microseconds=0.01):
     return pl.pallas_call(
         kernel,
         out_shape=out_shape,
@@ -261,7 +261,9 @@
         out_specs=jax.tree.map(lambda _: VMEM, out_shape),
         scratch_shapes=list(scratch),
         compiler_params=pltpu.CompilerParams(vmem_limit_bytes=megabytes * 1024 * 1024),
-        cost_estimate=pl.CostEstimate(flops=1000, bytes_accessed=1000, transcendentals=0),
+        cost_estimate=pl.CostEstimate(
+            flops=int(microseconds * 10**9), bytes_accessed=1000, transcendentals=0
+        ),
         name=name,
     )(*args)
 
@@ -300,9 +302,11 @@
     beside = swapped(sooner, "date", 1)
     if chain:
         first = lax.ppermute(held, "tile", ring)
+        third = lax.ppermute(held, "tile", [(b, a) for a, b in ring])
         first = after(first, across, beside)
         second = lax.ppermute(first, "tile", ring)
         first_other = swapped(first, "rep", 1)
+        third_other = swapped(third, "rep", 1)
         rest = pick(w_qkv, after(ids, first), share, part, True)
     else:
         first = ids
@@ -320,7 +324,6 @@
     columns = swapped(columns, "date", 2)
     if chain:
         second = after(second, first_other, beyond, columns, rest)
-        third = lax.ppermute(second, "tile", ring)
         second_other = swapped(second, "rep", 1)
         columns = after(columns, second)
     ups, ups_beside = call(
@@ -332,6 +335,8 @@
         4,
     )
     ups_beside = swapped(ups_beside, "date", 1)
+    if chain:
+        beyond = after(beyond, third_other)
 
     normed, unit, own_unit, own_inv = call(
         norm_kernel,
@@ -345,11 +350,10 @@
         [SMEM] + [VMEM] * (3 + groups),
         (visible, pos_table, gain2, bias2, tokens, near(beside), near(across), near(beyond)),
         12,
+        microseconds=2,
     )
     if chain:
-        third = after(third, second_other, ups_beside, normed)
-        third_other = swapped(third, "rep", 1)
-        pieces = [held, rest, first, first_other, second, second_other, third, third_other]
+        pieces = [held, rest, first, first_other, third, third_other, second, second_other]
     else:
         group = lax.axis_index("date")
         mine = [
@@ -388,6 +392,16 @@
     )
 
     close = swapped(cross, "date", 1)
+    both = call(
+        both_kernel,
+        "both",
+        pair,
+        [VMEM] * 2,
+        (near(close_context), near(far_context)),
+        2,
+        microseconds=10,
+    )
+    close = after(close, both)
     chip, total = call(
         merge_kernel,
         "merge",
@@ -396,8 +410,6 @@
         (near(passing), near(close), near(sums)),
         6,
     )
-    far_context = after(far_context, chip)
-    both = call(both_kernel, "both", pair, [VMEM] * 2, (near(close_context), near(far_context)), 2)
     far = swapped(chip, "date", 2)
     if owners == 4:
         total = call(

time: 74.6 us -> 73.3 us (0.983)
  waiting for transfers between devices: 41.3 us -> 25.2 us
  starting transfers between devices: 15.8 us -> 30.7 us
    ppermute x16, waiting for transfers between devices: 24.2 us -> 16.6 us  [swapped(): lax.ppermute(array, axis, [(i, i ^ bits) for i in range(lax.axis_size(axi...]
    ppermute x16, starting transfers between devices: 12.7 us -> 20 us  [swapped(): lax.ppermute(array, axis, [(i, i ^ bits) for i in range(lax.axis_size(axi...]
    ppermute x1, starting transfers between devices: 0.78 us -> 7.74 us  [local(): second = lax.ppermute(first, 'tile', ring)]
    ppermute x1, waiting for transfers between devices: 5.6 us -> 0.01 us  [local(): third = lax.ppermute(held, 'tile', [(b, a) for a, b in ring])]
    ppermute x1, waiting for transfers between devices: 2.14 us -> 0.43 us  [local(): second = lax.ppermute(first, 'tile', ring)]
    ppermute x1, waiting for transfers between devices: 9.45 us -> 8.2 us  [local(): first = lax.ppermute(held, 'tile', ring)]
  transfers between devices with their start and end apart: 19 -> 19, of which waited for: 11 -> 9; matrix products, arithmetic and copies ran while one was open for 0% -> 0% of each run, Pallas kernels for 9% -> 11%
where the time goes in v6:
time: 73.3 us; the launch traced here: 73.1 us
  starting transfers between devices  30.7 us (42%)
  waiting for transfers between devices  25.2 us (34%)
  Pallas kernels  16.3 us (22%)
  between operations  0.84 us (1%)
    ppermute x16, starting transfers between devices, swapped(): lax.ppermute(array, axis, [(i, i ^ bits) for i in range(lax.axis_size(axi...  20 us
    ppermute x16, waiting for transfers between devices, swapped(): lax.ppermute(array, axis, [(i, i ^ bits) for i in range(lax.axis_size(axi...  16.6 us
    pallas_call x12, Pallas kernels, call(): pl.pallas_call(kernel, out_shape=out_shape, in_specs=in_specs, out_specs=...  16.3 us
    ppermute x1, waiting for transfers between devices, local(): first = lax.ppermute(held, 'tile', ring)  8.2 us
    ppermute x1, starting transfers between devices, local(): second = lax.ppermute(first, 'tile', ring)  7.74 us
    ppermute x1, starting transfers between devices, local(): first = lax.ppermute(held, 'tile', ring)  1.58 us
  transfers between devices with their start and end apart: 19, of which 9 were waited for; matrix products, arithmetic and copies ran while one was open for 0% of the time, Pallas kernels for 11%

profile of v6, /device:TPU:0, one launch (start us, length us, event | category | flops | bytes accessed | tf_op | source)
XLA Modules:
  0.0 73.1 jit_solution(8260793827905967602)
XLA Ops:
  0.7 1.9 %pick.2.refs_0_ = bf16[160,960]{1,0:T(8,128)(2,1)S(1)} custom-call(s32[3]{0:T(128)S(1)} %pad_add_fusion.ids_ref, bf16[320,3840]{1,0:T(8,128)(2,1)} %w_ref.3), custom_call_target="tpu_custom_call" | custom-call | flops 10000000 | bytes 1000 | tf_op jit(solution)/shard_map/pick/pallas_call | solution.py:257
  2.6 3.0 %collective-permute-start.1 = (bf16[4,32,1280]{2,1,0:T(8,128)(2,1)S(1)}, bf16[4,32,1280]{2,1,0:T(8,128)(2,1)S(1)}, u32[]{:S(2)}, u32[]{:S(2)}) collective-permute-start(bf16[4,32,1280]{2,1,0:T(8,128)(2,1)S(1)} %copy-done.4), channel_id=1, source_target_pairs={{0,8},{4,12},{8,0},{12,4},{1,9},{5,13},{9,1},{13,5},{2,10},{6,14},... | collective-permute-start | bytes 983048 | tf_op jit(solution)/shard_map/ppermute | solution.py:245
  5.7 1.6 %collective-permute-start.2 = (bf16[160,960]{1,0:T(8,128)(2,1)S(1)}, bf16[160,960]{1,0:T(8,128)(2,1)S(1)}, u32[]{:S(2)}, u32[]{:S(2)}) collective-permute-start(bf16[160,960]{1,0:T(8,128)(2,1)S(1)} %pick.2.refs_0_), channel_id=1, source_target_pairs={{0,1},{1,3},{3,2},{2,0},{4,5},{5,7},{7,6},{6,4},{8,9},{9,11},{11,1... | collective-permute-start | bytes 921608 | tf_op jit(solution)/shard_map/ppermute | solution.py:304
  7.2 1.3 %collective-permute-start.4 = (bf16[160,960]{1,0:T(8,128)(2,1)S(1)}, bf16[160,960]{1,0:T(8,128)(2,1)S(1)}, u32[]{:S(2)}, u32[]{:S(2)}) collective-permute-start(bf16[160,960]{1,0:T(8,128)(2,1)S(1)} %pick.2.refs_0_), channel_id=1, source_target_pairs={{1,0},{3,1},{2,3},{0,2},{5,4},{7,5},{6,7},{4,6},{9,8},{11,9},{10,1... | collective-permute-start | bytes 921608 | tf_op jit(solution)/shard_map/ppermute | solution.py:305
  8.6 8.2 %collective-permute-done.2.refs_2_ = bf16[160,960]{1,0:T(8,128)(2,1)S(1)} collective-permute-done((bf16[160,960]{1,0:T(8,128)(2,1)S(1)}, bf16[160,960]{1,0:T(8,128)(2,1)S(1)}, u32[]{:S(2)}, u32[]{:S(2)}) %collective-permute-start.2) | collective-permute-done | bytes 307232 | tf_op jit(solution)/shard_map/ppermute | solution.py:304
  16.8 1.6 %collective-permute-start.8 = (bf16[160,960]{1,0:T(8,128)(2,1)S(1)}, bf16[160,960]{1,0:T(8,128)(2,1)S(1)}, u32[]{:S(2)}, u32[]{:S(2)}) collective-permute-start(bf16[160,960]{1,0:T(8,128)(2,1)S(1)} %collective-permute-done.2.refs_2_), channel_id=1, source_target_pairs={{0,16},{16,0},{1,17},{17,1},{2,18},{18,2},{3,19},{19,3},{4,20},{20... | collective-permute-start | bytes 921608 | tf_op jit(solution)/shard_map/ppermute | solution.py:245
  18.4 7.7 %collective-permute-start.7 = (bf16[160,960]{1,0:T(8,128)(2,1)S(1)}, bf16[160,960]{1,0:T(8,128)(2,1)S(1)}, u32[]{:S(2)}, u32[]{:S(2)}) collective-permute-start(bf16[160,960]{1,0:T(8,128)(2,1)S(1)} %collective-permute-done.2.refs_2_), channel_id=1, source_target_pairs={{0,1},{1,3},{3,2},{2,0},{4,5},{5,7},{7,6},{6,4},{8,9},{9,11},{11,1... | collective-permute-start | bytes 921608 | tf_op jit(solution)/shard_map/ppermute | solution.py:307
  27.8 1.9 %pick.3.refs_1_ = bf16[160,960]{1,0:T(8,128)(2,1)S(1)} custom-call(s32[3]{0:T(128)S(1)} %pad_add_fusion.ids_ref, bf16[320,3840]{1,0:T(8,128)(2,1)} %w_ref.3), custom_call_target="tpu_custom_call" | custom-call | flops 10000000 | bytes 1000 | tf_op jit(solution)/shard_map/pick/pallas_call | solution.py:257
  29.7 3.3 %collective-permute-done.6.columns_ref = bf16[4,32,640]{2,1,0:T(8,128)(2,1)S(1)} collective-permute-done((bf16[4,32,640]{2,1,0:T(8,128)(2,1)S(1)}, bf16[4,32,640]{2,1,0:T(8,128)(2,1)S(1)}, u32[]{:S(2)}, u32[]{:S(2)}) %collective-permute-start.6) | collective-permute-done | bytes 163872 | tf_op jit(solution)/shard_map/ppermute | solution.py:245
  33.4 1.2 %collective-permute-start.10 = (bf16[160,960]{1,0:T(8,128)(2,1)S(1)}, bf16[160,960]{1,0:T(8,128)(2,1)S(1)}, u32[]{:S(2)}, u32[]{:S(2)}) collective-permute-start(bf16[160,960]{1,0:T(8,128)(2,1)S(1)} %collective-permute-done.7.refs_6_), channel_id=1, source_target_pairs={{0,16},{16,0},{1,17},{17,1},{2,18},{18,2},{3,19},{19,3},{4,20},{20... | collective-permute-start | bytes 921608 | tf_op jit(solution)/shard_map/ppermute | solution.py:245
  34.6 1.2 %collective-permute-done.5.refs_5_ = bf16[160,960]{1,0:T(8,128)(2,1)S(1)} collective-permute-done((bf16[160,960]{1,0:T(8,128)(2,1)S(1)}, bf16[160,960]{1,0:T(8,128)(2,1)S(1)}, u32[]{:S(2)}, u32[]{:S(2)}) %collective-permute-start.5) | collective-permute-done | bytes 307232 | tf_op jit(solution)/shard_map/ppermute | solution.py:245
  35.8 0.8 %part.1 = (bf16[2,4,32,320]{3,2,1,0:T(8,128)(2,1)S(1)}, bf16[2,4,32,320]{3,2,1,0:T(8,128)(2,1)S(1)}) custom-call(s32[3]{0:T(128)S(1)} %pad_add_fusion.ids_ref, bf16[4,32,1280]{2,1,0:T(8,128)(2,1)S(1)} %copy-done, bf16[4,32,640]{2,1,0:T(8,128)(2,1)S(1)} %collective-permute-done.6.columns_ref), custom_call_target="tpu_custom_call" | custom-call | flops 10000000 | bytes 1000 | tf_op jit(solution)/shard_map/part/pallas_call | solution.py:257
  36.8 1.9 %norm.1 = (bf16[512,1280]{1,0:T(8,128)(2,1)S(1)}, bf16[512,1280]{1,0:T(8,128)(2,1)S(1)}, f32[4,32,1280]{2,1,0:T(8,128)S(1)}, f32[4,32,128]{2,1,0:T(8,128)S(1)}) custom-call(s32[4]{0:T(128)S(1)} %copy-done.5, bf16[256,1280]{1,0:T(8,128)(2,1)S(1)} %copy-done.3, f32[1,1280]{1,0:T(1,128)S(1)} %reshape.12.gain_ref, f32[1,1280]{1,0:T(1,128)S(1)} %reshape.13.bias_ref, ...), custom_call_target="tpu_custom_call" | custom-call | flops 2000000000 | bytes 1000 | tf_op jit(solution)/shard_map/norm/pallas_call | solution.py:257
  38.8 3.9 %collective-permute-done.10.refs_7_ = bf16[160,960]{1,0:T(8,128)(2,1)S(1)} collective-permute-done((bf16[160,960]{1,0:T(8,128)(2,1)S(1)}, bf16[160,960]{1,0:T(8,128)(2,1)S(1)}, u32[]{:S(2)}, u32[]{:S(2)}) %collective-permute-start.10) | collective-permute-done | bytes 307232 | tf_op jit(solution)/shard_map/ppermute | solution.py:245
  42.7 4.4 %attend.1 = (bf16[4,32,320]{2,1,0:T(8,128)(2,1)S(1)}, bf16[4,32,320]{2,1,0:T(8,128)(2,1)S(1)}, bf16[2,4,32,320]{3,2,1,0:T(8,128)(2,1)S(1)}, bf16[512,960]{1,0:T(8,128)(2,1)S(1)}, bf16[1280,960]{1,0:T(8,128)(2,1)S(1)}) custom-call(s32[3]{0:T(128)S(1)} %pad_add_fusion.ids_ref, s32[4]{0:T(128)S(1)} %copy-done.2, ...), custom_call_target="tpu_custom_call" | custom-call | flops 10000000 | bytes 1000 | tf_op jit(solution)/shard_map/attend/pallas_call | solution.py:257
  47.6 1.6 %back.1 = (bf16[4,32,1280]{2,1,0:T(8,128)(2,1)S(1)}, bf16[4,32,1280]{2,1,0:T(8,128)(2,1)S(1)}, bf16[272,1280]{1,0:T(8,128)(2,1)S(1)}, f32[2,1280]{1,0:T(2,128)S(1)}) custom-call(bf16[512,960]{1,0:T(8,128)(2,1)S(1)} %get-tuple-element.42.gqkv_ref, bf16[512,1280]{1,0:T(8,128)(2,1)S(1)} %get-tuple-element.43.unit_ref, ...), custom_call_target="tpu_custom_call" | custom-call | flops 10000000 | bytes 1000 | tf_op jit(solution)/shard_map/back/pallas_call | solution.py:257
  49.4 3.4 %collective-permute-done.12.far_ref.across_ref = bf16[2,4,32,320]{3,2,1,0:T(8,128)(2,1)S(1)} collective-permute-done((bf16[2,4,32,320]{3,2,1,0:T(8,128)(2,1)S(1)}, bf16[2,4,32,320]{3,2,1,0:T(8,128)(2,1)S(1)}, u32[]{:S(2)}, u32[]{:S(2)}) %collective-permute-start.12) | collective-permute-done | bytes 163872 | tf_op jit(solution)/shard_map/ppermute | solution.py:245
  53.5 9.7 %collective-permute-start.17 = (f32[2,1280]{1,0:T(2,128)S(1)}, f32[2,1280]{1,0:T(2,128)S(1)}, u32[]{:S(2)}, u32[]{:S(2)}) collective-permute-start(f32[2,1280]{1,0:T(2,128)S(1)} %get-tuple-element.58.refs_0_), channel_id=1, source_target_pairs={{0,3},{1,2},{2,1},{3,0},{4,7},{5,6},{6,5},{7,4},{8,11},{9,10},{10,... | collective-permute-start | bytes 30728 | tf_op jit(solution)/shard_map/ppermute | solution.py:245
  63.7 1.1 %collective-permute-done.17.refs_3_ = f32[2,1280]{1,0:T(2,128)S(1)} collective-permute-done((f32[2,1280]{1,0:T(2,128)S(1)}, f32[2,1280]{1,0:T(2,128)S(1)}, u32[]{:S(2)}, u32[]{:S(2)}) %collective-permute-start.17) | collective-permute-done | bytes 10272 | tf_op jit(solution)/shard_map/ppermute | solution.py:245
  64.8 2.9 %collective-permute-done.16.refs_2_ = f32[2,1280]{1,0:T(2,128)S(1)} collective-permute-done((f32[2,1280]{1,0:T(2,128)S(1)}, f32[2,1280]{1,0:T(2,128)S(1)}, u32[]{:S(2)}, u32[]{:S(2)}) %collective-permute-start.16) | collective-permute-done | bytes 10272 | tf_op jit(solution)/shard_map/ppermute | solution.py:245
  67.7 1.6 %collective-permute-start.18 = (f32[2,1280]{1,0:T(2,128)S(1)}, f32[2,1280]{1,0:T(2,128)S(1)}, u32[]{:S(2)}, u32[]{:S(2)}) collective-permute-start(f32[2,1280]{1,0:T(2,128)S(1)} %add.5.refs_0_), channel_id=1, source_target_pairs={{0,8},{4,12},{8,0},{12,4},{1,9},{5,13},{9,1},{13,5},{2,10},{6,14},... | collective-permute-start | bytes 30728 | tf_op jit(solution)/shard_map/ppermute | solution.py:245
  69.3 1.4 %home.1 = (f32[4,32,1280]{2,1,0:T(8,128)S(1)}, bf16[4,32,1280]{2,1,0:T(8,128)(2,1)}) custom-call(s32[3]{0:T(128)S(1)} %pad_add_fusion.ids_ref, bf16[4,32,1280]{2,1,0:T(8,128)(2,1)S(1)} %get-tuple-element.45.stay_ref, bf16[272,1280]{1,0:T(8,128)(2,1)S(1)} %collective-permute-done.11.close_ref, bf16[4,32,320]{2,1,0:T(8,128)(2,1)S(1)} %get-tuple-element.50.own_ref, ...), custom_call_target="tpu_custom_call" | custom-call | flops 10000000 | bytes 1000 | tf_op jit(solution)/shard_map/home/pallas_call | solution.py:257
  70.7 0.7 %collective-permute-done.18.refs_1_ = f32[2,1280]{1,0:T(2,128)S(1)} collective-permute-done((f32[2,1280]{1,0:T(2,128)S(1)}, f32[2,1280]{1,0:T(2,128)S(1)}, u32[]{:S(2)}, u32[]{:S(2)}) %collective-permute-start.18) | collective-permute-done | bytes 10272 | tf_op jit(solution)/shard_map/ppermute | solution.py:245
  71.5 1.6 %finish.1 = (bf16[4,32,1280]{2,1,0:T(8,128)(2,1)}, f32[2,1280]{1,0:T(2,128)}) custom-call(s32[3]{0:T(128)S(1)} %pad_add_fusion.ids_ref, s32[4]{0:T(128)S(1)} %copy-done.2, f32[4,32,1280]{2,1,0:T(8,128)S(1)} %get-tuple-element.52.unit_ref, f32[4,32,128]{2,1,0:T(8,128)S(1)} %get-tuple-element.53.inv_ref, f32[1,1280]{1,0:T(1,128)S(1)} %reshape.12.gain_ref, ...), custom_call_target="tpu_custom_call" | custom-call | flops 10000000 | bytes 1000 | tf_op jit(solution)/shard_map/finish/pallas_call | solution.py:257
  (45 shorter events, 4.3 us)
Async XLA Ops:
  0.6 26.0 %copy-start = (bf16[4,32,1280]{2,1,0:T(8,128)(2,1)S(1)}, bf16[4,32,1280]{2,1,0:T(8,128)(2,1)}, u32[]{:S(2)}) copy-start(bf16[4,32,1280]{2,1,0:T(8,128)(2,1)} %cotangent_ref.3) | copy-start | bytes 983044
  0.7 33.9 %copy-start.6 = (f32[1280]{0:T(1024)S(1)}, f32[1280]{0:T(1024)}, u32[]{:S(2)}) copy-start(f32[1280]{0:T(1024)} %param.15) | copy-start | bytes 15364
  0.7 33.9 %copy-start.7 = (f32[1280]{0:T(1024)S(1)}, f32[1280]{0:T(1024)}, u32[]{:S(2)}) copy-start(f32[1280]{0:T(1024)} %param.16) | copy-start | bytes 15364
  2.6 34.2 %copy-start.3 = (bf16[256,1280]{1,0:T(8,128)(2,1)S(1)}, bf16[256,1280]{1,0:T(8,128)(2,1)}, u32[]{:S(2)}) copy-start(bf16[256,1280]{1,0:T(8,128)(2,1)} %pos_ref.1) | copy-start | bytes 1966084
  2.6 34.2 %copy-start.5 = (s32[4]{0:T(128)S(1)}, s32[4]{0:T(128)}, u32[]{:S(2)}) copy-start(s32[4]{0:T(128)} %visible_ref.1) | copy-start | bytes 52
  2.6 14.1 %collective-permute-start.1 = (bf16[4,32,1280]{2,1,0:T(8,128)(2,1)S(1)}, bf16[4,32,1280]{2,1,0:T(8,128)(2,1)S(1)}, u32[]{:S(2)}, u32[]{:S(2)}) collective-permute-start(bf16[4,32,1280]{2,1,0:T(8,128)(2,1)S(1)} %copy-done.4), channel_id=1, source_target_pairs={{0,8},{4,12},{8,0},{12,4},{1,9},{5,13},{9,1},{13,5},{2,10},{6,14},... | collective-permute-start | bytes 983048 | tf_op jit(solution)/shard_map/ppermute | solution.py:245
  5.6 11.1 %collective-permute-start = (bf16[4,32,1280]{2,1,0:T(8,128)(2,1)S(1)}, bf16[4,32,1280]{2,1,0:T(8,128)(2,1)S(1)}, u32[]{:S(2)}, u32[]{:S(2)}) collective-permute-start(bf16[4,32,1280]{2,1,0:T(8,128)(2,1)S(1)} %copy-done.4), channel_id=1, source_target_pairs={{0,4},{4,0},{8,12},{12,8},{1,5},{5,1},{9,13},{13,9},{2,6},{6,2},{1... | collective-permute-start | bytes 983048 | tf_op jit(solution)/shard_map/ppermute | solution.py:245
  5.7 11.1 %collective-permute-start.2 = (bf16[160,960]{1,0:T(8,128)(2,1)S(1)}, bf16[160,960]{1,0:T(8,128)(2,1)S(1)}, u32[]{:S(2)}, u32[]{:S(2)}) collective-permute-start(bf16[160,960]{1,0:T(8,128)(2,1)S(1)} %pick.2.refs_0_), channel_id=1, source_target_pairs={{0,1},{1,3},{3,2},{2,0},{4,5},{5,7},{7,6},{6,4},{8,9},{9,11},{11,1... | collective-permute-start | bytes 921608 | tf_op jit(solution)/shard_map/ppermute | solution.py:304
  7.2 18.9 %collective-permute-start.4 = (bf16[160,960]{1,0:T(8,128)(2,1)S(1)}, bf16[160,960]{1,0:T(8,128)(2,1)S(1)}, u32[]{:S(2)}, u32[]{:S(2)}) collective-permute-start(bf16[160,960]{1,0:T(8,128)(2,1)S(1)} %pick.2.refs_0_), channel_id=1, source_target_pairs={{1,0},{3,1},{2,3},{0,2},{5,4},{7,5},{6,7},{4,6},{9,8},{11,9},{10,1... | collective-permute-start | bytes 921608 | tf_op jit(solution)/shard_map/ppermute | solution.py:305
  16.8 16.6 %collective-permute-start.3 = (bf16[4,32,1280]{2,1,0:T(8,128)(2,1)S(1)}, bf16[4,32,1280]{2,1,0:T(8,128)(2,1)S(1)}, u32[]{:S(2)}, u32[]{:S(2)}) collective-permute-start(bf16[4,32,1280]{2,1,0:T(8,128)(2,1)S(1)} %collective-permute-done.1.refs_2_), channel_id=1, source_target_pairs={{0,4},{4,0},{8,12},{12,8},{1,5},{5,1},{9,13},{13,9},{2,6},{6,2},{1... | collective-permute-start | bytes 983048 | tf_op jit(solution)/shard_map/ppermute | solution.py:245
  16.8 16.2 %collective-permute-start.8 = (bf16[160,960]{1,0:T(8,128)(2,1)S(1)}, bf16[160,960]{1,0:T(8,128)(2,1)S(1)}, u32[]{:S(2)}, u32[]{:S(2)}) collective-permute-start(bf16[160,960]{1,0:T(8,128)(2,1)S(1)} %collective-permute-done.2.refs_2_), channel_id=1, source_target_pairs={{0,16},{16,0},{1,17},{17,1},{2,18},{18,2},{3,19},{19,3},{4,20},{20... | collective-permute-start | bytes 921608 | tf_op jit(solution)/shard_map/ppermute | solution.py:245
  18.4 15.0 %collective-permute-start.7 = (bf16[160,960]{1,0:T(8,128)(2,1)S(1)}, bf16[160,960]{1,0:T(8,128)(2,1)S(1)}, u32[]{:S(2)}, u32[]{:S(2)}) collective-permute-start(bf16[160,960]{1,0:T(8,128)(2,1)S(1)} %collective-permute-done.2.refs_2_), channel_id=1, source_target_pairs={{0,1},{1,3},{3,2},{2,0},{4,5},{5,7},{7,6},{6,4},{8,9},{9,11},{11,1... | collective-permute-start | bytes 921608 | tf_op jit(solution)/shard_map/ppermute | solution.py:307
  26.1 9.7 %collective-permute-start.5 = (bf16[160,960]{1,0:T(8,128)(2,1)S(1)}, bf16[160,960]{1,0:T(8,128)(2,1)S(1)}, u32[]{:S(2)}, u32[]{:S(2)}) collective-permute-start(bf16[160,960]{1,0:T(8,128)(2,1)S(1)} %collective-permute-done.4.refs_4_), channel_id=1, source_target_pairs={{0,16},{16,0},{1,17},{17,1},{2,18},{18,2},{3,19},{19,3},{4,20},{20... | collective-permute-start | bytes 921608 | tf_op jit(solution)/shard_map/ppermute | solution.py:245
  27.2 5.8 %collective-permute-start.6 = (bf16[4,32,640]{2,1,0:T(8,128)(2,1)S(1)}, bf16[4,32,640]{2,1,0:T(8,128)(2,1)S(1)}, u32[]{:S(2)}, u32[]{:S(2)}) collective-permute-start(bf16[4,32,640]{2,1,0:T(8,128)(2,1)S(1)} %columns.1), channel_id=1, source_target_pairs={{0,8},{4,12},{8,0},{12,4},{1,9},{5,13},{9,1},{13,5},{2,10},{6,14},... | collective-permute-start | bytes 491528 | tf_op jit(solution)/shard_map/ppermute | solution.py:245
  33.4 9.2 %collective-permute-start.10 = (bf16[160,960]{1,0:T(8,128)(2,1)S(1)}, bf16[160,960]{1,0:T(8,128)(2,1)S(1)}, u32[]{:S(2)}, u32[]{:S(2)}) collective-permute-start(bf16[160,960]{1,0:T(8,128)(2,1)S(1)} %collective-permute-done.7.refs_6_), channel_id=1, source_target_pairs={{0,16},{16,0},{1,17},{17,1},{2,18},{18,2},{3,19},{19,3},{4,20},{20... | collective-permute-start | bytes 921608 | tf_op jit(solution)/shard_map/ppermute | solution.py:245
  36.7 2.0 %collective-permute-start.9 = (bf16[2,4,32,320]{3,2,1,0:T(8,128)(2,1)S(1)}, bf16[2,4,32,320]{3,2,1,0:T(8,128)(2,1)S(1)}, u32[]{:S(2)}, u32[]{:S(2)}) collective-permute-start(bf16[2,4,32,320]{3,2,1,0:T(8,128)(2,1)S(1)} %get-tuple-element.41), channel_id=1, source_target_pairs={{0,4},{4,0},{8,12},{12,8},{1,5},{5,1},{9,13},{13,9},{2,6},{6,2},{1... | collective-permute-start | bytes 491528 | tf_op jit(solution)/shard_map/ppermute | solution.py:245
  47.0 5.7 %collective-permute-start.12 = (bf16[2,4,32,320]{3,2,1,0:T(8,128)(2,1)S(1)}, bf16[2,4,32,320]{3,2,1,0:T(8,128)(2,1)S(1)}, u32[]{:S(2)}, u32[]{:S(2)}) collective-permute-start(bf16[2,4,32,320]{3,2,1,0:T(8,128)(2,1)S(1)} %get-tuple-element.48), channel_id=1, source_target_pairs={{0,8},{4,12},{8,0},{12,4},{1,9},{5,13},{9,1},{13,5},{2,10},{6,14},... | collective-permute-start | bytes 491528 | tf_op jit(solution)/shard_map/ppermute | solution.py:245
  49.3 3.5 %collective-permute-start.11 = (bf16[272,1280]{1,0:T(8,128)(2,1)S(1)}, bf16[272,1280]{1,0:T(8,128)(2,1)S(1)}, u32[]{:S(2)}, u32[]{:S(2)}) collective-permute-start(bf16[272,1280]{1,0:T(8,128)(2,1)S(1)} %get-tuple-element.46), channel_id=1, source_target_pairs={{0,4},{4,0},{8,12},{12,8},{1,5},{5,1},{9,13},{13,9},{2,6},{6,2},{1... | collective-permute-start | bytes 2088968 | tf_op jit(solution)/shard_map/ppermute | solution.py:245
  52.9 18.6 %collective-permute-start.14 = (bf16[4,32,1280]{2,1,0:T(8,128)(2,1)S(1)}, bf16[4,32,1280]{2,1,0:T(8,128)(2,1)S(1)}, u32[]{:S(2)}, u32[]{:S(2)}) collective-permute-start(bf16[4,32,1280]{2,1,0:T(8,128)(2,1)S(1)} %get-tuple-element.57), channel_id=1, source_target_pairs={{0,8},{4,12},{8,0},{12,4},{1,9},{5,13},{9,1},{13,5},{2,10},{6,14},... | collective-permute-start | bytes 983048 | tf_op jit(solution)/shard_map/ppermute | solution.py:245
  53.5 15.8 %collective-permute-start.13 = (bf16[2,4,32,320]{3,2,1,0:T(8,128)(2,1)S(1)}, bf16[2,4,32,320]{3,2,1,0:T(8,128)(2,1)S(1)}, u32[]{:S(2)}, u32[]{:S(2)}) collective-permute-start(bf16[2,4,32,320]{3,2,1,0:T(8,128)(2,1)S(1)} %both.1), channel_id=1, source_target_pairs={{0,4},{4,0},{8,12},{12,8},{1,5},{5,1},{9,13},{13,9},{2,6},{6,2},{1... | collective-permute-start | bytes 491528 | tf_op jit(solution)/shard_map/ppermute | solution.py:245
  53.5 11.3 %collective-permute-start.17 = (f32[2,1280]{1,0:T(2,128)S(1)}, f32[2,1280]{1,0:T(2,128)S(1)}, u32[]{:S(2)}, u32[]{:S(2)}) collective-permute-start(f32[2,1280]{1,0:T(2,128)S(1)} %get-tuple-element.58.refs_0_), channel_id=1, source_target_pairs={{0,3},{1,2},{2,1},{3,0},{4,7},{5,6},{6,5},{7,4},{8,11},{9,10},{10,... | collective-permute-start | bytes 30728 | tf_op jit(solution)/shard_map/ppermute | solution.py:245
  63.2 4.6 %collective-permute-start.16 = (f32[2,1280]{1,0:T(2,128)S(1)}, f32[2,1280]{1,0:T(2,128)S(1)}, u32[]{:S(2)}, u32[]{:S(2)}) collective-permute-start(f32[2,1280]{1,0:T(2,128)S(1)} %get-tuple-element.58.refs_0_), channel_id=1, source_target_pairs={{0,2},{1,3},{2,0},{3,1},{4,6},{5,7},{6,4},{7,5},{8,10},{9,11},{10,... | collective-permute-start | bytes 30728 | tf_op jit(solution)/shard_map/ppermute | solution.py:245
  63.2 4.6 %collective-permute-start.15 = (f32[2,1280]{1,0:T(2,128)S(1)}, f32[2,1280]{1,0:T(2,128)S(1)}, u32[]{:S(2)}, u32[]{:S(2)}) collective-permute-start(f32[2,1280]{1,0:T(2,128)S(1)} %get-tuple-element.58.refs_0_), channel_id=1, source_target_pairs={{0,1},{1,0},{2,3},{3,2},{4,5},{5,4},{6,7},{7,6},{8,9},{9,8},{10,11... | collective-permute-start | bytes 30728 | tf_op jit(solution)/shard_map/ppermute | solution.py:245
  67.7 3.7 %collective-permute-start.18 = (f32[2,1280]{1,0:T(2,128)S(1)}, f32[2,1280]{1,0:T(2,128)S(1)}, u32[]{:S(2)}, u32[]{:S(2)}) collective-permute-start(f32[2,1280]{1,0:T(2,128)S(1)} %add.5.refs_0_), channel_id=1, source_target_pairs={{0,8},{4,12},{8,0},{12,4},{1,9},{5,13},{9,1},{13,5},{2,10},{6,14},... | collective-permute-start | bytes 30728 | tf_op jit(solution)/shard_map/ppermute | solution.py:245
  (3 other events, 13.9 us)

commit v7 on v6

--- a/solution.py
+++ b/solution.py
@@ -107,7 +107,7 @@
     share = depth // 2
     spot = owner ^ (owner >> 1)
     firsts = []
-    for step in (0, 1, 3, 2):
+    for step in range(owners):
         back = lax.rem(spot + owners - step, owners)
         source = back ^ (back >> 1)
         firsts.append(pl.multiple_of(source * depth + rep * share, 16))
@@ -296,22 +296,24 @@
     ring = [(0, 1), (1, 3), (3, 2), (2, 0)]
     share = depth // 2
 
-    held = pick(w_qkv, ids, share, part, False) if chain else ids
-    sooner = after(tokens, held)
+    if chain:
+        held = pick(w_qkv, ids, share, part, False)
+        first = lax.ppermute(held, "tile", ring)
+        second = lax.ppermute(first, "tile", ring)
+        first_other = swapped(first, "rep", 1)
+        rest = pick(w_qkv, after(ids, first), share, part, True)
+        second = after(second, first_other, rest)
+        third = lax.ppermute(second, "tile", ring)
+        second_other = swapped(second, "rep", 1)
+        third = after(third, second_other)
+        third_other = swapped(third, "rep", 1)
+    else:
+        first = second = ids
+
+    sooner = after(tokens, first)
     across = swapped(sooner, "date", 2)
     beside = swapped(sooner, "date", 1)
-    if chain:
-        first = lax.ppermute(held, "tile", ring)
-        third = lax.ppermute(held, "tile", [(b, a) for a, b in ring])
-        first = after(first, across, beside)
-        second = lax.ppermute(first, "tile", ring)
-        first_other = swapped(first, "rep", 1)
-        third_other = swapped(third, "rep", 1)
-        rest = pick(w_qkv, after(ids, first), share, part, True)
-    else:
-        first = ids
-    across = after(across, first)
-    beyond = swapped(across, "date", 1)
+    beyond = swapped(after(across, second), "date", 1)
     pair = pltpu.VMEM((2, slots, rows, part), BF16)
     columns = call(
         functools.partial(columns_kernel, part),
@@ -322,10 +324,6 @@
         4,
     )
     columns = swapped(columns, "date", 2)
-    if chain:
-        second = after(second, first_other, beyond, columns, rest)
-        second_other = swapped(second, "rep", 1)
-        columns = after(columns, second)
     ups, ups_beside = call(
         functools.partial(part_kernel, part),
         "part",
@@ -333,10 +331,9 @@
         [SMEM, VMEM, VMEM],
         (ids, cotangent, near(columns)),
         4,
+        microseconds=2,
     )
     ups_beside = swapped(ups_beside, "date", 1)
-    if chain:
-        beyond = after(beyond, third_other)
 
     normed, unit, own_unit, own_inv = call(
         norm_kernel,
@@ -353,7 +350,7 @@
         microseconds=2,
     )
     if chain:
-        pieces = [held, rest, first, first_other, third, third_other, second, second_other]
+        pieces = [held, rest, first, first_other, second, second_other, third, third_other]
     else:
         group = lax.axis_index("date")
         mine = [

time: 73.3 us -> 66.6 us (0.909)
  starting transfers between devices: 30.7 us -> 20.3 us
  waiting for transfers between devices: 25.2 us -> 28.9 us
    ppermute x1, starting transfers between devices: 7.74 us -> 0.79 us  [local(): second = lax.ppermute(first, 'tile', ring)]
    ppermute x16, starting transfers between devices: 20 us -> 15.7 us  [swapped(): lax.ppermute(array, axis, [(i, i ^ bits) for i in range(lax.axis_size(axi...]
    ppermute x1, waiting for transfers between devices: 0.01 us -> 4.29 us  [local(): third = lax.ppermute(second, 'tile', ring)]
    ppermute x16, waiting for transfers between devices: 16.6 us -> 14 us  [swapped(): lax.ppermute(array, axis, [(i, i ^ bits) for i in range(lax.axis_size(axi...]
    ppermute x1, starting transfers between devices: 1.58 us -> 3.08 us  [local(): first = lax.ppermute(held, 'tile', ring)]
    ppermute x1, waiting for transfers between devices: 0.43 us -> 1.87 us  [local(): second = lax.ppermute(first, 'tile', ring)]
  transfers between devices with their start and end apart: 19 -> 19, of which waited for: 9 -> 10; matrix products, arithmetic and copies ran while one was open for 0% -> 0% of each run, Pallas kernels for 11% -> 13%
where the time goes in v7:
time: 66.6 us; the launch traced here: 66.5 us
  waiting for transfers between devices  28.9 us (43%)
  starting transfers between devices  20.3 us (30%)
  Pallas kernels  16.3 us (24%)
  between operations  0.84 us (1%)
    pallas_call x12, Pallas kernels, call(): pl.pallas_call(kernel, out_shape=out_shape, in_specs=in_specs, out_specs=...  16.3 us
    ppermute x16, starting transfers between devices, swapped(): lax.ppermute(array, axis, [(i, i ^ bits) for i in range(lax.axis_size(axi...  15.7 us
    ppermute x16, waiting for transfers between devices, swapped(): lax.ppermute(array, axis, [(i, i ^ bits) for i in range(lax.axis_size(axi...  14 us
    ppermute x1, waiting for transfers between devices, local(): first = lax.ppermute(held, 'tile', ring)  8.72 us
    ppermute x1, waiting for transfers between devices, local(): third = lax.ppermute(second, 'tile', ring)  4.29 us
    ppermute x1, starting transfers between devices, local(): first = lax.ppermute(held, 'tile', ring)  3.08 us
    ppermute x1, waiting for transfers between devices, local(): second = lax.ppermute(first, 'tile', ring)  1.87 us
  transfers between devices with their start and end apart: 19, of which 10 were waited for; matrix products, arithmetic and copies ran while one was open for 0% of the time, Pallas kernels for 13%

profile of v7, /device:TPU:0, one launch (start us, length us, event | category | flops | bytes accessed | tf_op | source)
XLA Modules:
  0.0 66.5 jit_solution(15038547287897954662)
XLA Ops:
  0.7 1.9 %pick.2.refs_0_ = bf16[160,960]{1,0:T(8,128)(2,1)S(1)} custom-call(s32[3]{0:T(128)S(1)} %pad_add_fusion.ids_ref, bf16[320,3840]{1,0:T(8,128)(2,1)} %w_ref.3), custom_call_target="tpu_custom_call" | custom-call | flops 10000000 | bytes 1000 | tf_op jit(solution)/shard_map/pick/pallas_call | solution.py:257
  2.6 3.1 %collective-permute-start = (bf16[160,960]{1,0:T(8,128)(2,1)S(1)}, bf16[160,960]{1,0:T(8,128)(2,1)S(1)}, u32[]{:S(2)}, u32[]{:S(2)}) collective-permute-start(bf16[160,960]{1,0:T(8,128)(2,1)S(1)} %pick.2.refs_0_), channel_id=1, source_target_pairs={{0,1},{1,3},{3,2},{2,0},{4,5},{5,7},{7,6},{6,4},{8,9},{9,11},{11,1... | collective-permute-start | bytes 921608 | tf_op jit(solution)/shard_map/ppermute | solution.py:301
  5.7 8.7 %collective-permute-done.refs_2_ = bf16[160,960]{1,0:T(8,128)(2,1)S(1)} collective-permute-done((bf16[160,960]{1,0:T(8,128)(2,1)S(1)}, bf16[160,960]{1,0:T(8,128)(2,1)S(1)}, u32[]{:S(2)}, u32[]{:S(2)}) %collective-permute-start) | collective-permute-done | bytes 307232 | tf_op jit(solution)/shard_map/ppermute | solution.py:301
  14.4 1.6 %collective-permute-start.4 = (bf16[160,960]{1,0:T(8,128)(2,1)S(1)}, bf16[160,960]{1,0:T(8,128)(2,1)S(1)}, u32[]{:S(2)}, u32[]{:S(2)}) collective-permute-start(bf16[160,960]{1,0:T(8,128)(2,1)S(1)} %collective-permute-done.refs_2_), channel_id=1, source_target_pairs={{0,16},{16,0},{1,17},{17,1},{2,18},{18,2},{3,19},{19,3},{4,20},{20... | collective-permute-start | bytes 921608 | tf_op jit(solution)/shard_map/ppermute | solution.py:245
  16.8 1.5 %collective-permute-start.2 = (bf16[4,32,1280]{2,1,0:T(8,128)(2,1)S(1)}, bf16[4,32,1280]{2,1,0:T(8,128)(2,1)S(1)}, u32[]{:S(2)}, u32[]{:S(2)}) collective-permute-start(bf16[4,32,1280]{2,1,0:T(8,128)(2,1)S(1)} %copy-done.4), channel_id=1, source_target_pairs={{0,8},{4,12},{8,0},{12,4},{1,9},{5,13},{9,1},{13,5},{2,10},{6,14},... | collective-permute-start | bytes 983048 | tf_op jit(solution)/shard_map/ppermute | solution.py:245
  18.3 1.9 %pick.3.refs_1_ = bf16[160,960]{1,0:T(8,128)(2,1)S(1)} custom-call(s32[3]{0:T(128)S(1)} %pad_add_fusion.ids_ref, bf16[320,3840]{1,0:T(8,128)(2,1)} %w_ref.3), custom_call_target="tpu_custom_call" | custom-call | flops 10000000 | bytes 1000 | tf_op jit(solution)/shard_map/pick/pallas_call | solution.py:257
  20.1 3.2 %collective-permute-done.4.refs_3_ = bf16[160,960]{1,0:T(8,128)(2,1)S(1)} collective-permute-done((bf16[160,960]{1,0:T(8,128)(2,1)S(1)}, bf16[160,960]{1,0:T(8,128)(2,1)S(1)}, u32[]{:S(2)}, u32[]{:S(2)}) %collective-permute-start.4) | collective-permute-done | bytes 307232 | tf_op jit(solution)/shard_map/ppermute | solution.py:245
  23.3 1.9 %collective-permute-done.3.refs_4_ = bf16[160,960]{1,0:T(8,128)(2,1)S(1)} collective-permute-done((bf16[160,960]{1,0:T(8,128)(2,1)S(1)}, bf16[160,960]{1,0:T(8,128)(2,1)S(1)}, u32[]{:S(2)}, u32[]{:S(2)}) %collective-permute-start.3) | collective-permute-done | bytes 307232 | tf_op jit(solution)/shard_map/ppermute | solution.py:302
  27.0 1.6 %collective-permute-start.6 = (bf16[4,32,640]{2,1,0:T(8,128)(2,1)S(1)}, bf16[4,32,640]{2,1,0:T(8,128)(2,1)S(1)}, u32[]{:S(2)}, u32[]{:S(2)}) collective-permute-start(bf16[4,32,640]{2,1,0:T(8,128)(2,1)S(1)} %columns.1), channel_id=1, source_target_pairs={{0,8},{4,12},{8,0},{12,4},{1,9},{5,13},{9,1},{13,5},{2,10},{6,14},... | collective-permute-start | bytes 491528 | tf_op jit(solution)/shard_map/ppermute | solution.py:245
  29.2 4.3 %collective-permute-done.9.refs_6_ = bf16[160,960]{1,0:T(8,128)(2,1)S(1)} collective-permute-done((bf16[160,960]{1,0:T(8,128)(2,1)S(1)}, bf16[160,960]{1,0:T(8,128)(2,1)S(1)}, u32[]{:S(2)}, u32[]{:S(2)}) %collective-permute-start.9) | collective-permute-done | bytes 307232 | tf_op jit(solution)/shard_map/ppermute | solution.py:306
  33.5 1.1 %collective-permute-start.10 = (bf16[160,960]{1,0:T(8,128)(2,1)S(1)}, bf16[160,960]{1,0:T(8,128)(2,1)S(1)}, u32[]{:S(2)}, u32[]{:S(2)}) collective-permute-start(bf16[160,960]{1,0:T(8,128)(2,1)S(1)} %collective-permute-done.9.refs_6_), channel_id=1, source_target_pairs={{0,16},{16,0},{1,17},{17,1},{2,18},{18,2},{3,19},{19,3},{4,20},{20... | collective-permute-start | bytes 921608 | tf_op jit(solution)/shard_map/ppermute | solution.py:245
  35.5 1.9 %norm.1 = (bf16[512,1280]{1,0:T(8,128)(2,1)S(1)}, bf16[512,1280]{1,0:T(8,128)(2,1)S(1)}, f32[4,32,1280]{2,1,0:T(8,128)S(1)}, f32[4,32,128]{2,1,0:T(8,128)S(1)}) custom-call(s32[4]{0:T(128)S(1)} %copy-done.5, bf16[256,1280]{1,0:T(8,128)(2,1)S(1)} %copy-done.3, f32[1,1280]{1,0:T(1,128)S(1)} %reshape.12.gain_ref, f32[1,1280]{1,0:T(1,128)S(1)} %reshape.13.bias_ref, ...), custom_call_target="tpu_custom_call" | custom-call | flops 2000000000 | bytes 1000 | tf_op jit(solution)/shard_map/norm/pallas_call | solution.py:257
  37.5 3.0 %collective-permute-done.10.refs_7_ = bf16[160,960]{1,0:T(8,128)(2,1)S(1)} collective-permute-done((bf16[160,960]{1,0:T(8,128)(2,1)S(1)}, bf16[160,960]{1,0:T(8,128)(2,1)S(1)}, u32[]{:S(2)}, u32[]{:S(2)}) %collective-permute-start.10) | collective-permute-done | bytes 307232 | tf_op jit(solution)/shard_map/ppermute | solution.py:245
  40.5 4.4 %attend.1 = (bf16[4,32,320]{2,1,0:T(8,128)(2,1)S(1)}, bf16[4,32,320]{2,1,0:T(8,128)(2,1)S(1)}, bf16[2,4,32,320]{3,2,1,0:T(8,128)(2,1)S(1)}, bf16[512,960]{1,0:T(8,128)(2,1)S(1)}, bf16[1280,960]{1,0:T(8,128)(2,1)S(1)}) custom-call(s32[3]{0:T(128)S(1)} %pad_add_fusion.ids_ref, s32[4]{0:T(128)S(1)} %copy-done.2, ...), custom_call_target="tpu_custom_call" | custom-call | flops 10000000 | bytes 1000 | tf_op jit(solution)/shard_map/attend/pallas_call | solution.py:257
  44.9 1.6 %collective-permute-start.12 = (bf16[2,4,32,320]{3,2,1,0:T(8,128)(2,1)S(1)}, bf16[2,4,32,320]{3,2,1,0:T(8,128)(2,1)S(1)}, u32[]{:S(2)}, u32[]{:S(2)}) collective-permute-start(bf16[2,4,32,320]{3,2,1,0:T(8,128)(2,1)S(1)} %get-tuple-element.44), channel_id=1, source_target_pairs={{0,8},{4,12},{8,0},{12,4},{1,9},{5,13},{9,1},{13,5},{2,10},{6,14},... | collective-permute-start | bytes 491528 | tf_op jit(solution)/shard_map/ppermute | solution.py:245
  46.5 1.6 %back.1 = (bf16[4,32,1280]{2,1,0:T(8,128)(2,1)S(1)}, bf16[4,32,1280]{2,1,0:T(8,128)(2,1)S(1)}, bf16[272,1280]{1,0:T(8,128)(2,1)S(1)}, f32[2,1280]{1,0:T(2,128)S(1)}) custom-call(bf16[512,960]{1,0:T(8,128)(2,1)S(1)} %get-tuple-element.38.gqkv_ref, bf16[512,1280]{1,0:T(8,128)(2,1)S(1)} %get-tuple-element.39.unit_ref, ...), custom_call_target="tpu_custom_call" | custom-call | flops 10000000 | bytes 1000 | tf_op jit(solution)/shard_map/back/pallas_call | solution.py:257
  48.2 2.5 %collective-permute-done.12.far_ref.across_ref = bf16[2,4,32,320]{3,2,1,0:T(8,128)(2,1)S(1)} collective-permute-done((bf16[2,4,32,320]{3,2,1,0:T(8,128)(2,1)S(1)}, bf16[2,4,32,320]{3,2,1,0:T(8,128)(2,1)S(1)}, u32[]{:S(2)}, u32[]{:S(2)}) %collective-permute-start.12) | collective-permute-done | bytes 163872 | tf_op jit(solution)/shard_map/ppermute | solution.py:245
  50.8 1.6 %collective-permute-start.14 = (bf16[4,32,1280]{2,1,0:T(8,128)(2,1)S(1)}, bf16[4,32,1280]{2,1,0:T(8,128)(2,1)S(1)}, u32[]{:S(2)}, u32[]{:S(2)}) collective-permute-start(bf16[4,32,1280]{2,1,0:T(8,128)(2,1)S(1)} %get-tuple-element.53), channel_id=1, source_target_pairs={{0,8},{4,12},{8,0},{12,4},{1,9},{5,13},{9,1},{13,5},{2,10},{6,14},... | collective-permute-start | bytes 983048 | tf_op jit(solution)/shard_map/ppermute | solution.py:245
  52.3 3.6 %collective-permute-start.17 = (f32[2,1280]{1,0:T(2,128)S(1)}, f32[2,1280]{1,0:T(2,128)S(1)}, u32[]{:S(2)}, u32[]{:S(2)}) collective-permute-start(f32[2,1280]{1,0:T(2,128)S(1)} %get-tuple-element.54.refs_0_), channel_id=1, source_target_pairs={{0,3},{1,2},{2,1},{3,0},{4,7},{5,6},{6,5},{7,4},{8,11},{9,10},{10,... | collective-permute-start | bytes 30728 | tf_op jit(solution)/shard_map/ppermute | solution.py:245
  55.9 1.6 %collective-permute-start.16 = (f32[2,1280]{1,0:T(2,128)S(1)}, f32[2,1280]{1,0:T(2,128)S(1)}, u32[]{:S(2)}, u32[]{:S(2)}) collective-permute-start(f32[2,1280]{1,0:T(2,128)S(1)} %get-tuple-element.54.refs_0_), channel_id=1, source_target_pairs={{0,2},{1,3},{2,0},{3,1},{4,6},{5,7},{6,4},{7,5},{8,10},{9,11},{10,... | collective-permute-start | bytes 30728 | tf_op jit(solution)/shard_map/ppermute | solution.py:245
  57.8 2.7 %collective-permute-done.16.refs_2_ = f32[2,1280]{1,0:T(2,128)S(1)} collective-permute-done((f32[2,1280]{1,0:T(2,128)S(1)}, f32[2,1280]{1,0:T(2,128)S(1)}, u32[]{:S(2)}, u32[]{:S(2)}) %collective-permute-start.16) | collective-permute-done | bytes 10272 | tf_op jit(solution)/shard_map/ppermute | solution.py:245
  61.7 1.4 %home.1 = (f32[4,32,1280]{2,1,0:T(8,128)S(1)}, bf16[4,32,1280]{2,1,0:T(8,128)(2,1)}) custom-call(s32[3]{0:T(128)S(1)} %pad_add_fusion.ids_ref, bf16[4,32,1280]{2,1,0:T(8,128)(2,1)S(1)} %get-tuple-element.41.stay_ref, bf16[272,1280]{1,0:T(8,128)(2,1)S(1)} %collective-permute-done.11.close_ref, bf16[4,32,320]{2,1,0:T(8,128)(2,1)S(1)} %get-tuple-element.46.own_ref, ...), custom_call_target="tpu_custom_call" | custom-call | flops 10000000 | bytes 1000 | tf_op jit(solution)/shard_map/home/pallas_call | solution.py:257
  63.2 1.7 %collective-permute-done.18.refs_1_ = f32[2,1280]{1,0:T(2,128)S(1)} collective-permute-done((f32[2,1280]{1,0:T(2,128)S(1)}, f32[2,1280]{1,0:T(2,128)S(1)}, u32[]{:S(2)}, u32[]{:S(2)}) %collective-permute-start.18) | collective-permute-done | bytes 10272 | tf_op jit(solution)/shard_map/ppermute | solution.py:245
  64.9 1.6 %finish.1 = (bf16[4,32,1280]{2,1,0:T(8,128)(2,1)}, f32[2,1280]{1,0:T(2,128)}) custom-call(s32[3]{0:T(128)S(1)} %pad_add_fusion.ids_ref, s32[4]{0:T(128)S(1)} %copy-done.2, f32[4,32,1280]{2,1,0:T(8,128)S(1)} %get-tuple-element.48.unit_ref, f32[4,32,128]{2,1,0:T(8,128)S(1)} %get-tuple-element.49.inv_ref, f32[1,1280]{1,0:T(1,128)S(1)} %reshape.12.gain_ref, ...), custom_call_target="tpu_custom_call" | custom-call | flops 10000000 | bytes 1000 | tf_op jit(solution)/shard_map/finish/pallas_call | solution.py:257
  (45 shorter events, 5.9 us)
Async XLA Ops:
  0.6 16.1 %copy-start.4 = (bf16[4,32,1280]{2,1,0:T(8,128)(2,1)S(1)}, bf16[4,32,1280]{2,1,0:T(8,128)(2,1)}, u32[]{:S(2)}) copy-start(bf16[4,32,1280]{2,1,0:T(8,128)(2,1)} %refs_0_.1) | copy-start | bytes 983044
  0.7 25.7 %copy-start = (bf16[4,32,1280]{2,1,0:T(8,128)(2,1)S(1)}, bf16[4,32,1280]{2,1,0:T(8,128)(2,1)}, u32[]{:S(2)}) copy-start(bf16[4,32,1280]{2,1,0:T(8,128)(2,1)} %cotangent_ref.3) | copy-start | bytes 983044
  0.7 28.4 %copy-start.6 = (f32[1280]{0:T(1024)S(1)}, f32[1280]{0:T(1024)}, u32[]{:S(2)}) copy-start(f32[1280]{0:T(1024)} %param.15) | copy-start | bytes 15364
  0.7 28.4 %copy-start.7 = (f32[1280]{0:T(1024)S(1)}, f32[1280]{0:T(1024)}, u32[]{:S(2)}) copy-start(f32[1280]{0:T(1024)} %param.16) | copy-start | bytes 15364
  2.6 11.8 %collective-permute-start = (bf16[160,960]{1,0:T(8,128)(2,1)S(1)}, bf16[160,960]{1,0:T(8,128)(2,1)S(1)}, u32[]{:S(2)}, u32[]{:S(2)}) collective-permute-start(bf16[160,960]{1,0:T(8,128)(2,1)S(1)} %pick.2.refs_0_), channel_id=1, source_target_pairs={{0,1},{1,3},{3,2},{2,0},{4,5},{5,7},{7,6},{6,4},{8,9},{9,11},{11,1... | collective-permute-start | bytes 921608 | tf_op jit(solution)/shard_map/ppermute | solution.py:301
  14.4 8.9 %collective-permute-start.4 = (bf16[160,960]{1,0:T(8,128)(2,1)S(1)}, bf16[160,960]{1,0:T(8,128)(2,1)S(1)}, u32[]{:S(2)}, u32[]{:S(2)}) collective-permute-start(bf16[160,960]{1,0:T(8,128)(2,1)S(1)} %collective-permute-done.refs_2_), channel_id=1, source_target_pairs={{0,16},{16,0},{1,17},{17,1},{2,18},{18,2},{3,19},{19,3},{4,20},{20... | collective-permute-start | bytes 921608 | tf_op jit(solution)/shard_map/ppermute | solution.py:245
  16.0 9.2 %collective-permute-start.3 = (bf16[160,960]{1,0:T(8,128)(2,1)S(1)}, bf16[160,960]{1,0:T(8,128)(2,1)S(1)}, u32[]{:S(2)}, u32[]{:S(2)}) collective-permute-start(bf16[160,960]{1,0:T(8,128)(2,1)S(1)} %collective-permute-done.refs_2_), channel_id=1, source_target_pairs={{0,1},{1,3},{3,2},{2,0},{4,5},{5,7},{7,6},{6,4},{8,9},{9,11},{11,1... | collective-permute-start | bytes 921608 | tf_op jit(solution)/shard_map/ppermute | solution.py:302
  16.8 11.8 %collective-permute-start.2 = (bf16[4,32,1280]{2,1,0:T(8,128)(2,1)S(1)}, bf16[4,32,1280]{2,1,0:T(8,128)(2,1)S(1)}, u32[]{:S(2)}, u32[]{:S(2)}) collective-permute-start(bf16[4,32,1280]{2,1,0:T(8,128)(2,1)S(1)} %copy-done.4), channel_id=1, source_target_pairs={{0,8},{4,12},{8,0},{12,4},{1,9},{5,13},{9,1},{13,5},{2,10},{6,14},... | collective-permute-start | bytes 983048 | tf_op jit(solution)/shard_map/ppermute | solution.py:245
  25.2 8.3 %collective-permute-start.9 = (bf16[160,960]{1,0:T(8,128)(2,1)S(1)}, bf16[160,960]{1,0:T(8,128)(2,1)S(1)}, u32[]{:S(2)}, u32[]{:S(2)}) collective-permute-start(bf16[160,960]{1,0:T(8,128)(2,1)S(1)} %collective-permute-done.3.refs_4_), channel_id=1, source_target_pairs={{0,1},{1,3},{3,2},{2,0},{4,5},{5,7},{7,6},{6,4},{8,9},{9,11},{11,1... | collective-permute-start | bytes 921608 | tf_op jit(solution)/shard_map/ppermute | solution.py:306
  26.0 7.5 %collective-permute-start.8 = (bf16[160,960]{1,0:T(8,128)(2,1)S(1)}, bf16[160,960]{1,0:T(8,128)(2,1)S(1)}, u32[]{:S(2)}, u32[]{:S(2)}) collective-permute-start(bf16[160,960]{1,0:T(8,128)(2,1)S(1)} %collective-permute-done.3.refs_4_), channel_id=1, source_target_pairs={{0,16},{16,0},{1,17},{17,1},{2,18},{18,2},{3,19},{19,3},{4,20},{20... | collective-permute-start | bytes 921608 | tf_op jit(solution)/shard_map/ppermute | solution.py:245
  27.0 7.5 %collective-permute-start.6 = (bf16[4,32,640]{2,1,0:T(8,128)(2,1)S(1)}, bf16[4,32,640]{2,1,0:T(8,128)(2,1)S(1)}, u32[]{:S(2)}, u32[]{:S(2)}) collective-permute-start(bf16[4,32,640]{2,1,0:T(8,128)(2,1)S(1)} %columns.1), channel_id=1, source_target_pairs={{0,8},{4,12},{8,0},{12,4},{1,9},{5,13},{9,1},{13,5},{2,10},{6,14},... | collective-permute-start | bytes 491528 | tf_op jit(solution)/shard_map/ppermute | solution.py:245
  28.6 6.9 %collective-permute-start.1 = (bf16[4,32,1280]{2,1,0:T(8,128)(2,1)S(1)}, bf16[4,32,1280]{2,1,0:T(8,128)(2,1)S(1)}, u32[]{:S(2)}, u32[]{:S(2)}) collective-permute-start(bf16[4,32,1280]{2,1,0:T(8,128)(2,1)S(1)} %copy-done.4), channel_id=1, source_target_pairs={{0,4},{4,0},{8,12},{12,8},{1,5},{5,1},{9,13},{13,9},{2,6},{6,2},{1... | collective-permute-start | bytes 983048 | tf_op jit(solution)/shard_map/ppermute | solution.py:245
  28.6 6.9 %collective-permute-start.5 = (bf16[4,32,1280]{2,1,0:T(8,128)(2,1)S(1)}, bf16[4,32,1280]{2,1,0:T(8,128)(2,1)S(1)}, u32[]{:S(2)}, u32[]{:S(2)}) collective-permute-start(bf16[4,32,1280]{2,1,0:T(8,128)(2,1)S(1)} %collective-permute-done.2.refs_2_), channel_id=1, source_target_pairs={{0,4},{4,0},{8,12},{12,8},{1,5},{5,1},{9,13},{13,9},{2,6},{6,2},{1... | collective-permute-start | bytes 983048 | tf_op jit(solution)/shard_map/ppermute | solution.py:245
  29.1 6.4 %copy-start.3 = (bf16[256,1280]{1,0:T(8,128)(2,1)S(1)}, bf16[256,1280]{1,0:T(8,128)(2,1)}, u32[]{:S(2)}) copy-start(bf16[256,1280]{1,0:T(8,128)(2,1)} %pos_ref.1) | copy-start | bytes 1966084
  33.5 7.1 %collective-permute-start.10 = (bf16[160,960]{1,0:T(8,128)(2,1)S(1)}, bf16[160,960]{1,0:T(8,128)(2,1)S(1)}, u32[]{:S(2)}, u32[]{:S(2)}) collective-permute-start(bf16[160,960]{1,0:T(8,128)(2,1)S(1)} %collective-permute-done.9.refs_6_), channel_id=1, source_target_pairs={{0,16},{16,0},{1,17},{17,1},{2,18},{18,2},{3,19},{19,3},{4,20},{20... | collective-permute-start | bytes 921608 | tf_op jit(solution)/shard_map/ppermute | solution.py:245
  35.4 2.1 %collective-permute-start.7 = (bf16[2,4,32,320]{3,2,1,0:T(8,128)(2,1)S(1)}, bf16[2,4,32,320]{3,2,1,0:T(8,128)(2,1)S(1)}, u32[]{:S(2)}, u32[]{:S(2)}) collective-permute-start(bf16[2,4,32,320]{3,2,1,0:T(8,128)(2,1)S(1)} %get-tuple-element.36), channel_id=1, source_target_pairs={{0,4},{4,0},{8,12},{12,8},{1,5},{5,1},{9,13},{13,9},{2,6},{6,2},{1... | collective-permute-start | bytes 491528 | tf_op jit(solution)/shard_map/ppermute | solution.py:245
  44.9 5.7 %collective-permute-start.12 = (bf16[2,4,32,320]{3,2,1,0:T(8,128)(2,1)S(1)}, bf16[2,4,32,320]{3,2,1,0:T(8,128)(2,1)S(1)}, u32[]{:S(2)}, u32[]{:S(2)}) collective-permute-start(bf16[2,4,32,320]{3,2,1,0:T(8,128)(2,1)S(1)} %get-tuple-element.44), channel_id=1, source_target_pairs={{0,8},{4,12},{8,0},{12,4},{1,9},{5,13},{9,1},{13,5},{2,10},{6,14},... | collective-permute-start | bytes 491528 | tf_op jit(solution)/shard_map/ppermute | solution.py:245
  48.1 2.6 %collective-permute-start.11 = (bf16[272,1280]{1,0:T(8,128)(2,1)S(1)}, bf16[272,1280]{1,0:T(8,128)(2,1)S(1)}, u32[]{:S(2)}, u32[]{:S(2)}) collective-permute-start(bf16[272,1280]{1,0:T(8,128)(2,1)S(1)} %get-tuple-element.42), channel_id=1, source_target_pairs={{0,4},{4,0},{8,12},{12,8},{1,5},{5,1},{9,13},{13,9},{2,6},{6,2},{1... | collective-permute-start | bytes 2088968 | tf_op jit(solution)/shard_map/ppermute | solution.py:245
  50.8 14.1 %collective-permute-start.14 = (bf16[4,32,1280]{2,1,0:T(8,128)(2,1)S(1)}, bf16[4,32,1280]{2,1,0:T(8,128)(2,1)S(1)}, u32[]{:S(2)}, u32[]{:S(2)}) collective-permute-start(bf16[4,32,1280]{2,1,0:T(8,128)(2,1)S(1)} %get-tuple-element.53), channel_id=1, source_target_pairs={{0,8},{4,12},{8,0},{12,4},{1,9},{5,13},{9,1},{13,5},{2,10},{6,14},... | collective-permute-start | bytes 983048 | tf_op jit(solution)/shard_map/ppermute | solution.py:245
  52.3 9.4 %collective-permute-start.13 = (bf16[2,4,32,320]{3,2,1,0:T(8,128)(2,1)S(1)}, bf16[2,4,32,320]{3,2,1,0:T(8,128)(2,1)S(1)}, u32[]{:S(2)}, u32[]{:S(2)}) collective-permute-start(bf16[2,4,32,320]{3,2,1,0:T(8,128)(2,1)S(1)} %both.1), channel_id=1, source_target_pairs={{0,4},{4,0},{8,12},{12,8},{1,5},{5,1},{9,13},{13,9},{2,6},{6,2},{1... | collective-permute-start | bytes 491528 | tf_op jit(solution)/shard_map/ppermute | solution.py:245
  52.3 5.5 %collective-permute-start.17 = (f32[2,1280]{1,0:T(2,128)S(1)}, f32[2,1280]{1,0:T(2,128)S(1)}, u32[]{:S(2)}, u32[]{:S(2)}) collective-permute-start(f32[2,1280]{1,0:T(2,128)S(1)} %get-tuple-element.54.refs_0_), channel_id=1, source_target_pairs={{0,3},{1,2},{2,1},{3,0},{4,7},{5,6},{6,5},{7,4},{8,11},{9,10},{10,... | collective-permute-start | bytes 30728 | tf_op jit(solution)/shard_map/ppermute | solution.py:245
  55.9 4.6 %collective-permute-start.16 = (f32[2,1280]{1,0:T(2,128)S(1)}, f32[2,1280]{1,0:T(2,128)S(1)}, u32[]{:S(2)}, u32[]{:S(2)}) collective-permute-start(f32[2,1280]{1,0:T(2,128)S(1)} %get-tuple-element.54.refs_0_), channel_id=1, source_target_pairs={{0,2},{1,3},{2,0},{3,1},{4,6},{5,7},{6,4},{7,5},{8,10},{9,11},{10,... | collective-permute-start | bytes 30728 | tf_op jit(solution)/shard_map/ppermute | solution.py:245
  57.5 3.7 %collective-permute-start.15 = (f32[2,1280]{1,0:T(2,128)S(1)}, f32[2,1280]{1,0:T(2,128)S(1)}, u32[]{:S(2)}, u32[]{:S(2)}) collective-permute-start(f32[2,1280]{1,0:T(2,128)S(1)} %get-tuple-element.54.refs_0_), channel_id=1, source_target_pairs={{0,1},{1,0},{2,3},{3,2},{4,5},{5,4},{6,7},{7,6},{8,9},{9,8},{10,11... | collective-permute-start | bytes 30728 | tf_op jit(solution)/shard_map/ppermute | solution.py:245
  61.2 3.7 %collective-permute-start.18 = (f32[2,1280]{1,0:T(2,128)S(1)}, f32[2,1280]{1,0:T(2,128)S(1)}, u32[]{:S(2)}, u32[]{:S(2)}) collective-permute-start(f32[2,1280]{1,0:T(2,128)S(1)} %add.5.refs_0_), channel_id=1, source_target_pairs={{0,8},{4,12},{8,0},{12,4},{1,9},{5,13},{9,1},{13,5},{2,10},{6,14},... | collective-permute-start | bytes 30728 | tf_op jit(solution)/shard_map/ppermute | solution.py:245
  (3 other events, 16.6 us)

commit v8 on v7

--- a/solution.py
+++ b/solution.py
@@ -37,8 +37,9 @@
     return start, wide, odd == 1
 
 
-def pick_kernel(part, other, ids_ref, w_ref, out_ref, windows, sems):
-    height = out_ref.shape[0]
+def pick_kernel(part, other, ids_ref, w_ref, *refs):
+    out_refs, windows, sems = refs[:-2], refs[-2], refs[-1]
+    height = windows.shape[1]
     channels = w_ref.shape[1] // 3
     half = 1 - ids_ref[0] if other else ids_ref[0]
     first = pl.multiple_of(half * height, 16)
@@ -59,39 +60,60 @@
     for i in range(3):
         window = windows[i]
         pieces.append(jnp.where(odd, window[:, wide - part :], window[:, :part]))
-    out_ref[...] = jnp.concatenate(pieces, axis=1)
-
-
-def columns_kernel(part, ids_ref, cotangent_ref, out_ref):
-    theirs = (1 - ids_ref[1] // 2) * (2 * part)
-    out_ref[...] = cotangent_ref[:, :, pl.ds(pl.multiple_of(theirs, 128), 2 * part)]
-
-
-def part_kernel(part, ids_ref, cotangent_ref, columns_ref, up_ref, out_ref):
-    ours = pl.multiple_of(ids_ref[1] // 2 * (2 * part), 128)
+    picked = jnp.concatenate(pieces, axis=1)
+    at = 0
+    for out_ref in out_refs:
+        out_ref[...] = picked[at : at + out_ref.shape[0]]
+        at += out_ref.shape[0]
+
+
+def chip_pair(ids_ref, part):
+    pair = ids_ref[1] // 2
+    return pl.multiple_of(pair * (2 * part), 128), pl.multiple_of((1 - pair) * (2 * part), 128)
+
+
+def pack_across_kernel(part, ids_ref, tokens_ref, cotangent_ref, out_ref):
+    width = tokens_ref.shape[2]
+    theirs = chip_pair(ids_ref, part)[1]
+    out_ref[:, :, :width] = tokens_ref[...]
+    out_ref[:, :, width:] = cotangent_ref[:, :, pl.ds(theirs, 2 * part)]
+
+
+def pack_beside_kernel(part, ids_ref, tokens_ref, cotangent_ref, across_ref, out_ref, up_ref):
+    width = tokens_ref.shape[2]
+    ours = chip_pair(ids_ref, part)[0]
     odd = lax.rem(ids_ref[1], 2) == 1
-    for i, block in enumerate((cotangent_ref[:, :, pl.ds(ours, 2 * part)], columns_ref[...])):
+    out_ref[:, :, :width] = tokens_ref[...]
+    out_ref[:, :, width : 2 * width] = across_ref[:, :, :width]
+    theirs = []
+    for i, block in enumerate((cotangent_ref[:, :, pl.ds(ours, 2 * part)], across_ref[:, :, width:])):
         low, high = block[:, :, :part], block[:, :, part:]
         up_ref[i] = jnp.where(odd, high, low)
-        out_ref[i] = jnp.where(odd, low, high)
-
-
-def norm_kernel(visible_ref, pos_ref, gain_ref, bias_ref, *refs):
-    token_refs = refs[:-4]
-    normed_ref, unit_ref, own_unit_ref, own_inv_ref = refs[-4:]
-    slots, rows, width = token_refs[0].shape
+        theirs.append(jnp.where(odd, low, high))
+    out_ref[:, :, 2 * width :] = jnp.concatenate(theirs, axis=2)
+
+
+def norm_kernel(visible_ref, pos_ref, gain_ref, bias_ref, tokens_ref, across_ref, beside_ref, *refs):
+    normed_ref, unit_ref, own_unit_ref, own_inv_ref = refs
+    slots, rows, width = tokens_ref.shape
     gain = gain_ref[...]
     bias = bias_ref[...]
     for p in range(slots):
         iota = lax.broadcasted_iota(jnp.int32, (8, pos_ref.shape[0]), 1)
         onehot = (iota == visible_ref[p]).astype(F32).astype(BF16)
         position = dot(onehot, pos_ref[...])[0:1]
-        for s, tokens_ref in enumerate(token_refs):
-            embedded = (tokens_ref[p].astype(F32) + position).astype(BF16).astype(F32)
+        groups = (
+            tokens_ref[p],
+            beside_ref[p, :, :width],
+            across_ref[p, :, :width],
+            beside_ref[p, :, width : 2 * width],
+        )
+        for s, tokens in enumerate(groups):
+            embedded = (tokens.astype(F32) + position).astype(BF16).astype(F32)
             centred = embedded - jnp.mean(embedded, axis=-1, keepdims=True)
             inv_std = lax.rsqrt(jnp.mean(centred * centred, axis=-1, keepdims=True) + 1e-06)
             unit = centred * inv_std
-            at = (p * len(token_refs) + s) * rows
+            at = (p * len(groups) + s) * rows
             normed_ref[at : at + rows] = (unit * gain + bias).astype(BF16)
             unit_ref[at : at + rows] = unit.astype(BF16)
             if s == 0:
@@ -99,31 +121,42 @@
                 own_inv_ref[p] = jnp.broadcast_to(inv_std, own_inv_ref.shape[1:])
 
 
-def piece_rows(ids_ref, count, depth):
-    if count == 1:
-        return [0]
+def put_pieces(ids_ref, depth, offset, piece_refs, weights):
+    owners = len(piece_refs) // 2 + 1
     rep, owner = ids_ref[0], ids_ref[2]
-    owners = count // 2
     share = depth // 2
     spot = owner ^ (owner >> 1)
-    firsts = []
-    for step in range(owners):
-        back = lax.rem(spot + owners - step, owners)
-        source = back ^ (back >> 1)
-        firsts.append(pl.multiple_of(source * depth + rep * share, 16))
-        firsts.append(pl.multiple_of(source * depth + (1 - rep) * share, 16))
-    return firsts
-
-
-def attend_kernel(count, depth, ids_ref, live_ref, normed_ref, valid_ref, up_ref, beside_ref, *refs):
+    for i, ref in enumerate(piece_refs):
+        back = lax.rem(spot + owners - (i // 2 + 1), owners)
+        half = 1 - rep if i % 2 else rep
+        first = (back ^ (back >> 1)) * depth + half * share + offset
+        weights[pl.ds(pl.multiple_of(first, 16), ref.shape[0]), :] = ref[...]
+
+
+def place_kernel(depth, ids_ref, low_ref, high_ref, rest_ref, *refs):
+    weights = refs[-1]
+    rep, own = ids_ref[0], ids_ref[2] * depth
+    share = depth // 2
+    low = pl.multiple_of(own + rep * share, 16)
+    weights[pl.ds(low, low_ref.shape[0]), :] = low_ref[...]
+    high = pl.multiple_of(own + rep * share + low_ref.shape[0], 16)
+    weights[pl.ds(high, high_ref.shape[0]), :] = high_ref[...]
+    rest = pl.multiple_of(own + (1 - rep) * share, 16)
+    weights[pl.ds(rest, rest_ref.shape[0]), :] = rest_ref[...]
+    put_pieces(ids_ref, depth, 0, refs[:-1], weights)
+
+
+def attend_kernel(
+    count, depth, ids_ref, live_ref, _, normed_ref, valid_ref, up_ref, beside_ref, *refs
+):
     piece_refs = refs[:count]
-    own_ref, close_ref, across_ref, gqkv_ref, weights, qkv_ref = refs[-6:]
+    own_ref, close_ref, across_ref, gqkv_ref, weights, qkv_ref = refs[count:]
     _, slots, rows, channels = up_ref.shape
     dates = valid_ref.shape[1]
     heads = channels // HEAD_DIM
     inv_scale = 1.0 / HEAD_DIM**0.5
-    for first, ref in zip(piece_rows(ids_ref, count, depth), piece_refs):
-        weights[pl.ds(first, ref.shape[0]), :] = ref[...]
+    if count:
+        put_pieces(ids_ref, depth, depth // 4, piece_refs, weights)
     qkv_ref[...] = dot(normed_ref[...], weights[...]).astype(BF16)
     row = lax.broadcasted_iota(jnp.int32, (dates, dates), 0)
     column = lax.broadcasted_iota(jnp.int32, (dates, dates), 1)
@@ -132,7 +165,8 @@
         span = slice(p * dates, (p + 1) * dates)
         alive = (live_ref[ids_ref[2]] > p // (BLOCK_ROWS // DG)).astype(F32)
         rows_qkv = qkv_ref[span, :]
-        upstream = [up_ref[0, p], beside_ref[0, p], up_ref[1, p], beside_ref[1, p]]
+        others = beside_ref[p, :, beside_ref.shape[2] - 2 * channels :]
+        upstream = [up_ref[0, p], others[:, :channels], up_ref[1, p], others[:, channels:]]
         upstream = jnp.concatenate(upstream, axis=0) * alive.astype(BF16)
         valid = valid_ref[p : p + 1, :].astype(F32)
         allowed = jnp.sum(jnp.where(same_date, valid, 0.0), axis=1, keepdims=True) > 0
@@ -253,13 +287,14 @@
     return pltpu.with_memory_space_constraint(array, pltpu.VMEM)
 
 
-def call(kernel, name, out_shape, in_specs, args, megabytes, scratch=(), microseconds=0.01):
+def call(kernel, name, out_shape, in_specs, args, megabytes, scratch=(), microseconds=0.01, aliases=()):
     return pl.pallas_call(
         kernel,
         out_shape=out_shape,
         in_specs=in_specs,
         out_specs=jax.tree.map(lambda _: VMEM, out_shape),
         scratch_shapes=list(scratch),
+        input_output_aliases=dict(aliases),
         compiler_params=pltpu.CompilerParams(vmem_limit_bytes=megabytes * 1024 * 1024),
         cost_estimate=pl.CostEstimate(
             flops=int(microseconds * 10**9), bytes_accessed=1000, transcendentals=0
@@ -273,7 +308,9 @@
     return call(
         functools.partial(pick_kernel, part, other),
         "pick",
-        pltpu.VMEM((share, 3 * part), BF16),
+        (pltpu.VMEM((share, 3 * part), BF16),)
+        if other
+        else (pltpu.VMEM((share // 2, 3 * part), BF16),) * 2,
         [SMEM, HBM],
         (ids, pltpu.with_memory_space_constraint(w_qkv, pltpu.HBM)),
         4,
@@ -292,48 +329,48 @@
     ids = jnp.stack([lax.axis_index(name) for name in ("rep", "date", "tile")]).astype(jnp.int32)
     gain2, bias2 = norm_gain.reshape(1, width), norm_bias.reshape(1, width)
 
-    chain = owners == 4 and lax.axis_size("rep") == 2 and depth % 32 == 0
+    chain = owners == 4 and lax.axis_size("rep") == 2 and depth % 64 == 0
     ring = [(0, 1), (1, 3), (3, 2), (2, 0)]
     share = depth // 2
-
     if chain:
-        held = pick(w_qkv, ids, share, part, False)
-        first = lax.ppermute(held, "tile", ring)
-        second = lax.ppermute(first, "tile", ring)
-        first_other = swapped(first, "rep", 1)
-        rest = pick(w_qkv, after(ids, first), share, part, True)
-        second = after(second, first_other, rest)
-        third = lax.ppermute(second, "tile", ring)
-        second_other = swapped(second, "rep", 1)
-        third = after(third, second_other)
-        third_other = swapped(third, "rep", 1)
+        low, high = pick(w_qkv, ids, share, part, False)
+        chains = []
+        for held in (low, high):
+            first = lax.ppermute(held, "tile", ring)
+            second = lax.ppermute(first, "tile", ring)
+            first_other = swapped(first, "rep", 1)
+            if chains:
+                (rest,) = pick(w_qkv, after(ids, first), share, part, True)
+                first_other = after(first_other, rest)
+            second = after(second, first_other)
+            third = lax.ppermute(second, "tile", ring)
+            second_other = swapped(second, "rep", 1)
+            third = after(third, second_other)
+            third_other = swapped(third, "rep", 1)
+            chains.append((first, first_other, second, second_other, third, third_other))
+        first, later = chains[0][0], chains[1][2]
     else:
-        first = second = ids
-
-    sooner = after(tokens, first)
-    across = swapped(sooner, "date", 2)
-    beside = swapped(sooner, "date", 1)
-    beyond = swapped(after(across, second), "date", 1)
+        first = later = ids
+
+    across = call(
+        functools.partial(pack_across_kernel, part),
+        "pack_across",
+        pltpu.VMEM((slots, rows, width + 2 * part), BF16),
+        [SMEM, VMEM, VMEM],
+        (after(ids, first), tokens, cotangent),
+        6,
+    )
+    across = swapped(across, "date", 2)
     pair = pltpu.VMEM((2, slots, rows, part), BF16)
-    columns = call(
-        functools.partial(columns_kernel, part),
-        "columns",
-        pltpu.VMEM((slots, rows, 2 * part), BF16),
-        [SMEM, VMEM],
-        (after(ids, first), cotangent),
-        4,
-    )
-    columns = swapped(columns, "date", 2)
-    ups, ups_beside = call(
-        functools.partial(part_kernel, part),
-        "part",
-        (pair, pair),
-        [SMEM, VMEM, VMEM],
-        (ids, cotangent, near(columns)),
-        4,
-        microseconds=2,
-    )
-    ups_beside = swapped(ups_beside, "date", 1)
+    beside, ups = call(
+        functools.partial(pack_beside_kernel, part),
+        "pack_beside",
+        (pltpu.VMEM((slots, rows, 2 * width + 2 * part), BF16), pair),
+        [SMEM, VMEM, VMEM, VMEM],
+        (after(ids, later), tokens, cotangent, near(across)),
+        6,
+    )
+    beside = swapped(beside, "date", 1)
 
     normed, unit, own_unit, own_inv = call(
         norm_kernel,
@@ -344,20 +381,32 @@
             pltpu.VMEM((slots, rows, width), F32),
             pltpu.VMEM((slots, rows, 128), F32),
         ),
-        [SMEM] + [VMEM] * (3 + groups),
-        (visible, pos_table, gain2, bias2, tokens, near(beside), near(across), near(beyond)),
+        [SMEM] + [VMEM] * 6,
+        (visible, pos_table, gain2, bias2, tokens, near(across), near(beside)),
         12,
         microseconds=2,
     )
+    whole = pltpu.VMEM((width, 3 * part), BF16)
     if chain:
-        pieces = [held, rest, first, first_other, second, second_other, third, third_other]
+        own = [near(piece) for piece in (low, high, rest)]
+        pieces = [near(piece) for piece in chains[0]]
+        weights = call(
+            functools.partial(place_kernel, depth),
+            "place",
+            whole,
+            [SMEM] + [VMEM] * (len(own) + len(pieces)),
+            (ids, *own, *pieces),
+            4,
+            microseconds=8,
+        )
+        pieces = [near(piece) for piece in chains[1]]
     else:
         group = lax.axis_index("date")
         mine = [
             lax.dynamic_slice_in_dim(w_qkv, i * channels + group * part, part, 1) for i in range(3)
         ]
-        pieces = [lax.all_gather(jnp.concatenate(mine, axis=1), "tile", axis=0, tiled=True)]
-    pieces = [near(piece) for piece in pieces]
+        weights = lax.all_gather(jnp.concatenate(mine, axis=1), "tile", axis=0, tiled=True)
+        pieces = []
 
     piece = pltpu.VMEM((slots, rows, part), BF16)
     context, close_context, far_context, gqkv, weights = call(
@@ -368,11 +417,12 @@
             piece,
             pair,
             pltpu.VMEM((slots * dates, 3 * part), BF16),
-            pltpu.VMEM((width, 3 * part), BF16),
+            whole,
         ),
-        [SMEM] * 2 + [VMEM] * (4 + len(pieces)),
-        (ids, live, near(normed), valid, near(ups), near(ups_beside), *pieces),
+        [SMEM] * 2 + [VMEM] * (5 + len(pieces)),
+        (ids, live, near(weights), near(normed), valid, near(ups), near(beside), *pieces),
         20,
+        aliases=((2, 4),),
         scratch=(pltpu.VMEM((slots * dates, 3 * part), BF16),),
     )
     far_context = swapped(far_context, "date", 2)

time: 66.6 us -> 65.8 us (0.988)
  waiting for transfers between devices: 28.9 us -> 21.2 us
  starting transfers between devices: 20.3 us -> 26.5 us
    ppermute x1 -> x2, starting transfers between devices: 0.79 us -> 5.56 us  [local(): third = lax.ppermute(second, 'tile', ring)]
    ppermute x1 -> x2, waiting for transfers between devices: 4.29 us -> 0.67 us  [local(): third = lax.ppermute(second, 'tile', ring)]
    ppermute x1 -> x2, starting transfers between devices: 0.79 us -> 4.17 us  [local(): second = lax.ppermute(first, 'tile', ring)]
    ppermute x16, starting transfers between devices: 15.7 us -> 13 us  [swapped(): lax.ppermute(array, axis, [(i, i ^ bits) for i in range(lax.axis_size(axi...]
    ppermute x1 -> x2, waiting for transfers between devices: 8.72 us -> 6.97 us  [local(): first = lax.ppermute(held, 'tile', ring)]
    ppermute x1 -> x2, waiting for transfers between devices: 1.87 us -> 0.48 us  [local(): second = lax.ppermute(first, 'tile', ring)]
    ppermute x16, waiting for transfers between devices: 14 us -> 13.1 us  [swapped(): lax.ppermute(array, axis, [(i, i ^ bits) for i in range(lax.axis_size(axi...]
    ppermute x1 -> x2, starting transfers between devices: 3.08 us -> 3.86 us  [local(): first = lax.ppermute(held, 'tile', ring)]
  transfers between devices with their start and end apart: 19 -> 22, of which waited for: 10 -> 16; matrix products, arithmetic and copies ran while one was open for 0% -> 0% of each run, Pallas kernels for 13% -> 13%
where the time goes in v8:
time: 65.8 us; the launch traced here: 65.6 us
  starting transfers between devices  26.5 us (40%)
  waiting for transfers between devices  21.2 us (32%)
  Pallas kernels  16.8 us (26%)
  between operations  0.88 us (1%)
    pallas_call x13, Pallas kernels, call(): pl.pallas_call(kernel, out_shape=out_shape, in_specs=in_specs, out_specs=...  16.8 us
    ppermute x16, waiting for transfers between devices, swapped(): lax.ppermute(array, axis, [(i, i ^ bits) for i in range(lax.axis_size(axi...  13.1 us
    ppermute x16, starting transfers between devices, swapped(): lax.ppermute(array, axis, [(i, i ^ bits) for i in range(lax.axis_size(axi...  13 us
    ppermute x2, waiting for transfers between devices, local(): first = lax.ppermute(held, 'tile', ring)  6.97 us
    ppermute x2, starting transfers between devices, local(): third = lax.ppermute(second, 'tile', ring)  5.56 us
    ppermute x2, starting transfers between devices, local(): second = lax.ppermute(first, 'tile', ring)  4.17 us
    ppermute x2, starting transfers between devices, local(): first = lax.ppermute(held, 'tile', ring)  3.86 us
  transfers between devices with their start and end apart: 22, of which 16 were waited for; matrix products, arithmetic and copies ran while one was open for 0% of the time, Pallas kernels for 13%

profile of v8, /device:TPU:0, one launch (start us, length us, event | category | flops | bytes accessed | tf_op | source)
XLA Modules:
  0.0 65.6 jit_solution(3683922151558473445)
XLA Ops:
  0.7 1.9 %pick.2 = (bf16[80,960]{1,0:T(8,128)(2,1)S(1)}, bf16[80,960]{1,0:T(8,128)(2,1)S(1)}) custom-call(s32[3]{0:T(128)S(1)} %pad_add_fusion.ids_ref, bf16[320,3840]{1,0:T(8,128)(2,1)} %w_ref.3), custom_call_target="tpu_custom_call" | custom-call | flops 10000000 | bytes 1000 | tf_op jit(solution)/shard_map/pick/pallas_call | solution.py:291
  2.6 3.1 %collective-permute-start.1 = (bf16[80,960]{1,0:T(8,128)(2,1)S(1)}, bf16[80,960]{1,0:T(8,128)(2,1)S(1)}, u32[]{:S(2)}, u32[]{:S(2)}) collective-permute-start(bf16[80,960]{1,0:T(8,128)(2,1)S(1)} %get-tuple-element.35.low_ref), channel_id=1, source_target_pairs={{0,1},{1,3},{3,2},{2,0},{4,5},{5,7},{7,6},{6,4},{8,9},{9,11},{11,1... | collective-permute-start | bytes 460808 | tf_op jit(solution)/shard_map/ppermute | solution.py:339
  5.7 5.2 %collective-permute-done.1.refs_0_ = bf16[80,960]{1,0:T(8,128)(2,1)S(1)} collective-permute-done((bf16[80,960]{1,0:T(8,128)(2,1)S(1)}, bf16[80,960]{1,0:T(8,128)(2,1)S(1)}, u32[]{:S(2)}, u32[]{:S(2)}) %collective-permute-start.1) | collective-permute-done | bytes 153632 | tf_op jit(solution)/shard_map/ppermute | solution.py:339
  11.5 1.6 %collective-permute-start.7 = (bf16[4,32,1920]{2,1,0:T(8,128)(2,1)S(1)}, bf16[4,32,1920]{2,1,0:T(8,128)(2,1)S(1)}, u32[]{:S(2)}, u32[]{:S(2)}) collective-permute-start(bf16[4,32,1920]{2,1,0:T(8,128)(2,1)S(1)} %pack_across.1), channel_id=1, source_target_pairs={{0,8},{4,12},{8,0},{12,4},{1,9},{5,13},{9,1},{13,5},{2,10},{6,14},... | collective-permute-start | bytes 1474568 | tf_op jit(solution)/shard_map/ppermute | solution.py:279
  13.9 3.4 %collective-permute-start.3 = (bf16[80,960]{1,0:T(8,128)(2,1)S(1)}, bf16[80,960]{1,0:T(8,128)(2,1)S(1)}, u32[]{:S(2)}, u32[]{:S(2)}) collective-permute-start(bf16[80,960]{1,0:T(8,128)(2,1)S(1)} %collective-permute-done.1.refs_0_), channel_id=1, source_target_pairs={{0,1},{1,3},{3,2},{2,0},{4,5},{5,7},{7,6},{6,4},{8,9},{9,11},{11,1... | collective-permute-start | bytes 460808 | tf_op jit(solution)/shard_map/ppermute | solution.py:340
  17.3 1.5 %collective-permute-start.2 = (bf16[80,960]{1,0:T(8,128)(2,1)S(1)}, bf16[80,960]{1,0:T(8,128)(2,1)S(1)}, u32[]{:S(2)}, u32[]{:S(2)}) collective-permute-start(bf16[80,960]{1,0:T(8,128)(2,1)S(1)} %collective-permute-done.1.refs_0_), channel_id=1, source_target_pairs={{0,16},{16,0},{1,17},{17,1},{2,18},{18,2},{3,19},{19,3},{4,20},{20... | collective-permute-start | bytes 460808 | tf_op jit(solution)/shard_map/ppermute | solution.py:279
  18.8 1.8 %collective-permute-done.refs_0_ = bf16[80,960]{1,0:T(8,128)(2,1)S(1)} collective-permute-done((bf16[80,960]{1,0:T(8,128)(2,1)S(1)}, bf16[80,960]{1,0:T(8,128)(2,1)S(1)}, u32[]{:S(2)}, u32[]{:S(2)}) %collective-permute-start) | collective-permute-done | bytes 153632 | tf_op jit(solution)/shard_map/ppermute | solution.py:339
  20.6 1.5 %collective-permute-start.9 = (bf16[80,960]{1,0:T(8,128)(2,1)S(1)}, bf16[80,960]{1,0:T(8,128)(2,1)S(1)}, u32[]{:S(2)}, u32[]{:S(2)}) collective-permute-start(bf16[80,960]{1,0:T(8,128)(2,1)S(1)} %collective-permute-done.refs_0_), channel_id=1, source_target_pairs={{0,16},{16,0},{1,17},{17,1},{2,18},{18,2},{3,19},{19,3},{4,20},{20... | collective-permute-start | bytes 460808 | tf_op jit(solution)/shard_map/ppermute | solution.py:279
  23.3 3.0 %collective-permute-start.5 = (bf16[80,960]{1,0:T(8,128)(2,1)S(1)}, bf16[80,960]{1,0:T(8,128)(2,1)S(1)}, u32[]{:S(2)}, u32[]{:S(2)}) collective-permute-start(bf16[80,960]{1,0:T(8,128)(2,1)S(1)} %collective-permute-done.3.refs_2_), channel_id=1, source_target_pairs={{0,1},{1,3},{3,2},{2,0},{4,5},{5,7},{7,6},{6,4},{8,9},{9,11},{11,1... | collective-permute-start | bytes 460808 | tf_op jit(solution)/shard_map/ppermute | solution.py:346
  26.8 1.9 %pick.3.rest_ref = bf16[160,960]{1,0:T(8,128)(2,1)S(1)} custom-call(s32[3]{0:T(128)S(1)} %pad_add_fusion.ids_ref, bf16[320,3840]{1,0:T(8,128)(2,1)} %w_ref.3), custom_call_target="tpu_custom_call" | custom-call | flops 10000000 | bytes 1000 | tf_op jit(solution)/shard_map/pick/pallas_call | solution.py:291
  29.0 2.6 %collective-permute-start.12 = (bf16[80,960]{1,0:T(8,128)(2,1)S(1)}, bf16[80,960]{1,0:T(8,128)(2,1)S(1)}, u32[]{:S(2)}, u32[]{:S(2)}) collective-permute-start(bf16[80,960]{1,0:T(8,128)(2,1)S(1)} %collective-permute-done.8.refs_2_), channel_id=1, source_target_pairs={{0,1},{1,3},{3,2},{2,0},{4,5},{5,7},{7,6},{6,4},{8,9},{9,11},{11,1... | collective-permute-start | bytes 460808 | tf_op jit(solution)/shard_map/ppermute | solution.py:346
  31.8 1.4 %collective-permute-done.4.refs_3_ = bf16[80,960]{1,0:T(8,128)(2,1)S(1)} collective-permute-done((bf16[80,960]{1,0:T(8,128)(2,1)S(1)}, bf16[80,960]{1,0:T(8,128)(2,1)S(1)}, u32[]{:S(2)}, u32[]{:S(2)}) %collective-permute-start.4) | collective-permute-done | bytes 153632 | tf_op jit(solution)/shard_map/ppermute | solution.py:279
  35.3 1.7 %collective-permute-done.11.refs_3_ = bf16[80,960]{1,0:T(8,128)(2,1)S(1)} collective-permute-done((bf16[80,960]{1,0:T(8,128)(2,1)S(1)}, bf16[80,960]{1,0:T(8,128)(2,1)S(1)}, u32[]{:S(2)}, u32[]{:S(2)}) %collective-permute-start.11) | collective-permute-done | bytes 153632 | tf_op jit(solution)/shard_map/ppermute | solution.py:279
  37.0 2.4 %collective-permute-done.6.refs_5_ = bf16[80,960]{1,0:T(8,128)(2,1)S(1)} collective-permute-done((bf16[80,960]{1,0:T(8,128)(2,1)S(1)}, bf16[80,960]{1,0:T(8,128)(2,1)S(1)}, u32[]{:S(2)}, u32[]{:S(2)}) %collective-permute-start.6) | collective-permute-done | bytes 153632 | tf_op jit(solution)/shard_map/ppermute | solution.py:279
  40.1 1.9 %norm.1 = (bf16[512,1280]{1,0:T(8,128)(2,1)S(1)}, bf16[512,1280]{1,0:T(8,128)(2,1)S(1)}, f32[4,32,1280]{2,1,0:T(8,128)S(1)}, f32[4,32,128]{2,1,0:T(8,128)S(1)}) custom-call(s32[4]{0:T(128)S(1)} %copy-done.5, bf16[256,1280]{1,0:T(8,128)(2,1)S(1)} %copy-done.4, f32[1,1280]{1,0:T(1,128)S(1)} %reshape.12.gain_ref, f32[1,1280]{1,0:T(1,128)S(1)} %reshape.13.bias_ref, ...), custom_call_target="tpu_custom_call" | custom-call | flops 2000000000 | bytes 1000 | tf_op jit(solution)/shard_map/norm/pallas_call | solution.py:291
  42.3 4.3 %attend.1 = (bf16[4,32,320]{2,1,0:T(8,128)(2,1)S(1)}, bf16[4,32,320]{2,1,0:T(8,128)(2,1)S(1)}, bf16[2,4,32,320]{3,2,1,0:T(8,128)(2,1)S(1)}, bf16[512,960]{1,0:T(8,128)(2,1)S(1)}, bf16[1280,960]{1,0:T(8,128)(2,1)S(1)}) custom-call(s32[3]{0:T(128)S(1)} %pad_add_fusion.ids_ref, s32[4]{0:T(128)S(1)} %copy-done.3, ...), custom_call_target="tpu_custom_call", output_to_operand_aliasing={{4}: (2, {})} | custom-call | flops 10000000 | bytes 1000 | tf_op jit(solution)/shard_map/attend/pallas_call | solution.py:291
  47.1 1.6 %back.1 = (bf16[4,32,1280]{2,1,0:T(8,128)(2,1)S(1)}, bf16[4,32,1280]{2,1,0:T(8,128)(2,1)S(1)}, bf16[272,1280]{1,0:T(8,128)(2,1)S(1)}, f32[2,1280]{1,0:T(2,128)S(1)}) custom-call(bf16[512,960]{1,0:T(8,128)(2,1)S(1)} %get-tuple-element.48.gqkv_ref, bf16[512,1280]{1,0:T(8,128)(2,1)S(1)} %get-tuple-element.49.unit_ref, ...), custom_call_target="tpu_custom_call" | custom-call | flops 10000000 | bytes 1000 | tf_op jit(solution)/shard_map/back/pallas_call | solution.py:291
  48.9 3.4 %collective-permute-done.15.far_ref.across_ref = bf16[2,4,32,320]{3,2,1,0:T(8,128)(2,1)S(1)} collective-permute-done((bf16[2,4,32,320]{3,2,1,0:T(8,128)(2,1)S(1)}, bf16[2,4,32,320]{3,2,1,0:T(8,128)(2,1)S(1)}, u32[]{:S(2)}, u32[]{:S(2)}) %collective-permute-start.15) | collective-permute-done | bytes 163872 | tf_op jit(solution)/shard_map/ppermute | solution.py:279
  53.0 2.1 %collective-permute-start.20 = (f32[2,1280]{1,0:T(2,128)S(1)}, f32[2,1280]{1,0:T(2,128)S(1)}, u32[]{:S(2)}, u32[]{:S(2)}) collective-permute-start(f32[2,1280]{1,0:T(2,128)S(1)} %get-tuple-element.64.refs_0_), channel_id=1, source_target_pairs={{0,3},{1,2},{2,1},{3,0},{4,7},{5,6},{6,5},{7,4},{8,11},{9,10},{10,... | collective-permute-start | bytes 30728 | tf_op jit(solution)/shard_map/ppermute | solution.py:279
  55.1 1.5 %collective-permute-start.19 = (f32[2,1280]{1,0:T(2,128)S(1)}, f32[2,1280]{1,0:T(2,128)S(1)}, u32[]{:S(2)}, u32[]{:S(2)}) collective-permute-start(f32[2,1280]{1,0:T(2,128)S(1)} %get-tuple-element.64.refs_0_), channel_id=1, source_target_pairs={{0,2},{1,3},{2,0},{3,1},{4,6},{5,7},{6,4},{7,5},{8,10},{9,11},{10,... | collective-permute-start | bytes 30728 | tf_op jit(solution)/shard_map/ppermute | solution.py:279
  58.5 1.2 %collective-permute-done.19.refs_2_ = f32[2,1280]{1,0:T(2,128)S(1)} collective-permute-done((f32[2,1280]{1,0:T(2,128)S(1)}, f32[2,1280]{1,0:T(2,128)S(1)}, u32[]{:S(2)}, u32[]{:S(2)}) %collective-permute-start.19) | collective-permute-done | bytes 10272 | tf_op jit(solution)/shard_map/ppermute | solution.py:279
  60.3 1.5 %collective-permute-start.21 = (f32[2,1280]{1,0:T(2,128)S(1)}, f32[2,1280]{1,0:T(2,128)S(1)}, u32[]{:S(2)}, u32[]{:S(2)}) collective-permute-start(f32[2,1280]{1,0:T(2,128)S(1)} %add.5.refs_0_), channel_id=1, source_target_pairs={{0,8},{4,12},{8,0},{12,4},{1,9},{5,13},{9,1},{13,5},{2,10},{6,14},... | collective-permute-start | bytes 30728 | tf_op jit(solution)/shard_map/ppermute | solution.py:279
  61.8 1.4 %home.1 = (f32[4,32,1280]{2,1,0:T(8,128)S(1)}, bf16[4,32,1280]{2,1,0:T(8,128)(2,1)}) custom-call(s32[3]{0:T(128)S(1)} %pad_add_fusion.ids_ref, bf16[4,32,1280]{2,1,0:T(8,128)(2,1)S(1)} %get-tuple-element.51.stay_ref, bf16[272,1280]{1,0:T(8,128)(2,1)S(1)} %collective-permute-done.14.close_ref, bf16[4,32,320]{2,1,0:T(8,128)(2,1)S(1)} %get-tuple-element.56.own_ref, ...), custom_call_target="tpu_custom_call" | custom-call | flops 10000000 | bytes 1000 | tf_op jit(solution)/shard_map/home/pallas_call | solution.py:291
  64.0 1.6 %finish.1 = (bf16[4,32,1280]{2,1,0:T(8,128)(2,1)}, f32[2,1280]{1,0:T(2,128)}) custom-call(s32[3]{0:T(128)S(1)} %pad_add_fusion.ids_ref, s32[4]{0:T(128)S(1)} %copy-done.3, f32[4,32,1280]{2,1,0:T(8,128)S(1)} %get-tuple-element.58.unit_ref, f32[4,32,128]{2,1,0:T(8,128)S(1)} %get-tuple-element.59.inv_ref, f32[1,1280]{1,0:T(1,128)S(1)} %reshape.12.gain_ref, ...), custom_call_target="tpu_custom_call" | custom-call | flops 10000000 | bytes 1000 | tf_op jit(solution)/shard_map/finish/pallas_call | solution.py:291
  (52 shorter events, 11.3 us)
Async XLA Ops:
  2.6 32.1 %copy-start.6 = (f32[1280]{0:T(1024)S(1)}, f32[1280]{0:T(1024)}, u32[]{:S(2)}) copy-start(f32[1280]{0:T(1024)} %param.15) | copy-start | bytes 15364
  2.6 32.1 %copy-start.7 = (f32[1280]{0:T(1024)S(1)}, f32[1280]{0:T(1024)}, u32[]{:S(2)}) copy-start(f32[1280]{0:T(1024)} %param.16) | copy-start | bytes 15364
  2.6 8.3 %collective-permute-start.1 = (bf16[80,960]{1,0:T(8,128)(2,1)S(1)}, bf16[80,960]{1,0:T(8,128)(2,1)S(1)}, u32[]{:S(2)}, u32[]{:S(2)}) collective-permute-start(bf16[80,960]{1,0:T(8,128)(2,1)S(1)} %get-tuple-element.35.low_ref), channel_id=1, source_target_pairs={{0,1},{1,3},{3,2},{2,0},{4,5},{5,7},{7,6},{6,4},{8,9},{9,11},{11,1... | collective-permute-start | bytes 460808 | tf_op jit(solution)/shard_map/ppermute | solution.py:339
  11.5 22.2 %collective-permute-start.7 = (bf16[4,32,1920]{2,1,0:T(8,128)(2,1)S(1)}, bf16[4,32,1920]{2,1,0:T(8,128)(2,1)S(1)}, u32[]{:S(2)}, u32[]{:S(2)}) collective-permute-start(bf16[4,32,1920]{2,1,0:T(8,128)(2,1)S(1)} %pack_across.1), channel_id=1, source_target_pairs={{0,8},{4,12},{8,0},{12,4},{1,9},{5,13},{9,1},{13,5},{2,10},{6,14},... | collective-permute-start | bytes 1474568 | tf_op jit(solution)/shard_map/ppermute | solution.py:279
  13.1 7.4 %collective-permute-start = (bf16[80,960]{1,0:T(8,128)(2,1)S(1)}, bf16[80,960]{1,0:T(8,128)(2,1)S(1)}, u32[]{:S(2)}, u32[]{:S(2)}) collective-permute-start(bf16[80,960]{1,0:T(8,128)(2,1)S(1)} %get-tuple-element.36.high_ref), channel_id=1, source_target_pairs={{0,1},{1,3},{3,2},{2,0},{4,5},{5,7},{7,6},{6,4},{8,9},{9,11},{11,1... | collective-permute-start | bytes 460808 | tf_op jit(solution)/shard_map/ppermute | solution.py:339
  13.9 9.1 %collective-permute-start.3 = (bf16[80,960]{1,0:T(8,128)(2,1)S(1)}, bf16[80,960]{1,0:T(8,128)(2,1)S(1)}, u32[]{:S(2)}, u32[]{:S(2)}) collective-permute-start(bf16[80,960]{1,0:T(8,128)(2,1)S(1)} %collective-permute-done.1.refs_0_), channel_id=1, source_target_pairs={{0,1},{1,3},{3,2},{2,0},{4,5},{5,7},{7,6},{6,4},{8,9},{9,11},{11,1... | collective-permute-start | bytes 460808 | tf_op jit(solution)/shard_map/ppermute | solution.py:340
  17.3 6.0 %collective-permute-start.2 = (bf16[80,960]{1,0:T(8,128)(2,1)S(1)}, bf16[80,960]{1,0:T(8,128)(2,1)S(1)}, u32[]{:S(2)}, u32[]{:S(2)}) collective-permute-start(bf16[80,960]{1,0:T(8,128)(2,1)S(1)} %collective-permute-done.1.refs_0_), channel_id=1, source_target_pairs={{0,16},{16,0},{1,17},{17,1},{2,18},{18,2},{3,19},{19,3},{4,20},{20... | collective-permute-start | bytes 460808 | tf_op jit(solution)/shard_map/ppermute | solution.py:279
  20.6 8.1 %collective-permute-start.9 = (bf16[80,960]{1,0:T(8,128)(2,1)S(1)}, bf16[80,960]{1,0:T(8,128)(2,1)S(1)}, u32[]{:S(2)}, u32[]{:S(2)}) collective-permute-start(bf16[80,960]{1,0:T(8,128)(2,1)S(1)} %collective-permute-done.refs_0_), channel_id=1, source_target_pairs={{0,16},{16,0},{1,17},{17,1},{2,18},{18,2},{3,19},{19,3},{4,20},{20... | collective-permute-start | bytes 460808 | tf_op jit(solution)/shard_map/ppermute | solution.py:279
  22.1 7.0 %collective-permute-start.8 = (bf16[80,960]{1,0:T(8,128)(2,1)S(1)}, bf16[80,960]{1,0:T(8,128)(2,1)S(1)}, u32[]{:S(2)}, u32[]{:S(2)}) collective-permute-start(bf16[80,960]{1,0:T(8,128)(2,1)S(1)} %collective-permute-done.refs_0_), channel_id=1, source_target_pairs={{0,1},{1,3},{3,2},{2,0},{4,5},{5,7},{7,6},{6,4},{8,9},{9,11},{11,1... | collective-permute-start | bytes 460808 | tf_op jit(solution)/shard_map/ppermute | solution.py:340
  23.3 8.5 %collective-permute-start.5 = (bf16[80,960]{1,0:T(8,128)(2,1)S(1)}, bf16[80,960]{1,0:T(8,128)(2,1)S(1)}, u32[]{:S(2)}, u32[]{:S(2)}) collective-permute-start(bf16[80,960]{1,0:T(8,128)(2,1)S(1)} %collective-permute-done.3.refs_2_), channel_id=1, source_target_pairs={{0,1},{1,3},{3,2},{2,0},{4,5},{5,7},{7,6},{6,4},{8,9},{9,11},{11,1... | collective-permute-start | bytes 460808 | tf_op jit(solution)/shard_map/ppermute | solution.py:346
  26.3 7.0 %collective-permute-start.4 = (bf16[80,960]{1,0:T(8,128)(2,1)S(1)}, bf16[80,960]{1,0:T(8,128)(2,1)S(1)}, u32[]{:S(2)}, u32[]{:S(2)}) collective-permute-start(bf16[80,960]{1,0:T(8,128)(2,1)S(1)} %collective-permute-done.3.refs_2_), channel_id=1, source_target_pairs={{0,16},{16,0},{1,17},{17,1},{2,18},{18,2},{3,19},{19,3},{4,20},{20... | collective-permute-start | bytes 460808 | tf_op jit(solution)/shard_map/ppermute | solution.py:279
  29.0 6.2 %collective-permute-start.12 = (bf16[80,960]{1,0:T(8,128)(2,1)S(1)}, bf16[80,960]{1,0:T(8,128)(2,1)S(1)}, u32[]{:S(2)}, u32[]{:S(2)}) collective-permute-start(bf16[80,960]{1,0:T(8,128)(2,1)S(1)} %collective-permute-done.8.refs_2_), channel_id=1, source_target_pairs={{0,1},{1,3},{3,2},{2,0},{4,5},{5,7},{7,6},{6,4},{8,9},{9,11},{11,1... | collective-permute-start | bytes 460808 | tf_op jit(solution)/shard_map/ppermute | solution.py:346
  31.6 5.3 %collective-permute-start.11 = (bf16[80,960]{1,0:T(8,128)(2,1)S(1)}, bf16[80,960]{1,0:T(8,128)(2,1)S(1)}, u32[]{:S(2)}, u32[]{:S(2)}) collective-permute-start(bf16[80,960]{1,0:T(8,128)(2,1)S(1)} %collective-permute-done.8.refs_2_), channel_id=1, source_target_pairs={{0,16},{16,0},{1,17},{17,1},{2,18},{18,2},{3,19},{19,3},{4,20},{20... | collective-permute-start | bytes 460808 | tf_op jit(solution)/shard_map/ppermute | solution.py:279
  33.2 6.1 %collective-permute-start.6 = (bf16[80,960]{1,0:T(8,128)(2,1)S(1)}, bf16[80,960]{1,0:T(8,128)(2,1)S(1)}, u32[]{:S(2)}, u32[]{:S(2)}) collective-permute-start(bf16[80,960]{1,0:T(8,128)(2,1)S(1)} %collective-permute-done.5.refs_4_), channel_id=1, source_target_pairs={{0,16},{16,0},{1,17},{17,1},{2,18},{18,2},{3,19},{19,3},{4,20},{20... | collective-permute-start | bytes 460808 | tf_op jit(solution)/shard_map/ppermute | solution.py:279
  34.6 5.4 %collective-permute-start.10 = (bf16[4,32,3200]{2,1,0:T(8,128)(2,1)S(1)}, bf16[4,32,3200]{2,1,0:T(8,128)(2,1)S(1)}, u32[]{:S(2)}, u32[]{:S(2)}) collective-permute-start(bf16[4,32,3200]{2,1,0:T(8,128)(2,1)S(1)} %get-tuple-element.44), channel_id=1, source_target_pairs={{0,4},{4,0},{8,12},{12,8},{1,5},{5,1},{9,13},{13,9},{2,6},{6,2},{1... | collective-permute-start | bytes 2457608 | tf_op jit(solution)/shard_map/ppermute | solution.py:279
  36.9 5.3 %collective-permute-start.13 = (bf16[80,960]{1,0:T(8,128)(2,1)S(1)}, bf16[80,960]{1,0:T(8,128)(2,1)S(1)}, u32[]{:S(2)}, u32[]{:S(2)}) collective-permute-start(bf16[80,960]{1,0:T(8,128)(2,1)S(1)} %collective-permute-done.12.refs_4_), channel_id=1, source_target_pairs={{0,16},{16,0},{1,17},{17,1},{2,18},{18,2},{3,19},{19,3},{4,20},{20... | collective-permute-start | bytes 460808 | tf_op jit(solution)/shard_map/ppermute | solution.py:279
  46.5 5.7 %collective-permute-start.15 = (bf16[2,4,32,320]{3,2,1,0:T(8,128)(2,1)S(1)}, bf16[2,4,32,320]{3,2,1,0:T(8,128)(2,1)S(1)}, u32[]{:S(2)}, u32[]{:S(2)}) collective-permute-start(bf16[2,4,32,320]{3,2,1,0:T(8,128)(2,1)S(1)} %get-tuple-element.54), channel_id=1, source_target_pairs={{0,8},{4,12},{8,0},{12,4},{1,9},{5,13},{9,1},{13,5},{2,10},{6,14},... | collective-permute-start | bytes 491528 | tf_op jit(solution)/shard_map/ppermute | solution.py:279
  48.8 3.5 %collective-permute-start.14 = (bf16[272,1280]{1,0:T(8,128)(2,1)S(1)}, bf16[272,1280]{1,0:T(8,128)(2,1)S(1)}, u32[]{:S(2)}, u32[]{:S(2)}) collective-permute-start(bf16[272,1280]{1,0:T(8,128)(2,1)S(1)} %get-tuple-element.52), channel_id=1, source_target_pairs={{0,4},{4,0},{8,12},{12,8},{1,5},{5,1},{9,13},{13,9},{2,6},{6,2},{1... | collective-permute-start | bytes 2088968 | tf_op jit(solution)/shard_map/ppermute | solution.py:279
  52.4 11.6 %collective-permute-start.17 = (bf16[4,32,1280]{2,1,0:T(8,128)(2,1)S(1)}, bf16[4,32,1280]{2,1,0:T(8,128)(2,1)S(1)}, u32[]{:S(2)}, u32[]{:S(2)}) collective-permute-start(bf16[4,32,1280]{2,1,0:T(8,128)(2,1)S(1)} %get-tuple-element.63), channel_id=1, source_target_pairs={{0,8},{4,12},{8,0},{12,4},{1,9},{5,13},{9,1},{13,5},{2,10},{6,14},... | collective-permute-start | bytes 983048 | tf_op jit(solution)/shard_map/ppermute | solution.py:279
  53.0 8.9 %collective-permute-start.16 = (bf16[2,4,32,320]{3,2,1,0:T(8,128)(2,1)S(1)}, bf16[2,4,32,320]{3,2,1,0:T(8,128)(2,1)S(1)}, u32[]{:S(2)}, u32[]{:S(2)}) collective-permute-start(bf16[2,4,32,320]{3,2,1,0:T(8,128)(2,1)S(1)} %both.1), channel_id=1, source_target_pairs={{0,4},{4,0},{8,12},{12,8},{1,5},{5,1},{9,13},{13,9},{2,6},{6,2},{1... | collective-permute-start | bytes 491528 | tf_op jit(solution)/shard_map/ppermute | solution.py:279
  53.0 5.5 %collective-permute-start.20 = (f32[2,1280]{1,0:T(2,128)S(1)}, f32[2,1280]{1,0:T(2,128)S(1)}, u32[]{:S(2)}, u32[]{:S(2)}) collective-permute-start(f32[2,1280]{1,0:T(2,128)S(1)} %get-tuple-element.64.refs_0_), channel_id=1, source_target_pairs={{0,3},{1,2},{2,1},{3,0},{4,7},{5,6},{6,5},{7,4},{8,11},{9,10},{10,... | collective-permute-start | bytes 30728 | tf_op jit(solution)/shard_map/ppermute | solution.py:279
  55.1 4.6 %collective-permute-start.19 = (f32[2,1280]{1,0:T(2,128)S(1)}, f32[2,1280]{1,0:T(2,128)S(1)}, u32[]{:S(2)}, u32[]{:S(2)}) collective-permute-start(f32[2,1280]{1,0:T(2,128)S(1)} %get-tuple-element.64.refs_0_), channel_id=1, source_target_pairs={{0,2},{1,3},{2,0},{3,1},{4,6},{5,7},{6,4},{7,5},{8,10},{9,11},{10,... | collective-permute-start | bytes 30728 | tf_op jit(solution)/shard_map/ppermute | solution.py:279
  56.7 3.7 %collective-permute-start.18 = (f32[2,1280]{1,0:T(2,128)S(1)}, f32[2,1280]{1,0:T(2,128)S(1)}, u32[]{:S(2)}, u32[]{:S(2)}) collective-permute-start(f32[2,1280]{1,0:T(2,128)S(1)} %get-tuple-element.64.refs_0_), channel_id=1, source_target_pairs={{0,1},{1,0},{2,3},{3,2},{4,5},{5,4},{6,7},{7,6},{8,9},{9,8},{10,11... | collective-permute-start | bytes 30728 | tf_op jit(solution)/shard_map/ppermute | solution.py:279
  60.3 3.7 %collective-permute-start.21 = (f32[2,1280]{1,0:T(2,128)S(1)}, f32[2,1280]{1,0:T(2,128)S(1)}, u32[]{:S(2)}, u32[]{:S(2)}) collective-permute-start(f32[2,1280]{1,0:T(2,128)S(1)} %add.5.refs_0_), channel_id=1, source_target_pairs={{0,8},{4,12},{8,0},{12,4},{1,9},{5,13},{9,1},{13,5},{2,10},{6,14},... | collective-permute-start | bytes 30728 | tf_op jit(solution)/shard_map/ppermute | solution.py:279
  (6 other events, 35.6 us)

commit v9 on v8

--- a/solution.py
+++ b/solution.py
@@ -121,13 +121,13 @@
                 own_inv_ref[p] = jnp.broadcast_to(inv_std, own_inv_ref.shape[1:])
 
 
-def put_pieces(ids_ref, depth, offset, piece_refs, weights):
-    owners = len(piece_refs) // 2 + 1
+def put_pieces(ids_ref, depth, offset, steps, piece_refs, weights):
+    owners = 4
     rep, owner = ids_ref[0], ids_ref[2]
     share = depth // 2
     spot = owner ^ (owner >> 1)
     for i, ref in enumerate(piece_refs):
-        back = lax.rem(spot + owners - (i // 2 + 1), owners)
+        back = lax.rem(spot + owners - steps[i // 2], owners)
         half = 1 - rep if i % 2 else rep
         first = (back ^ (back >> 1)) * depth + half * share + offset
         weights[pl.ds(pl.multiple_of(first, 16), ref.shape[0]), :] = ref[...]
@@ -143,7 +143,8 @@
     weights[pl.ds(high, high_ref.shape[0]), :] = high_ref[...]
     rest = pl.multiple_of(own + (1 - rep) * share, 16)
     weights[pl.ds(rest, rest_ref.shape[0]), :] = rest_ref[...]
-    put_pieces(ids_ref, depth, 0, refs[:-1], weights)
+    put_pieces(ids_ref, depth, 0, (1, 2, 3), refs[:6], weights)
+    put_pieces(ids_ref, depth, depth // 4, (1, 2), refs[6:-1], weights)
 
 
 def attend_kernel(
@@ -156,7 +157,7 @@
     heads = channels // HEAD_DIM
     inv_scale = 1.0 / HEAD_DIM**0.5
     if count:
-        put_pieces(ids_ref, depth, depth // 4, piece_refs, weights)
+        put_pieces(ids_ref, depth, depth // 4, (3,), piece_refs, weights)
     qkv_ref[...] = dot(normed_ref[...], weights[...]).astype(BF16)
     row = lax.broadcasted_iota(jnp.int32, (dates, dates), 0)
     column = lax.broadcasted_iota(jnp.int32, (dates, dates), 1)
@@ -337,18 +338,19 @@
         chains = []
         for held in (low, high):
             first = lax.ppermute(held, "tile", ring)
+            if chains:
+                (rest,) = pick(w_qkv, after(ids, held), share, part, True)
+                first = after(first, rest)
             second = lax.ppermute(first, "tile", ring)
             first_other = swapped(first, "rep", 1)
-            if chains:
-                (rest,) = pick(w_qkv, after(ids, first), share, part, True)
-                first_other = after(first_other, rest)
             second = after(second, first_other)
             third = lax.ppermute(second, "tile", ring)
             second_other = swapped(second, "rep", 1)
-            third = after(third, second_other)
+            if not chains:
+                third = after(third, second_other)
             third_other = swapped(third, "rep", 1)
             chains.append((first, first_other, second, second_other, third, third_other))
-        first, later = chains[0][0], chains[1][2]
+        first, later = chains[1][0], chains[1][2]
     else:
         first = later = ids
 
@@ -389,7 +391,7 @@
     whole = pltpu.VMEM((width, 3 * part), BF16)
     if chain:
         own = [near(piece) for piece in (low, high, rest)]
-        pieces = [near(piece) for piece in chains[0]]
+        pieces = [near(piece) for piece in chains[0] + chains[1][:4]]
         weights = call(
             functools.partial(place_kernel, depth),
             "place",
@@ -399,7 +401,7 @@
             4,
             microseconds=8,
         )
-        pieces = [near(piece) for piece in chains[1]]
+        pieces = [near(piece) for piece in chains[1][4:]]
     else:
         group = lax.axis_index("date")
         mine = [
@@ -458,18 +460,6 @@
         6,
     )
     far = swapped(chip, "date", 2)
-    if owners == 4:
-        total = call(
-            add_kernel,
-            "add",
-            pairs,
-            [VMEM] * owners,
-            [near(total)] + [near(swapped(total, "tile", s)) for s in range(1, owners)],
-            2,
-        )
-    else:
-        total = lax.psum(total, "tile")
-    far_total = swapped(total, "date", 2)
     both = swapped(both, "date", 1)
     home, attended = call(
         home_kernel,
@@ -480,6 +470,20 @@
         6,
         scratch=(pltpu.VMEM((groups, slots, rows, part), BF16),),
     )
+    if owners == 4:
+        tiles = [swapped(total, "tile", s) for s in range(1, owners)]
+        tiles[0] = after(tiles[0], home)
+        total = call(
+            add_kernel,
+            "add",
+            pairs,
+            [VMEM] * owners,
+            [near(total)] + [near(tile) for tile in tiles],
+            2,
+        )
+    else:
+        total = lax.psum(total, "tile")
+    far_total = swapped(total, "date", 2)
     grad_tokens, grad_norm = call(
         finish_kernel,
         "finish",

time: 65.8 us -> 65.8 us (level)
  starting transfers between devices: 26.5 us -> 31.3 us
  waiting for transfers between devices: 21.2 us -> 16.5 us
    ppermute x2, waiting for transfers between devices: 6.97 us -> 1.74 us  [local(): first = lax.ppermute(held, 'tile', ring)]
    ppermute x16, starting transfers between devices: 13 us -> 16.7 us  [swapped(): lax.ppermute(array, axis, [(i, i ^ bits) for i in range(lax.axis_size(axi...]
    ppermute x2, starting transfers between devices: 3.86 us -> 5.67 us  [local(): first = lax.ppermute(held, 'tile', ring)]
    ppermute x2, waiting for transfers between devices: 0.48 us -> 1.79 us  [local(): second = lax.ppermute(first, 'tile', ring)]
    ppermute x2, starting transfers between devices: 5.56 us -> 4.72 us  [local(): third = lax.ppermute(second, 'tile', ring)]
    ppermute x2, waiting for transfers between devices: 0.67 us -> 0.01 us  [local(): third = lax.ppermute(second, 'tile', ring)]
  transfers between devices with their start and end apart: 22 -> 22, of which waited for: 16 -> 10; matrix products, arithmetic and copies ran while one was open for 0% -> 0% of each run, Pallas kernels for 13% -> 14%
where the time goes in v9:
time: 65.8 us; the launch traced here: 65.6 us
  starting transfers between devices  31.3 us (48%)
  Pallas kernels  16.9 us (26%)
  waiting for transfers between devices  16.5 us (25%)
  between operations  0.87 us (1%)
    pallas_call x13, Pallas kernels, call(): pl.pallas_call(kernel, out_shape=out_shape, in_specs=in_specs, out_specs=...  16.9 us
    ppermute x16, starting transfers between devices, swapped(): lax.ppermute(array, axis, [(i, i ^ bits) for i in range(lax.axis_size(axi...  16.7 us
    ppermute x16, waiting for transfers between devices, swapped(): lax.ppermute(array, axis, [(i, i ^ bits) for i in range(lax.axis_size(axi...  13 us
    ppermute x2, starting transfers between devices, local(): first = lax.ppermute(held, 'tile', ring)  5.67 us
    ppermute x2, starting transfers between devices, local(): third = lax.ppermute(second, 'tile', ring)  4.72 us
    ppermute x2, starting transfers between devices, local(): second = lax.ppermute(first, 'tile', ring)  4.22 us
    ppermute x2, waiting for transfers between devices, local(): second = lax.ppermute(first, 'tile', ring)  1.79 us
    ppermute x2, waiting for transfers between devices, local(): first = lax.ppermute(held, 'tile', ring)  1.74 us
  transfers between devices with their start and end apart: 22, of which 10 were waited for; matrix products, arithmetic and copies ran while one was open for 0% of the time, Pallas kernels for 14%

profile of v9, /device:TPU:0, one launch (start us, length us, event | category | flops | bytes accessed | tf_op | source)
XLA Modules:
  0.0 65.6 jit_solution(12814710796709159199)
XLA Ops:
  0.7 1.9 %pick.2 = (bf16[80,960]{1,0:T(8,128)(2,1)S(1)}, bf16[80,960]{1,0:T(8,128)(2,1)S(1)}) custom-call(s32[3]{0:T(128)S(1)} %pad_add_fusion.ids_ref, bf16[320,3840]{1,0:T(8,128)(2,1)} %w_ref.3), custom_call_target="tpu_custom_call" | custom-call | flops 10000000 | bytes 1000 | tf_op jit(solution)/shard_map/pick/pallas_call | solution.py:292
  2.6 3.1 %collective-permute-start.6 = (bf16[80,960]{1,0:T(8,128)(2,1)S(1)}, bf16[80,960]{1,0:T(8,128)(2,1)S(1)}, u32[]{:S(2)}, u32[]{:S(2)}) collective-permute-start(bf16[80,960]{1,0:T(8,128)(2,1)S(1)} %get-tuple-element.36.high_ref), channel_id=1, source_target_pairs={{0,1},{1,3},{3,2},{2,0},{4,5},{5,7},{7,6},{6,4},{8,9},{9,11},{11,1... | collective-permute-start | bytes 460808 | tf_op jit(solution)/shard_map/ppermute | solution.py:340
  5.7 2.6 %collective-permute-start = (bf16[80,960]{1,0:T(8,128)(2,1)S(1)}, bf16[80,960]{1,0:T(8,128)(2,1)S(1)}, u32[]{:S(2)}, u32[]{:S(2)}) collective-permute-start(bf16[80,960]{1,0:T(8,128)(2,1)S(1)} %get-tuple-element.35.low_ref), channel_id=1, source_target_pairs={{0,1},{1,3},{3,2},{2,0},{4,5},{5,7},{7,6},{6,4},{8,9},{9,11},{11,1... | collective-permute-start | bytes 460808 | tf_op jit(solution)/shard_map/ppermute | solution.py:340
  8.3 1.9 %pick.3.rest_ref = bf16[160,960]{1,0:T(8,128)(2,1)S(1)} custom-call(s32[3]{0:T(128)S(1)} %pad_add_fusion.ids_ref, bf16[320,3840]{1,0:T(8,128)(2,1)} %w_ref.3), custom_call_target="tpu_custom_call" | custom-call | flops 10000000 | bytes 1000 | tf_op jit(solution)/shard_map/pick/pallas_call | solution.py:292
  10.1 1.6 %collective-permute-done.6.refs_6_ = bf16[80,960]{1,0:T(8,128)(2,1)S(1)} collective-permute-done((bf16[80,960]{1,0:T(8,128)(2,1)S(1)}, bf16[80,960]{1,0:T(8,128)(2,1)S(1)}, u32[]{:S(2)}, u32[]{:S(2)}) %collective-permute-start.6) | collective-permute-done | bytes 153632 | tf_op jit(solution)/shard_map/ppermute | solution.py:340
  12.3 1.9 %collective-permute-start.10 = (bf16[4,32,1920]{2,1,0:T(8,128)(2,1)S(1)}, bf16[4,32,1920]{2,1,0:T(8,128)(2,1)S(1)}, u32[]{:S(2)}, u32[]{:S(2)}) collective-permute-start(bf16[4,32,1920]{2,1,0:T(8,128)(2,1)S(1)} %pack_across.1), channel_id=1, source_target_pairs={{0,8},{4,12},{8,0},{12,4},{1,9},{5,13},{9,1},{13,5},{2,10},{6,14},... | collective-permute-start | bytes 1474568 | tf_op jit(solution)/shard_map/ppermute | solution.py:280
  15.2 1.5 %collective-permute-start.1 = (bf16[80,960]{1,0:T(8,128)(2,1)S(1)}, bf16[80,960]{1,0:T(8,128)(2,1)S(1)}, u32[]{:S(2)}, u32[]{:S(2)}) collective-permute-start(bf16[80,960]{1,0:T(8,128)(2,1)S(1)} %collective-permute-done.refs_0_), channel_id=1, source_target_pairs={{0,16},{16,0},{1,17},{17,1},{2,18},{18,2},{3,19},{19,3},{4,20},{20... | collective-permute-start | bytes 460808 | tf_op jit(solution)/shard_map/ppermute | solution.py:280
  16.7 3.4 %collective-permute-start.8 = (bf16[80,960]{1,0:T(8,128)(2,1)S(1)}, bf16[80,960]{1,0:T(8,128)(2,1)S(1)}, u32[]{:S(2)}, u32[]{:S(2)}) collective-permute-start(bf16[80,960]{1,0:T(8,128)(2,1)S(1)} %collective-permute-done.6.refs_6_), channel_id=1, source_target_pairs={{0,1},{1,3},{3,2},{2,0},{4,5},{5,7},{7,6},{6,4},{8,9},{9,11},{11,1... | collective-permute-start | bytes 460808 | tf_op jit(solution)/shard_map/ppermute | solution.py:344
  20.6 1.8 %collective-permute-done.2.refs_2_ = bf16[80,960]{1,0:T(8,128)(2,1)S(1)} collective-permute-done((bf16[80,960]{1,0:T(8,128)(2,1)S(1)}, bf16[80,960]{1,0:T(8,128)(2,1)S(1)}, u32[]{:S(2)}, u32[]{:S(2)}) %collective-permute-start.2) | collective-permute-done | bytes 153632 | tf_op jit(solution)/shard_map/ppermute | solution.py:344
  22.4 2.8 %collective-permute-start.4 = (bf16[80,960]{1,0:T(8,128)(2,1)S(1)}, bf16[80,960]{1,0:T(8,128)(2,1)S(1)}, u32[]{:S(2)}, u32[]{:S(2)}) collective-permute-start(bf16[80,960]{1,0:T(8,128)(2,1)S(1)} %collective-permute-done.2.refs_2_), channel_id=1, source_target_pairs={{0,1},{1,3},{3,2},{2,0},{4,5},{5,7},{7,6},{6,4},{8,9},{9,11},{11,1... | collective-permute-start | bytes 460808 | tf_op jit(solution)/shard_map/ppermute | solution.py:347
  25.3 1.5 %collective-permute-start.3 = (bf16[80,960]{1,0:T(8,128)(2,1)S(1)}, bf16[80,960]{1,0:T(8,128)(2,1)S(1)}, u32[]{:S(2)}, u32[]{:S(2)}) collective-permute-start(bf16[80,960]{1,0:T(8,128)(2,1)S(1)} %collective-permute-done.2.refs_2_), channel_id=1, source_target_pairs={{0,16},{16,0},{1,17},{17,1},{2,18},{18,2},{3,19},{19,3},{4,20},{20... | collective-permute-start | bytes 460808 | tf_op jit(solution)/shard_map/ppermute | solution.py:280
  26.9 1.9 %collective-permute-start.12 = (bf16[80,960]{1,0:T(8,128)(2,1)S(1)}, bf16[80,960]{1,0:T(8,128)(2,1)S(1)}, u32[]{:S(2)}, u32[]{:S(2)}) collective-permute-start(bf16[80,960]{1,0:T(8,128)(2,1)S(1)} %collective-permute-done.8.refs_8_), channel_id=1, source_target_pairs={{0,1},{1,3},{3,2},{2,0},{4,5},{5,7},{7,6},{6,4},{8,9},{9,11},{11,1... | collective-permute-start | bytes 460808 | tf_op jit(solution)/shard_map/ppermute | solution.py:347
  28.8 1.5 %collective-permute-start.9 = (bf16[80,960]{1,0:T(8,128)(2,1)S(1)}, bf16[80,960]{1,0:T(8,128)(2,1)S(1)}, u32[]{:S(2)}, u32[]{:S(2)}) collective-permute-start(bf16[80,960]{1,0:T(8,128)(2,1)S(1)} %collective-permute-done.8.refs_8_), channel_id=1, source_target_pairs={{0,16},{16,0},{1,17},{17,1},{2,18},{18,2},{3,19},{19,3},{4,20},{20... | collective-permute-start | bytes 460808 | tf_op jit(solution)/shard_map/ppermute | solution.py:280
  31.5 2.3 %collective-permute-start.5 = (bf16[80,960]{1,0:T(8,128)(2,1)S(1)}, bf16[80,960]{1,0:T(8,128)(2,1)S(1)}, u32[]{:S(2)}, u32[]{:S(2)}) collective-permute-start(bf16[80,960]{1,0:T(8,128)(2,1)S(1)} %collective-permute-done.4.refs_4_), channel_id=1, source_target_pairs={{0,16},{16,0},{1,17},{17,1},{2,18},{18,2},{3,19},{19,3},{4,20},{20... | collective-permute-start | bytes 460808 | tf_op jit(solution)/shard_map/ppermute | solution.py:280
  34.9 2.5 %collective-permute-done.5.refs_5_ = bf16[80,960]{1,0:T(8,128)(2,1)S(1)} collective-permute-done((bf16[80,960]{1,0:T(8,128)(2,1)S(1)}, bf16[80,960]{1,0:T(8,128)(2,1)S(1)}, u32[]{:S(2)}, u32[]{:S(2)}) %collective-permute-start.5) | collective-permute-done | bytes 153632 | tf_op jit(solution)/shard_map/ppermute | solution.py:280
  38.2 1.9 %norm.1 = (bf16[512,1280]{1,0:T(8,128)(2,1)S(1)}, bf16[512,1280]{1,0:T(8,128)(2,1)S(1)}, f32[4,32,1280]{2,1,0:T(8,128)S(1)}, f32[4,32,128]{2,1,0:T(8,128)S(1)}) custom-call(s32[4]{0:T(128)S(1)} %copy-done.5, bf16[256,1280]{1,0:T(8,128)(2,1)S(1)} %copy-done.4, f32[1,1280]{1,0:T(1,128)S(1)} %reshape.12.gain_ref, f32[1,1280]{1,0:T(1,128)S(1)} %reshape.13.bias_ref, ...), custom_call_target="tpu_custom_call" | custom-call | flops 2000000000 | bytes 1000 | tf_op jit(solution)/shard_map/norm/pallas_call | solution.py:292
  41.5 4.2 %attend.1 = (bf16[4,32,320]{2,1,0:T(8,128)(2,1)S(1)}, bf16[4,32,320]{2,1,0:T(8,128)(2,1)S(1)}, bf16[2,4,32,320]{3,2,1,0:T(8,128)(2,1)S(1)}, bf16[512,960]{1,0:T(8,128)(2,1)S(1)}, bf16[1280,960]{1,0:T(8,128)(2,1)S(1)}) custom-call(s32[3]{0:T(128)S(1)} %pad_add_fusion.ids_ref, s32[4]{0:T(128)S(1)} %copy-done.3, ...), custom_call_target="tpu_custom_call", output_to_operand_aliasing={{4}: (2, {})} | custom-call | flops 10000000 | bytes 1000 | tf_op jit(solution)/shard_map/attend/pallas_call | solution.py:292
  45.7 1.6 %collective-permute-start.15 = (bf16[2,4,32,320]{3,2,1,0:T(8,128)(2,1)S(1)}, bf16[2,4,32,320]{3,2,1,0:T(8,128)(2,1)S(1)}, u32[]{:S(2)}, u32[]{:S(2)}) collective-permute-start(bf16[2,4,32,320]{3,2,1,0:T(8,128)(2,1)S(1)} %get-tuple-element.53), channel_id=1, source_target_pairs={{0,8},{4,12},{8,0},{12,4},{1,9},{5,13},{9,1},{13,5},{2,10},{6,14},... | collective-permute-start | bytes 491528 | tf_op jit(solution)/shard_map/ppermute | solution.py:280
  47.3 1.6 %back.1 = (bf16[4,32,1280]{2,1,0:T(8,128)(2,1)S(1)}, bf16[4,32,1280]{2,1,0:T(8,128)(2,1)S(1)}, bf16[272,1280]{1,0:T(8,128)(2,1)S(1)}, f32[2,1280]{1,0:T(2,128)S(1)}) custom-call(bf16[512,960]{1,0:T(8,128)(2,1)S(1)} %get-tuple-element.47.gqkv_ref, bf16[512,1280]{1,0:T(8,128)(2,1)S(1)} %get-tuple-element.48.unit_ref, ...), custom_call_target="tpu_custom_call" | custom-call | flops 10000000 | bytes 1000 | tf_op jit(solution)/shard_map/back/pallas_call | solution.py:292
  49.0 3.3 %collective-permute-done.15.far_ref.across_ref = bf16[2,4,32,320]{3,2,1,0:T(8,128)(2,1)S(1)} collective-permute-done((bf16[2,4,32,320]{3,2,1,0:T(8,128)(2,1)S(1)}, bf16[2,4,32,320]{3,2,1,0:T(8,128)(2,1)S(1)}, u32[]{:S(2)}, u32[]{:S(2)}) %collective-permute-start.15) | collective-permute-done | bytes 163872 | tf_op jit(solution)/shard_map/ppermute | solution.py:280
  52.4 1.6 %collective-permute-start.17 = (bf16[4,32,1280]{2,1,0:T(8,128)(2,1)S(1)}, bf16[4,32,1280]{2,1,0:T(8,128)(2,1)S(1)}, u32[]{:S(2)}, u32[]{:S(2)}) collective-permute-start(bf16[4,32,1280]{2,1,0:T(8,128)(2,1)S(1)} %get-tuple-element.62), channel_id=1, source_target_pairs={{0,8},{4,12},{8,0},{12,4},{1,9},{5,13},{9,1},{13,5},{2,10},{6,14},... | collective-permute-start | bytes 983048 | tf_op jit(solution)/shard_map/ppermute | solution.py:280
  55.5 2.0 %collective-permute-start.19 = (f32[2,1280]{1,0:T(2,128)S(1)}, f32[2,1280]{1,0:T(2,128)S(1)}, u32[]{:S(2)}, u32[]{:S(2)}) collective-permute-start(f32[2,1280]{1,0:T(2,128)S(1)} %get-tuple-element.63.refs_0_), channel_id=1, source_target_pairs={{0,2},{1,3},{2,0},{3,1},{4,6},{5,7},{6,4},{7,5},{8,10},{9,11},{10,... | collective-permute-start | bytes 30728 | tf_op jit(solution)/shard_map/ppermute | solution.py:280
  60.9 3.1 %collective-permute-done.21.refs_1_ = f32[2,1280]{1,0:T(2,128)S(1)} collective-permute-done((f32[2,1280]{1,0:T(2,128)S(1)}, f32[2,1280]{1,0:T(2,128)S(1)}, u32[]{:S(2)}, u32[]{:S(2)}) %collective-permute-start.21) | collective-permute-done | bytes 10272 | tf_op jit(solution)/shard_map/ppermute | solution.py:280
  64.0 1.6 %finish.1 = (bf16[4,32,1280]{2,1,0:T(8,128)(2,1)}, f32[2,1280]{1,0:T(2,128)}) custom-call(s32[3]{0:T(128)S(1)} %pad_add_fusion.ids_ref, s32[4]{0:T(128)S(1)} %copy-done.3, f32[4,32,1280]{2,1,0:T(8,128)S(1)} %get-tuple-element.57.unit_ref, f32[4,32,128]{2,1,0:T(8,128)S(1)} %get-tuple-element.58.inv_ref, f32[1,1280]{1,0:T(1,128)S(1)} %reshape.12.gain_ref, ...), custom_call_target="tpu_custom_call" | custom-call | flops 10000000 | bytes 1000 | tf_op jit(solution)/shard_map/finish/pallas_call | solution.py:292
  (52 shorter events, 11.7 us)
Async XLA Ops:
  2.6 9.1 %collective-permute-start.6 = (bf16[80,960]{1,0:T(8,128)(2,1)S(1)}, bf16[80,960]{1,0:T(8,128)(2,1)S(1)}, u32[]{:S(2)}, u32[]{:S(2)}) collective-permute-start(bf16[80,960]{1,0:T(8,128)(2,1)S(1)} %get-tuple-element.36.high_ref), channel_id=1, source_target_pairs={{0,1},{1,3},{3,2},{2,0},{4,5},{5,7},{7,6},{6,4},{8,9},{9,11},{11,1... | collective-permute-start | bytes 460808 | tf_op jit(solution)/shard_map/ppermute | solution.py:340
  5.7 29.1 %copy-start.6 = (f32[1280]{0:T(1024)S(1)}, f32[1280]{0:T(1024)}, u32[]{:S(2)}) copy-start(f32[1280]{0:T(1024)} %param.15) | copy-start | bytes 15364
  5.7 29.1 %copy-start.7 = (f32[1280]{0:T(1024)S(1)}, f32[1280]{0:T(1024)}, u32[]{:S(2)}) copy-start(f32[1280]{0:T(1024)} %param.16) | copy-start | bytes 15364
  5.7 8.7 %collective-permute-start = (bf16[80,960]{1,0:T(8,128)(2,1)S(1)}, bf16[80,960]{1,0:T(8,128)(2,1)S(1)}, u32[]{:S(2)}, u32[]{:S(2)}) collective-permute-start(bf16[80,960]{1,0:T(8,128)(2,1)S(1)} %get-tuple-element.35.low_ref), channel_id=1, source_target_pairs={{0,1},{1,3},{3,2},{2,0},{4,5},{5,7},{7,6},{6,4},{8,9},{9,11},{11,1... | collective-permute-start | bytes 460808 | tf_op jit(solution)/shard_map/ppermute | solution.py:340
  12.3 21.5 %collective-permute-start.10 = (bf16[4,32,1920]{2,1,0:T(8,128)(2,1)S(1)}, bf16[4,32,1920]{2,1,0:T(8,128)(2,1)S(1)}, u32[]{:S(2)}, u32[]{:S(2)}) collective-permute-start(bf16[4,32,1920]{2,1,0:T(8,128)(2,1)S(1)} %pack_across.1), channel_id=1, source_target_pairs={{0,8},{4,12},{8,0},{12,4},{1,9},{5,13},{9,1},{13,5},{2,10},{6,14},... | collective-permute-start | bytes 1474568 | tf_op jit(solution)/shard_map/ppermute | solution.py:280
  14.4 8.0 %collective-permute-start.2 = (bf16[80,960]{1,0:T(8,128)(2,1)S(1)}, bf16[80,960]{1,0:T(8,128)(2,1)S(1)}, u32[]{:S(2)}, u32[]{:S(2)}) collective-permute-start(bf16[80,960]{1,0:T(8,128)(2,1)S(1)} %collective-permute-done.refs_0_), channel_id=1, source_target_pairs={{0,1},{1,3},{3,2},{2,0},{4,5},{5,7},{7,6},{6,4},{8,9},{9,11},{11,1... | collective-permute-start | bytes 460808 | tf_op jit(solution)/shard_map/ppermute | solution.py:344
  15.2 7.2 %collective-permute-start.1 = (bf16[80,960]{1,0:T(8,128)(2,1)S(1)}, bf16[80,960]{1,0:T(8,128)(2,1)S(1)}, u32[]{:S(2)}, u32[]{:S(2)}) collective-permute-start(bf16[80,960]{1,0:T(8,128)(2,1)S(1)} %collective-permute-done.refs_0_), channel_id=1, source_target_pairs={{0,16},{16,0},{1,17},{17,1},{2,18},{18,2},{3,19},{19,3},{4,20},{20... | collective-permute-start | bytes 460808 | tf_op jit(solution)/shard_map/ppermute | solution.py:280
  16.7 10.1 %collective-permute-start.8 = (bf16[80,960]{1,0:T(8,128)(2,1)S(1)}, bf16[80,960]{1,0:T(8,128)(2,1)S(1)}, u32[]{:S(2)}, u32[]{:S(2)}) collective-permute-start(bf16[80,960]{1,0:T(8,128)(2,1)S(1)} %collective-permute-done.6.refs_6_), channel_id=1, source_target_pairs={{0,1},{1,3},{3,2},{2,0},{4,5},{5,7},{7,6},{6,4},{8,9},{9,11},{11,1... | collective-permute-start | bytes 460808 | tf_op jit(solution)/shard_map/ppermute | solution.py:344
  20.1 6.8 %collective-permute-start.7 = (bf16[80,960]{1,0:T(8,128)(2,1)S(1)}, bf16[80,960]{1,0:T(8,128)(2,1)S(1)}, u32[]{:S(2)}, u32[]{:S(2)}) collective-permute-start(bf16[80,960]{1,0:T(8,128)(2,1)S(1)} %collective-permute-done.6.refs_6_), channel_id=1, source_target_pairs={{0,16},{16,0},{1,17},{17,1},{2,18},{18,2},{3,19},{19,3},{4,20},{20... | collective-permute-start | bytes 460808 | tf_op jit(solution)/shard_map/ppermute | solution.py:280
  22.4 7.9 %collective-permute-start.4 = (bf16[80,960]{1,0:T(8,128)(2,1)S(1)}, bf16[80,960]{1,0:T(8,128)(2,1)S(1)}, u32[]{:S(2)}, u32[]{:S(2)}) collective-permute-start(bf16[80,960]{1,0:T(8,128)(2,1)S(1)} %collective-permute-done.2.refs_2_), channel_id=1, source_target_pairs={{0,1},{1,3},{3,2},{2,0},{4,5},{5,7},{7,6},{6,4},{8,9},{9,11},{11,1... | collective-permute-start | bytes 460808 | tf_op jit(solution)/shard_map/ppermute | solution.py:347
  25.3 6.2 %collective-permute-start.3 = (bf16[80,960]{1,0:T(8,128)(2,1)S(1)}, bf16[80,960]{1,0:T(8,128)(2,1)S(1)}, u32[]{:S(2)}, u32[]{:S(2)}) collective-permute-start(bf16[80,960]{1,0:T(8,128)(2,1)S(1)} %collective-permute-done.2.refs_2_), channel_id=1, source_target_pairs={{0,16},{16,0},{1,17},{17,1},{2,18},{18,2},{3,19},{19,3},{4,20},{20... | collective-permute-start | bytes 460808 | tf_op jit(solution)/shard_map/ppermute | solution.py:280
  26.9 7.9 %collective-permute-start.12 = (bf16[80,960]{1,0:T(8,128)(2,1)S(1)}, bf16[80,960]{1,0:T(8,128)(2,1)S(1)}, u32[]{:S(2)}, u32[]{:S(2)}) collective-permute-start(bf16[80,960]{1,0:T(8,128)(2,1)S(1)} %collective-permute-done.8.refs_8_), channel_id=1, source_target_pairs={{0,1},{1,3},{3,2},{2,0},{4,5},{5,7},{7,6},{6,4},{8,9},{9,11},{11,1... | collective-permute-start | bytes 460808 | tf_op jit(solution)/shard_map/ppermute | solution.py:347
  28.8 6.1 %collective-permute-start.9 = (bf16[80,960]{1,0:T(8,128)(2,1)S(1)}, bf16[80,960]{1,0:T(8,128)(2,1)S(1)}, u32[]{:S(2)}, u32[]{:S(2)}) collective-permute-start(bf16[80,960]{1,0:T(8,128)(2,1)S(1)} %collective-permute-done.8.refs_8_), channel_id=1, source_target_pairs={{0,16},{16,0},{1,17},{17,1},{2,18},{18,2},{3,19},{19,3},{4,20},{20... | collective-permute-start | bytes 460808 | tf_op jit(solution)/shard_map/ppermute | solution.py:280
  31.5 6.0 %collective-permute-start.5 = (bf16[80,960]{1,0:T(8,128)(2,1)S(1)}, bf16[80,960]{1,0:T(8,128)(2,1)S(1)}, u32[]{:S(2)}, u32[]{:S(2)}) collective-permute-start(bf16[80,960]{1,0:T(8,128)(2,1)S(1)} %collective-permute-done.4.refs_4_), channel_id=1, source_target_pairs={{0,16},{16,0},{1,17},{17,1},{2,18},{18,2},{3,19},{19,3},{4,20},{20... | collective-permute-start | bytes 460808 | tf_op jit(solution)/shard_map/ppermute | solution.py:280
  34.7 3.5 %collective-permute-start.11 = (bf16[4,32,3200]{2,1,0:T(8,128)(2,1)S(1)}, bf16[4,32,3200]{2,1,0:T(8,128)(2,1)S(1)}, u32[]{:S(2)}, u32[]{:S(2)}) collective-permute-start(bf16[4,32,3200]{2,1,0:T(8,128)(2,1)S(1)} %get-tuple-element.44), channel_id=1, source_target_pairs={{0,4},{4,0},{8,12},{12,8},{1,5},{5,1},{9,13},{13,9},{2,6},{6,2},{1... | collective-permute-start | bytes 2457608 | tf_op jit(solution)/shard_map/ppermute | solution.py:280
  34.8 6.6 %collective-permute-start.13 = (bf16[80,960]{1,0:T(8,128)(2,1)S(1)}, bf16[80,960]{1,0:T(8,128)(2,1)S(1)}, u32[]{:S(2)}, u32[]{:S(2)}) collective-permute-start(bf16[80,960]{1,0:T(8,128)(2,1)S(1)} %collective-permute-done.12.refs_0_), channel_id=1, source_target_pairs={{0,16},{16,0},{1,17},{17,1},{2,18},{18,2},{3,19},{19,3},{4,20},{20... | collective-permute-start | bytes 460808 | tf_op jit(solution)/shard_map/ppermute | solution.py:280
  45.7 6.6 %collective-permute-start.15 = (bf16[2,4,32,320]{3,2,1,0:T(8,128)(2,1)S(1)}, bf16[2,4,32,320]{3,2,1,0:T(8,128)(2,1)S(1)}, u32[]{:S(2)}, u32[]{:S(2)}) collective-permute-start(bf16[2,4,32,320]{3,2,1,0:T(8,128)(2,1)S(1)} %get-tuple-element.53), channel_id=1, source_target_pairs={{0,8},{4,12},{8,0},{12,4},{1,9},{5,13},{9,1},{13,5},{2,10},{6,14},... | collective-permute-start | bytes 491528 | tf_op jit(solution)/shard_map/ppermute | solution.py:280
  48.9 3.4 %collective-permute-start.14 = (bf16[272,1280]{1,0:T(8,128)(2,1)S(1)}, bf16[272,1280]{1,0:T(8,128)(2,1)S(1)}, u32[]{:S(2)}, u32[]{:S(2)}) collective-permute-start(bf16[272,1280]{1,0:T(8,128)(2,1)S(1)} %get-tuple-element.51), channel_id=1, source_target_pairs={{0,4},{4,0},{8,12},{12,8},{1,5},{5,1},{9,13},{13,9},{2,6},{6,2},{1... | collective-permute-start | bytes 2088968 | tf_op jit(solution)/shard_map/ppermute | solution.py:280
  52.4 11.6 %collective-permute-start.17 = (bf16[4,32,1280]{2,1,0:T(8,128)(2,1)S(1)}, bf16[4,32,1280]{2,1,0:T(8,128)(2,1)S(1)}, u32[]{:S(2)}, u32[]{:S(2)}) collective-permute-start(bf16[4,32,1280]{2,1,0:T(8,128)(2,1)S(1)} %get-tuple-element.62), channel_id=1, source_target_pairs={{0,8},{4,12},{8,0},{12,4},{1,9},{5,13},{9,1},{13,5},{2,10},{6,14},... | collective-permute-start | bytes 983048 | tf_op jit(solution)/shard_map/ppermute | solution.py:280
  54.0 3.5 %collective-permute-start.16 = (bf16[2,4,32,320]{3,2,1,0:T(8,128)(2,1)S(1)}, bf16[2,4,32,320]{3,2,1,0:T(8,128)(2,1)S(1)}, u32[]{:S(2)}, u32[]{:S(2)}) collective-permute-start(bf16[2,4,32,320]{3,2,1,0:T(8,128)(2,1)S(1)} %both.1), channel_id=1, source_target_pairs={{0,4},{4,0},{8,12},{12,8},{1,5},{5,1},{9,13},{13,9},{2,6},{6,2},{1... | collective-permute-start | bytes 491528 | tf_op jit(solution)/shard_map/ppermute | solution.py:280
  54.0 4.9 %collective-permute-start.18 = (f32[2,1280]{1,0:T(2,128)S(1)}, f32[2,1280]{1,0:T(2,128)S(1)}, u32[]{:S(2)}, u32[]{:S(2)}) collective-permute-start(f32[2,1280]{1,0:T(2,128)S(1)} %get-tuple-element.63.refs_0_), channel_id=1, source_target_pairs={{0,1},{1,0},{2,3},{3,2},{4,5},{5,4},{6,7},{7,6},{8,9},{9,8},{10,11... | collective-permute-start | bytes 30728 | tf_op jit(solution)/shard_map/ppermute | solution.py:280
  54.8 5.5 %collective-permute-start.20 = (f32[2,1280]{1,0:T(2,128)S(1)}, f32[2,1280]{1,0:T(2,128)S(1)}, u32[]{:S(2)}, u32[]{:S(2)}) collective-permute-start(f32[2,1280]{1,0:T(2,128)S(1)} %get-tuple-element.63.refs_0_), channel_id=1, source_target_pairs={{0,3},{1,2},{2,1},{3,0},{4,7},{5,6},{6,5},{7,4},{8,11},{9,10},{10,... | collective-permute-start | bytes 30728 | tf_op jit(solution)/shard_map/ppermute | solution.py:280
  55.5 4.8 %collective-permute-start.19 = (f32[2,1280]{1,0:T(2,128)S(1)}, f32[2,1280]{1,0:T(2,128)S(1)}, u32[]{:S(2)}, u32[]{:S(2)}) collective-permute-start(f32[2,1280]{1,0:T(2,128)S(1)} %get-tuple-element.63.refs_0_), channel_id=1, source_target_pairs={{0,2},{1,3},{2,0},{3,1},{4,6},{5,7},{6,4},{7,5},{8,10},{9,11},{10,... | collective-permute-start | bytes 30728 | tf_op jit(solution)/shard_map/ppermute | solution.py:280
  60.3 3.7 %collective-permute-start.21 = (f32[2,1280]{1,0:T(2,128)S(1)}, f32[2,1280]{1,0:T(2,128)S(1)}, u32[]{:S(2)}, u32[]{:S(2)}) collective-permute-start(f32[2,1280]{1,0:T(2,128)S(1)} %add.5.refs_0_), channel_id=1, source_target_pairs={{0,8},{4,12},{8,0},{12,4},{1,9},{5,13},{9,1},{13,5},{2,10},{6,14},... | collective-permute-start | bytes 30728 | tf_op jit(solution)/shard_map/ppermute | solution.py:280
  (6 other events, 35.4 us)

commit v10 on v9

--- a/solution.py
+++ b/solution.py
@@ -199,7 +199,6 @@
 def back_kernel(gqkv_ref, unit_ref, weights, stay_ref, pass_ref, cross_ref, sums_ref):
     slots, rows, width = stay_ref.shape
     dates = gqkv_ref.shape[0] // slots
-    tail = 2 * slots * rows
     step = 256
     for n in range(width // step):
         lanes = slice(n * step, (n + 1) * step)
@@ -216,19 +215,13 @@
         gain_sum = jnp.sum(partial * unit_ref[:, lanes].astype(F32), axis=0, keepdims=True)
         sums = jnp.concatenate([gain_sum, jnp.sum(partial, axis=0, keepdims=True)], axis=0)
         sums_ref[:, lanes] = sums
-        high = sums.astype(BF16)
-        rest = (sums - high.astype(F32)).astype(BF16)
-        fill = jnp.zeros((cross_ref.shape[0] - tail - 4, step), BF16)
-        cross_ref[tail:, lanes] = jnp.concatenate([high, rest, fill], axis=0)
-
-
-def merge_kernel(pass_ref, close_ref, sums_ref, out_ref, total_ref):
+
+
+def merge_kernel(pass_ref, close_ref, out_ref):
     slots, rows, width = out_ref.shape
     for p in range(slots):
         at = (slots + p) * rows
         out_ref[p] = (pass_ref[p].astype(F32) + close_ref[at : at + rows].astype(F32)).astype(BF16)
-    sums = close_ref[2 * slots * rows :].astype(F32)
-    total_ref[...] = sums_ref[...] + sums[0:2] + sums[2:4]
 
 
 def both_kernel(close_ref, far_ref, both_ref):
@@ -434,13 +427,16 @@
     stay, passing, cross, sums = call(
         back_kernel,
         "back",
-        (block, block, pltpu.VMEM((2 * slots * rows + 16, width), BF16), pairs),
+        (block, block, pltpu.VMEM((2 * slots * rows, width), BF16), pairs),
         [VMEM] * 3,
         (near(gqkv), near(unit), near(weights)),
         12,
     )
 
     close = swapped(cross, "date", 1)
+    tiles = [sums]
+    if owners == 4:
+        tiles += [swapped(sums, "tile", s) for s in range(1, owners)]
     both = call(
         both_kernel,
         "both",
@@ -448,17 +444,10 @@
         [VMEM] * 2,
         (near(close_context), near(far_context)),
         2,
-        microseconds=10,
-    )
-    close = after(close, both)
-    chip, total = call(
-        merge_kernel,
-        "merge",
-        (block, pairs),
-        [VMEM] * 3,
-        (near(passing), near(close), near(sums)),
-        6,
-    )
+        microseconds=6.5,
+    )
+    close = after(close, both, *tiles[1:])
+    chip = call(merge_kernel, "merge", block, [VMEM] * 2, (near(passing), near(close)), 6)
     far = swapped(chip, "date", 2)
     both = swapped(both, "date", 1)
     home, attended = call(
@@ -471,19 +460,11 @@
         scratch=(pltpu.VMEM((groups, slots, rows, part), BF16),),
     )
     if owners == 4:
-        tiles = [swapped(total, "tile", s) for s in range(1, owners)]
-        tiles[0] = after(tiles[0], home)
-        total = call(
-            add_kernel,
-            "add",
-            pairs,
-            [VMEM] * owners,
-            [near(total)] + [near(tile) for tile in tiles],
-            2,
-        )
+        tiles = [near(tile) for tile in tiles]
+        total = call(add_kernel, "add", pairs, [VMEM] * owners, tiles, 2)
     else:
-        total = lax.psum(total, "tile")
-    far_total = swapped(total, "date", 2)
+        total = lax.psum(sums, "tile")
+    totals = [total] + [swapped(total, "date", s) for s in range(1, groups)]
     grad_tokens, grad_norm = call(
         finish_kernel,
         "finish",
@@ -491,8 +472,8 @@
             jax.ShapeDtypeStruct((slots, rows, width), BF16),
             jax.ShapeDtypeStruct((2, width), F32),
         ),
-        [SMEM] * 2 + [VMEM] * 7,
-        (ids, live, near(own_unit), near(own_inv), gain2, near(home), near(far), total, far_total),
+        [SMEM] * 2 + [VMEM] * (5 + groups),
+        (ids, live, near(own_unit), near(own_inv), gain2, near(home), near(far), *totals),
         6,
     )
     return attended, grad_tokens, grad_norm

time: 65.8 us -> 66.4 us (level)
  starting transfers between devices: 31.3 us -> 32.8 us
  waiting for transfers between devices: 16.5 us -> 15.6 us
    ppermute x16 -> x18, starting transfers between devices: 16.7 us -> 18.2 us  [swapped(): lax.ppermute(array, axis, [(i, i ^ bits) for i in range(lax.axis_size(axi...]
    ppermute x16 -> x18, waiting for transfers between devices: 13 us -> 12.1 us  [swapped(): lax.ppermute(array, axis, [(i, i ^ bits) for i in range(lax.axis_size(axi...]
  transfers between devices with their start and end apart: 22 -> 24, of which waited for: 10 -> 11; matrix products, arithmetic and copies ran while one was open for 0% -> 0% of each run, Pallas kernels for 14% -> 14%
where the time goes in v10:
time: 66.4 us; the launch traced here: 66.3 us
  starting transfers between devices  32.8 us (49%)
  Pallas kernels  16.8 us (25%)
  waiting for transfers between devices  15.6 us (23%)
  between operations  0.86 us (1%)
    ppermute x18, starting transfers between devices, swapped(): lax.ppermute(array, axis, [(i, i ^ bits) for i in range(lax.axis_size(axi...  18.2 us
    pallas_call x13, Pallas kernels, call(): pl.pallas_call(kernel, out_shape=out_shape, in_specs=in_specs, out_specs=...  16.8 us
    ppermute x18, waiting for transfers between devices, swapped(): lax.ppermute(array, axis, [(i, i ^ bits) for i in range(lax.axis_size(axi...  12.1 us
    ppermute x2, starting transfers between devices, local(): first = lax.ppermute(held, 'tile', ring)  5.67 us
    ppermute x2, starting transfers between devices, local(): third = lax.ppermute(second, 'tile', ring)  4.72 us
    ppermute x2, starting transfers between devices, local(): second = lax.ppermute(first, 'tile', ring)  4.22 us
    ppermute x2, waiting for transfers between devices, local(): second = lax.ppermute(first, 'tile', ring)  1.79 us
    ppermute x2, waiting for transfers between devices, local(): first = lax.ppermute(held, 'tile', ring)  1.74 us
  transfers between devices with their start and end apart: 24, of which 11 were waited for; matrix products, arithmetic and copies ran while one was open for 0% of the time, Pallas kernels for 14%

profile of v10, /device:TPU:0, one launch (start us, length us, event | category | flops | bytes accessed | tf_op | source)
XLA Modules:
  0.0 66.3 jit_solution(15862771174366937753)
XLA Ops:
  0.7 1.9 %pick.2 = (bf16[80,960]{1,0:T(8,128)(2,1)S(1)}, bf16[80,960]{1,0:T(8,128)(2,1)S(1)}) custom-call(s32[3]{0:T(128)S(1)} %pad_add_fusion.ids_ref, bf16[320,3840]{1,0:T(8,128)(2,1)} %w_ref.3), custom_call_target="tpu_custom_call" | custom-call | flops 10000000 | bytes 1000 | tf_op jit(solution)/shard_map/pick/pallas_call | solution.py:285
  2.6 3.1 %collective-permute-start.6 = (bf16[80,960]{1,0:T(8,128)(2,1)S(1)}, bf16[80,960]{1,0:T(8,128)(2,1)S(1)}, u32[]{:S(2)}, u32[]{:S(2)}) collective-permute-start(bf16[80,960]{1,0:T(8,128)(2,1)S(1)} %get-tuple-element.33.high_ref), channel_id=1, source_target_pairs={{0,1},{1,3},{3,2},{2,0},{4,5},{5,7},{7,6},{6,4},{8,9},{9,11},{11,1... | collective-permute-start | bytes 460808 | tf_op jit(solution)/shard_map/ppermute | solution.py:333
  5.7 2.6 %collective-permute-start = (bf16[80,960]{1,0:T(8,128)(2,1)S(1)}, bf16[80,960]{1,0:T(8,128)(2,1)S(1)}, u32[]{:S(2)}, u32[]{:S(2)}) collective-permute-start(bf16[80,960]{1,0:T(8,128)(2,1)S(1)} %get-tuple-element.32.low_ref), channel_id=1, source_target_pairs={{0,1},{1,3},{3,2},{2,0},{4,5},{5,7},{7,6},{6,4},{8,9},{9,11},{11,1... | collective-permute-start | bytes 460808 | tf_op jit(solution)/shard_map/ppermute | solution.py:333
  8.3 1.9 %pick.3.rest_ref = bf16[160,960]{1,0:T(8,128)(2,1)S(1)} custom-call(s32[3]{0:T(128)S(1)} %pad_add_fusion.ids_ref, bf16[320,3840]{1,0:T(8,128)(2,1)} %w_ref.3), custom_call_target="tpu_custom_call" | custom-call | flops 10000000 | bytes 1000 | tf_op jit(solution)/shard_map/pick/pallas_call | solution.py:285
  10.1 1.6 %collective-permute-done.6.refs_6_ = bf16[80,960]{1,0:T(8,128)(2,1)S(1)} collective-permute-done((bf16[80,960]{1,0:T(8,128)(2,1)S(1)}, bf16[80,960]{1,0:T(8,128)(2,1)S(1)}, u32[]{:S(2)}, u32[]{:S(2)}) %collective-permute-start.6) | collective-permute-done | bytes 153632 | tf_op jit(solution)/shard_map/ppermute | solution.py:333
  12.3 1.9 %collective-permute-start.10 = (bf16[4,32,1920]{2,1,0:T(8,128)(2,1)S(1)}, bf16[4,32,1920]{2,1,0:T(8,128)(2,1)S(1)}, u32[]{:S(2)}, u32[]{:S(2)}) collective-permute-start(bf16[4,32,1920]{2,1,0:T(8,128)(2,1)S(1)} %pack_across.1), channel_id=1, source_target_pairs={{0,8},{4,12},{8,0},{12,4},{1,9},{5,13},{9,1},{13,5},{2,10},{6,14},... | collective-permute-start | bytes 1474568 | tf_op jit(solution)/shard_map/ppermute | solution.py:273
  15.2 1.5 %collective-permute-start.1 = (bf16[80,960]{1,0:T(8,128)(2,1)S(1)}, bf16[80,960]{1,0:T(8,128)(2,1)S(1)}, u32[]{:S(2)}, u32[]{:S(2)}) collective-permute-start(bf16[80,960]{1,0:T(8,128)(2,1)S(1)} %collective-permute-done.refs_0_), channel_id=1, source_target_pairs={{0,16},{16,0},{1,17},{17,1},{2,18},{18,2},{3,19},{19,3},{4,20},{20... | collective-permute-start | bytes 460808 | tf_op jit(solution)/shard_map/ppermute | solution.py:273
  16.7 3.4 %collective-permute-start.8 = (bf16[80,960]{1,0:T(8,128)(2,1)S(1)}, bf16[80,960]{1,0:T(8,128)(2,1)S(1)}, u32[]{:S(2)}, u32[]{:S(2)}) collective-permute-start(bf16[80,960]{1,0:T(8,128)(2,1)S(1)} %collective-permute-done.6.refs_6_), channel_id=1, source_target_pairs={{0,1},{1,3},{3,2},{2,0},{4,5},{5,7},{7,6},{6,4},{8,9},{9,11},{11,1... | collective-permute-start | bytes 460808 | tf_op jit(solution)/shard_map/ppermute | solution.py:337
  20.6 1.8 %collective-permute-done.2.refs_2_ = bf16[80,960]{1,0:T(8,128)(2,1)S(1)} collective-permute-done((bf16[80,960]{1,0:T(8,128)(2,1)S(1)}, bf16[80,960]{1,0:T(8,128)(2,1)S(1)}, u32[]{:S(2)}, u32[]{:S(2)}) %collective-permute-start.2) | collective-permute-done | bytes 153632 | tf_op jit(solution)/shard_map/ppermute | solution.py:337
  22.4 2.8 %collective-permute-start.4 = (bf16[80,960]{1,0:T(8,128)(2,1)S(1)}, bf16[80,960]{1,0:T(8,128)(2,1)S(1)}, u32[]{:S(2)}, u32[]{:S(2)}) collective-permute-start(bf16[80,960]{1,0:T(8,128)(2,1)S(1)} %collective-permute-done.2.refs_2_), channel_id=1, source_target_pairs={{0,1},{1,3},{3,2},{2,0},{4,5},{5,7},{7,6},{6,4},{8,9},{9,11},{11,1... | collective-permute-start | bytes 460808 | tf_op jit(solution)/shard_map/ppermute | solution.py:340
  25.3 1.5 %collective-permute-start.3 = (bf16[80,960]{1,0:T(8,128)(2,1)S(1)}, bf16[80,960]{1,0:T(8,128)(2,1)S(1)}, u32[]{:S(2)}, u32[]{:S(2)}) collective-permute-start(bf16[80,960]{1,0:T(8,128)(2,1)S(1)} %collective-permute-done.2.refs_2_), channel_id=1, source_target_pairs={{0,16},{16,0},{1,17},{17,1},{2,18},{18,2},{3,19},{19,3},{4,20},{20... | collective-permute-start | bytes 460808 | tf_op jit(solution)/shard_map/ppermute | solution.py:273
  26.9 1.9 %collective-permute-start.12 = (bf16[80,960]{1,0:T(8,128)(2,1)S(1)}, bf16[80,960]{1,0:T(8,128)(2,1)S(1)}, u32[]{:S(2)}, u32[]{:S(2)}) collective-permute-start(bf16[80,960]{1,0:T(8,128)(2,1)S(1)} %collective-permute-done.8.refs_8_), channel_id=1, source_target_pairs={{0,1},{1,3},{3,2},{2,0},{4,5},{5,7},{7,6},{6,4},{8,9},{9,11},{11,1... | collective-permute-start | bytes 460808 | tf_op jit(solution)/shard_map/ppermute | solution.py:340
  31.5 2.3 %collective-permute-start.5 = (bf16[80,960]{1,0:T(8,128)(2,1)S(1)}, bf16[80,960]{1,0:T(8,128)(2,1)S(1)}, u32[]{:S(2)}, u32[]{:S(2)}) collective-permute-start(bf16[80,960]{1,0:T(8,128)(2,1)S(1)} %collective-permute-done.4.refs_4_), channel_id=1, source_target_pairs={{0,16},{16,0},{1,17},{17,1},{2,18},{18,2},{3,19},{19,3},{4,20},{20... | collective-permute-start | bytes 460808 | tf_op jit(solution)/shard_map/ppermute | solution.py:273
  34.9 2.5 %collective-permute-done.5.refs_5_ = bf16[80,960]{1,0:T(8,128)(2,1)S(1)} collective-permute-done((bf16[80,960]{1,0:T(8,128)(2,1)S(1)}, bf16[80,960]{1,0:T(8,128)(2,1)S(1)}, u32[]{:S(2)}, u32[]{:S(2)}) %collective-permute-start.5) | collective-permute-done | bytes 153632 | tf_op jit(solution)/shard_map/ppermute | solution.py:273
  38.2 1.9 %norm.1 = (bf16[512,1280]{1,0:T(8,128)(2,1)S(1)}, bf16[512,1280]{1,0:T(8,128)(2,1)S(1)}, f32[4,32,1280]{2,1,0:T(8,128)S(1)}, f32[4,32,128]{2,1,0:T(8,128)S(1)}) custom-call(s32[4]{0:T(128)S(1)} %copy-done.5, bf16[256,1280]{1,0:T(8,128)(2,1)S(1)} %copy-done.4, f32[1,1280]{1,0:T(1,128)S(1)} %reshape.12.gain_ref, f32[1,1280]{1,0:T(1,128)S(1)} %reshape.13.bias_ref, ...), custom_call_target="tpu_custom_call" | custom-call | flops 2000000000 | bytes 1000 | tf_op jit(solution)/shard_map/norm/pallas_call | solution.py:285
  41.5 4.2 %attend.1 = (bf16[4,32,320]{2,1,0:T(8,128)(2,1)S(1)}, bf16[4,32,320]{2,1,0:T(8,128)(2,1)S(1)}, bf16[2,4,32,320]{3,2,1,0:T(8,128)(2,1)S(1)}, bf16[512,960]{1,0:T(8,128)(2,1)S(1)}, bf16[1280,960]{1,0:T(8,128)(2,1)S(1)}) custom-call(s32[3]{0:T(128)S(1)} %pad_add_fusion.ids_ref, s32[4]{0:T(128)S(1)} %copy-done.3, ...), custom_call_target="tpu_custom_call", output_to_operand_aliasing={{4}: (2, {})} | custom-call | flops 10000000 | bytes 1000 | tf_op jit(solution)/shard_map/attend/pallas_call | solution.py:285
  45.7 1.6 %collective-permute-start.15 = (bf16[2,4,32,320]{3,2,1,0:T(8,128)(2,1)S(1)}, bf16[2,4,32,320]{3,2,1,0:T(8,128)(2,1)S(1)}, u32[]{:S(2)}, u32[]{:S(2)}) collective-permute-start(bf16[2,4,32,320]{3,2,1,0:T(8,128)(2,1)S(1)} %get-tuple-element.50), channel_id=1, source_target_pairs={{0,8},{4,12},{8,0},{12,4},{1,9},{5,13},{9,1},{13,5},{2,10},{6,14},... | collective-permute-start | bytes 491528 | tf_op jit(solution)/shard_map/ppermute | solution.py:273
  47.3 1.6 %back.1 = (bf16[4,32,1280]{2,1,0:T(8,128)(2,1)S(1)}, bf16[4,32,1280]{2,1,0:T(8,128)(2,1)S(1)}, bf16[256,1280]{1,0:T(8,128)(2,1)S(1)}, f32[2,1280]{1,0:T(2,128)S(1)}) custom-call(bf16[512,960]{1,0:T(8,128)(2,1)S(1)} %get-tuple-element.44.gqkv_ref, bf16[512,1280]{1,0:T(8,128)(2,1)S(1)} %get-tuple-element.45.unit_ref, ...), custom_call_target="tpu_custom_call" | custom-call | flops 10000000 | bytes 1000 | tf_op jit(solution)/shard_map/back/pallas_call | solution.py:285
  49.6 1.8 %collective-permute-start.17 = (f32[2,1280]{1,0:T(2,128)S(1)}, f32[2,1280]{1,0:T(2,128)S(1)}, u32[]{:S(2)}, u32[]{:S(2)}) collective-permute-start(f32[2,1280]{1,0:T(2,128)S(1)} %get-tuple-element.51.refs_0_), channel_id=1, source_target_pairs={{0,2},{1,3},{2,0},{3,1},{4,6},{5,7},{6,4},{7,5},{8,10},{9,11},{10,... | collective-permute-start | bytes 30728 | tf_op jit(solution)/shard_map/ppermute | solution.py:273
  51.3 2.1 %collective-permute-start.16 = (f32[2,1280]{1,0:T(2,128)S(1)}, f32[2,1280]{1,0:T(2,128)S(1)}, u32[]{:S(2)}, u32[]{:S(2)}) collective-permute-start(f32[2,1280]{1,0:T(2,128)S(1)} %get-tuple-element.51.refs_0_), channel_id=1, source_target_pairs={{0,1},{1,0},{2,3},{3,2},{4,5},{5,4},{6,7},{7,6},{8,9},{9,8},{10,11... | collective-permute-start | bytes 30728 | tf_op jit(solution)/shard_map/ppermute | solution.py:273
  55.8 1.6 %collective-permute-start.23 = (f32[2,1280]{1,0:T(2,128)S(1)}, f32[2,1280]{1,0:T(2,128)S(1)}, u32[]{:S(2)}, u32[]{:S(2)}) collective-permute-start(f32[2,1280]{1,0:T(2,128)S(1)} %add.5.refs_0_), channel_id=1, source_target_pairs={{0,12},{4,8},{8,4},{12,0},{1,13},{5,9},{9,5},{13,1},{2,14},{6,10},... | collective-permute-start | bytes 30728 | tf_op jit(solution)/shard_map/ppermute | solution.py:273
  59.4 3.4 %collective-permute-done.23.refs_3_ = f32[2,1280]{1,0:T(2,128)S(1)} collective-permute-done((f32[2,1280]{1,0:T(2,128)S(1)}, f32[2,1280]{1,0:T(2,128)S(1)}, u32[]{:S(2)}, u32[]{:S(2)}) %collective-permute-start.23) | collective-permute-done | bytes 10272 | tf_op jit(solution)/shard_map/ppermute | solution.py:273
  62.8 1.9 %collective-permute-done.22.refs_2_ = f32[2,1280]{1,0:T(2,128)S(1)} collective-permute-done((f32[2,1280]{1,0:T(2,128)S(1)}, f32[2,1280]{1,0:T(2,128)S(1)}, u32[]{:S(2)}, u32[]{:S(2)}) %collective-permute-start.22) | collective-permute-done | bytes 10272 | tf_op jit(solution)/shard_map/ppermute | solution.py:273
  64.7 1.6 %finish.1 = (bf16[4,32,1280]{2,1,0:T(8,128)(2,1)}, f32[2,1280]{1,0:T(2,128)}) custom-call(s32[3]{0:T(128)S(1)} %pad_add_fusion.ids_ref, s32[4]{0:T(128)S(1)} %copy-done.3, f32[4,32,1280]{2,1,0:T(8,128)S(1)} %get-tuple-element.55.unit_ref, f32[4,32,128]{2,1,0:T(8,128)S(1)} %get-tuple-element.56.inv_ref, f32[1,1280]{1,0:T(1,128)S(1)} %reshape.12.gain_ref, ...), custom_call_target="tpu_custom_call" | custom-call | flops 10000000 | bytes 1000 | tf_op jit(solution)/shard_map/finish/pallas_call | solution.py:285
  (56 shorter events, 13.1 us)
Async XLA Ops:
  2.6 9.1 %collective-permute-start.6 = (bf16[80,960]{1,0:T(8,128)(2,1)S(1)}, bf16[80,960]{1,0:T(8,128)(2,1)S(1)}, u32[]{:S(2)}, u32[]{:S(2)}) collective-permute-start(bf16[80,960]{1,0:T(8,128)(2,1)S(1)} %get-tuple-element.33.high_ref), channel_id=1, source_target_pairs={{0,1},{1,3},{3,2},{2,0},{4,5},{5,7},{7,6},{6,4},{8,9},{9,11},{11,1... | collective-permute-start | bytes 460808 | tf_op jit(solution)/shard_map/ppermute | solution.py:333
  5.7 8.7 %collective-permute-start = (bf16[80,960]{1,0:T(8,128)(2,1)S(1)}, bf16[80,960]{1,0:T(8,128)(2,1)S(1)}, u32[]{:S(2)}, u32[]{:S(2)}) collective-permute-start(bf16[80,960]{1,0:T(8,128)(2,1)S(1)} %get-tuple-element.32.low_ref), channel_id=1, source_target_pairs={{0,1},{1,3},{3,2},{2,0},{4,5},{5,7},{7,6},{6,4},{8,9},{9,11},{11,1... | collective-permute-start | bytes 460808 | tf_op jit(solution)/shard_map/ppermute | solution.py:333
  12.3 21.5 %collective-permute-start.10 = (bf16[4,32,1920]{2,1,0:T(8,128)(2,1)S(1)}, bf16[4,32,1920]{2,1,0:T(8,128)(2,1)S(1)}, u32[]{:S(2)}, u32[]{:S(2)}) collective-permute-start(bf16[4,32,1920]{2,1,0:T(8,128)(2,1)S(1)} %pack_across.1), channel_id=1, source_target_pairs={{0,8},{4,12},{8,0},{12,4},{1,9},{5,13},{9,1},{13,5},{2,10},{6,14},... | collective-permute-start | bytes 1474568 | tf_op jit(solution)/shard_map/ppermute | solution.py:273
  14.4 8.0 %collective-permute-start.2 = (bf16[80,960]{1,0:T(8,128)(2,1)S(1)}, bf16[80,960]{1,0:T(8,128)(2,1)S(1)}, u32[]{:S(2)}, u32[]{:S(2)}) collective-permute-start(bf16[80,960]{1,0:T(8,128)(2,1)S(1)} %collective-permute-done.refs_0_), channel_id=1, source_target_pairs={{0,1},{1,3},{3,2},{2,0},{4,5},{5,7},{7,6},{6,4},{8,9},{9,11},{11,1... | collective-permute-start | bytes 460808 | tf_op jit(solution)/shard_map/ppermute | solution.py:337
  15.2 7.2 %collective-permute-start.1 = (bf16[80,960]{1,0:T(8,128)(2,1)S(1)}, bf16[80,960]{1,0:T(8,128)(2,1)S(1)}, u32[]{:S(2)}, u32[]{:S(2)}) collective-permute-start(bf16[80,960]{1,0:T(8,128)(2,1)S(1)} %collective-permute-done.refs_0_), channel_id=1, source_target_pairs={{0,16},{16,0},{1,17},{17,1},{2,18},{18,2},{3,19},{19,3},{4,20},{20... | collective-permute-start | bytes 460808 | tf_op jit(solution)/shard_map/ppermute | solution.py:273
  16.7 10.1 %collective-permute-start.8 = (bf16[80,960]{1,0:T(8,128)(2,1)S(1)}, bf16[80,960]{1,0:T(8,128)(2,1)S(1)}, u32[]{:S(2)}, u32[]{:S(2)}) collective-permute-start(bf16[80,960]{1,0:T(8,128)(2,1)S(1)} %collective-permute-done.6.refs_6_), channel_id=1, source_target_pairs={{0,1},{1,3},{3,2},{2,0},{4,5},{5,7},{7,6},{6,4},{8,9},{9,11},{11,1... | collective-permute-start | bytes 460808 | tf_op jit(solution)/shard_map/ppermute | solution.py:337
  20.1 6.8 %collective-permute-start.7 = (bf16[80,960]{1,0:T(8,128)(2,1)S(1)}, bf16[80,960]{1,0:T(8,128)(2,1)S(1)}, u32[]{:S(2)}, u32[]{:S(2)}) collective-permute-start(bf16[80,960]{1,0:T(8,128)(2,1)S(1)} %collective-permute-done.6.refs_6_), channel_id=1, source_target_pairs={{0,16},{16,0},{1,17},{17,1},{2,18},{18,2},{3,19},{19,3},{4,20},{20... | collective-permute-start | bytes 460808 | tf_op jit(solution)/shard_map/ppermute | solution.py:273
  22.4 7.9 %collective-permute-start.4 = (bf16[80,960]{1,0:T(8,128)(2,1)S(1)}, bf16[80,960]{1,0:T(8,128)(2,1)S(1)}, u32[]{:S(2)}, u32[]{:S(2)}) collective-permute-start(bf16[80,960]{1,0:T(8,128)(2,1)S(1)} %collective-permute-done.2.refs_2_), channel_id=1, source_target_pairs={{0,1},{1,3},{3,2},{2,0},{4,5},{5,7},{7,6},{6,4},{8,9},{9,11},{11,1... | collective-permute-start | bytes 460808 | tf_op jit(solution)/shard_map/ppermute | solution.py:340
  25.3 6.2 %collective-permute-start.3 = (bf16[80,960]{1,0:T(8,128)(2,1)S(1)}, bf16[80,960]{1,0:T(8,128)(2,1)S(1)}, u32[]{:S(2)}, u32[]{:S(2)}) collective-permute-start(bf16[80,960]{1,0:T(8,128)(2,1)S(1)} %collective-permute-done.2.refs_2_), channel_id=1, source_target_pairs={{0,16},{16,0},{1,17},{17,1},{2,18},{18,2},{3,19},{19,3},{4,20},{20... | collective-permute-start | bytes 460808 | tf_op jit(solution)/shard_map/ppermute | solution.py:273
  26.9 7.9 %collective-permute-start.12 = (bf16[80,960]{1,0:T(8,128)(2,1)S(1)}, bf16[80,960]{1,0:T(8,128)(2,1)S(1)}, u32[]{:S(2)}, u32[]{:S(2)}) collective-permute-start(bf16[80,960]{1,0:T(8,128)(2,1)S(1)} %collective-permute-done.8.refs_8_), channel_id=1, source_target_pairs={{0,1},{1,3},{3,2},{2,0},{4,5},{5,7},{7,6},{6,4},{8,9},{9,11},{11,1... | collective-permute-start | bytes 460808 | tf_op jit(solution)/shard_map/ppermute | solution.py:340
  28.8 6.1 %collective-permute-start.9 = (bf16[80,960]{1,0:T(8,128)(2,1)S(1)}, bf16[80,960]{1,0:T(8,128)(2,1)S(1)}, u32[]{:S(2)}, u32[]{:S(2)}) collective-permute-start(bf16[80,960]{1,0:T(8,128)(2,1)S(1)} %collective-permute-done.8.refs_8_), channel_id=1, source_target_pairs={{0,16},{16,0},{1,17},{17,1},{2,18},{18,2},{3,19},{19,3},{4,20},{20... | collective-permute-start | bytes 460808 | tf_op jit(solution)/shard_map/ppermute | solution.py:273
  31.5 6.0 %collective-permute-start.5 = (bf16[80,960]{1,0:T(8,128)(2,1)S(1)}, bf16[80,960]{1,0:T(8,128)(2,1)S(1)}, u32[]{:S(2)}, u32[]{:S(2)}) collective-permute-start(bf16[80,960]{1,0:T(8,128)(2,1)S(1)} %collective-permute-done.4.refs_4_), channel_id=1, source_target_pairs={{0,16},{16,0},{1,17},{17,1},{2,18},{18,2},{3,19},{19,3},{4,20},{20... | collective-permute-start | bytes 460808 | tf_op jit(solution)/shard_map/ppermute | solution.py:273
  34.7 3.5 %collective-permute-start.11 = (bf16[4,32,3200]{2,1,0:T(8,128)(2,1)S(1)}, bf16[4,32,3200]{2,1,0:T(8,128)(2,1)S(1)}, u32[]{:S(2)}, u32[]{:S(2)}) collective-permute-start(bf16[4,32,3200]{2,1,0:T(8,128)(2,1)S(1)} %get-tuple-element.41), channel_id=1, source_target_pairs={{0,4},{4,0},{8,12},{12,8},{1,5},{5,1},{9,13},{13,9},{2,6},{6,2},{1... | collective-permute-start | bytes 2457608 | tf_op jit(solution)/shard_map/ppermute | solution.py:273
  34.8 6.6 %collective-permute-start.13 = (bf16[80,960]{1,0:T(8,128)(2,1)S(1)}, bf16[80,960]{1,0:T(8,128)(2,1)S(1)}, u32[]{:S(2)}, u32[]{:S(2)}) collective-permute-start(bf16[80,960]{1,0:T(8,128)(2,1)S(1)} %collective-permute-done.12.refs_0_), channel_id=1, source_target_pairs={{0,16},{16,0},{1,17},{17,1},{2,18},{18,2},{3,19},{19,3},{4,20},{20... | collective-permute-start | bytes 460808 | tf_op jit(solution)/shard_map/ppermute | solution.py:273
  45.7 7.7 %collective-permute-start.15 = (bf16[2,4,32,320]{3,2,1,0:T(8,128)(2,1)S(1)}, bf16[2,4,32,320]{3,2,1,0:T(8,128)(2,1)S(1)}, u32[]{:S(2)}, u32[]{:S(2)}) collective-permute-start(bf16[2,4,32,320]{3,2,1,0:T(8,128)(2,1)S(1)} %get-tuple-element.50), channel_id=1, source_target_pairs={{0,8},{4,12},{8,0},{12,4},{1,9},{5,13},{9,1},{13,5},{2,10},{6,14},... | collective-permute-start | bytes 491528 | tf_op jit(solution)/shard_map/ppermute | solution.py:273
  48.9 6.2 %collective-permute-start.14 = (bf16[256,1280]{1,0:T(8,128)(2,1)S(1)}, bf16[256,1280]{1,0:T(8,128)(2,1)S(1)}, u32[]{:S(2)}, u32[]{:S(2)}) collective-permute-start(bf16[256,1280]{1,0:T(8,128)(2,1)S(1)} %get-tuple-element.48), channel_id=1, source_target_pairs={{0,4},{4,0},{8,12},{12,8},{1,5},{5,1},{9,13},{13,9},{2,6},{6,2},{1... | collective-permute-start | bytes 1966088 | tf_op jit(solution)/shard_map/ppermute | solution.py:273
  49.0 5.6 %collective-permute-start.18 = (f32[2,1280]{1,0:T(2,128)S(1)}, f32[2,1280]{1,0:T(2,128)S(1)}, u32[]{:S(2)}, u32[]{:S(2)}) collective-permute-start(f32[2,1280]{1,0:T(2,128)S(1)} %get-tuple-element.51.refs_0_), channel_id=1, source_target_pairs={{0,3},{1,2},{2,1},{3,0},{4,7},{5,6},{6,5},{7,4},{8,11},{9,10},{10,... | collective-permute-start | bytes 30728 | tf_op jit(solution)/shard_map/ppermute | solution.py:273
  49.6 5.0 %collective-permute-start.17 = (f32[2,1280]{1,0:T(2,128)S(1)}, f32[2,1280]{1,0:T(2,128)S(1)}, u32[]{:S(2)}, u32[]{:S(2)}) collective-permute-start(f32[2,1280]{1,0:T(2,128)S(1)} %get-tuple-element.51.refs_0_), channel_id=1, source_target_pairs={{0,2},{1,3},{2,0},{3,1},{4,6},{5,7},{6,4},{7,5},{8,10},{9,11},{10,... | collective-permute-start | bytes 30728 | tf_op jit(solution)/shard_map/ppermute | solution.py:273
  51.3 3.7 %collective-permute-start.16 = (f32[2,1280]{1,0:T(2,128)S(1)}, f32[2,1280]{1,0:T(2,128)S(1)}, u32[]{:S(2)}, u32[]{:S(2)}) collective-permute-start(f32[2,1280]{1,0:T(2,128)S(1)} %get-tuple-element.51.refs_0_), channel_id=1, source_target_pairs={{0,1},{1,0},{2,3},{3,2},{4,5},{5,4},{6,7},{7,6},{8,9},{9,8},{10,11... | collective-permute-start | bytes 30728 | tf_op jit(solution)/shard_map/ppermute | solution.py:273
  55.2 9.5 %collective-permute-start.20 = (bf16[4,32,1280]{2,1,0:T(8,128)(2,1)S(1)}, bf16[4,32,1280]{2,1,0:T(8,128)(2,1)S(1)}, u32[]{:S(2)}, u32[]{:S(2)}) collective-permute-start(bf16[4,32,1280]{2,1,0:T(8,128)(2,1)S(1)} %merge.1), channel_id=1, source_target_pairs={{0,8},{4,12},{8,0},{12,4},{1,9},{5,13},{9,1},{13,5},{2,10},{6,14},... | collective-permute-start | bytes 983048 | tf_op jit(solution)/shard_map/ppermute | solution.py:273
  55.8 2.2 %collective-permute-start.19 = (bf16[2,4,32,320]{3,2,1,0:T(8,128)(2,1)S(1)}, bf16[2,4,32,320]{3,2,1,0:T(8,128)(2,1)S(1)}, u32[]{:S(2)}, u32[]{:S(2)}) collective-permute-start(bf16[2,4,32,320]{3,2,1,0:T(8,128)(2,1)S(1)} %both.1), channel_id=1, source_target_pairs={{0,4},{4,0},{8,12},{12,8},{1,5},{5,1},{9,13},{13,9},{2,6},{6,2},{1... | collective-permute-start | bytes 491528 | tf_op jit(solution)/shard_map/ppermute | solution.py:273
  55.8 7.0 %collective-permute-start.23 = (f32[2,1280]{1,0:T(2,128)S(1)}, f32[2,1280]{1,0:T(2,128)S(1)}, u32[]{:S(2)}, u32[]{:S(2)}) collective-permute-start(f32[2,1280]{1,0:T(2,128)S(1)} %add.5.refs_0_), channel_id=1, source_target_pairs={{0,12},{4,8},{8,4},{12,0},{1,13},{5,9},{9,5},{13,1},{2,14},{6,10},... | collective-permute-start | bytes 30728 | tf_op jit(solution)/shard_map/ppermute | solution.py:273
  57.4 7.3 %collective-permute-start.22 = (f32[2,1280]{1,0:T(2,128)S(1)}, f32[2,1280]{1,0:T(2,128)S(1)}, u32[]{:S(2)}, u32[]{:S(2)}) collective-permute-start(f32[2,1280]{1,0:T(2,128)S(1)} %add.5.refs_0_), channel_id=1, source_target_pairs={{0,8},{4,12},{8,0},{12,4},{1,9},{5,13},{9,1},{13,5},{2,10},{6,14},... | collective-permute-start | bytes 30728 | tf_op jit(solution)/shard_map/ppermute | solution.py:273
  57.9 6.7 %collective-permute-start.21 = (f32[2,1280]{1,0:T(2,128)S(1)}, f32[2,1280]{1,0:T(2,128)S(1)}, u32[]{:S(2)}, u32[]{:S(2)}) collective-permute-start(f32[2,1280]{1,0:T(2,128)S(1)} %add.5.refs_0_), channel_id=1, source_target_pairs={{0,4},{4,0},{8,12},{12,8},{1,5},{5,1},{9,13},{13,9},{2,6},{6,2},{1... | collective-permute-start | bytes 30728 | tf_op jit(solution)/shard_map/ppermute | solution.py:273
  (8 other events, 93.6 us)

commit v11 on v9

--- a/solution.py
+++ b/solution.py
@@ -441,16 +441,6 @@
     )
 
     close = swapped(cross, "date", 1)
-    both = call(
-        both_kernel,
-        "both",
-        pair,
-        [VMEM] * 2,
-        (near(close_context), near(far_context)),
-        2,
-        microseconds=10,
-    )
-    close = after(close, both)
     chip, total = call(
         merge_kernel,
         "merge",
@@ -460,6 +450,20 @@
         6,
     )
     far = swapped(chip, "date", 2)
+    if owners == 4:
+        total = call(
+            add_kernel,
+            "add",
+            pairs,
+            [VMEM] * owners,
+            [near(total)] + [near(swapped(total, "tile", s)) for s in range(1, owners)],
+            2,
+        )
+    else:
+        total = lax.psum(total, "tile")
+    far_total = swapped(total, "date", 2)
+    far_context = after(far_context, total)
+    both = call(both_kernel, "both", pair, [VMEM] * 2, (near(close_context), near(far_context)), 2)
     both = swapped(both, "date", 1)
     home, attended = call(
         home_kernel,
@@ -470,20 +474,6 @@
         6,
         scratch=(pltpu.VMEM((groups, slots, rows, part), BF16),),
     )
-    if owners == 4:
-        tiles = [swapped(total, "tile", s) for s in range(1, owners)]
-        tiles[0] = after(tiles[0], home)
-        total = call(
-            add_kernel,
-            "add",
-            pairs,
-            [VMEM] * owners,
-            [near(total)] + [near(tile) for tile in tiles],
-            2,
-        )
-    else:
-        total = lax.psum(total, "tile")
-    far_total = swapped(total, "date", 2)
     grad_tokens, grad_norm = call(
         finish_kernel,
         "finish",

time: 65.8 us -> 63.8 us (0.970)
  waiting for transfers between devices: 16.5 us -> 13.5 us
  starting transfers between devices: 31.3 us -> 32.2 us
    ppermute x16, waiting for transfers between devices: 13 us -> 9.99 us  [swapped(): lax.ppermute(array, axis, [(i, i ^ bits) for i in range(lax.axis_size(axi...]
    ppermute x16, starting transfers between devices: 16.7 us -> 17.6 us  [swapped(): lax.ppermute(array, axis, [(i, i ^ bits) for i in range(lax.axis_size(axi...]
  transfers between devices with their start and end apart: 22 -> 22, of which waited for: 10 -> 12; matrix products, arithmetic and copies ran while one was open for 0% -> 0% of each run, Pallas kernels for 14% -> 12%
where the time goes in v11:
time: 63.8 us; the launch traced here: 63.6 us
  starting transfers between devices  32.2 us (50%)
  Pallas kernels  16.9 us (26%)
  waiting for transfers between devices  13.5 us (21%)
  between operations  0.87 us (1%)
    ppermute x16, starting transfers between devices, swapped(): lax.ppermute(array, axis, [(i, i ^ bits) for i in range(lax.axis_size(axi...  17.6 us
    pallas_call x13, Pallas kernels, call(): pl.pallas_call(kernel, out_shape=out_shape, in_specs=in_specs, out_specs=...  16.9 us
    ppermute x16, waiting for transfers between devices, swapped(): lax.ppermute(array, axis, [(i, i ^ bits) for i in range(lax.axis_size(axi...  9.99 us
    ppermute x2, starting transfers between devices, local(): first = lax.ppermute(held, 'tile', ring)  5.67 us
    ppermute x2, starting transfers between devices, local(): third = lax.ppermute(second, 'tile', ring)  4.72 us
    ppermute x2, starting transfers between devices, local(): second = lax.ppermute(first, 'tile', ring)  4.22 us
    ppermute x2, waiting for transfers between devices, local(): second = lax.ppermute(first, 'tile', ring)  1.79 us
    ppermute x2, waiting for transfers between devices, local(): first = lax.ppermute(held, 'tile', ring)  1.74 us
  transfers between devices with their start and end apart: 22, of which 12 were waited for; matrix products, arithmetic and copies ran while one was open for 0% of the time, Pallas kernels for 12%

profile of v11, /device:TPU:0, one launch (start us, length us, event | category | flops | bytes accessed | tf_op | source)
XLA Modules:
  0.0 63.6 jit_solution(183636575213839909)
XLA Ops:
  0.7 1.9 %pick.2 = (bf16[80,960]{1,0:T(8,128)(2,1)S(1)}, bf16[80,960]{1,0:T(8,128)(2,1)S(1)}) custom-call(s32[3]{0:T(128)S(1)} %pad_add_fusion.ids_ref, bf16[320,3840]{1,0:T(8,128)(2,1)} %w_ref.3), custom_call_target="tpu_custom_call" | custom-call | flops 10000000 | bytes 1000 | tf_op jit(solution)/shard_map/pick/pallas_call | solution.py:292
  2.6 3.1 %collective-permute-start.6 = (bf16[80,960]{1,0:T(8,128)(2,1)S(1)}, bf16[80,960]{1,0:T(8,128)(2,1)S(1)}, u32[]{:S(2)}, u32[]{:S(2)}) collective-permute-start(bf16[80,960]{1,0:T(8,128)(2,1)S(1)} %get-tuple-element.35.high_ref), channel_id=1, source_target_pairs={{0,1},{1,3},{3,2},{2,0},{4,5},{5,7},{7,6},{6,4},{8,9},{9,11},{11,1... | collective-permute-start | bytes 460808 | tf_op jit(solution)/shard_map/ppermute | solution.py:340
  5.7 2.6 %collective-permute-start = (bf16[80,960]{1,0:T(8,128)(2,1)S(1)}, bf16[80,960]{1,0:T(8,128)(2,1)S(1)}, u32[]{:S(2)}, u32[]{:S(2)}) collective-permute-start(bf16[80,960]{1,0:T(8,128)(2,1)S(1)} %get-tuple-element.34.low_ref), channel_id=1, source_target_pairs={{0,1},{1,3},{3,2},{2,0},{4,5},{5,7},{7,6},{6,4},{8,9},{9,11},{11,1... | collective-permute-start | bytes 460808 | tf_op jit(solution)/shard_map/ppermute | solution.py:340
  8.3 1.9 %pick.3.rest_ref = bf16[160,960]{1,0:T(8,128)(2,1)S(1)} custom-call(s32[3]{0:T(128)S(1)} %pad_add_fusion.ids_ref, bf16[320,3840]{1,0:T(8,128)(2,1)} %w_ref.3), custom_call_target="tpu_custom_call" | custom-call | flops 10000000 | bytes 1000 | tf_op jit(solution)/shard_map/pick/pallas_call | solution.py:292
  10.1 1.6 %collective-permute-done.6.refs_6_ = bf16[80,960]{1,0:T(8,128)(2,1)S(1)} collective-permute-done((bf16[80,960]{1,0:T(8,128)(2,1)S(1)}, bf16[80,960]{1,0:T(8,128)(2,1)S(1)}, u32[]{:S(2)}, u32[]{:S(2)}) %collective-permute-start.6) | collective-permute-done | bytes 153632 | tf_op jit(solution)/shard_map/ppermute | solution.py:340
  12.3 1.9 %collective-permute-start.10 = (bf16[4,32,1920]{2,1,0:T(8,128)(2,1)S(1)}, bf16[4,32,1920]{2,1,0:T(8,128)(2,1)S(1)}, u32[]{:S(2)}, u32[]{:S(2)}) collective-permute-start(bf16[4,32,1920]{2,1,0:T(8,128)(2,1)S(1)} %pack_across.1), channel_id=1, source_target_pairs={{0,8},{4,12},{8,0},{12,4},{1,9},{5,13},{9,1},{13,5},{2,10},{6,14},... | collective-permute-start | bytes 1474568 | tf_op jit(solution)/shard_map/ppermute | solution.py:280
  15.2 1.5 %collective-permute-start.1 = (bf16[80,960]{1,0:T(8,128)(2,1)S(1)}, bf16[80,960]{1,0:T(8,128)(2,1)S(1)}, u32[]{:S(2)}, u32[]{:S(2)}) collective-permute-start(bf16[80,960]{1,0:T(8,128)(2,1)S(1)} %collective-permute-done.refs_0_), channel_id=1, source_target_pairs={{0,16},{16,0},{1,17},{17,1},{2,18},{18,2},{3,19},{19,3},{4,20},{20... | collective-permute-start | bytes 460808 | tf_op jit(solution)/shard_map/ppermute | solution.py:280
  16.7 3.4 %collective-permute-start.8 = (bf16[80,960]{1,0:T(8,128)(2,1)S(1)}, bf16[80,960]{1,0:T(8,128)(2,1)S(1)}, u32[]{:S(2)}, u32[]{:S(2)}) collective-permute-start(bf16[80,960]{1,0:T(8,128)(2,1)S(1)} %collective-permute-done.6.refs_6_), channel_id=1, source_target_pairs={{0,1},{1,3},{3,2},{2,0},{4,5},{5,7},{7,6},{6,4},{8,9},{9,11},{11,1... | collective-permute-start | bytes 460808 | tf_op jit(solution)/shard_map/ppermute | solution.py:344
  20.6 1.8 %collective-permute-done.2.refs_2_ = bf16[80,960]{1,0:T(8,128)(2,1)S(1)} collective-permute-done((bf16[80,960]{1,0:T(8,128)(2,1)S(1)}, bf16[80,960]{1,0:T(8,128)(2,1)S(1)}, u32[]{:S(2)}, u32[]{:S(2)}) %collective-permute-start.2) | collective-permute-done | bytes 153632 | tf_op jit(solution)/shard_map/ppermute | solution.py:344
  22.4 2.8 %collective-permute-start.4 = (bf16[80,960]{1,0:T(8,128)(2,1)S(1)}, bf16[80,960]{1,0:T(8,128)(2,1)S(1)}, u32[]{:S(2)}, u32[]{:S(2)}) collective-permute-start(bf16[80,960]{1,0:T(8,128)(2,1)S(1)} %collective-permute-done.2.refs_2_), channel_id=1, source_target_pairs={{0,1},{1,3},{3,2},{2,0},{4,5},{5,7},{7,6},{6,4},{8,9},{9,11},{11,1... | collective-permute-start | bytes 460808 | tf_op jit(solution)/shard_map/ppermute | solution.py:347
  25.3 1.5 %collective-permute-start.3 = (bf16[80,960]{1,0:T(8,128)(2,1)S(1)}, bf16[80,960]{1,0:T(8,128)(2,1)S(1)}, u32[]{:S(2)}, u32[]{:S(2)}) collective-permute-start(bf16[80,960]{1,0:T(8,128)(2,1)S(1)} %collective-permute-done.2.refs_2_), channel_id=1, source_target_pairs={{0,16},{16,0},{1,17},{17,1},{2,18},{18,2},{3,19},{19,3},{4,20},{20... | collective-permute-start | bytes 460808 | tf_op jit(solution)/shard_map/ppermute | solution.py:280
  26.9 1.9 %collective-permute-start.12 = (bf16[80,960]{1,0:T(8,128)(2,1)S(1)}, bf16[80,960]{1,0:T(8,128)(2,1)S(1)}, u32[]{:S(2)}, u32[]{:S(2)}) collective-permute-start(bf16[80,960]{1,0:T(8,128)(2,1)S(1)} %collective-permute-done.8.refs_8_), channel_id=1, source_target_pairs={{0,1},{1,3},{3,2},{2,0},{4,5},{5,7},{7,6},{6,4},{8,9},{9,11},{11,1... | collective-permute-start | bytes 460808 | tf_op jit(solution)/shard_map/ppermute | solution.py:347
  28.8 1.5 %collective-permute-start.9 = (bf16[80,960]{1,0:T(8,128)(2,1)S(1)}, bf16[80,960]{1,0:T(8,128)(2,1)S(1)}, u32[]{:S(2)}, u32[]{:S(2)}) collective-permute-start(bf16[80,960]{1,0:T(8,128)(2,1)S(1)} %collective-permute-done.8.refs_8_), channel_id=1, source_target_pairs={{0,16},{16,0},{1,17},{17,1},{2,18},{18,2},{3,19},{19,3},{4,20},{20... | collective-permute-start | bytes 460808 | tf_op jit(solution)/shard_map/ppermute | solution.py:280
  31.5 2.3 %collective-permute-start.5 = (bf16[80,960]{1,0:T(8,128)(2,1)S(1)}, bf16[80,960]{1,0:T(8,128)(2,1)S(1)}, u32[]{:S(2)}, u32[]{:S(2)}) collective-permute-start(bf16[80,960]{1,0:T(8,128)(2,1)S(1)} %collective-permute-done.4.refs_4_), channel_id=1, source_target_pairs={{0,16},{16,0},{1,17},{17,1},{2,18},{18,2},{3,19},{19,3},{4,20},{20... | collective-permute-start | bytes 460808 | tf_op jit(solution)/shard_map/ppermute | solution.py:280
  34.9 2.5 %collective-permute-done.5.refs_5_ = bf16[80,960]{1,0:T(8,128)(2,1)S(1)} collective-permute-done((bf16[80,960]{1,0:T(8,128)(2,1)S(1)}, bf16[80,960]{1,0:T(8,128)(2,1)S(1)}, u32[]{:S(2)}, u32[]{:S(2)}) %collective-permute-start.5) | collective-permute-done | bytes 153632 | tf_op jit(solution)/shard_map/ppermute | solution.py:280
  38.2 1.9 %norm.1 = (bf16[512,1280]{1,0:T(8,128)(2,1)S(1)}, bf16[512,1280]{1,0:T(8,128)(2,1)S(1)}, f32[4,32,1280]{2,1,0:T(8,128)S(1)}, f32[4,32,128]{2,1,0:T(8,128)S(1)}) custom-call(s32[4]{0:T(128)S(1)} %copy-done.5, bf16[256,1280]{1,0:T(8,128)(2,1)S(1)} %copy-done.4, f32[1,1280]{1,0:T(1,128)S(1)} %reshape.12.gain_ref, f32[1,1280]{1,0:T(1,128)S(1)} %reshape.13.bias_ref, ...), custom_call_target="tpu_custom_call" | custom-call | flops 2000000000 | bytes 1000 | tf_op jit(solution)/shard_map/norm/pallas_call | solution.py:292
  41.5 4.2 %attend.1 = (bf16[4,32,320]{2,1,0:T(8,128)(2,1)S(1)}, bf16[4,32,320]{2,1,0:T(8,128)(2,1)S(1)}, bf16[2,4,32,320]{3,2,1,0:T(8,128)(2,1)S(1)}, bf16[512,960]{1,0:T(8,128)(2,1)S(1)}, bf16[1280,960]{1,0:T(8,128)(2,1)S(1)}) custom-call(s32[3]{0:T(128)S(1)} %pad_add_fusion.ids_ref, s32[4]{0:T(128)S(1)} %copy-done.3, ...), custom_call_target="tpu_custom_call", output_to_operand_aliasing={{4}: (2, {})} | custom-call | flops 10000000 | bytes 1000 | tf_op jit(solution)/shard_map/attend/pallas_call | solution.py:292
  45.7 1.6 %back.1 = (bf16[4,32,1280]{2,1,0:T(8,128)(2,1)S(1)}, bf16[4,32,1280]{2,1,0:T(8,128)(2,1)S(1)}, bf16[272,1280]{1,0:T(8,128)(2,1)S(1)}, f32[2,1280]{1,0:T(2,128)S(1)}) custom-call(bf16[512,960]{1,0:T(8,128)(2,1)S(1)} %get-tuple-element.46.gqkv_ref, bf16[512,1280]{1,0:T(8,128)(2,1)S(1)} %get-tuple-element.47.unit_ref, ...), custom_call_target="tpu_custom_call" | custom-call | flops 10000000 | bytes 1000 | tf_op jit(solution)/shard_map/back/pallas_call | solution.py:292
  47.4 1.6 %collective-permute-start.15 = (bf16[2,4,32,320]{3,2,1,0:T(8,128)(2,1)S(1)}, bf16[2,4,32,320]{3,2,1,0:T(8,128)(2,1)S(1)}, u32[]{:S(2)}, u32[]{:S(2)}) collective-permute-start(bf16[2,4,32,320]{3,2,1,0:T(8,128)(2,1)S(1)} %get-tuple-element.53), channel_id=1, source_target_pairs={{0,8},{4,12},{8,0},{12,4},{1,9},{5,13},{9,1},{13,5},{2,10},{6,14},... | collective-permute-start | bytes 491528 | tf_op jit(solution)/shard_map/ppermute | solution.py:280
  49.7 1.6 %collective-permute-start.20 = (bf16[4,32,1280]{2,1,0:T(8,128)(2,1)S(1)}, bf16[4,32,1280]{2,1,0:T(8,128)(2,1)S(1)}, u32[]{:S(2)}, u32[]{:S(2)}) collective-permute-start(bf16[4,32,1280]{2,1,0:T(8,128)(2,1)S(1)} %get-tuple-element.62), channel_id=1, source_target_pairs={{0,8},{4,12},{8,0},{12,4},{1,9},{5,13},{9,1},{13,5},{2,10},{6,14},... | collective-permute-start | bytes 983048 | tf_op jit(solution)/shard_map/ppermute | solution.py:280
  51.8 1.8 %collective-permute-start.17 = (f32[2,1280]{1,0:T(2,128)S(1)}, f32[2,1280]{1,0:T(2,128)S(1)}, u32[]{:S(2)}, u32[]{:S(2)}) collective-permute-start(f32[2,1280]{1,0:T(2,128)S(1)} %get-tuple-element.56.refs_0_), channel_id=1, source_target_pairs={{0,2},{1,3},{2,0},{3,1},{4,6},{5,7},{6,4},{7,5},{8,10},{9,11},{10,... | collective-permute-start | bytes 30728 | tf_op jit(solution)/shard_map/ppermute | solution.py:280
  53.5 2.1 %collective-permute-start.16 = (f32[2,1280]{1,0:T(2,128)S(1)}, f32[2,1280]{1,0:T(2,128)S(1)}, u32[]{:S(2)}, u32[]{:S(2)}) collective-permute-start(f32[2,1280]{1,0:T(2,128)S(1)} %get-tuple-element.56.refs_0_), channel_id=1, source_target_pairs={{0,1},{1,0},{2,3},{3,2},{4,5},{5,4},{6,7},{7,6},{8,9},{9,8},{10,11... | collective-permute-start | bytes 30728 | tf_op jit(solution)/shard_map/ppermute | solution.py:280
  60.2 1.8 %collective-permute-done.21.refs_1_ = f32[2,1280]{1,0:T(2,128)S(1)} collective-permute-done((f32[2,1280]{1,0:T(2,128)S(1)}, f32[2,1280]{1,0:T(2,128)S(1)}, u32[]{:S(2)}, u32[]{:S(2)}) %collective-permute-start.21) | collective-permute-done | bytes 10272 | tf_op jit(solution)/shard_map/ppermute | solution.py:280
  62.0 1.6 %finish.1 = (bf16[4,32,1280]{2,1,0:T(8,128)(2,1)}, f32[2,1280]{1,0:T(2,128)}) custom-call(s32[3]{0:T(128)S(1)} %pad_add_fusion.ids_ref, s32[4]{0:T(128)S(1)} %copy-done.3, f32[4,32,1280]{2,1,0:T(8,128)S(1)} %get-tuple-element.59.unit_ref, f32[4,32,128]{2,1,0:T(8,128)S(1)} %get-tuple-element.60.inv_ref, f32[1,1280]{1,0:T(1,128)S(1)} %reshape.12.gain_ref, ...), custom_call_target="tpu_custom_call" | custom-call | flops 10000000 | bytes 1000 | tf_op jit(solution)/shard_map/finish/pallas_call | solution.py:292
  (52 shorter events, 12.5 us)
Async XLA Ops:
  2.6 9.1 %collective-permute-start.6 = (bf16[80,960]{1,0:T(8,128)(2,1)S(1)}, bf16[80,960]{1,0:T(8,128)(2,1)S(1)}, u32[]{:S(2)}, u32[]{:S(2)}) collective-permute-start(bf16[80,960]{1,0:T(8,128)(2,1)S(1)} %get-tuple-element.35.high_ref), channel_id=1, source_target_pairs={{0,1},{1,3},{3,2},{2,0},{4,5},{5,7},{7,6},{6,4},{8,9},{9,11},{11,1... | collective-permute-start | bytes 460808 | tf_op jit(solution)/shard_map/ppermute | solution.py:340
  5.7 29.1 %copy-start.6 = (f32[1280]{0:T(1024)S(1)}, f32[1280]{0:T(1024)}, u32[]{:S(2)}) copy-start(f32[1280]{0:T(1024)} %param.15) | copy-start | bytes 15364
  5.7 29.1 %copy-start.7 = (f32[1280]{0:T(1024)S(1)}, f32[1280]{0:T(1024)}, u32[]{:S(2)}) copy-start(f32[1280]{0:T(1024)} %param.16) | copy-start | bytes 15364
  5.7 8.7 %collective-permute-start = (bf16[80,960]{1,0:T(8,128)(2,1)S(1)}, bf16[80,960]{1,0:T(8,128)(2,1)S(1)}, u32[]{:S(2)}, u32[]{:S(2)}) collective-permute-start(bf16[80,960]{1,0:T(8,128)(2,1)S(1)} %get-tuple-element.34.low_ref), channel_id=1, source_target_pairs={{0,1},{1,3},{3,2},{2,0},{4,5},{5,7},{7,6},{6,4},{8,9},{9,11},{11,1... | collective-permute-start | bytes 460808 | tf_op jit(solution)/shard_map/ppermute | solution.py:340
  12.3 21.5 %collective-permute-start.10 = (bf16[4,32,1920]{2,1,0:T(8,128)(2,1)S(1)}, bf16[4,32,1920]{2,1,0:T(8,128)(2,1)S(1)}, u32[]{:S(2)}, u32[]{:S(2)}) collective-permute-start(bf16[4,32,1920]{2,1,0:T(8,128)(2,1)S(1)} %pack_across.1), channel_id=1, source_target_pairs={{0,8},{4,12},{8,0},{12,4},{1,9},{5,13},{9,1},{13,5},{2,10},{6,14},... | collective-permute-start | bytes 1474568 | tf_op jit(solution)/shard_map/ppermute | solution.py:280
  14.4 8.0 %collective-permute-start.2 = (bf16[80,960]{1,0:T(8,128)(2,1)S(1)}, bf16[80,960]{1,0:T(8,128)(2,1)S(1)}, u32[]{:S(2)}, u32[]{:S(2)}) collective-permute-start(bf16[80,960]{1,0:T(8,128)(2,1)S(1)} %collective-permute-done.refs_0_), channel_id=1, source_target_pairs={{0,1},{1,3},{3,2},{2,0},{4,5},{5,7},{7,6},{6,4},{8,9},{9,11},{11,1... | collective-permute-start | bytes 460808 | tf_op jit(solution)/shard_map/ppermute | solution.py:344
  15.2 7.2 %collective-permute-start.1 = (bf16[80,960]{1,0:T(8,128)(2,1)S(1)}, bf16[80,960]{1,0:T(8,128)(2,1)S(1)}, u32[]{:S(2)}, u32[]{:S(2)}) collective-permute-start(bf16[80,960]{1,0:T(8,128)(2,1)S(1)} %collective-permute-done.refs_0_), channel_id=1, source_target_pairs={{0,16},{16,0},{1,17},{17,1},{2,18},{18,2},{3,19},{19,3},{4,20},{20... | collective-permute-start | bytes 460808 | tf_op jit(solution)/shard_map/ppermute | solution.py:280
  16.7 10.1 %collective-permute-start.8 = (bf16[80,960]{1,0:T(8,128)(2,1)S(1)}, bf16[80,960]{1,0:T(8,128)(2,1)S(1)}, u32[]{:S(2)}, u32[]{:S(2)}) collective-permute-start(bf16[80,960]{1,0:T(8,128)(2,1)S(1)} %collective-permute-done.6.refs_6_), channel_id=1, source_target_pairs={{0,1},{1,3},{3,2},{2,0},{4,5},{5,7},{7,6},{6,4},{8,9},{9,11},{11,1... | collective-permute-start | bytes 460808 | tf_op jit(solution)/shard_map/ppermute | solution.py:344
  20.1 6.8 %collective-permute-start.7 = (bf16[80,960]{1,0:T(8,128)(2,1)S(1)}, bf16[80,960]{1,0:T(8,128)(2,1)S(1)}, u32[]{:S(2)}, u32[]{:S(2)}) collective-permute-start(bf16[80,960]{1,0:T(8,128)(2,1)S(1)} %collective-permute-done.6.refs_6_), channel_id=1, source_target_pairs={{0,16},{16,0},{1,17},{17,1},{2,18},{18,2},{3,19},{19,3},{4,20},{20... | collective-permute-start | bytes 460808 | tf_op jit(solution)/shard_map/ppermute | solution.py:280
  22.4 7.9 %collective-permute-start.4 = (bf16[80,960]{1,0:T(8,128)(2,1)S(1)}, bf16[80,960]{1,0:T(8,128)(2,1)S(1)}, u32[]{:S(2)}, u32[]{:S(2)}) collective-permute-start(bf16[80,960]{1,0:T(8,128)(2,1)S(1)} %collective-permute-done.2.refs_2_), channel_id=1, source_target_pairs={{0,1},{1,3},{3,2},{2,0},{4,5},{5,7},{7,6},{6,4},{8,9},{9,11},{11,1... | collective-permute-start | bytes 460808 | tf_op jit(solution)/shard_map/ppermute | solution.py:347
  25.3 6.2 %collective-permute-start.3 = (bf16[80,960]{1,0:T(8,128)(2,1)S(1)}, bf16[80,960]{1,0:T(8,128)(2,1)S(1)}, u32[]{:S(2)}, u32[]{:S(2)}) collective-permute-start(bf16[80,960]{1,0:T(8,128)(2,1)S(1)} %collective-permute-done.2.refs_2_), channel_id=1, source_target_pairs={{0,16},{16,0},{1,17},{17,1},{2,18},{18,2},{3,19},{19,3},{4,20},{20... | collective-permute-start | bytes 460808 | tf_op jit(solution)/shard_map/ppermute | solution.py:280
  26.9 7.9 %collective-permute-start.12 = (bf16[80,960]{1,0:T(8,128)(2,1)S(1)}, bf16[80,960]{1,0:T(8,128)(2,1)S(1)}, u32[]{:S(2)}, u32[]{:S(2)}) collective-permute-start(bf16[80,960]{1,0:T(8,128)(2,1)S(1)} %collective-permute-done.8.refs_8_), channel_id=1, source_target_pairs={{0,1},{1,3},{3,2},{2,0},{4,5},{5,7},{7,6},{6,4},{8,9},{9,11},{11,1... | collective-permute-start | bytes 460808 | tf_op jit(solution)/shard_map/ppermute | solution.py:347
  28.8 6.1 %collective-permute-start.9 = (bf16[80,960]{1,0:T(8,128)(2,1)S(1)}, bf16[80,960]{1,0:T(8,128)(2,1)S(1)}, u32[]{:S(2)}, u32[]{:S(2)}) collective-permute-start(bf16[80,960]{1,0:T(8,128)(2,1)S(1)} %collective-permute-done.8.refs_8_), channel_id=1, source_target_pairs={{0,16},{16,0},{1,17},{17,1},{2,18},{18,2},{3,19},{19,3},{4,20},{20... | collective-permute-start | bytes 460808 | tf_op jit(solution)/shard_map/ppermute | solution.py:280
  31.5 6.0 %collective-permute-start.5 = (bf16[80,960]{1,0:T(8,128)(2,1)S(1)}, bf16[80,960]{1,0:T(8,128)(2,1)S(1)}, u32[]{:S(2)}, u32[]{:S(2)}) collective-permute-start(bf16[80,960]{1,0:T(8,128)(2,1)S(1)} %collective-permute-done.4.refs_4_), channel_id=1, source_target_pairs={{0,16},{16,0},{1,17},{17,1},{2,18},{18,2},{3,19},{19,3},{4,20},{20... | collective-permute-start | bytes 460808 | tf_op jit(solution)/shard_map/ppermute | solution.py:280
  34.7 3.5 %collective-permute-start.11 = (bf16[4,32,3200]{2,1,0:T(8,128)(2,1)S(1)}, bf16[4,32,3200]{2,1,0:T(8,128)(2,1)S(1)}, u32[]{:S(2)}, u32[]{:S(2)}) collective-permute-start(bf16[4,32,3200]{2,1,0:T(8,128)(2,1)S(1)} %get-tuple-element.43), channel_id=1, source_target_pairs={{0,4},{4,0},{8,12},{12,8},{1,5},{5,1},{9,13},{13,9},{2,6},{6,2},{1... | collective-permute-start | bytes 2457608 | tf_op jit(solution)/shard_map/ppermute | solution.py:280
  34.8 6.6 %collective-permute-start.13 = (bf16[80,960]{1,0:T(8,128)(2,1)S(1)}, bf16[80,960]{1,0:T(8,128)(2,1)S(1)}, u32[]{:S(2)}, u32[]{:S(2)}) collective-permute-start(bf16[80,960]{1,0:T(8,128)(2,1)S(1)} %collective-permute-done.12.refs_0_), channel_id=1, source_target_pairs={{0,16},{16,0},{1,17},{17,1},{2,18},{18,2},{3,19},{19,3},{4,20},{20... | collective-permute-start | bytes 460808 | tf_op jit(solution)/shard_map/ppermute | solution.py:280
  47.4 2.2 %collective-permute-start.14 = (bf16[272,1280]{1,0:T(8,128)(2,1)S(1)}, bf16[272,1280]{1,0:T(8,128)(2,1)S(1)}, u32[]{:S(2)}, u32[]{:S(2)}) collective-permute-start(bf16[272,1280]{1,0:T(8,128)(2,1)S(1)} %get-tuple-element.50), channel_id=1, source_target_pairs={{0,4},{4,0},{8,12},{12,8},{1,5},{5,1},{9,13},{13,9},{2,6},{6,2},{1... | collective-permute-start | bytes 2088968 | tf_op jit(solution)/shard_map/ppermute | solution.py:280
  47.4 9.8 %collective-permute-start.15 = (bf16[2,4,32,320]{3,2,1,0:T(8,128)(2,1)S(1)}, bf16[2,4,32,320]{3,2,1,0:T(8,128)(2,1)S(1)}, u32[]{:S(2)}, u32[]{:S(2)}) collective-permute-start(bf16[2,4,32,320]{3,2,1,0:T(8,128)(2,1)S(1)} %get-tuple-element.53), channel_id=1, source_target_pairs={{0,8},{4,12},{8,0},{12,4},{1,9},{5,13},{9,1},{13,5},{2,10},{6,14},... | collective-permute-start | bytes 491528 | tf_op jit(solution)/shard_map/ppermute | solution.py:280
  49.7 12.3 %collective-permute-start.20 = (bf16[4,32,1280]{2,1,0:T(8,128)(2,1)S(1)}, bf16[4,32,1280]{2,1,0:T(8,128)(2,1)S(1)}, u32[]{:S(2)}, u32[]{:S(2)}) collective-permute-start(bf16[4,32,1280]{2,1,0:T(8,128)(2,1)S(1)} %get-tuple-element.62), channel_id=1, source_target_pairs={{0,8},{4,12},{8,0},{12,4},{1,9},{5,13},{9,1},{13,5},{2,10},{6,14},... | collective-permute-start | bytes 983048 | tf_op jit(solution)/shard_map/ppermute | solution.py:280
  51.2 5.5 %collective-permute-start.18 = (f32[2,1280]{1,0:T(2,128)S(1)}, f32[2,1280]{1,0:T(2,128)S(1)}, u32[]{:S(2)}, u32[]{:S(2)}) collective-permute-start(f32[2,1280]{1,0:T(2,128)S(1)} %get-tuple-element.56.refs_0_), channel_id=1, source_target_pairs={{0,3},{1,2},{2,1},{3,0},{4,7},{5,6},{6,5},{7,4},{8,11},{9,10},{10,... | collective-permute-start | bytes 30728 | tf_op jit(solution)/shard_map/ppermute | solution.py:280
  51.8 4.9 %collective-permute-start.17 = (f32[2,1280]{1,0:T(2,128)S(1)}, f32[2,1280]{1,0:T(2,128)S(1)}, u32[]{:S(2)}, u32[]{:S(2)}) collective-permute-start(f32[2,1280]{1,0:T(2,128)S(1)} %get-tuple-element.56.refs_0_), channel_id=1, source_target_pairs={{0,2},{1,3},{2,0},{3,1},{4,6},{5,7},{6,4},{7,5},{8,10},{9,11},{10,... | collective-permute-start | bytes 30728 | tf_op jit(solution)/shard_map/ppermute | solution.py:280
  53.5 3.7 %collective-permute-start.16 = (f32[2,1280]{1,0:T(2,128)S(1)}, f32[2,1280]{1,0:T(2,128)S(1)}, u32[]{:S(2)}, u32[]{:S(2)}) collective-permute-start(f32[2,1280]{1,0:T(2,128)S(1)} %get-tuple-element.56.refs_0_), channel_id=1, source_target_pairs={{0,1},{1,0},{2,3},{3,2},{4,5},{5,4},{6,7},{7,6},{8,9},{9,8},{10,11... | collective-permute-start | bytes 30728 | tf_op jit(solution)/shard_map/ppermute | solution.py:280
  57.3 1.5 %collective-permute-start.19 = (bf16[2,4,32,320]{3,2,1,0:T(8,128)(2,1)S(1)}, bf16[2,4,32,320]{3,2,1,0:T(8,128)(2,1)S(1)}, u32[]{:S(2)}, u32[]{:S(2)}) collective-permute-start(bf16[2,4,32,320]{3,2,1,0:T(8,128)(2,1)S(1)} %both.1), channel_id=1, source_target_pairs={{0,4},{4,0},{8,12},{12,8},{1,5},{5,1},{9,13},{13,9},{2,6},{6,2},{1... | collective-permute-start | bytes 491528 | tf_op jit(solution)/shard_map/ppermute | solution.py:280
  57.4 4.6 %collective-permute-start.21 = (f32[2,1280]{1,0:T(2,128)S(1)}, f32[2,1280]{1,0:T(2,128)S(1)}, u32[]{:S(2)}, u32[]{:S(2)}) collective-permute-start(f32[2,1280]{1,0:T(2,128)S(1)} %add.5.refs_0_), channel_id=1, source_target_pairs={{0,8},{4,12},{8,0},{12,4},{1,9},{5,13},{9,1},{13,5},{2,10},{6,14},... | collective-permute-start | bytes 30728 | tf_op jit(solution)/shard_map/ppermute | solution.py:280
  (6 other events, 35.4 us)

commit v12 on v11

--- a/solution.py
+++ b/solution.py
@@ -346,13 +346,11 @@
             second = after(second, first_other)
             third = lax.ppermute(second, "tile", ring)
             second_other = swapped(second, "rep", 1)
-            if not chains:
-                third = after(third, second_other)
             third_other = swapped(third, "rep", 1)
             chains.append((first, first_other, second, second_other, third, third_other))
-        first, later = chains[1][0], chains[1][2]
+        first, later = chains[1][0], (chains[1][2], chains[0][3])
     else:
-        first = later = ids
+        first, later = ids, ()
 
     across = call(
         functools.partial(pack_across_kernel, part),
@@ -369,7 +367,7 @@
         "pack_beside",
         (pltpu.VMEM((slots, rows, 2 * width + 2 * part), BF16), pair),
         [SMEM, VMEM, VMEM, VMEM],
-        (after(ids, later), tokens, cotangent, near(across)),
+        (after(ids, *later), tokens, cotangent, near(across)),
         6,
     )
     beside = swapped(beside, "date", 1)

time: 63.8 us -> 62.4 us (0.978)
  waiting for transfers between devices: 13.5 us -> 12.4 us
    ppermute x16, waiting for transfers between devices: 9.99 us -> 8.83 us  [swapped(): lax.ppermute(array, axis, [(i, i ^ bits) for i in range(lax.axis_size(axi...]
where the time goes in v12:
time: 62.4 us; the launch traced here: 62.3 us
  starting transfers between devices  32.1 us (51%)
  Pallas kernels  16.9 us (27%)
  waiting for transfers between devices  12.4 us (20%)
  between operations  0.86 us (1%)
    ppermute x16, starting transfers between devices, swapped(): lax.ppermute(array, axis, [(i, i ^ bits) for i in range(lax.axis_size(axi...  17.4 us
    pallas_call x13, Pallas kernels, call(): pl.pallas_call(kernel, out_shape=out_shape, in_specs=in_specs, out_specs=...  16.9 us
    ppermute x16, waiting for transfers between devices, swapped(): lax.ppermute(array, axis, [(i, i ^ bits) for i in range(lax.axis_size(axi...  8.83 us
    ppermute x2, starting transfers between devices, local(): first = lax.ppermute(held, 'tile', ring)  5.67 us
    ppermute x2, starting transfers between devices, local(): third = lax.ppermute(second, 'tile', ring)  4.72 us
    ppermute x2, starting transfers between devices, local(): second = lax.ppermute(first, 'tile', ring)  4.22 us
    ppermute x2, waiting for transfers between devices, local(): second = lax.ppermute(first, 'tile', ring)  1.79 us
    ppermute x2, waiting for transfers between devices, local(): first = lax.ppermute(held, 'tile', ring)  1.74 us
  transfers between devices with their start and end apart: 22, of which 12 were waited for; matrix products, arithmetic and copies ran while one was open for 0% of the time, Pallas kernels for 12%

profile of v12, /device:TPU:0, one launch (start us, length us, event | category | flops | bytes accessed | tf_op | source)
XLA Modules:
  0.0 62.3 jit_solution(4438856410429300942)
XLA Ops:
  0.7 1.9 %pick.2 = (bf16[80,960]{1,0:T(8,128)(2,1)S(1)}, bf16[80,960]{1,0:T(8,128)(2,1)S(1)}) custom-call(s32[3]{0:T(128)S(1)} %pad_add_fusion.ids_ref, bf16[320,3840]{1,0:T(8,128)(2,1)} %w_ref.3), custom_call_target="tpu_custom_call" | custom-call | flops 10000000 | bytes 1000 | tf_op jit(solution)/shard_map/pick/pallas_call | solution.py:292
  2.6 3.1 %collective-permute-start.6 = (bf16[80,960]{1,0:T(8,128)(2,1)S(1)}, bf16[80,960]{1,0:T(8,128)(2,1)S(1)}, u32[]{:S(2)}, u32[]{:S(2)}) collective-permute-start(bf16[80,960]{1,0:T(8,128)(2,1)S(1)} %get-tuple-element.34.high_ref), channel_id=1, source_target_pairs={{0,1},{1,3},{3,2},{2,0},{4,5},{5,7},{7,6},{6,4},{8,9},{9,11},{11,1... | collective-permute-start | bytes 460808 | tf_op jit(solution)/shard_map/ppermute | solution.py:340
  5.7 2.6 %collective-permute-start = (bf16[80,960]{1,0:T(8,128)(2,1)S(1)}, bf16[80,960]{1,0:T(8,128)(2,1)S(1)}, u32[]{:S(2)}, u32[]{:S(2)}) collective-permute-start(bf16[80,960]{1,0:T(8,128)(2,1)S(1)} %get-tuple-element.33.low_ref), channel_id=1, source_target_pairs={{0,1},{1,3},{3,2},{2,0},{4,5},{5,7},{7,6},{6,4},{8,9},{9,11},{11,1... | collective-permute-start | bytes 460808 | tf_op jit(solution)/shard_map/ppermute | solution.py:340
  8.3 1.9 %pick.3.rest_ref = bf16[160,960]{1,0:T(8,128)(2,1)S(1)} custom-call(s32[3]{0:T(128)S(1)} %pad_add_fusion.ids_ref, bf16[320,3840]{1,0:T(8,128)(2,1)} %w_ref.3), custom_call_target="tpu_custom_call" | custom-call | flops 10000000 | bytes 1000 | tf_op jit(solution)/shard_map/pick/pallas_call | solution.py:292
  10.1 1.6 %collective-permute-done.6.refs_6_ = bf16[80,960]{1,0:T(8,128)(2,1)S(1)} collective-permute-done((bf16[80,960]{1,0:T(8,128)(2,1)S(1)}, bf16[80,960]{1,0:T(8,128)(2,1)S(1)}, u32[]{:S(2)}, u32[]{:S(2)}) %collective-permute-start.6) | collective-permute-done | bytes 153632 | tf_op jit(solution)/shard_map/ppermute | solution.py:340
  12.3 1.9 %collective-permute-start.10 = (bf16[4,32,1920]{2,1,0:T(8,128)(2,1)S(1)}, bf16[4,32,1920]{2,1,0:T(8,128)(2,1)S(1)}, u32[]{:S(2)}, u32[]{:S(2)}) collective-permute-start(bf16[4,32,1920]{2,1,0:T(8,128)(2,1)S(1)} %pack_across.1), channel_id=1, source_target_pairs={{0,8},{4,12},{8,0},{12,4},{1,9},{5,13},{9,1},{13,5},{2,10},{6,14},... | collective-permute-start | bytes 1474568 | tf_op jit(solution)/shard_map/ppermute | solution.py:280
  15.2 1.5 %collective-permute-start.1 = (bf16[80,960]{1,0:T(8,128)(2,1)S(1)}, bf16[80,960]{1,0:T(8,128)(2,1)S(1)}, u32[]{:S(2)}, u32[]{:S(2)}) collective-permute-start(bf16[80,960]{1,0:T(8,128)(2,1)S(1)} %collective-permute-done.refs_0_), channel_id=1, source_target_pairs={{0,16},{16,0},{1,17},{17,1},{2,18},{18,2},{3,19},{19,3},{4,20},{20... | collective-permute-start | bytes 460808 | tf_op jit(solution)/shard_map/ppermute | solution.py:280
  16.7 3.4 %collective-permute-start.8 = (bf16[80,960]{1,0:T(8,128)(2,1)S(1)}, bf16[80,960]{1,0:T(8,128)(2,1)S(1)}, u32[]{:S(2)}, u32[]{:S(2)}) collective-permute-start(bf16[80,960]{1,0:T(8,128)(2,1)S(1)} %collective-permute-done.6.refs_6_), channel_id=1, source_target_pairs={{0,1},{1,3},{3,2},{2,0},{4,5},{5,7},{7,6},{6,4},{8,9},{9,11},{11,1... | collective-permute-start | bytes 460808 | tf_op jit(solution)/shard_map/ppermute | solution.py:344
  20.6 1.8 %collective-permute-done.2.refs_2_ = bf16[80,960]{1,0:T(8,128)(2,1)S(1)} collective-permute-done((bf16[80,960]{1,0:T(8,128)(2,1)S(1)}, bf16[80,960]{1,0:T(8,128)(2,1)S(1)}, u32[]{:S(2)}, u32[]{:S(2)}) %collective-permute-start.2) | collective-permute-done | bytes 153632 | tf_op jit(solution)/shard_map/ppermute | solution.py:344
  22.4 2.8 %collective-permute-start.4 = (bf16[80,960]{1,0:T(8,128)(2,1)S(1)}, bf16[80,960]{1,0:T(8,128)(2,1)S(1)}, u32[]{:S(2)}, u32[]{:S(2)}) collective-permute-start(bf16[80,960]{1,0:T(8,128)(2,1)S(1)} %collective-permute-done.2.refs_2_), channel_id=1, source_target_pairs={{0,1},{1,3},{3,2},{2,0},{4,5},{5,7},{7,6},{6,4},{8,9},{9,11},{11,1... | collective-permute-start | bytes 460808 | tf_op jit(solution)/shard_map/ppermute | solution.py:347
  25.3 1.6 %collective-permute-start.3 = (bf16[80,960]{1,0:T(8,128)(2,1)S(1)}, bf16[80,960]{1,0:T(8,128)(2,1)S(1)}, u32[]{:S(2)}, u32[]{:S(2)}) collective-permute-start(bf16[80,960]{1,0:T(8,128)(2,1)S(1)} %collective-permute-done.2.refs_2_), channel_id=1, source_target_pairs={{0,16},{16,0},{1,17},{17,1},{2,18},{18,2},{3,19},{19,3},{4,20},{20... | collective-permute-start | bytes 460808 | tf_op jit(solution)/shard_map/ppermute | solution.py:280
  26.9 1.9 %collective-permute-start.12 = (bf16[80,960]{1,0:T(8,128)(2,1)S(1)}, bf16[80,960]{1,0:T(8,128)(2,1)S(1)}, u32[]{:S(2)}, u32[]{:S(2)}) collective-permute-start(bf16[80,960]{1,0:T(8,128)(2,1)S(1)} %collective-permute-done.8.refs_8_), channel_id=1, source_target_pairs={{0,1},{1,3},{3,2},{2,0},{4,5},{5,7},{7,6},{6,4},{8,9},{9,11},{11,1... | collective-permute-start | bytes 460808 | tf_op jit(solution)/shard_map/ppermute | solution.py:347
  28.8 1.5 %collective-permute-start.9 = (bf16[80,960]{1,0:T(8,128)(2,1)S(1)}, bf16[80,960]{1,0:T(8,128)(2,1)S(1)}, u32[]{:S(2)}, u32[]{:S(2)}) collective-permute-start(bf16[80,960]{1,0:T(8,128)(2,1)S(1)} %collective-permute-done.8.refs_8_), channel_id=1, source_target_pairs={{0,16},{16,0},{1,17},{17,1},{2,18},{18,2},{3,19},{19,3},{4,20},{20... | collective-permute-start | bytes 460808 | tf_op jit(solution)/shard_map/ppermute | solution.py:280
  30.9 1.5 %collective-permute-done.3.refs_3_ = bf16[80,960]{1,0:T(8,128)(2,1)S(1)} collective-permute-done((bf16[80,960]{1,0:T(8,128)(2,1)S(1)}, bf16[80,960]{1,0:T(8,128)(2,1)S(1)}, u32[]{:S(2)}, u32[]{:S(2)}) %collective-permute-start.3) | collective-permute-done | bytes 153632 | tf_op jit(solution)/shard_map/ppermute | solution.py:280
  36.7 1.9 %norm.1 = (bf16[512,1280]{1,0:T(8,128)(2,1)S(1)}, bf16[512,1280]{1,0:T(8,128)(2,1)S(1)}, f32[4,32,1280]{2,1,0:T(8,128)S(1)}, f32[4,32,128]{2,1,0:T(8,128)S(1)}) custom-call(s32[4]{0:T(128)S(1)} %copy-done.5, bf16[256,1280]{1,0:T(8,128)(2,1)S(1)} %copy-done.4, f32[1,1280]{1,0:T(1,128)S(1)} %reshape.12.gain_ref, f32[1,1280]{1,0:T(1,128)S(1)} %reshape.13.bias_ref, ...), custom_call_target="tpu_custom_call" | custom-call | flops 2000000000 | bytes 1000 | tf_op jit(solution)/shard_map/norm/pallas_call | solution.py:292
  38.7 1.4 %collective-permute-done.13.refs_1_ = bf16[80,960]{1,0:T(8,128)(2,1)S(1)} collective-permute-done((bf16[80,960]{1,0:T(8,128)(2,1)S(1)}, bf16[80,960]{1,0:T(8,128)(2,1)S(1)}, u32[]{:S(2)}, u32[]{:S(2)}) %collective-permute-start.13) | collective-permute-done | bytes 153632 | tf_op jit(solution)/shard_map/ppermute | solution.py:280
  40.1 4.2 %attend.1 = (bf16[4,32,320]{2,1,0:T(8,128)(2,1)S(1)}, bf16[4,32,320]{2,1,0:T(8,128)(2,1)S(1)}, bf16[2,4,32,320]{3,2,1,0:T(8,128)(2,1)S(1)}, bf16[512,960]{1,0:T(8,128)(2,1)S(1)}, bf16[1280,960]{1,0:T(8,128)(2,1)S(1)}) custom-call(s32[3]{0:T(128)S(1)} %pad_add_fusion.ids_ref, s32[4]{0:T(128)S(1)} %copy-done.3, ...), custom_call_target="tpu_custom_call", output_to_operand_aliasing={{4}: (2, {})} | custom-call | flops 10000000 | bytes 1000 | tf_op jit(solution)/shard_map/attend/pallas_call | solution.py:292
  44.4 1.6 %back.1 = (bf16[4,32,1280]{2,1,0:T(8,128)(2,1)S(1)}, bf16[4,32,1280]{2,1,0:T(8,128)(2,1)S(1)}, bf16[272,1280]{1,0:T(8,128)(2,1)S(1)}, f32[2,1280]{1,0:T(2,128)S(1)}) custom-call(bf16[512,960]{1,0:T(8,128)(2,1)S(1)} %get-tuple-element.44.gqkv_ref, bf16[512,1280]{1,0:T(8,128)(2,1)S(1)} %get-tuple-element.45.unit_ref, ...), custom_call_target="tpu_custom_call" | custom-call | flops 10000000 | bytes 1000 | tf_op jit(solution)/shard_map/back/pallas_call | solution.py:292
  46.1 1.6 %collective-permute-start.15 = (bf16[2,4,32,320]{3,2,1,0:T(8,128)(2,1)S(1)}, bf16[2,4,32,320]{3,2,1,0:T(8,128)(2,1)S(1)}, u32[]{:S(2)}, u32[]{:S(2)}) collective-permute-start(bf16[2,4,32,320]{3,2,1,0:T(8,128)(2,1)S(1)} %get-tuple-element.51), channel_id=1, source_target_pairs={{0,8},{4,12},{8,0},{12,4},{1,9},{5,13},{9,1},{13,5},{2,10},{6,14},... | collective-permute-start | bytes 491528 | tf_op jit(solution)/shard_map/ppermute | solution.py:280
  48.3 1.6 %collective-permute-start.20 = (bf16[4,32,1280]{2,1,0:T(8,128)(2,1)S(1)}, bf16[4,32,1280]{2,1,0:T(8,128)(2,1)S(1)}, u32[]{:S(2)}, u32[]{:S(2)}) collective-permute-start(bf16[4,32,1280]{2,1,0:T(8,128)(2,1)S(1)} %get-tuple-element.60), channel_id=1, source_target_pairs={{0,8},{4,12},{8,0},{12,4},{1,9},{5,13},{9,1},{13,5},{2,10},{6,14},... | collective-permute-start | bytes 983048 | tf_op jit(solution)/shard_map/ppermute | solution.py:280
  49.9 1.9 %collective-permute-start.18 = (f32[2,1280]{1,0:T(2,128)S(1)}, f32[2,1280]{1,0:T(2,128)S(1)}, u32[]{:S(2)}, u32[]{:S(2)}) collective-permute-start(f32[2,1280]{1,0:T(2,128)S(1)} %get-tuple-element.54.refs_0_), channel_id=1, source_target_pairs={{0,3},{1,2},{2,1},{3,0},{4,7},{5,6},{6,5},{7,4},{8,11},{9,10},{10,... | collective-permute-start | bytes 30728 | tf_op jit(solution)/shard_map/ppermute | solution.py:280
  52.5 1.8 %collective-permute-start.16 = (f32[2,1280]{1,0:T(2,128)S(1)}, f32[2,1280]{1,0:T(2,128)S(1)}, u32[]{:S(2)}, u32[]{:S(2)}) collective-permute-start(f32[2,1280]{1,0:T(2,128)S(1)} %get-tuple-element.54.refs_0_), channel_id=1, source_target_pairs={{0,1},{1,0},{2,3},{3,2},{4,5},{5,4},{6,7},{7,6},{8,9},{9,8},{10,11... | collective-permute-start | bytes 30728 | tf_op jit(solution)/shard_map/ppermute | solution.py:280
  57.9 1.4 %home.1 = (f32[4,32,1280]{2,1,0:T(8,128)S(1)}, bf16[4,32,1280]{2,1,0:T(8,128)(2,1)}) custom-call(s32[3]{0:T(128)S(1)} %pad_add_fusion.ids_ref, bf16[4,32,1280]{2,1,0:T(8,128)(2,1)S(1)} %get-tuple-element.47.stay_ref, bf16[272,1280]{1,0:T(8,128)(2,1)S(1)} %collective-permute-done.14.close_ref, bf16[4,32,320]{2,1,0:T(8,128)(2,1)S(1)} %get-tuple-element.49.own_ref, ...), custom_call_target="tpu_custom_call" | custom-call | flops 10000000 | bytes 1000 | tf_op jit(solution)/shard_map/home/pallas_call | solution.py:292
  60.6 1.6 %finish.1 = (bf16[4,32,1280]{2,1,0:T(8,128)(2,1)}, f32[2,1280]{1,0:T(2,128)}) custom-call(s32[3]{0:T(128)S(1)} %pad_add_fusion.ids_ref, s32[4]{0:T(128)S(1)} %copy-done.3, f32[4,32,1280]{2,1,0:T(8,128)S(1)} %get-tuple-element.57.unit_ref, f32[4,32,128]{2,1,0:T(8,128)S(1)} %get-tuple-element.58.inv_ref, f32[1,1280]{1,0:T(1,128)S(1)} %reshape.12.gain_ref, ...), custom_call_target="tpu_custom_call" | custom-call | flops 10000000 | bytes 1000 | tf_op jit(solution)/shard_map/finish/pallas_call | solution.py:292
  (52 shorter events, 13.4 us)
Async XLA Ops:
  2.6 9.1 %collective-permute-start.6 = (bf16[80,960]{1,0:T(8,128)(2,1)S(1)}, bf16[80,960]{1,0:T(8,128)(2,1)S(1)}, u32[]{:S(2)}, u32[]{:S(2)}) collective-permute-start(bf16[80,960]{1,0:T(8,128)(2,1)S(1)} %get-tuple-element.34.high_ref), channel_id=1, source_target_pairs={{0,1},{1,3},{3,2},{2,0},{4,5},{5,7},{7,6},{6,4},{8,9},{9,11},{11,1... | collective-permute-start | bytes 460808 | tf_op jit(solution)/shard_map/ppermute | solution.py:340
  5.7 27.7 %copy-start.6 = (f32[1280]{0:T(1024)S(1)}, f32[1280]{0:T(1024)}, u32[]{:S(2)}) copy-start(f32[1280]{0:T(1024)} %param.15) | copy-start | bytes 15364
  5.7 27.7 %copy-start.7 = (f32[1280]{0:T(1024)S(1)}, f32[1280]{0:T(1024)}, u32[]{:S(2)}) copy-start(f32[1280]{0:T(1024)} %param.16) | copy-start | bytes 15364
  5.7 8.7 %collective-permute-start = (bf16[80,960]{1,0:T(8,128)(2,1)S(1)}, bf16[80,960]{1,0:T(8,128)(2,1)S(1)}, u32[]{:S(2)}, u32[]{:S(2)}) collective-permute-start(bf16[80,960]{1,0:T(8,128)(2,1)S(1)} %get-tuple-element.33.low_ref), channel_id=1, source_target_pairs={{0,1},{1,3},{3,2},{2,0},{4,5},{5,7},{7,6},{6,4},{8,9},{9,11},{11,1... | collective-permute-start | bytes 460808 | tf_op jit(solution)/shard_map/ppermute | solution.py:340
  12.3 20.1 %collective-permute-start.10 = (bf16[4,32,1920]{2,1,0:T(8,128)(2,1)S(1)}, bf16[4,32,1920]{2,1,0:T(8,128)(2,1)S(1)}, u32[]{:S(2)}, u32[]{:S(2)}) collective-permute-start(bf16[4,32,1920]{2,1,0:T(8,128)(2,1)S(1)} %pack_across.1), channel_id=1, source_target_pairs={{0,8},{4,12},{8,0},{12,4},{1,9},{5,13},{9,1},{13,5},{2,10},{6,14},... | collective-permute-start | bytes 1474568 | tf_op jit(solution)/shard_map/ppermute | solution.py:280
  14.4 8.0 %collective-permute-start.2 = (bf16[80,960]{1,0:T(8,128)(2,1)S(1)}, bf16[80,960]{1,0:T(8,128)(2,1)S(1)}, u32[]{:S(2)}, u32[]{:S(2)}) collective-permute-start(bf16[80,960]{1,0:T(8,128)(2,1)S(1)} %collective-permute-done.refs_0_), channel_id=1, source_target_pairs={{0,1},{1,3},{3,2},{2,0},{4,5},{5,7},{7,6},{6,4},{8,9},{9,11},{11,1... | collective-permute-start | bytes 460808 | tf_op jit(solution)/shard_map/ppermute | solution.py:344
  15.2 7.2 %collective-permute-start.1 = (bf16[80,960]{1,0:T(8,128)(2,1)S(1)}, bf16[80,960]{1,0:T(8,128)(2,1)S(1)}, u32[]{:S(2)}, u32[]{:S(2)}) collective-permute-start(bf16[80,960]{1,0:T(8,128)(2,1)S(1)} %collective-permute-done.refs_0_), channel_id=1, source_target_pairs={{0,16},{16,0},{1,17},{17,1},{2,18},{18,2},{3,19},{19,3},{4,20},{20... | collective-permute-start | bytes 460808 | tf_op jit(solution)/shard_map/ppermute | solution.py:280
  16.7 10.1 %collective-permute-start.8 = (bf16[80,960]{1,0:T(8,128)(2,1)S(1)}, bf16[80,960]{1,0:T(8,128)(2,1)S(1)}, u32[]{:S(2)}, u32[]{:S(2)}) collective-permute-start(bf16[80,960]{1,0:T(8,128)(2,1)S(1)} %collective-permute-done.6.refs_6_), channel_id=1, source_target_pairs={{0,1},{1,3},{3,2},{2,0},{4,5},{5,7},{7,6},{6,4},{8,9},{9,11},{11,1... | collective-permute-start | bytes 460808 | tf_op jit(solution)/shard_map/ppermute | solution.py:344
  20.1 6.8 %collective-permute-start.7 = (bf16[80,960]{1,0:T(8,128)(2,1)S(1)}, bf16[80,960]{1,0:T(8,128)(2,1)S(1)}, u32[]{:S(2)}, u32[]{:S(2)}) collective-permute-start(bf16[80,960]{1,0:T(8,128)(2,1)S(1)} %collective-permute-done.6.refs_6_), channel_id=1, source_target_pairs={{0,16},{16,0},{1,17},{17,1},{2,18},{18,2},{3,19},{19,3},{4,20},{20... | collective-permute-start | bytes 460808 | tf_op jit(solution)/shard_map/ppermute | solution.py:280
  22.4 7.9 %collective-permute-start.4 = (bf16[80,960]{1,0:T(8,128)(2,1)S(1)}, bf16[80,960]{1,0:T(8,128)(2,1)S(1)}, u32[]{:S(2)}, u32[]{:S(2)}) collective-permute-start(bf16[80,960]{1,0:T(8,128)(2,1)S(1)} %collective-permute-done.2.refs_2_), channel_id=1, source_target_pairs={{0,1},{1,3},{3,2},{2,0},{4,5},{5,7},{7,6},{6,4},{8,9},{9,11},{11,1... | collective-permute-start | bytes 460808 | tf_op jit(solution)/shard_map/ppermute | solution.py:347
  25.3 7.1 %collective-permute-start.3 = (bf16[80,960]{1,0:T(8,128)(2,1)S(1)}, bf16[80,960]{1,0:T(8,128)(2,1)S(1)}, u32[]{:S(2)}, u32[]{:S(2)}) collective-permute-start(bf16[80,960]{1,0:T(8,128)(2,1)S(1)} %collective-permute-done.2.refs_2_), channel_id=1, source_target_pairs={{0,16},{16,0},{1,17},{17,1},{2,18},{18,2},{3,19},{19,3},{4,20},{20... | collective-permute-start | bytes 460808 | tf_op jit(solution)/shard_map/ppermute | solution.py:280
  26.9 6.6 %collective-permute-start.12 = (bf16[80,960]{1,0:T(8,128)(2,1)S(1)}, bf16[80,960]{1,0:T(8,128)(2,1)S(1)}, u32[]{:S(2)}, u32[]{:S(2)}) collective-permute-start(bf16[80,960]{1,0:T(8,128)(2,1)S(1)} %collective-permute-done.8.refs_8_), channel_id=1, source_target_pairs={{0,1},{1,3},{3,2},{2,0},{4,5},{5,7},{7,6},{6,4},{8,9},{9,11},{11,1... | collective-permute-start | bytes 460808 | tf_op jit(solution)/shard_map/ppermute | solution.py:347
  28.8 6.1 %collective-permute-start.9 = (bf16[80,960]{1,0:T(8,128)(2,1)S(1)}, bf16[80,960]{1,0:T(8,128)(2,1)S(1)}, u32[]{:S(2)}, u32[]{:S(2)}) collective-permute-start(bf16[80,960]{1,0:T(8,128)(2,1)S(1)} %collective-permute-done.8.refs_8_), channel_id=1, source_target_pairs={{0,16},{16,0},{1,17},{17,1},{2,18},{18,2},{3,19},{19,3},{4,20},{20... | collective-permute-start | bytes 460808 | tf_op jit(solution)/shard_map/ppermute | solution.py:280
  30.3 5.7 %collective-permute-start.5 = (bf16[80,960]{1,0:T(8,128)(2,1)S(1)}, bf16[80,960]{1,0:T(8,128)(2,1)S(1)}, u32[]{:S(2)}, u32[]{:S(2)}) collective-permute-start(bf16[80,960]{1,0:T(8,128)(2,1)S(1)} %collective-permute-done.4.refs_4_), channel_id=1, source_target_pairs={{0,16},{16,0},{1,17},{17,1},{2,18},{18,2},{3,19},{19,3},{4,20},{20... | collective-permute-start | bytes 460808 | tf_op jit(solution)/shard_map/ppermute | solution.py:280
  33.3 3.4 %collective-permute-start.11 = (bf16[4,32,3200]{2,1,0:T(8,128)(2,1)S(1)}, bf16[4,32,3200]{2,1,0:T(8,128)(2,1)S(1)}, u32[]{:S(2)}, u32[]{:S(2)}) collective-permute-start(bf16[4,32,3200]{2,1,0:T(8,128)(2,1)S(1)} %get-tuple-element.41), channel_id=1, source_target_pairs={{0,4},{4,0},{8,12},{12,8},{1,5},{5,1},{9,13},{13,9},{2,6},{6,2},{1... | collective-permute-start | bytes 2457608 | tf_op jit(solution)/shard_map/ppermute | solution.py:280
  33.5 6.6 %collective-permute-start.13 = (bf16[80,960]{1,0:T(8,128)(2,1)S(1)}, bf16[80,960]{1,0:T(8,128)(2,1)S(1)}, u32[]{:S(2)}, u32[]{:S(2)}) collective-permute-start(bf16[80,960]{1,0:T(8,128)(2,1)S(1)} %collective-permute-done.12.refs_0_), channel_id=1, source_target_pairs={{0,16},{16,0},{1,17},{17,1},{2,18},{18,2},{3,19},{19,3},{4,20},{20... | collective-permute-start | bytes 460808 | tf_op jit(solution)/shard_map/ppermute | solution.py:280
  46.0 2.2 %collective-permute-start.14 = (bf16[272,1280]{1,0:T(8,128)(2,1)S(1)}, bf16[272,1280]{1,0:T(8,128)(2,1)S(1)}, u32[]{:S(2)}, u32[]{:S(2)}) collective-permute-start(bf16[272,1280]{1,0:T(8,128)(2,1)S(1)} %get-tuple-element.48), channel_id=1, source_target_pairs={{0,4},{4,0},{8,12},{12,8},{1,5},{5,1},{9,13},{13,9},{2,6},{6,2},{1... | collective-permute-start | bytes 2088968 | tf_op jit(solution)/shard_map/ppermute | solution.py:280
  46.1 10.3 %collective-permute-start.15 = (bf16[2,4,32,320]{3,2,1,0:T(8,128)(2,1)S(1)}, bf16[2,4,32,320]{3,2,1,0:T(8,128)(2,1)S(1)}, u32[]{:S(2)}, u32[]{:S(2)}) collective-permute-start(bf16[2,4,32,320]{3,2,1,0:T(8,128)(2,1)S(1)} %get-tuple-element.51), channel_id=1, source_target_pairs={{0,8},{4,12},{8,0},{12,4},{1,9},{5,13},{9,1},{13,5},{2,10},{6,14},... | collective-permute-start | bytes 491528 | tf_op jit(solution)/shard_map/ppermute | solution.py:280
  48.3 12.3 %collective-permute-start.20 = (bf16[4,32,1280]{2,1,0:T(8,128)(2,1)S(1)}, bf16[4,32,1280]{2,1,0:T(8,128)(2,1)S(1)}, u32[]{:S(2)}, u32[]{:S(2)}) collective-permute-start(bf16[4,32,1280]{2,1,0:T(8,128)(2,1)S(1)} %get-tuple-element.60), channel_id=1, source_target_pairs={{0,8},{4,12},{8,0},{12,4},{1,9},{5,13},{9,1},{13,5},{2,10},{6,14},... | collective-permute-start | bytes 983048 | tf_op jit(solution)/shard_map/ppermute | solution.py:280
  49.9 5.5 %collective-permute-start.18 = (f32[2,1280]{1,0:T(2,128)S(1)}, f32[2,1280]{1,0:T(2,128)S(1)}, u32[]{:S(2)}, u32[]{:S(2)}) collective-permute-start(f32[2,1280]{1,0:T(2,128)S(1)} %get-tuple-element.54.refs_0_), channel_id=1, source_target_pairs={{0,3},{1,2},{2,1},{3,0},{4,7},{5,6},{6,5},{7,4},{8,11},{9,10},{10,... | collective-permute-start | bytes 30728 | tf_op jit(solution)/shard_map/ppermute | solution.py:280
  51.8 4.6 %collective-permute-start.17 = (f32[2,1280]{1,0:T(2,128)S(1)}, f32[2,1280]{1,0:T(2,128)S(1)}, u32[]{:S(2)}, u32[]{:S(2)}) collective-permute-start(f32[2,1280]{1,0:T(2,128)S(1)} %get-tuple-element.54.refs_0_), channel_id=1, source_target_pairs={{0,2},{1,3},{2,0},{3,1},{4,6},{5,7},{6,4},{7,5},{8,10},{9,11},{10,... | collective-permute-start | bytes 30728 | tf_op jit(solution)/shard_map/ppermute | solution.py:280
  52.5 3.8 %collective-permute-start.16 = (f32[2,1280]{1,0:T(2,128)S(1)}, f32[2,1280]{1,0:T(2,128)S(1)}, u32[]{:S(2)}, u32[]{:S(2)}) collective-permute-start(f32[2,1280]{1,0:T(2,128)S(1)} %get-tuple-element.54.refs_0_), channel_id=1, source_target_pairs={{0,1},{1,0},{2,3},{3,2},{4,5},{5,4},{6,7},{7,6},{8,9},{9,8},{10,11... | collective-permute-start | bytes 30728 | tf_op jit(solution)/shard_map/ppermute | solution.py:280
  56.4 1.5 %collective-permute-start.19 = (bf16[2,4,32,320]{3,2,1,0:T(8,128)(2,1)S(1)}, bf16[2,4,32,320]{3,2,1,0:T(8,128)(2,1)S(1)}, u32[]{:S(2)}, u32[]{:S(2)}) collective-permute-start(bf16[2,4,32,320]{3,2,1,0:T(8,128)(2,1)S(1)} %both.1), channel_id=1, source_target_pairs={{0,4},{4,0},{8,12},{12,8},{1,5},{5,1},{9,13},{13,9},{2,6},{6,2},{1... | collective-permute-start | bytes 491528 | tf_op jit(solution)/shard_map/ppermute | solution.py:280
  56.5 4.2 %collective-permute-start.21 = (f32[2,1280]{1,0:T(2,128)S(1)}, f32[2,1280]{1,0:T(2,128)S(1)}, u32[]{:S(2)}, u32[]{:S(2)}) collective-permute-start(f32[2,1280]{1,0:T(2,128)S(1)} %add.5.refs_0_), channel_id=1, source_target_pairs={{0,8},{4,12},{8,0},{12,4},{1,9},{5,13},{9,1},{13,5},{2,10},{6,14},... | collective-permute-start | bytes 30728 | tf_op jit(solution)/shard_map/ppermute | solution.py:280
  (6 other events, 35.4 us)

commit v13 on v12

--- a/solution.py
+++ b/solution.py
@@ -343,9 +343,8 @@
                 first = after(first, rest)
             second = lax.ppermute(first, "tile", ring)
             first_other = swapped(first, "rep", 1)
-            second = after(second, first_other)
             third = lax.ppermute(second, "tile", ring)
-            second_other = swapped(second, "rep", 1)
+            second_other = swapped(after(second, first_other), "rep", 1)
             third_other = swapped(third, "rep", 1)
             chains.append((first, first_other, second, second_other, third, third_other))
         first, later = chains[1][0], (chains[1][2], chains[0][3])

time: 62.4 us -> 62 us (level)
  starting transfers between devices: 32.1 us -> 30.4 us
  waiting for transfers between devices: 12.4 us -> 13.6 us
    ppermute x2, starting transfers between devices: 4.72 us -> 3.33 us  [local(): third = lax.ppermute(second, 'tile', ring)]
    ppermute x2, waiting for transfers between devices: 1.79 us -> 3.12 us  [local(): second = lax.ppermute(first, 'tile', ring)]
  transfers between devices with their start and end apart: 22 -> 22, of which waited for: 12 -> 14; matrix products, arithmetic and copies ran while one was open for 0% -> 0% of each run, Pallas kernels for 12% -> 12%
where the time goes in v13:
time: 62 us; the launch traced here: 61.8 us
  starting transfers between devices  30.4 us (49%)
  Pallas kernels  16.9 us (27%)
  waiting for transfers between devices  13.6 us (22%)
  between operations  0.85 us (1%)
    ppermute x16, starting transfers between devices, swapped(): lax.ppermute(array, axis, [(i, i ^ bits) for i in range(lax.axis_size(axi...  17.2 us
    pallas_call x13, Pallas kernels, call(): pl.pallas_call(kernel, out_shape=out_shape, in_specs=in_specs, out_specs=...  16.9 us
    ppermute x16, waiting for transfers between devices, swapped(): lax.ppermute(array, axis, [(i, i ^ bits) for i in range(lax.axis_size(axi...  8.38 us
    ppermute x2, starting transfers between devices, local(): first = lax.ppermute(held, 'tile', ring)  5.67 us
    ppermute x2, starting transfers between devices, local(): second = lax.ppermute(first, 'tile', ring)  4.22 us
    ppermute x2, starting transfers between devices, local(): third = lax.ppermute(second, 'tile', ring)  3.33 us
    ppermute x2, waiting for transfers between devices, local(): second = lax.ppermute(first, 'tile', ring)  3.12 us
    ppermute x2, waiting for transfers between devices, local(): first = lax.ppermute(held, 'tile', ring)  1.74 us
  transfers between devices with their start and end apart: 22, of which 14 were waited for; matrix products, arithmetic and copies ran while one was open for 0% of the time, Pallas kernels for 12%

profile of v13, /device:TPU:0, one launch (start us, length us, event | category | flops | bytes accessed | tf_op | source)
XLA Modules:
  0.0 61.8 jit_solution(11199323817327704774)
XLA Ops:
  0.7 1.9 %pick.2 = (bf16[80,960]{1,0:T(8,128)(2,1)S(1)}, bf16[80,960]{1,0:T(8,128)(2,1)S(1)}) custom-call(s32[3]{0:T(128)S(1)} %pad_add_fusion.ids_ref, bf16[320,3840]{1,0:T(8,128)(2,1)} %w_ref.3), custom_call_target="tpu_custom_call" | custom-call | flops 10000000 | bytes 1000 | tf_op jit(solution)/shard_map/pick/pallas_call | solution.py:292
  2.6 3.1 %collective-permute-start.6 = (bf16[80,960]{1,0:T(8,128)(2,1)S(1)}, bf16[80,960]{1,0:T(8,128)(2,1)S(1)}, u32[]{:S(2)}, u32[]{:S(2)}) collective-permute-start(bf16[80,960]{1,0:T(8,128)(2,1)S(1)} %get-tuple-element.34.high_ref), channel_id=1, source_target_pairs={{0,1},{1,3},{3,2},{2,0},{4,5},{5,7},{7,6},{6,4},{8,9},{9,11},{11,1... | collective-permute-start | bytes 460808 | tf_op jit(solution)/shard_map/ppermute | solution.py:340
  5.7 2.6 %collective-permute-start = (bf16[80,960]{1,0:T(8,128)(2,1)S(1)}, bf16[80,960]{1,0:T(8,128)(2,1)S(1)}, u32[]{:S(2)}, u32[]{:S(2)}) collective-permute-start(bf16[80,960]{1,0:T(8,128)(2,1)S(1)} %get-tuple-element.33.low_ref), channel_id=1, source_target_pairs={{0,1},{1,3},{3,2},{2,0},{4,5},{5,7},{7,6},{6,4},{8,9},{9,11},{11,1... | collective-permute-start | bytes 460808 | tf_op jit(solution)/shard_map/ppermute | solution.py:340
  8.3 1.9 %pick.3.rest_ref = bf16[160,960]{1,0:T(8,128)(2,1)S(1)} custom-call(s32[3]{0:T(128)S(1)} %pad_add_fusion.ids_ref, bf16[320,3840]{1,0:T(8,128)(2,1)} %w_ref.3), custom_call_target="tpu_custom_call" | custom-call | flops 10000000 | bytes 1000 | tf_op jit(solution)/shard_map/pick/pallas_call | solution.py:292
  10.1 1.6 %collective-permute-done.6.refs_6_ = bf16[80,960]{1,0:T(8,128)(2,1)S(1)} collective-permute-done((bf16[80,960]{1,0:T(8,128)(2,1)S(1)}, bf16[80,960]{1,0:T(8,128)(2,1)S(1)}, u32[]{:S(2)}, u32[]{:S(2)}) %collective-permute-start.6) | collective-permute-done | bytes 153632 | tf_op jit(solution)/shard_map/ppermute | solution.py:340
  12.3 1.9 %collective-permute-start.10 = (bf16[4,32,1920]{2,1,0:T(8,128)(2,1)S(1)}, bf16[4,32,1920]{2,1,0:T(8,128)(2,1)S(1)}, u32[]{:S(2)}, u32[]{:S(2)}) collective-permute-start(bf16[4,32,1920]{2,1,0:T(8,128)(2,1)S(1)} %pack_across.1), channel_id=1, source_target_pairs={{0,8},{4,12},{8,0},{12,4},{1,9},{5,13},{9,1},{13,5},{2,10},{6,14},... | collective-permute-start | bytes 1474568 | tf_op jit(solution)/shard_map/ppermute | solution.py:280
  15.2 1.5 %collective-permute-start.1 = (bf16[80,960]{1,0:T(8,128)(2,1)S(1)}, bf16[80,960]{1,0:T(8,128)(2,1)S(1)}, u32[]{:S(2)}, u32[]{:S(2)}) collective-permute-start(bf16[80,960]{1,0:T(8,128)(2,1)S(1)} %collective-permute-done.refs_0_), channel_id=1, source_target_pairs={{0,16},{16,0},{1,17},{17,1},{2,18},{18,2},{3,19},{19,3},{4,20},{20... | collective-permute-start | bytes 460808 | tf_op jit(solution)/shard_map/ppermute | solution.py:280
  16.7 3.4 %collective-permute-start.8 = (bf16[80,960]{1,0:T(8,128)(2,1)S(1)}, bf16[80,960]{1,0:T(8,128)(2,1)S(1)}, u32[]{:S(2)}, u32[]{:S(2)}) collective-permute-start(bf16[80,960]{1,0:T(8,128)(2,1)S(1)} %collective-permute-done.6.refs_6_), channel_id=1, source_target_pairs={{0,1},{1,3},{3,2},{2,0},{4,5},{5,7},{7,6},{6,4},{8,9},{9,11},{11,1... | collective-permute-start | bytes 460808 | tf_op jit(solution)/shard_map/ppermute | solution.py:344
  20.6 1.8 %collective-permute-done.2.refs_2_ = bf16[80,960]{1,0:T(8,128)(2,1)S(1)} collective-permute-done((bf16[80,960]{1,0:T(8,128)(2,1)S(1)}, bf16[80,960]{1,0:T(8,128)(2,1)S(1)}, u32[]{:S(2)}, u32[]{:S(2)}) %collective-permute-start.2) | collective-permute-done | bytes 153632 | tf_op jit(solution)/shard_map/ppermute | solution.py:344
  23.1 1.5 %collective-permute-start.3 = (bf16[80,960]{1,0:T(8,128)(2,1)S(1)}, bf16[80,960]{1,0:T(8,128)(2,1)S(1)}, u32[]{:S(2)}, u32[]{:S(2)}) collective-permute-start(bf16[80,960]{1,0:T(8,128)(2,1)S(1)} %collective-permute-done.2.refs_2_), channel_id=1, source_target_pairs={{0,16},{16,0},{1,17},{17,1},{2,18},{18,2},{3,19},{19,3},{4,20},{20... | collective-permute-start | bytes 460808 | tf_op jit(solution)/shard_map/ppermute | solution.py:280
  24.6 1.3 %collective-permute-done.8.refs_8_ = bf16[80,960]{1,0:T(8,128)(2,1)S(1)} collective-permute-done((bf16[80,960]{1,0:T(8,128)(2,1)S(1)}, bf16[80,960]{1,0:T(8,128)(2,1)S(1)}, u32[]{:S(2)}, u32[]{:S(2)}) %collective-permute-start.8) | collective-permute-done | bytes 153632 | tf_op jit(solution)/shard_map/ppermute | solution.py:344
  26.1 2.7 %collective-permute-start.12 = (bf16[80,960]{1,0:T(8,128)(2,1)S(1)}, bf16[80,960]{1,0:T(8,128)(2,1)S(1)}, u32[]{:S(2)}, u32[]{:S(2)}) collective-permute-start(bf16[80,960]{1,0:T(8,128)(2,1)S(1)} %collective-permute-done.8.refs_8_), channel_id=1, source_target_pairs={{0,1},{1,3},{3,2},{2,0},{4,5},{5,7},{7,6},{6,4},{8,9},{9,11},{11,1... | collective-permute-start | bytes 460808 | tf_op jit(solution)/shard_map/ppermute | solution.py:346
  28.8 1.5 %collective-permute-start.9 = (bf16[80,960]{1,0:T(8,128)(2,1)S(1)}, bf16[80,960]{1,0:T(8,128)(2,1)S(1)}, u32[]{:S(2)}, u32[]{:S(2)}) collective-permute-start(bf16[80,960]{1,0:T(8,128)(2,1)S(1)} %collective-permute-done.8.refs_8_), channel_id=1, source_target_pairs={{0,16},{16,0},{1,17},{17,1},{2,18},{18,2},{3,19},{19,3},{4,20},{20... | collective-permute-start | bytes 460808 | tf_op jit(solution)/shard_map/ppermute | solution.py:280
  32.3 1.2 %collective-permute-start.13 = (bf16[80,960]{1,0:T(8,128)(2,1)S(1)}, bf16[80,960]{1,0:T(8,128)(2,1)S(1)}, u32[]{:S(2)}, u32[]{:S(2)}) collective-permute-start(bf16[80,960]{1,0:T(8,128)(2,1)S(1)} %collective-permute-done.12.refs_0_), channel_id=1, source_target_pairs={{0,16},{16,0},{1,17},{17,1},{2,18},{18,2},{3,19},{19,3},{4,20},{20... | collective-permute-start | bytes 460808 | tf_op jit(solution)/shard_map/ppermute | solution.py:280
  34.1 2.4 %collective-permute-done.5.refs_5_ = bf16[80,960]{1,0:T(8,128)(2,1)S(1)} collective-permute-done((bf16[80,960]{1,0:T(8,128)(2,1)S(1)}, bf16[80,960]{1,0:T(8,128)(2,1)S(1)}, u32[]{:S(2)}, u32[]{:S(2)}) %collective-permute-start.5) | collective-permute-done | bytes 153632 | tf_op jit(solution)/shard_map/ppermute | solution.py:280
  37.3 1.9 %norm.1 = (bf16[512,1280]{1,0:T(8,128)(2,1)S(1)}, bf16[512,1280]{1,0:T(8,128)(2,1)S(1)}, f32[4,32,1280]{2,1,0:T(8,128)S(1)}, f32[4,32,128]{2,1,0:T(8,128)S(1)}) custom-call(s32[4]{0:T(128)S(1)} %copy-done.5, bf16[256,1280]{1,0:T(8,128)(2,1)S(1)} %copy-done.4, f32[1,1280]{1,0:T(1,128)S(1)} %reshape.12.gain_ref, f32[1,1280]{1,0:T(1,128)S(1)} %reshape.13.bias_ref, ...), custom_call_target="tpu_custom_call" | custom-call | flops 2000000000 | bytes 1000 | tf_op jit(solution)/shard_map/norm/pallas_call | solution.py:292
  39.4 4.2 %attend.1 = (bf16[4,32,320]{2,1,0:T(8,128)(2,1)S(1)}, bf16[4,32,320]{2,1,0:T(8,128)(2,1)S(1)}, bf16[2,4,32,320]{3,2,1,0:T(8,128)(2,1)S(1)}, bf16[512,960]{1,0:T(8,128)(2,1)S(1)}, bf16[1280,960]{1,0:T(8,128)(2,1)S(1)}) custom-call(s32[3]{0:T(128)S(1)} %pad_add_fusion.ids_ref, s32[4]{0:T(128)S(1)} %copy-done.3, ...), custom_call_target="tpu_custom_call", output_to_operand_aliasing={{4}: (2, {})} | custom-call | flops 10000000 | bytes 1000 | tf_op jit(solution)/shard_map/attend/pallas_call | solution.py:292
  43.6 1.6 %back.1 = (bf16[4,32,1280]{2,1,0:T(8,128)(2,1)S(1)}, bf16[4,32,1280]{2,1,0:T(8,128)(2,1)S(1)}, bf16[272,1280]{1,0:T(8,128)(2,1)S(1)}, f32[2,1280]{1,0:T(2,128)S(1)}) custom-call(bf16[512,960]{1,0:T(8,128)(2,1)S(1)} %get-tuple-element.44.gqkv_ref, bf16[512,1280]{1,0:T(8,128)(2,1)S(1)} %get-tuple-element.45.unit_ref, ...), custom_call_target="tpu_custom_call" | custom-call | flops 10000000 | bytes 1000 | tf_op jit(solution)/shard_map/back/pallas_call | solution.py:292
  45.3 1.6 %collective-permute-start.15 = (bf16[2,4,32,320]{3,2,1,0:T(8,128)(2,1)S(1)}, bf16[2,4,32,320]{3,2,1,0:T(8,128)(2,1)S(1)}, u32[]{:S(2)}, u32[]{:S(2)}) collective-permute-start(bf16[2,4,32,320]{3,2,1,0:T(8,128)(2,1)S(1)} %get-tuple-element.51), channel_id=1, source_target_pairs={{0,8},{4,12},{8,0},{12,4},{1,9},{5,13},{9,1},{13,5},{2,10},{6,14},... | collective-permute-start | bytes 491528 | tf_op jit(solution)/shard_map/ppermute | solution.py:280
  47.6 1.6 %collective-permute-start.20 = (bf16[4,32,1280]{2,1,0:T(8,128)(2,1)S(1)}, bf16[4,32,1280]{2,1,0:T(8,128)(2,1)S(1)}, u32[]{:S(2)}, u32[]{:S(2)}) collective-permute-start(bf16[4,32,1280]{2,1,0:T(8,128)(2,1)S(1)} %get-tuple-element.60), channel_id=1, source_target_pairs={{0,8},{4,12},{8,0},{12,4},{1,9},{5,13},{9,1},{13,5},{2,10},{6,14},... | collective-permute-start | bytes 983048 | tf_op jit(solution)/shard_map/ppermute | solution.py:280
  49.1 2.6 %collective-permute-start.18 = (f32[2,1280]{1,0:T(2,128)S(1)}, f32[2,1280]{1,0:T(2,128)S(1)}, u32[]{:S(2)}, u32[]{:S(2)}) collective-permute-start(f32[2,1280]{1,0:T(2,128)S(1)} %get-tuple-element.54.refs_0_), channel_id=1, source_target_pairs={{0,3},{1,2},{2,1},{3,0},{4,7},{5,6},{6,5},{7,4},{8,11},{9,10},{10,... | collective-permute-start | bytes 30728 | tf_op jit(solution)/shard_map/ppermute | solution.py:280
  54.6 1.7 %collective-permute-done.17.refs_2_ = f32[2,1280]{1,0:T(2,128)S(1)} collective-permute-done((f32[2,1280]{1,0:T(2,128)S(1)}, f32[2,1280]{1,0:T(2,128)S(1)}, u32[]{:S(2)}, u32[]{:S(2)}) %collective-permute-start.17) | collective-permute-done | bytes 10272 | tf_op jit(solution)/shard_map/ppermute | solution.py:280
  57.9 1.4 %home.1 = (f32[4,32,1280]{2,1,0:T(8,128)S(1)}, bf16[4,32,1280]{2,1,0:T(8,128)(2,1)}) custom-call(s32[3]{0:T(128)S(1)} %pad_add_fusion.ids_ref, bf16[4,32,1280]{2,1,0:T(8,128)(2,1)S(1)} %get-tuple-element.47.stay_ref, bf16[272,1280]{1,0:T(8,128)(2,1)S(1)} %collective-permute-done.14.close_ref, bf16[4,32,320]{2,1,0:T(8,128)(2,1)S(1)} %get-tuple-element.49.own_ref, ...), custom_call_target="tpu_custom_call" | custom-call | flops 10000000 | bytes 1000 | tf_op jit(solution)/shard_map/home/pallas_call | solution.py:292
  60.2 1.6 %finish.1 = (bf16[4,32,1280]{2,1,0:T(8,128)(2,1)}, f32[2,1280]{1,0:T(2,128)}) custom-call(s32[3]{0:T(128)S(1)} %pad_add_fusion.ids_ref, s32[4]{0:T(128)S(1)} %copy-done.3, f32[4,32,1280]{2,1,0:T(8,128)S(1)} %get-tuple-element.57.unit_ref, f32[4,32,128]{2,1,0:T(8,128)S(1)} %get-tuple-element.58.inv_ref, f32[1,1280]{1,0:T(1,128)S(1)} %reshape.12.gain_ref, ...), custom_call_target="tpu_custom_call" | custom-call | flops 10000000 | bytes 1000 | tf_op jit(solution)/shard_map/finish/pallas_call | solution.py:292
  (52 shorter events, 12.4 us)
Async XLA Ops:
  2.6 9.1 %collective-permute-start.6 = (bf16[80,960]{1,0:T(8,128)(2,1)S(1)}, bf16[80,960]{1,0:T(8,128)(2,1)S(1)}, u32[]{:S(2)}, u32[]{:S(2)}) collective-permute-start(bf16[80,960]{1,0:T(8,128)(2,1)S(1)} %get-tuple-element.34.high_ref), channel_id=1, source_target_pairs={{0,1},{1,3},{3,2},{2,0},{4,5},{5,7},{7,6},{6,4},{8,9},{9,11},{11,1... | collective-permute-start | bytes 460808 | tf_op jit(solution)/shard_map/ppermute | solution.py:340
  5.7 26.3 %copy-start.6 = (f32[1280]{0:T(1024)S(1)}, f32[1280]{0:T(1024)}, u32[]{:S(2)}) copy-start(f32[1280]{0:T(1024)} %param.15) | copy-start | bytes 15364
  5.7 26.3 %copy-start.7 = (f32[1280]{0:T(1024)S(1)}, f32[1280]{0:T(1024)}, u32[]{:S(2)}) copy-start(f32[1280]{0:T(1024)} %param.16) | copy-start | bytes 15364
  5.7 8.7 %collective-permute-start = (bf16[80,960]{1,0:T(8,128)(2,1)S(1)}, bf16[80,960]{1,0:T(8,128)(2,1)S(1)}, u32[]{:S(2)}, u32[]{:S(2)}) collective-permute-start(bf16[80,960]{1,0:T(8,128)(2,1)S(1)} %get-tuple-element.33.low_ref), channel_id=1, source_target_pairs={{0,1},{1,3},{3,2},{2,0},{4,5},{5,7},{7,6},{6,4},{8,9},{9,11},{11,1... | collective-permute-start | bytes 460808 | tf_op jit(solution)/shard_map/ppermute | solution.py:340
  12.3 18.7 %collective-permute-start.10 = (bf16[4,32,1920]{2,1,0:T(8,128)(2,1)S(1)}, bf16[4,32,1920]{2,1,0:T(8,128)(2,1)S(1)}, u32[]{:S(2)}, u32[]{:S(2)}) collective-permute-start(bf16[4,32,1920]{2,1,0:T(8,128)(2,1)S(1)} %pack_across.1), channel_id=1, source_target_pairs={{0,8},{4,12},{8,0},{12,4},{1,9},{5,13},{9,1},{13,5},{2,10},{6,14},... | collective-permute-start | bytes 1474568 | tf_op jit(solution)/shard_map/ppermute | solution.py:280
  14.4 8.0 %collective-permute-start.2 = (bf16[80,960]{1,0:T(8,128)(2,1)S(1)}, bf16[80,960]{1,0:T(8,128)(2,1)S(1)}, u32[]{:S(2)}, u32[]{:S(2)}) collective-permute-start(bf16[80,960]{1,0:T(8,128)(2,1)S(1)} %collective-permute-done.refs_0_), channel_id=1, source_target_pairs={{0,1},{1,3},{3,2},{2,0},{4,5},{5,7},{7,6},{6,4},{8,9},{9,11},{11,1... | collective-permute-start | bytes 460808 | tf_op jit(solution)/shard_map/ppermute | solution.py:344
  15.2 7.9 %collective-permute-start.1 = (bf16[80,960]{1,0:T(8,128)(2,1)S(1)}, bf16[80,960]{1,0:T(8,128)(2,1)S(1)}, u32[]{:S(2)}, u32[]{:S(2)}) collective-permute-start(bf16[80,960]{1,0:T(8,128)(2,1)S(1)} %collective-permute-done.refs_0_), channel_id=1, source_target_pairs={{0,16},{16,0},{1,17},{17,1},{2,18},{18,2},{3,19},{19,3},{4,20},{20... | collective-permute-start | bytes 460808 | tf_op jit(solution)/shard_map/ppermute | solution.py:280
  16.7 9.2 %collective-permute-start.8 = (bf16[80,960]{1,0:T(8,128)(2,1)S(1)}, bf16[80,960]{1,0:T(8,128)(2,1)S(1)}, u32[]{:S(2)}, u32[]{:S(2)}) collective-permute-start(bf16[80,960]{1,0:T(8,128)(2,1)S(1)} %collective-permute-done.6.refs_6_), channel_id=1, source_target_pairs={{0,1},{1,3},{3,2},{2,0},{4,5},{5,7},{7,6},{6,4},{8,9},{9,11},{11,1... | collective-permute-start | bytes 460808 | tf_op jit(solution)/shard_map/ppermute | solution.py:344
  20.1 6.0 %collective-permute-start.7 = (bf16[80,960]{1,0:T(8,128)(2,1)S(1)}, bf16[80,960]{1,0:T(8,128)(2,1)S(1)}, u32[]{:S(2)}, u32[]{:S(2)}) collective-permute-start(bf16[80,960]{1,0:T(8,128)(2,1)S(1)} %collective-permute-done.6.refs_6_), channel_id=1, source_target_pairs={{0,16},{16,0},{1,17},{17,1},{2,18},{18,2},{3,19},{19,3},{4,20},{20... | collective-permute-start | bytes 460808 | tf_op jit(solution)/shard_map/ppermute | solution.py:280
  22.4 7.9 %collective-permute-start.4 = (bf16[80,960]{1,0:T(8,128)(2,1)S(1)}, bf16[80,960]{1,0:T(8,128)(2,1)S(1)}, u32[]{:S(2)}, u32[]{:S(2)}) collective-permute-start(bf16[80,960]{1,0:T(8,128)(2,1)S(1)} %collective-permute-done.2.refs_2_), channel_id=1, source_target_pairs={{0,1},{1,3},{3,2},{2,0},{4,5},{5,7},{7,6},{6,4},{8,9},{9,11},{11,1... | collective-permute-start | bytes 460808 | tf_op jit(solution)/shard_map/ppermute | solution.py:346
  23.1 7.9 %collective-permute-start.3 = (bf16[80,960]{1,0:T(8,128)(2,1)S(1)}, bf16[80,960]{1,0:T(8,128)(2,1)S(1)}, u32[]{:S(2)}, u32[]{:S(2)}) collective-permute-start(bf16[80,960]{1,0:T(8,128)(2,1)S(1)} %collective-permute-done.2.refs_2_), channel_id=1, source_target_pairs={{0,16},{16,0},{1,17},{17,1},{2,18},{18,2},{3,19},{19,3},{4,20},{20... | collective-permute-start | bytes 460808 | tf_op jit(solution)/shard_map/ppermute | solution.py:280
  26.1 6.2 %collective-permute-start.12 = (bf16[80,960]{1,0:T(8,128)(2,1)S(1)}, bf16[80,960]{1,0:T(8,128)(2,1)S(1)}, u32[]{:S(2)}, u32[]{:S(2)}) collective-permute-start(bf16[80,960]{1,0:T(8,128)(2,1)S(1)} %collective-permute-done.8.refs_8_), channel_id=1, source_target_pairs={{0,1},{1,3},{3,2},{2,0},{4,5},{5,7},{7,6},{6,4},{8,9},{9,11},{11,1... | collective-permute-start | bytes 460808 | tf_op jit(solution)/shard_map/ppermute | solution.py:346
  28.8 5.3 %collective-permute-start.9 = (bf16[80,960]{1,0:T(8,128)(2,1)S(1)}, bf16[80,960]{1,0:T(8,128)(2,1)S(1)}, u32[]{:S(2)}, u32[]{:S(2)}) collective-permute-start(bf16[80,960]{1,0:T(8,128)(2,1)S(1)} %collective-permute-done.8.refs_8_), channel_id=1, source_target_pairs={{0,16},{16,0},{1,17},{17,1},{2,18},{18,2},{3,19},{19,3},{4,20},{20... | collective-permute-start | bytes 460808 | tf_op jit(solution)/shard_map/ppermute | solution.py:280
  30.3 6.2 %collective-permute-start.5 = (bf16[80,960]{1,0:T(8,128)(2,1)S(1)}, bf16[80,960]{1,0:T(8,128)(2,1)S(1)}, u32[]{:S(2)}, u32[]{:S(2)}) collective-permute-start(bf16[80,960]{1,0:T(8,128)(2,1)S(1)} %collective-permute-done.4.refs_4_), channel_id=1, source_target_pairs={{0,16},{16,0},{1,17},{17,1},{2,18},{18,2},{3,19},{19,3},{4,20},{20... | collective-permute-start | bytes 460808 | tf_op jit(solution)/shard_map/ppermute | solution.py:280
  31.8 5.4 %collective-permute-start.11 = (bf16[4,32,3200]{2,1,0:T(8,128)(2,1)S(1)}, bf16[4,32,3200]{2,1,0:T(8,128)(2,1)S(1)}, u32[]{:S(2)}, u32[]{:S(2)}) collective-permute-start(bf16[4,32,3200]{2,1,0:T(8,128)(2,1)S(1)} %get-tuple-element.41), channel_id=1, source_target_pairs={{0,4},{4,0},{8,12},{12,8},{1,5},{5,1},{9,13},{13,9},{2,6},{6,2},{1... | collective-permute-start | bytes 2457608 | tf_op jit(solution)/shard_map/ppermute | solution.py:280
  32.3 7.0 %collective-permute-start.13 = (bf16[80,960]{1,0:T(8,128)(2,1)S(1)}, bf16[80,960]{1,0:T(8,128)(2,1)S(1)}, u32[]{:S(2)}, u32[]{:S(2)}) collective-permute-start(bf16[80,960]{1,0:T(8,128)(2,1)S(1)} %collective-permute-done.12.refs_0_), channel_id=1, source_target_pairs={{0,16},{16,0},{1,17},{17,1},{2,18},{18,2},{3,19},{19,3},{4,20},{20... | collective-permute-start | bytes 460808 | tf_op jit(solution)/shard_map/ppermute | solution.py:280
  45.3 2.2 %collective-permute-start.14 = (bf16[272,1280]{1,0:T(8,128)(2,1)S(1)}, bf16[272,1280]{1,0:T(8,128)(2,1)S(1)}, u32[]{:S(2)}, u32[]{:S(2)}) collective-permute-start(bf16[272,1280]{1,0:T(8,128)(2,1)S(1)} %get-tuple-element.48), channel_id=1, source_target_pairs={{0,4},{4,0},{8,12},{12,8},{1,5},{5,1},{9,13},{13,9},{2,6},{6,2},{1... | collective-permute-start | bytes 2088968 | tf_op jit(solution)/shard_map/ppermute | solution.py:280
  45.3 11.0 %collective-permute-start.15 = (bf16[2,4,32,320]{3,2,1,0:T(8,128)(2,1)S(1)}, bf16[2,4,32,320]{3,2,1,0:T(8,128)(2,1)S(1)}, u32[]{:S(2)}, u32[]{:S(2)}) collective-permute-start(bf16[2,4,32,320]{3,2,1,0:T(8,128)(2,1)S(1)} %get-tuple-element.51), channel_id=1, source_target_pairs={{0,8},{4,12},{8,0},{12,4},{1,9},{5,13},{9,1},{13,5},{2,10},{6,14},... | collective-permute-start | bytes 491528 | tf_op jit(solution)/shard_map/ppermute | solution.py:280
  47.6 12.6 %collective-permute-start.20 = (bf16[4,32,1280]{2,1,0:T(8,128)(2,1)S(1)}, bf16[4,32,1280]{2,1,0:T(8,128)(2,1)S(1)}, u32[]{:S(2)}, u32[]{:S(2)}) collective-permute-start(bf16[4,32,1280]{2,1,0:T(8,128)(2,1)S(1)} %get-tuple-element.60), channel_id=1, source_target_pairs={{0,8},{4,12},{8,0},{12,4},{1,9},{5,13},{9,1},{13,5},{2,10},{6,14},... | collective-permute-start | bytes 983048 | tf_op jit(solution)/shard_map/ppermute | solution.py:280
  49.1 5.5 %collective-permute-start.18 = (f32[2,1280]{1,0:T(2,128)S(1)}, f32[2,1280]{1,0:T(2,128)S(1)}, u32[]{:S(2)}, u32[]{:S(2)}) collective-permute-start(f32[2,1280]{1,0:T(2,128)S(1)} %get-tuple-element.54.refs_0_), channel_id=1, source_target_pairs={{0,3},{1,2},{2,1},{3,0},{4,7},{5,6},{6,5},{7,4},{8,11},{9,10},{10,... | collective-permute-start | bytes 30728 | tf_op jit(solution)/shard_map/ppermute | solution.py:280
  51.8 4.6 %collective-permute-start.17 = (f32[2,1280]{1,0:T(2,128)S(1)}, f32[2,1280]{1,0:T(2,128)S(1)}, u32[]{:S(2)}, u32[]{:S(2)}) collective-permute-start(f32[2,1280]{1,0:T(2,128)S(1)} %get-tuple-element.54.refs_0_), channel_id=1, source_target_pairs={{0,2},{1,3},{2,0},{3,1},{4,6},{5,7},{6,4},{7,5},{8,10},{9,11},{10,... | collective-permute-start | bytes 30728 | tf_op jit(solution)/shard_map/ppermute | solution.py:280
  52.5 3.8 %collective-permute-start.16 = (f32[2,1280]{1,0:T(2,128)S(1)}, f32[2,1280]{1,0:T(2,128)S(1)}, u32[]{:S(2)}, u32[]{:S(2)}) collective-permute-start(f32[2,1280]{1,0:T(2,128)S(1)} %get-tuple-element.54.refs_0_), channel_id=1, source_target_pairs={{0,1},{1,0},{2,3},{3,2},{4,5},{5,4},{6,7},{7,6},{8,9},{9,8},{10,11... | collective-permute-start | bytes 30728 | tf_op jit(solution)/shard_map/ppermute | solution.py:280
  56.4 1.5 %collective-permute-start.19 = (bf16[2,4,32,320]{3,2,1,0:T(8,128)(2,1)S(1)}, bf16[2,4,32,320]{3,2,1,0:T(8,128)(2,1)S(1)}, u32[]{:S(2)}, u32[]{:S(2)}) collective-permute-start(bf16[2,4,32,320]{3,2,1,0:T(8,128)(2,1)S(1)} %both.1), channel_id=1, source_target_pairs={{0,4},{4,0},{8,12},{12,8},{1,5},{5,1},{9,13},{13,9},{2,6},{6,2},{1... | collective-permute-start | bytes 491528 | tf_op jit(solution)/shard_map/ppermute | solution.py:280
  56.5 3.7 %collective-permute-start.21 = (f32[2,1280]{1,0:T(2,128)S(1)}, f32[2,1280]{1,0:T(2,128)S(1)}, u32[]{:S(2)}, u32[]{:S(2)}) collective-permute-start(f32[2,1280]{1,0:T(2,128)S(1)} %add.5.refs_0_), channel_id=1, source_target_pairs={{0,8},{4,12},{8,0},{12,4},{1,9},{5,13},{9,1},{13,5},{2,10},{6,14},... | collective-permute-start | bytes 30728 | tf_op jit(solution)/shard_map/ppermute | solution.py:280
  (6 other events, 36.9 us)

commit v14 on v12

--- a/solution.py
+++ b/solution.py
@@ -343,12 +343,11 @@
                 first = after(first, rest)
             second = lax.ppermute(first, "tile", ring)
             first_other = swapped(first, "rep", 1)
-            second = after(second, first_other)
             third = lax.ppermute(second, "tile", ring)
             second_other = swapped(second, "rep", 1)
             third_other = swapped(third, "rep", 1)
             chains.append((first, first_other, second, second_other, third, third_other))
-        first, later = chains[1][0], (chains[1][2], chains[0][3])
+        first, later = chains[1][0], (chains[1][2], chains[0][3], chains[0][1], chains[1][1])
     else:
         first, later = ids, ()
 

time: 62.4 us -> 62 us (level)
  starting transfers between devices: 32.1 us -> 29.4 us
  waiting for transfers between devices: 12.4 us -> 14.6 us
    ppermute x2, starting transfers between devices: 4.72 us -> 2.71 us  [local(): third = lax.ppermute(second, 'tile', ring)]
    ppermute x2, waiting for transfers between devices: 0.01 us -> 1.45 us  [local(): third = lax.ppermute(second, 'tile', ring)]
    ppermute x2, waiting for transfers between devices: 1.79 us -> 3.12 us  [local(): second = lax.ppermute(first, 'tile', ring)]
    ppermute x16, starting transfers between devices: 17.4 us -> 16.8 us  [swapped(): lax.ppermute(array, axis, [(i, i ^ bits) for i in range(lax.axis_size(axi...]
  transfers between devices with their start and end apart: 22 -> 22, of which waited for: 12 -> 13; matrix products, arithmetic and copies ran while one was open for 0% -> 0% of each run, Pallas kernels for 12% -> 12%
where the time goes in v14:
time: 62 us; the launch traced here: 61.8 us
  starting transfers between devices  29.4 us (47%)
  Pallas kernels  16.9 us (27%)
  waiting for transfers between devices  14.6 us (24%)
  between operations  0.85 us (1%)
    pallas_call x13, Pallas kernels, call(): pl.pallas_call(kernel, out_shape=out_shape, in_specs=in_specs, out_specs=...  16.9 us
    ppermute x16, starting transfers between devices, swapped(): lax.ppermute(array, axis, [(i, i ^ bits) for i in range(lax.axis_size(axi...  16.8 us
    ppermute x16, waiting for transfers between devices, swapped(): lax.ppermute(array, axis, [(i, i ^ bits) for i in range(lax.axis_size(axi...  8.27 us
    ppermute x2, starting transfers between devices, local(): first = lax.ppermute(held, 'tile', ring)  5.67 us
    ppermute x2, starting transfers between devices, local(): second = lax.ppermute(first, 'tile', ring)  4.22 us
    ppermute x2, waiting for transfers between devices, local(): second = lax.ppermute(first, 'tile', ring)  3.12 us
    ppermute x2, starting transfers between devices, local(): third = lax.ppermute(second, 'tile', ring)  2.71 us
    ppermute x2, waiting for transfers between devices, local(): first = lax.ppermute(held, 'tile', ring)  1.74 us
  transfers between devices with their start and end apart: 22, of which 13 were waited for; matrix products, arithmetic and copies ran while one was open for 0% of the time, Pallas kernels for 12%

profile of v14, /device:TPU:0, one launch (start us, length us, event | category | flops | bytes accessed | tf_op | source)
XLA Modules:
  0.0 61.8 jit_solution(7267690488434041726)
XLA Ops:
  0.7 1.9 %pick.2 = (bf16[80,960]{1,0:T(8,128)(2,1)S(1)}, bf16[80,960]{1,0:T(8,128)(2,1)S(1)}) custom-call(s32[3]{0:T(128)S(1)} %pad_add_fusion.ids_ref, bf16[320,3840]{1,0:T(8,128)(2,1)} %w_ref.3), custom_call_target="tpu_custom_call" | custom-call | flops 10000000 | bytes 1000 | tf_op jit(solution)/shard_map/pick/pallas_call | solution.py:292
  2.6 3.1 %collective-permute-start.6 = (bf16[80,960]{1,0:T(8,128)(2,1)S(1)}, bf16[80,960]{1,0:T(8,128)(2,1)S(1)}, u32[]{:S(2)}, u32[]{:S(2)}) collective-permute-start(bf16[80,960]{1,0:T(8,128)(2,1)S(1)} %get-tuple-element.32.high_ref), channel_id=1, source_target_pairs={{0,1},{1,3},{3,2},{2,0},{4,5},{5,7},{7,6},{6,4},{8,9},{9,11},{11,1... | collective-permute-start | bytes 460808 | tf_op jit(solution)/shard_map/ppermute | solution.py:340
  5.7 2.6 %collective-permute-start = (bf16[80,960]{1,0:T(8,128)(2,1)S(1)}, bf16[80,960]{1,0:T(8,128)(2,1)S(1)}, u32[]{:S(2)}, u32[]{:S(2)}) collective-permute-start(bf16[80,960]{1,0:T(8,128)(2,1)S(1)} %get-tuple-element.31.low_ref), channel_id=1, source_target_pairs={{0,1},{1,3},{3,2},{2,0},{4,5},{5,7},{7,6},{6,4},{8,9},{9,11},{11,1... | collective-permute-start | bytes 460808 | tf_op jit(solution)/shard_map/ppermute | solution.py:340
  8.3 1.9 %pick.3.rest_ref = bf16[160,960]{1,0:T(8,128)(2,1)S(1)} custom-call(s32[3]{0:T(128)S(1)} %pad_add_fusion.ids_ref, bf16[320,3840]{1,0:T(8,128)(2,1)} %w_ref.3), custom_call_target="tpu_custom_call" | custom-call | flops 10000000 | bytes 1000 | tf_op jit(solution)/shard_map/pick/pallas_call | solution.py:292
  10.1 1.6 %collective-permute-done.6.refs_6_ = bf16[80,960]{1,0:T(8,128)(2,1)S(1)} collective-permute-done((bf16[80,960]{1,0:T(8,128)(2,1)S(1)}, bf16[80,960]{1,0:T(8,128)(2,1)S(1)}, u32[]{:S(2)}, u32[]{:S(2)}) %collective-permute-start.6) | collective-permute-done | bytes 153632 | tf_op jit(solution)/shard_map/ppermute | solution.py:340
  12.3 1.9 %collective-permute-start.10 = (bf16[4,32,1920]{2,1,0:T(8,128)(2,1)S(1)}, bf16[4,32,1920]{2,1,0:T(8,128)(2,1)S(1)}, u32[]{:S(2)}, u32[]{:S(2)}) collective-permute-start(bf16[4,32,1920]{2,1,0:T(8,128)(2,1)S(1)} %pack_across.1), channel_id=1, source_target_pairs={{0,8},{4,12},{8,0},{12,4},{1,9},{5,13},{9,1},{13,5},{2,10},{6,14},... | collective-permute-start | bytes 1474568 | tf_op jit(solution)/shard_map/ppermute | solution.py:280
  15.2 1.5 %collective-permute-start.1 = (bf16[80,960]{1,0:T(8,128)(2,1)S(1)}, bf16[80,960]{1,0:T(8,128)(2,1)S(1)}, u32[]{:S(2)}, u32[]{:S(2)}) collective-permute-start(bf16[80,960]{1,0:T(8,128)(2,1)S(1)} %collective-permute-done.refs_0_), channel_id=1, source_target_pairs={{0,16},{16,0},{1,17},{17,1},{2,18},{18,2},{3,19},{19,3},{4,20},{20... | collective-permute-start | bytes 460808 | tf_op jit(solution)/shard_map/ppermute | solution.py:280
  16.7 3.4 %collective-permute-start.8 = (bf16[80,960]{1,0:T(8,128)(2,1)S(1)}, bf16[80,960]{1,0:T(8,128)(2,1)S(1)}, u32[]{:S(2)}, u32[]{:S(2)}) collective-permute-start(bf16[80,960]{1,0:T(8,128)(2,1)S(1)} %collective-permute-done.6.refs_6_), channel_id=1, source_target_pairs={{0,1},{1,3},{3,2},{2,0},{4,5},{5,7},{7,6},{6,4},{8,9},{9,11},{11,1... | collective-permute-start | bytes 460808 | tf_op jit(solution)/shard_map/ppermute | solution.py:344
  20.6 1.8 %collective-permute-done.2.refs_2_ = bf16[80,960]{1,0:T(8,128)(2,1)S(1)} collective-permute-done((bf16[80,960]{1,0:T(8,128)(2,1)S(1)}, bf16[80,960]{1,0:T(8,128)(2,1)S(1)}, u32[]{:S(2)}, u32[]{:S(2)}) %collective-permute-start.2) | collective-permute-done | bytes 153632 | tf_op jit(solution)/shard_map/ppermute | solution.py:344
  23.1 1.5 %collective-permute-start.3 = (bf16[80,960]{1,0:T(8,128)(2,1)S(1)}, bf16[80,960]{1,0:T(8,128)(2,1)S(1)}, u32[]{:S(2)}, u32[]{:S(2)}) collective-permute-start(bf16[80,960]{1,0:T(8,128)(2,1)S(1)} %collective-permute-done.2.refs_2_), channel_id=1, source_target_pairs={{0,16},{16,0},{1,17},{17,1},{2,18},{18,2},{3,19},{19,3},{4,20},{20... | collective-permute-start | bytes 460808 | tf_op jit(solution)/shard_map/ppermute | solution.py:280
  24.6 1.3 %collective-permute-done.8.refs_8_ = bf16[80,960]{1,0:T(8,128)(2,1)S(1)} collective-permute-done((bf16[80,960]{1,0:T(8,128)(2,1)S(1)}, bf16[80,960]{1,0:T(8,128)(2,1)S(1)}, u32[]{:S(2)}, u32[]{:S(2)}) %collective-permute-start.8) | collective-permute-done | bytes 153632 | tf_op jit(solution)/shard_map/ppermute | solution.py:344
  25.9 2.1 %collective-permute-start.12 = (bf16[80,960]{1,0:T(8,128)(2,1)S(1)}, bf16[80,960]{1,0:T(8,128)(2,1)S(1)}, u32[]{:S(2)}, u32[]{:S(2)}) collective-permute-start(bf16[80,960]{1,0:T(8,128)(2,1)S(1)} %collective-permute-done.8.refs_8_), channel_id=1, source_target_pairs={{0,1},{1,3},{3,2},{2,0},{4,5},{5,7},{7,6},{6,4},{8,9},{9,11},{11,1... | collective-permute-start | bytes 460808 | tf_op jit(solution)/shard_map/ppermute | solution.py:346
  29.5 1.2 %collective-permute-start.5 = (bf16[80,960]{1,0:T(8,128)(2,1)S(1)}, bf16[80,960]{1,0:T(8,128)(2,1)S(1)}, u32[]{:S(2)}, u32[]{:S(2)}) collective-permute-start(bf16[80,960]{1,0:T(8,128)(2,1)S(1)} %collective-permute-done.4.refs_4_), channel_id=1, source_target_pairs={{0,16},{16,0},{1,17},{17,1},{2,18},{18,2},{3,19},{19,3},{4,20},{20... | collective-permute-start | bytes 460808 | tf_op jit(solution)/shard_map/ppermute | solution.py:280
  32.2 1.4 %collective-permute-start.13 = (bf16[80,960]{1,0:T(8,128)(2,1)S(1)}, bf16[80,960]{1,0:T(8,128)(2,1)S(1)}, u32[]{:S(2)}, u32[]{:S(2)}) collective-permute-start(bf16[80,960]{1,0:T(8,128)(2,1)S(1)} %collective-permute-done.12.refs_0_), channel_id=1, source_target_pairs={{0,16},{16,0},{1,17},{17,1},{2,18},{18,2},{3,19},{19,3},{4,20},{20... | collective-permute-start | bytes 460808 | tf_op jit(solution)/shard_map/ppermute | solution.py:280
  33.5 1.6 %collective-permute-done.5.refs_5_ = bf16[80,960]{1,0:T(8,128)(2,1)S(1)} collective-permute-done((bf16[80,960]{1,0:T(8,128)(2,1)S(1)}, bf16[80,960]{1,0:T(8,128)(2,1)S(1)}, u32[]{:S(2)}, u32[]{:S(2)}) %collective-permute-start.5) | collective-permute-done | bytes 153632 | tf_op jit(solution)/shard_map/ppermute | solution.py:280
  35.9 1.9 %norm.1 = (bf16[512,1280]{1,0:T(8,128)(2,1)S(1)}, bf16[512,1280]{1,0:T(8,128)(2,1)S(1)}, f32[4,32,1280]{2,1,0:T(8,128)S(1)}, f32[4,32,128]{2,1,0:T(8,128)S(1)}) custom-call(s32[4]{0:T(128)S(1)} %copy-done.5, bf16[256,1280]{1,0:T(8,128)(2,1)S(1)} %copy-done.4, f32[1,1280]{1,0:T(1,128)S(1)} %reshape.12.gain_ref, f32[1,1280]{1,0:T(1,128)S(1)} %reshape.13.bias_ref, ...), custom_call_target="tpu_custom_call" | custom-call | flops 2000000000 | bytes 1000 | tf_op jit(solution)/shard_map/norm/pallas_call | solution.py:292
  38.6 4.2 %attend.1 = (bf16[4,32,320]{2,1,0:T(8,128)(2,1)S(1)}, bf16[4,32,320]{2,1,0:T(8,128)(2,1)S(1)}, bf16[2,4,32,320]{3,2,1,0:T(8,128)(2,1)S(1)}, bf16[512,960]{1,0:T(8,128)(2,1)S(1)}, bf16[1280,960]{1,0:T(8,128)(2,1)S(1)}) custom-call(s32[3]{0:T(128)S(1)} %pad_add_fusion.ids_ref, s32[4]{0:T(128)S(1)} %copy-done.3, ...), custom_call_target="tpu_custom_call", output_to_operand_aliasing={{4}: (2, {})} | custom-call | flops 10000000 | bytes 1000 | tf_op jit(solution)/shard_map/attend/pallas_call | solution.py:292
  42.8 1.6 %back.1 = (bf16[4,32,1280]{2,1,0:T(8,128)(2,1)S(1)}, bf16[4,32,1280]{2,1,0:T(8,128)(2,1)S(1)}, bf16[272,1280]{1,0:T(8,128)(2,1)S(1)}, f32[2,1280]{1,0:T(2,128)S(1)}) custom-call(bf16[512,960]{1,0:T(8,128)(2,1)S(1)} %get-tuple-element.40.gqkv_ref, bf16[512,1280]{1,0:T(8,128)(2,1)S(1)} %get-tuple-element.41.unit_ref, ...), custom_call_target="tpu_custom_call" | custom-call | flops 10000000 | bytes 1000 | tf_op jit(solution)/shard_map/back/pallas_call | solution.py:292
  44.5 1.6 %collective-permute-start.15 = (bf16[2,4,32,320]{3,2,1,0:T(8,128)(2,1)S(1)}, bf16[2,4,32,320]{3,2,1,0:T(8,128)(2,1)S(1)}, u32[]{:S(2)}, u32[]{:S(2)}) collective-permute-start(bf16[2,4,32,320]{3,2,1,0:T(8,128)(2,1)S(1)} %get-tuple-element.47), channel_id=1, source_target_pairs={{0,8},{4,12},{8,0},{12,4},{1,9},{5,13},{9,1},{13,5},{2,10},{6,14},... | collective-permute-start | bytes 491528 | tf_op jit(solution)/shard_map/ppermute | solution.py:280
  46.8 1.6 %collective-permute-start.20 = (bf16[4,32,1280]{2,1,0:T(8,128)(2,1)S(1)}, bf16[4,32,1280]{2,1,0:T(8,128)(2,1)S(1)}, u32[]{:S(2)}, u32[]{:S(2)}) collective-permute-start(bf16[4,32,1280]{2,1,0:T(8,128)(2,1)S(1)} %get-tuple-element.56), channel_id=1, source_target_pairs={{0,8},{4,12},{8,0},{12,4},{1,9},{5,13},{9,1},{13,5},{2,10},{6,14},... | collective-permute-start | bytes 983048 | tf_op jit(solution)/shard_map/ppermute | solution.py:280
  48.3 3.4 %collective-permute-start.18 = (f32[2,1280]{1,0:T(2,128)S(1)}, f32[2,1280]{1,0:T(2,128)S(1)}, u32[]{:S(2)}, u32[]{:S(2)}) collective-permute-start(f32[2,1280]{1,0:T(2,128)S(1)} %get-tuple-element.50.refs_0_), channel_id=1, source_target_pairs={{0,3},{1,2},{2,1},{3,0},{4,7},{5,6},{6,5},{7,4},{8,11},{9,10},{10,... | collective-permute-start | bytes 30728 | tf_op jit(solution)/shard_map/ppermute | solution.py:280
  53.8 2.5 %collective-permute-done.17.refs_2_ = f32[2,1280]{1,0:T(2,128)S(1)} collective-permute-done((f32[2,1280]{1,0:T(2,128)S(1)}, f32[2,1280]{1,0:T(2,128)S(1)}, u32[]{:S(2)}, u32[]{:S(2)}) %collective-permute-start.17) | collective-permute-done | bytes 10272 | tf_op jit(solution)/shard_map/ppermute | solution.py:280
  57.9 1.4 %home.1 = (f32[4,32,1280]{2,1,0:T(8,128)S(1)}, bf16[4,32,1280]{2,1,0:T(8,128)(2,1)}) custom-call(s32[3]{0:T(128)S(1)} %pad_add_fusion.ids_ref, bf16[4,32,1280]{2,1,0:T(8,128)(2,1)S(1)} %get-tuple-element.43.stay_ref, bf16[272,1280]{1,0:T(8,128)(2,1)S(1)} %collective-permute-done.14.close_ref, bf16[4,32,320]{2,1,0:T(8,128)(2,1)S(1)} %get-tuple-element.45.own_ref, ...), custom_call_target="tpu_custom_call" | custom-call | flops 10000000 | bytes 1000 | tf_op jit(solution)/shard_map/home/pallas_call | solution.py:292
  60.2 1.6 %finish.1 = (bf16[4,32,1280]{2,1,0:T(8,128)(2,1)}, f32[2,1280]{1,0:T(2,128)}) custom-call(s32[3]{0:T(128)S(1)} %pad_add_fusion.ids_ref, s32[4]{0:T(128)S(1)} %copy-done.3, f32[4,32,1280]{2,1,0:T(8,128)S(1)} %get-tuple-element.53.unit_ref, f32[4,32,128]{2,1,0:T(8,128)S(1)} %get-tuple-element.54.inv_ref, f32[1,1280]{1,0:T(1,128)S(1)} %reshape.12.gain_ref, ...), custom_call_target="tpu_custom_call" | custom-call | flops 10000000 | bytes 1000 | tf_op jit(solution)/shard_map/finish/pallas_call | solution.py:292
  (52 shorter events, 12.4 us)
Async XLA Ops:
  2.6 9.1 %collective-permute-start.6 = (bf16[80,960]{1,0:T(8,128)(2,1)S(1)}, bf16[80,960]{1,0:T(8,128)(2,1)S(1)}, u32[]{:S(2)}, u32[]{:S(2)}) collective-permute-start(bf16[80,960]{1,0:T(8,128)(2,1)S(1)} %get-tuple-element.32.high_ref), channel_id=1, source_target_pairs={{0,1},{1,3},{3,2},{2,0},{4,5},{5,7},{7,6},{6,4},{8,9},{9,11},{11,1... | collective-permute-start | bytes 460808 | tf_op jit(solution)/shard_map/ppermute | solution.py:340
  5.7 26.0 %copy-start.6 = (f32[1280]{0:T(1024)S(1)}, f32[1280]{0:T(1024)}, u32[]{:S(2)}) copy-start(f32[1280]{0:T(1024)} %param.15) | copy-start | bytes 15364
  5.7 26.0 %copy-start.7 = (f32[1280]{0:T(1024)S(1)}, f32[1280]{0:T(1024)}, u32[]{:S(2)}) copy-start(f32[1280]{0:T(1024)} %param.16) | copy-start | bytes 15364
  5.7 8.7 %collective-permute-start = (bf16[80,960]{1,0:T(8,128)(2,1)S(1)}, bf16[80,960]{1,0:T(8,128)(2,1)S(1)}, u32[]{:S(2)}, u32[]{:S(2)}) collective-permute-start(bf16[80,960]{1,0:T(8,128)(2,1)S(1)} %get-tuple-element.31.low_ref), channel_id=1, source_target_pairs={{0,1},{1,3},{3,2},{2,0},{4,5},{5,7},{7,6},{6,4},{8,9},{9,11},{11,1... | collective-permute-start | bytes 460808 | tf_op jit(solution)/shard_map/ppermute | solution.py:340
  12.3 18.4 %collective-permute-start.10 = (bf16[4,32,1920]{2,1,0:T(8,128)(2,1)S(1)}, bf16[4,32,1920]{2,1,0:T(8,128)(2,1)S(1)}, u32[]{:S(2)}, u32[]{:S(2)}) collective-permute-start(bf16[4,32,1920]{2,1,0:T(8,128)(2,1)S(1)} %pack_across.1), channel_id=1, source_target_pairs={{0,8},{4,12},{8,0},{12,4},{1,9},{5,13},{9,1},{13,5},{2,10},{6,14},... | collective-permute-start | bytes 1474568 | tf_op jit(solution)/shard_map/ppermute | solution.py:280
  14.4 8.0 %collective-permute-start.2 = (bf16[80,960]{1,0:T(8,128)(2,1)S(1)}, bf16[80,960]{1,0:T(8,128)(2,1)S(1)}, u32[]{:S(2)}, u32[]{:S(2)}) collective-permute-start(bf16[80,960]{1,0:T(8,128)(2,1)S(1)} %collective-permute-done.refs_0_), channel_id=1, source_target_pairs={{0,1},{1,3},{3,2},{2,0},{4,5},{5,7},{7,6},{6,4},{8,9},{9,11},{11,1... | collective-permute-start | bytes 460808 | tf_op jit(solution)/shard_map/ppermute | solution.py:344
  15.2 7.9 %collective-permute-start.1 = (bf16[80,960]{1,0:T(8,128)(2,1)S(1)}, bf16[80,960]{1,0:T(8,128)(2,1)S(1)}, u32[]{:S(2)}, u32[]{:S(2)}) collective-permute-start(bf16[80,960]{1,0:T(8,128)(2,1)S(1)} %collective-permute-done.refs_0_), channel_id=1, source_target_pairs={{0,16},{16,0},{1,17},{17,1},{2,18},{18,2},{3,19},{19,3},{4,20},{20... | collective-permute-start | bytes 460808 | tf_op jit(solution)/shard_map/ppermute | solution.py:280
  16.7 9.2 %collective-permute-start.8 = (bf16[80,960]{1,0:T(8,128)(2,1)S(1)}, bf16[80,960]{1,0:T(8,128)(2,1)S(1)}, u32[]{:S(2)}, u32[]{:S(2)}) collective-permute-start(bf16[80,960]{1,0:T(8,128)(2,1)S(1)} %collective-permute-done.6.refs_6_), channel_id=1, source_target_pairs={{0,1},{1,3},{3,2},{2,0},{4,5},{5,7},{7,6},{6,4},{8,9},{9,11},{11,1... | collective-permute-start | bytes 460808 | tf_op jit(solution)/shard_map/ppermute | solution.py:344
  20.1 7.9 %collective-permute-start.7 = (bf16[80,960]{1,0:T(8,128)(2,1)S(1)}, bf16[80,960]{1,0:T(8,128)(2,1)S(1)}, u32[]{:S(2)}, u32[]{:S(2)}) collective-permute-start(bf16[80,960]{1,0:T(8,128)(2,1)S(1)} %collective-permute-done.6.refs_6_), channel_id=1, source_target_pairs={{0,16},{16,0},{1,17},{17,1},{2,18},{18,2},{3,19},{19,3},{4,20},{20... | collective-permute-start | bytes 460808 | tf_op jit(solution)/shard_map/ppermute | solution.py:280
  22.4 7.1 %collective-permute-start.4 = (bf16[80,960]{1,0:T(8,128)(2,1)S(1)}, bf16[80,960]{1,0:T(8,128)(2,1)S(1)}, u32[]{:S(2)}, u32[]{:S(2)}) collective-permute-start(bf16[80,960]{1,0:T(8,128)(2,1)S(1)} %collective-permute-done.2.refs_2_), channel_id=1, source_target_pairs={{0,1},{1,3},{3,2},{2,0},{4,5},{5,7},{7,6},{6,4},{8,9},{9,11},{11,1... | collective-permute-start | bytes 460808 | tf_op jit(solution)/shard_map/ppermute | solution.py:346
  23.1 7.6 %collective-permute-start.3 = (bf16[80,960]{1,0:T(8,128)(2,1)S(1)}, bf16[80,960]{1,0:T(8,128)(2,1)S(1)}, u32[]{:S(2)}, u32[]{:S(2)}) collective-permute-start(bf16[80,960]{1,0:T(8,128)(2,1)S(1)} %collective-permute-done.2.refs_2_), channel_id=1, source_target_pairs={{0,16},{16,0},{1,17},{17,1},{2,18},{18,2},{3,19},{19,3},{4,20},{20... | collective-permute-start | bytes 460808 | tf_op jit(solution)/shard_map/ppermute | solution.py:280
  25.9 6.2 %collective-permute-start.12 = (bf16[80,960]{1,0:T(8,128)(2,1)S(1)}, bf16[80,960]{1,0:T(8,128)(2,1)S(1)}, u32[]{:S(2)}, u32[]{:S(2)}) collective-permute-start(bf16[80,960]{1,0:T(8,128)(2,1)S(1)} %collective-permute-done.8.refs_8_), channel_id=1, source_target_pairs={{0,1},{1,3},{3,2},{2,0},{4,5},{5,7},{7,6},{6,4},{8,9},{9,11},{11,1... | collective-permute-start | bytes 460808 | tf_op jit(solution)/shard_map/ppermute | solution.py:346
  28.0 5.5 %collective-permute-start.9 = (bf16[80,960]{1,0:T(8,128)(2,1)S(1)}, bf16[80,960]{1,0:T(8,128)(2,1)S(1)}, u32[]{:S(2)}, u32[]{:S(2)}) collective-permute-start(bf16[80,960]{1,0:T(8,128)(2,1)S(1)} %collective-permute-done.8.refs_8_), channel_id=1, source_target_pairs={{0,16},{16,0},{1,17},{17,1},{2,18},{18,2},{3,19},{19,3},{4,20},{20... | collective-permute-start | bytes 460808 | tf_op jit(solution)/shard_map/ppermute | solution.py:280
  29.5 5.6 %collective-permute-start.5 = (bf16[80,960]{1,0:T(8,128)(2,1)S(1)}, bf16[80,960]{1,0:T(8,128)(2,1)S(1)}, u32[]{:S(2)}, u32[]{:S(2)}) collective-permute-start(bf16[80,960]{1,0:T(8,128)(2,1)S(1)} %collective-permute-done.4.refs_4_), channel_id=1, source_target_pairs={{0,16},{16,0},{1,17},{17,1},{2,18},{18,2},{3,19},{19,3},{4,20},{20... | collective-permute-start | bytes 460808 | tf_op jit(solution)/shard_map/ppermute | solution.py:280
  31.6 4.3 %collective-permute-start.11 = (bf16[4,32,3200]{2,1,0:T(8,128)(2,1)S(1)}, bf16[4,32,3200]{2,1,0:T(8,128)(2,1)S(1)}, u32[]{:S(2)}, u32[]{:S(2)}) collective-permute-start(bf16[4,32,3200]{2,1,0:T(8,128)(2,1)S(1)} %get-tuple-element.37), channel_id=1, source_target_pairs={{0,4},{4,0},{8,12},{12,8},{1,5},{5,1},{9,13},{13,9},{2,6},{6,2},{1... | collective-permute-start | bytes 2457608 | tf_op jit(solution)/shard_map/ppermute | solution.py:280
  32.2 6.4 %collective-permute-start.13 = (bf16[80,960]{1,0:T(8,128)(2,1)S(1)}, bf16[80,960]{1,0:T(8,128)(2,1)S(1)}, u32[]{:S(2)}, u32[]{:S(2)}) collective-permute-start(bf16[80,960]{1,0:T(8,128)(2,1)S(1)} %collective-permute-done.12.refs_0_), channel_id=1, source_target_pairs={{0,16},{16,0},{1,17},{17,1},{2,18},{18,2},{3,19},{19,3},{4,20},{20... | collective-permute-start | bytes 460808 | tf_op jit(solution)/shard_map/ppermute | solution.py:280
  44.5 2.2 %collective-permute-start.14 = (bf16[272,1280]{1,0:T(8,128)(2,1)S(1)}, bf16[272,1280]{1,0:T(8,128)(2,1)S(1)}, u32[]{:S(2)}, u32[]{:S(2)}) collective-permute-start(bf16[272,1280]{1,0:T(8,128)(2,1)S(1)} %get-tuple-element.44), channel_id=1, source_target_pairs={{0,4},{4,0},{8,12},{12,8},{1,5},{5,1},{9,13},{13,9},{2,6},{6,2},{1... | collective-permute-start | bytes 2088968 | tf_op jit(solution)/shard_map/ppermute | solution.py:280
  44.5 11.8 %collective-permute-start.15 = (bf16[2,4,32,320]{3,2,1,0:T(8,128)(2,1)S(1)}, bf16[2,4,32,320]{3,2,1,0:T(8,128)(2,1)S(1)}, u32[]{:S(2)}, u32[]{:S(2)}) collective-permute-start(bf16[2,4,32,320]{3,2,1,0:T(8,128)(2,1)S(1)} %get-tuple-element.47), channel_id=1, source_target_pairs={{0,8},{4,12},{8,0},{12,4},{1,9},{5,13},{9,1},{13,5},{2,10},{6,14},... | collective-permute-start | bytes 491528 | tf_op jit(solution)/shard_map/ppermute | solution.py:280
  46.8 13.4 %collective-permute-start.20 = (bf16[4,32,1280]{2,1,0:T(8,128)(2,1)S(1)}, bf16[4,32,1280]{2,1,0:T(8,128)(2,1)S(1)}, u32[]{:S(2)}, u32[]{:S(2)}) collective-permute-start(bf16[4,32,1280]{2,1,0:T(8,128)(2,1)S(1)} %get-tuple-element.56), channel_id=1, source_target_pairs={{0,8},{4,12},{8,0},{12,4},{1,9},{5,13},{9,1},{13,5},{2,10},{6,14},... | collective-permute-start | bytes 983048 | tf_op jit(solution)/shard_map/ppermute | solution.py:280
  48.3 5.5 %collective-permute-start.18 = (f32[2,1280]{1,0:T(2,128)S(1)}, f32[2,1280]{1,0:T(2,128)S(1)}, u32[]{:S(2)}, u32[]{:S(2)}) collective-permute-start(f32[2,1280]{1,0:T(2,128)S(1)} %get-tuple-element.50.refs_0_), channel_id=1, source_target_pairs={{0,3},{1,2},{2,1},{3,0},{4,7},{5,6},{6,5},{7,4},{8,11},{9,10},{10,... | collective-permute-start | bytes 30728 | tf_op jit(solution)/shard_map/ppermute | solution.py:280
  51.8 4.6 %collective-permute-start.17 = (f32[2,1280]{1,0:T(2,128)S(1)}, f32[2,1280]{1,0:T(2,128)S(1)}, u32[]{:S(2)}, u32[]{:S(2)}) collective-permute-start(f32[2,1280]{1,0:T(2,128)S(1)} %get-tuple-element.50.refs_0_), channel_id=1, source_target_pairs={{0,2},{1,3},{2,0},{3,1},{4,6},{5,7},{6,4},{7,5},{8,10},{9,11},{10,... | collective-permute-start | bytes 30728 | tf_op jit(solution)/shard_map/ppermute | solution.py:280
  52.5 3.8 %collective-permute-start.16 = (f32[2,1280]{1,0:T(2,128)S(1)}, f32[2,1280]{1,0:T(2,128)S(1)}, u32[]{:S(2)}, u32[]{:S(2)}) collective-permute-start(f32[2,1280]{1,0:T(2,128)S(1)} %get-tuple-element.50.refs_0_), channel_id=1, source_target_pairs={{0,1},{1,0},{2,3},{3,2},{4,5},{5,4},{6,7},{7,6},{8,9},{9,8},{10,11... | collective-permute-start | bytes 30728 | tf_op jit(solution)/shard_map/ppermute | solution.py:280
  56.4 1.5 %collective-permute-start.19 = (bf16[2,4,32,320]{3,2,1,0:T(8,128)(2,1)S(1)}, bf16[2,4,32,320]{3,2,1,0:T(8,128)(2,1)S(1)}, u32[]{:S(2)}, u32[]{:S(2)}) collective-permute-start(bf16[2,4,32,320]{3,2,1,0:T(8,128)(2,1)S(1)} %both.1), channel_id=1, source_target_pairs={{0,4},{4,0},{8,12},{12,8},{1,5},{5,1},{9,13},{13,9},{2,6},{6,2},{1... | collective-permute-start | bytes 491528 | tf_op jit(solution)/shard_map/ppermute | solution.py:280
  56.5 3.7 %collective-permute-start.21 = (f32[2,1280]{1,0:T(2,128)S(1)}, f32[2,1280]{1,0:T(2,128)S(1)}, u32[]{:S(2)}, u32[]{:S(2)}) collective-permute-start(f32[2,1280]{1,0:T(2,128)S(1)} %add.5.refs_0_), channel_id=1, source_target_pairs={{0,8},{4,12},{8,0},{12,4},{1,9},{5,13},{9,1},{13,5},{2,10},{6,14},... | collective-permute-start | bytes 30728 | tf_op jit(solution)/shard_map/ppermute | solution.py:280
  (6 other events, 35.8 us)
